TPU v7x, 32 devices: a whole 2x2x4 slice. The times are simulated.
32 devices in a mesh: fsdp: 8 (over z, y), tensor: 4 (over x, core).
Axes of the slice: x: 2, y: 2, z: 4, core: 2. Of those that a mesh axis runs over, the one named last changes fastest.
Arguments:
- context: bfloat16 [2048, 4096], P('fsdp', 'tensor'), may hold values from -6 to 6
- cotangent: bfloat16 [2048, 8192], P('fsdp', 'tensor'), may hold values from -0.125 to 0.125
- block_table: int32 [4, 128], P('tensor'), may hold values from 0 to 127, each once within a row
- left_stat: float32 [4, 128, 256, 256], P('tensor', 'fsdp'), may hold values from -1 to 5, as said below
- right_stat: float32 [4, 128, 256, 256], P('tensor', 'fsdp'), may hold values from -1 to 5, as said below
- root_left: float32 [4, 128, 256, 256], P('tensor', 'fsdp'), may hold values from -1 to 5, as said below
- root_right: float32 [4, 128, 256, 256], P('tensor', 'fsdp'), may hold values from -1 to 5, as said below
- second_moment: float32 [4, 128, 256, 256], P('tensor', 'fsdp'), may hold values from 0.3 to 3
Outputs:
- left_new: float32 [4, 128, 256, 256], P('tensor', 'fsdp')
- right_new: float32 [4, 128, 256, 256], P('tensor', 'fsdp')
- second_new: float32 [4, 128, 256, 256], P('tensor', 'fsdp')
- search_direction: bfloat16 [4, 1024, 8192], P('tensor', 'fsdp')
Inputs may be any that keep to these rules, and one draw needn't show every extreme that they name: Each row of block_table names every block 0 to 127 once. `left_stat`: symmetric, with positive diagonal. `right_stat`: symmetric, with positive diagonal. `root_left`: symmetric, with positive diagonal. `root_right`: symmetric, with positive diagonal.
All inputs are finite; a program needn't handle non-finite values.
Results may differ from a plain program's by a relative error of at most 0.017.
Values may be sent and summed in bfloat16 or wider, within the bound.
No kernel may reach another device: no remote copies, remote signals or barrier semaphores. Data moves between devices by JAX's collectives and lax.ppermute only.
A program may use at most 128 MiB of HBM per device.

v0:
```python
import jax
import jax.numpy as jnp
from jax import lax
from jax.sharding import PartitionSpec as P

decay_rate = 0.95


def per_device(
    context, cotangent, block_table, left_stat, right_stat, root_left, root_right, second_moment
):
    full_cot = lax.all_gather(cotangent, "tensor", axis=1, tiled=True)
    tokens_here, band_rows = context.shape
    model_width = full_cot.shape[1]
    block_size = left_stat.shape[-1]
    slot_count = left_stat.shape[1]
    groups = lax.axis_size("fsdp")
    position = lax.axis_index("fsdp")
    owner_table = block_table[0]
    col_bands = model_width // block_size
    strip_rows = band_rows // groups
    per_band = block_size // strip_rows
    my_blocks = lax.dynamic_slice_in_dim(owner_table, position * slot_count, slot_count)
    ctx_bands = context.reshape(tokens_here, band_rows // block_size, block_size)
    cot_bands = full_cot.reshape(tokens_here, col_bands, block_size)
    left_part = jnp.take(ctx_bands, owner_table // col_bands, axis=1)
    right_part = jnp.take(cot_bands, owner_table % col_bands, axis=1)
    blocks = jnp.einsum("tnb,tnc->nbc", left_part, right_part, preferred_element_type=jnp.float32)
    gradient = lax.psum_scatter(
        blocks.reshape(slot_count * block_size * lax.axis_size("fsdp"), block_size).astype(
            jnp.bfloat16
        ),
        "fsdp",
        scatter_dimension=0,
        tiled=True,
    ).astype(jnp.float32)
    gradient = gradient.reshape(slot_count, block_size, block_size)
    highest = lax.Precision.HIGHEST
    gram_left = jnp.einsum("sij,skj->sik", gradient, gradient, precision=highest)
    gram_right = jnp.einsum("sji,sjk->sik", gradient, gradient, precision=highest)
    left_new = decay_rate * left_stat[0] + (1.0 - decay_rate) * gram_left / block_size
    right_new = decay_rate * right_stat[0] + (1.0 - decay_rate) * gram_right / block_size
    second_new = decay_rate * second_moment[0] + (1.0 - decay_rate) * gradient * gradient
    adam_step = gradient / (jnp.sqrt(second_new) + 1e-08)
    shaped = jnp.einsum("sij,sjk->sik", root_left[0], gradient, precision=highest)
    shaped = jnp.einsum("sij,sjk->sik", shaped, root_right[0], precision=highest)
    graft_ratio = jnp.sqrt(jnp.sum(adam_step * adam_step, axis=(1, 2))) / jnp.sqrt(
        jnp.sum(shaped * shaped, axis=(1, 2)) + 1e-06
    )
    direction = (shaped * graft_ratio[:, None, None]).astype(jnp.bfloat16)
    by_strip = direction.reshape(slot_count, per_band, strip_rows, block_size)
    targets = jnp.arange(groups, dtype=jnp.int32)
    chosen = jnp.take(by_strip, targets % per_band, axis=1)
    keep_mask = ((my_blocks // col_bands)[:, None] == (targets // per_band)[None, :]).astype(
        jnp.bfloat16
    )
    outgoing_rows = jnp.swapaxes(chosen * keep_mask[:, :, None, None], 0, 1)
    returned = lax.all_to_all(outgoing_rows, "fsdp", split_axis=0, concat_axis=0, tiled=True)
    wanted = position // per_band * col_bands + jnp.arange(col_bands, dtype=jnp.int32)
    slot_ids = jnp.arange(owner_table.shape[0], dtype=jnp.int32)
    located = jnp.sum(
        jnp.where(owner_table[None, :] == wanted[:, None], slot_ids[None, :], 0), axis=1
    )
    flat_pieces = returned.reshape(groups * slot_count, strip_rows, block_size)
    pieces = jnp.take(flat_pieces, located, axis=0)
    result = jnp.swapaxes(pieces, 0, 1).reshape(strip_rows, model_width)
    return (left_new[None], right_new[None], second_new[None], result[None])


def solution(mesh):
    return jax.shard_map(
        per_device,
        mesh=mesh,
        in_specs=(
            P("fsdp", "tensor"),
            P("fsdp", "tensor"),
            P("tensor", None),
            P("tensor", "fsdp", None, None),
            P("tensor", "fsdp", None, None),
            P("tensor", "fsdp", None, None),
            P("tensor", "fsdp", None, None),
            P("tensor", "fsdp", None, None),
        ),
        out_specs=(
            P("tensor", "fsdp", None, None),
            P("tensor", "fsdp", None, None),
            P("tensor", "fsdp", None, None),
            P("tensor", "fsdp", None),
        ),
        check_vma=False,
    )
```

profile of v0, /device:TPU:8, one launch (start us, length us, event | category | flops | bytes accessed | tf_op | source)
XLA Modules:
  0.0 607.5 jit_solution(4367768409369643779)
XLA Ops:
  7.2 0.0 copy-start.3
  7.2 0.0 all-gather.2.cloned.1.call-start
  7.2 2.3 copy.30
  9.5 0.0 all-gather.2.cloned.1.call-update
  9.5 0.0 reduce-scatter.2.cloned.1.call-start
  9.6 1.2 copy.28
  10.8 0.2 copy.29
  11.0 0.0 copy-done.3
  11.1 8.2 %gather_fusion = bf16[128,256,256]{2,1,0:T(8,128)(2,1)} fusion(bf16[256,4,256]{2,0,1:T(8,128)(2,1)S(1)} %copy.29, s32[1024]{0:T(1024)S(1)} %get-tuple-element.21), kind=kCustom, calls=%fused_computation | custom fusion | bytes 33554944 | tf_op jit(solution)/shard_map/jit(_take)/gather | solution.py:26
  19.3 26.6 %all-gather.2.cloned.1.call-done = bf16[256,8192]{0,1:T(8,128)(2,1)} async-done(((bf16[256,2048]{0,1:T(8,128)(2,1)}), bf16[256,8192]{0,1:T(8,128)(2,1)}) %all-gather.2.cloned.1.call-update) | async-done | bytes 4194320 | tf_op jit(solution)/shard_map/all_gather | solution.py:12
  45.8 6.4 %copy.31 = bf16[256,32,256]{2,0,1:T(8,128)(2,1)} copy(bf16[256,32,256]{0,2,1:T(8,128)(2,1)} %bitcast.100) | data formatting | bytes 8388608 | tf_op jit(solution)/shard_map/reshape | solution.py:25
  52.2 10.6 %gather_fusion.1 = bf16[128,256,256]{2,1,0:T(8,128)(2,1)} fusion(bf16[256,32,256]{2,0,1:T(8,128)(2,1)} %copy.31, s32[1024]{0:T(1024)S(1)} %get-tuple-element.20), kind=kCustom, calls=%fused_computation.1 | custom fusion | bytes 33554944 | tf_op jit(solution)/shard_map/jit(_take)/gather | solution.py:27
  62.8 19.8 %fusion.7 = bf16[128,256,256]{2,1,0:T(8,128)(2,1)} fusion(bf16[128,256,256]{2,1,0:T(8,128)(2,1)} %gather_fusion.1, pred[128]{0:T(512)(128)(4,1)S(1)} %get-tuple-element.15, bf16[128,256,256]{2,1,0:T(8,128)(2,1)} %gather_fusion, pred[128]{0:T(512)(128)(4,1)S(1)} %get-tuple-element.14), kind=kOutput, calls=%fused_computation.11 | convolution fusion | flops 4320133120 | bytes 50331904 | tf_op jit(solution)/shard_map/tnb,tnc->nbc/dot_general | solution.py:28
  82.5 0.0 reduce-scatter.2.cloned.1.call-update
  82.6 0.1 and_select_fusion.1
  82.7 0.1 compare_convert_fusion
  82.8 281.3 %reduce-scatter.2.cloned.1.call-done = bf16[4096,256]{1,0:T(8,128)(2,1)} async-done(((bf16[32768,256]{1,0:T(8,128)(2,1)}), bf16[4096,256]{1,0:T(8,128)(2,1)}) %reduce-scatter.2.cloned.1.call-update) | async-done | bytes 2097168 | tf_op jit(solution)/shard_map/reduce_scatter | solution.py:29
  364.0 0.0 copy-start
  364.0 6.2 %broadcast_multiply_fusion = (f32[1,16,256,256]{3,2,1,0:T(8,128)S(1)}, f32[1,16,256,256]{3,2,1,0:T(8,128)}) fusion(f32[1,16,256,256]{3,2,1,0:T(8,128)} %param.15, bf16[1,16,256,256]{3,2,1,0:T(8,128)(2,1)} %bitcast.93), kind=kLoop, calls=%fused_computation.34 | loop fusion | flops 5242880 | bytes 14680064 | tf_op jit(solution)/shard_map/mul | solution.py:43
  370.2 0.0 copy-done
  370.2 2.5 fusion.25
  372.8 0.0 copy-start.2
  372.8 4.7 fusion.21
  377.5 0.0 copy-done.2
  377.5 5.9 multiply_reduce_fusion
  383.5 0.1 reduce_sum.39
  383.6 4.0 multiply_convert_fusion
  387.6 6.0 gather_fusion.2
  393.6 7.5 %select_multiply_fusion = bf16[8,16,128,256]{3,2,1,0:T(8,128)(2,1)} fusion(bf16[8,16,128,256]{3,2,1,0:T(8,128)(2,1)} %gather_fusion.2, pred[8]{0:T(512)(128)(4,1)S(1)} %compare_and_fusion, bf16[8,16]{1,0:T(8,128)(2,1)S(1)} %compare_convert_fusion), kind=kLoop, calls=%fused_computation.13 | loop fusion | flops 8388608 | bytes 16777480 | tf_op jit(solution)/shard_map/mul | solution.py:57
  401.1 6.8 %all-to-all-start = ((bf16[8,16,128,256]{3,2,1,0:T(8,128)(2,1)}), bf16[8,16,128,256]{3,2,1,0:T(8,128)(2,1)}, u32[]{:S(2)}, u32[]{:S(2)}) async-start(bf16[8,16,128,256]{3,2,1,0:T(8,128)(2,1)} %select_multiply_fusion), calls=%async_computation.1 | async-start | bytes 16777216 | tf_op jit(solution)/shard_map/all_to_all | solution.py:58
  407.9 0.2 select_reduce_fusion
  408.2 0.0 copy-start.1
  408.2 5.4 fusion.23
  413.5 0.0 copy-done.1
  413.5 3.0 fusion.24
  416.5 172.4 %all-to-all-done = bf16[8,16,128,256]{3,2,1,0:T(8,128)(2,1)} async-done(((bf16[8,16,128,256]{3,2,1,0:T(8,128)(2,1)}), bf16[8,16,128,256]{3,2,1,0:T(8,128)(2,1)}, u32[]{:S(2)}, u32[]{:S(2)}) %all-to-all-start) | async-done | bytes 8388640 | tf_op jit(solution)/shard_map/all_to_all | solution.py:58
  588.9 4.1 gather_fusion.3
  593.0 1.6 select_bitcast_fusion
  594.6 3.2 copy.36
  597.8 2.9 copy.37
  (13 shorter events, 0.1 us)
Async XLA Ops:
  7.2 3.9 copy-start.3
  7.2 38.6 %all-gather.2.cloned.1.call-start = ((), (), s32[]{:S(2)}) async-start(), calls=%async_computation.2 | async-start | bytes 5242880 | tf_op jit(solution)/shard_map/all_gather | solution.py:12
  9.5 354.5 %reduce-scatter.2.cloned.1.call-start = ((), (), s32[]{:S(2)}) async-start(), calls=%async_computation.3 | async-start | bytes 18874368 | tf_op jit(solution)/shard_map/reduce_scatter | solution.py:29
  364.0 6.2 %copy-start = (bf16[4096,256]{1,0:T(8,128)(2,1)S(1)}, bf16[4096,256]{1,0:T(8,128)(2,1)}, u32[]{:S(2)}) copy-start(bf16[4096,256]{1,0:T(8,128)(2,1)} %reduce-scatter.2.cloned.1.call-done) | copy-start | bytes 6291460
  372.8 4.8 copy-start.2
  401.1 187.8 %all-to-all-start = ((bf16[8,16,128,256]{3,2,1,0:T(8,128)(2,1)}), bf16[8,16,128,256]{3,2,1,0:T(8,128)(2,1)}, u32[]{:S(2)}, u32[]{:S(2)}) async-start(bf16[8,16,128,256]{3,2,1,0:T(8,128)(2,1)} %select_multiply_fusion), calls=%async_computation.1 | async-start | bytes 16777216 | tf_op jit(solution)/shard_map/all_to_all | solution.py:58
  408.2 5.4 copy-start.1
Sparse Core Ops, SparseCore 0:
  10.1 35.6 all-gather.1
  82.7 281.3 reduce-scatter.1
where the time goes:
time: 612 us; the launch traced here: 608 us
  waiting for transfers between devices  480 us (78%)
  local copies, waits for them, and re-layouts  45.1 us (7%)
  matrix products  38.8 us (6%)
  other arithmetic  22.3 us (4%)
  between operations  14.2 us (2%)
  starting transfers between devices  6.93 us (1%)
    reduce_scatter x1, waiting for transfers between devices, per_device(): lax.psum_scatter(blocks.reshape(slot_count * block_size * lax.axis_size('...  281 us
    all_to_all x1, waiting for transfers between devices, per_device(): lax.all_to_all(outgoing_rows, 'fsdp', split_axis=0, concat_axis=0, tiled=...  172 us
    all_gather x1, waiting for transfers between devices, per_device(): full_cot = lax.all_gather(cotangent, 'tensor', axis=1, tiled=True)  26.6 us
    dot_general x1, matrix products, per_device(): jnp.einsum('tnb,tnc->nbc', left_part, right_part, preferred_element_type=...  19.8 us
  transfers between devices with their start and end apart: 3, of which 3 were waited for; matrix products, arithmetic and copies ran while one was open for 3% of the time, Pallas kernels for 0%

commit v1 on v0

--- a/solution.py
+++ b/solution.py
@@ -1,12 +1,17 @@
+import functools
+
 import jax
 import jax.numpy as jnp
 from jax import lax
+from jax.experimental import pallas as pl
+from jax.experimental.pallas import tpu as pltpu
 from jax.sharding import PartitionSpec as P
 
 decay_rate = 0.95
-
-
-def per_device(
+MIB = 1024 * 1024
+
+
+def general_plan(
     context, cotangent, block_table, left_stat, right_stat, root_left, root_right, second_moment
 ):
     full_cot = lax.all_gather(cotangent, "tensor", axis=1, tiled=True)
@@ -67,6 +72,353 @@
     return (left_new[None], right_new[None], second_new[None], result[None])
 
 
+def swap(value, axis, offset):
+    count = lax.axis_size(axis)
+    return lax.ppermute(value, axis, [(i, i ^ offset) for i in range(count)])
+
+
+def strip_kernel(groups, strip, meta, cot_ref, *refs):
+    outs, turned = refs[:groups], refs[groups]
+    position = meta[0]
+    turned[...] = cot_ref[...].T
+    for k in range(groups):
+        start = pl.multiple_of((position ^ k) * strip, strip)
+        outs[k][0] = turned[pl.ds(start, strip), :]
+
+
+def cot_strips(meta, cotangent, groups, block):
+    tokens, width = cotangent.shape
+    bands, strip = width // block, block // groups
+    return pl.pallas_call(
+        functools.partial(strip_kernel, groups, strip),
+        grid_spec=pltpu.PrefetchScalarGridSpec(
+            num_scalar_prefetch=1,
+            grid=(bands,),
+            in_specs=[pl.BlockSpec((tokens, block), lambda c, meta: (0, c))],
+            out_specs=[pl.BlockSpec((1, strip, tokens), lambda c, meta: (c, 0, 0))] * groups,
+            scratch_shapes=[pltpu.VMEM((block, tokens), jnp.bfloat16)],
+        ),
+        out_shape=[jax.ShapeDtypeStruct((bands, strip, tokens), jnp.bfloat16)] * groups,
+        compiler_params=pltpu.CompilerParams(vmem_limit_bytes=16 * MIB),
+        cost_estimate=pl.CostEstimate(
+            flops=0, bytes_accessed=4 * tokens * width, transcendentals=0
+        ),
+        name="cot_strips",
+    )(meta, cotangent)
+
+
+def gradient_kernel(groups, ranks, slots, bands, strip, block, meta, *refs):
+    cots, ctxs = refs[:ranks], refs[ranks : ranks + groups]
+    outs = refs[ranks + groups : ranks + 2 * groups]
+    lhs, rhs, strips, sems = refs[ranks + 2 * groups :]
+    tokens = ctxs[0].shape[0]
+    rows = lhs.shape[1]
+    position, rank = meta[0], meta[1]
+    copies = []
+    for k in range(groups):
+        copies.append(
+            pltpu.make_async_copy(
+                ctxs[k], rhs.at[pl.ds(k * tokens, tokens), :], sems.at[ranks * groups + k]
+            )
+        )
+    for t in range(ranks):
+        for k in range(groups):
+            copies.append(
+                pltpu.make_async_copy(
+                    cots[t].at[k],
+                    lhs.at[t, :, pl.ds(k * tokens, tokens)],
+                    sems.at[t * groups + k],
+                )
+            )
+    for copy in copies:
+        copy.start()
+    for copy in copies:
+        copy.wait()
+    for t in range(ranks):
+        strips[pl.ds(t * rows, rows), :] = jnp.dot(
+            lhs[t], rhs[...], preferred_element_type=jnp.float32
+        ).astype(jnp.bfloat16)
+    own_bands = bands // ranks
+
+    def place(s, carry):
+        for k in range(groups):
+            block_id = meta[2 + (position ^ k) * slots + s]
+            row_band, col_band = lax.div(block_id, bands), lax.rem(block_id, bands)
+            piece = lax.div(col_band, own_bands) ^ rank
+            start = piece * rows + lax.rem(col_band, own_bands) * strip
+            outs[k][s] = strips[
+                pl.ds(pl.multiple_of(start, strip), strip),
+                pl.ds(pl.multiple_of(row_band * block, block), block),
+            ]
+        return carry
+
+    lax.fori_loop(0, slots, place, 0)
+
+
+def gradient_strips(meta, cots, ctxs, slots, bands, block):
+    groups, ranks = len(ctxs), len(cots)
+    tokens, band_rows = ctxs[0].shape
+    rows, strip = cots[0].shape[1], block // groups
+    flops = 2 * ranks * rows * groups * tokens * band_rows
+    return pl.pallas_call(
+        functools.partial(gradient_kernel, groups, ranks, slots, bands, strip, block),
+        grid_spec=pltpu.PrefetchScalarGridSpec(
+            num_scalar_prefetch=1,
+            grid=(),
+            in_specs=[pl.BlockSpec(memory_space=pl.ANY)] * (ranks + groups),
+            out_specs=[pl.BlockSpec(memory_space=pltpu.VMEM)] * groups,
+            scratch_shapes=[
+                pltpu.VMEM((ranks, rows, groups * tokens), jnp.bfloat16),
+                pltpu.VMEM((groups * tokens, band_rows), jnp.bfloat16),
+                pltpu.VMEM((ranks * rows, band_rows), jnp.bfloat16),
+                pltpu.SemaphoreType.DMA(((ranks + 1) * groups,)),
+            ],
+        ),
+        out_shape=[jax.ShapeDtypeStruct((slots, strip, block), jnp.bfloat16)] * groups,
+        compiler_params=pltpu.CompilerParams(vmem_limit_bytes=48 * MIB),
+        cost_estimate=pl.CostEstimate(
+            flops=flops,
+            bytes_accessed=2 * groups * (ranks * rows * tokens + tokens * band_rows + slots * strip * block),
+            transcendentals=0,
+        ),
+        name="gradient_strips",
+    )(meta, *cots, *ctxs)
+
+
+def gather_block(groups, strip, position, grads, turned):
+    for k in range(groups):
+        start = pl.multiple_of((position ^ k) * strip, strip)
+        turned[pl.ds(start, strip), :] = grads[k][0]
+
+
+def direction_kernel(groups, strip, sub, meta, second_ref, left_ref, right_ref, *refs):
+    grads, outs, turned, rows = refs[:groups], refs[groups : 2 * groups], refs[-2], refs[-1]
+    position = meta[0]
+    gather_block(groups, strip, position, grads, turned)
+    grad_bf16 = turned[...].T
+    grad = grad_bf16.astype(jnp.float32)
+    second = decay_rate * second_ref[0, 0] + (1.0 - decay_rate) * grad * grad
+    adam = grad / (jnp.sqrt(second) + 1e-08)
+    half = jnp.dot(
+        left_ref[0, 0].astype(jnp.bfloat16), grad_bf16, preferred_element_type=jnp.float32
+    )
+    shaped = jnp.dot(
+        half.astype(jnp.bfloat16),
+        right_ref[0, 0].astype(jnp.bfloat16),
+        preferred_element_type=jnp.float32,
+    )
+    adam_sum = jnp.sum(adam * adam, keepdims=True)
+    shaped_sum = jnp.sum(shaped * shaped, keepdims=True)
+    ratio = jnp.sqrt(adam_sum) / jnp.sqrt(shaped_sum + 1e-06)
+    rows[...] = (shaped * ratio).astype(jnp.bfloat16)
+    halves = outs[0].shape[1]
+    for k in range(groups):
+        for h in range(halves):
+            start = pl.multiple_of(h * groups * sub + (position ^ k) * sub, sub)
+            outs[k][0, h] = rows[pl.ds(start, sub), :]
+
+
+def directions(meta, grads, second, root_left, root_right, halves, sub):
+    groups = len(grads)
+    slots, strip, block = grads[0].shape
+    stat = pl.BlockSpec((1, 1, block, block), lambda s, meta: (0, s, 0, 0))
+    return pl.pallas_call(
+        functools.partial(direction_kernel, groups, strip, sub),
+        grid_spec=pltpu.PrefetchScalarGridSpec(
+            num_scalar_prefetch=1,
+            grid=(slots,),
+            in_specs=[stat] * 3
+            + [pl.BlockSpec((1, strip, block), lambda s, meta: (s, 0, 0))] * groups,
+            out_specs=[pl.BlockSpec((1, halves, sub, block), lambda s, meta: (s, 0, 0, 0))]
+            * groups,
+            scratch_shapes=[
+                pltpu.VMEM((block, block), jnp.bfloat16),
+                pltpu.VMEM((block, block), jnp.bfloat16),
+            ],
+        ),
+        out_shape=[jax.ShapeDtypeStruct((slots, halves, sub, block), jnp.bfloat16)] * groups,
+        compiler_params=pltpu.CompilerParams(vmem_limit_bytes=32 * MIB),
+        cost_estimate=pl.CostEstimate(
+            flops=4 * slots * block**3,
+            bytes_accessed=16 * slots * block * block,
+            transcendentals=0,
+        ),
+        name="directions",
+    )(meta, second, root_left, root_right, *grads)
+
+
+def statistics_kernel(groups, strip, meta, left_ref, right_ref, second_ref, *refs):
+    grads = refs[:groups]
+    left_out, right_out, second_out, turned = refs[groups:]
+    gather_block(groups, strip, meta[0], grads, turned)
+    block = turned.shape[0]
+    grad_t = turned[...]
+    grad_bf16 = grad_t.T
+    grad = grad_bf16.astype(jnp.float32)
+    gram_left = jnp.dot(grad_bf16, grad_t, preferred_element_type=jnp.float32)
+    gram_right = jnp.dot(grad_t, grad_bf16, preferred_element_type=jnp.float32)
+    left_out[0, 0] = decay_rate * left_ref[0, 0] + (1.0 - decay_rate) * gram_left / block
+    right_out[0, 0] = decay_rate * right_ref[0, 0] + (1.0 - decay_rate) * gram_right / block
+    second_out[0, 0] = decay_rate * second_ref[0, 0] + (1.0 - decay_rate) * grad * grad
+
+
+def statistics(meta, grads, left_stat, right_stat, second):
+    groups = len(grads)
+    slots, strip, block = grads[0].shape
+    stat = pl.BlockSpec((1, 1, block, block), lambda s, meta: (0, s, 0, 0))
+    return pl.pallas_call(
+        functools.partial(statistics_kernel, groups, strip),
+        grid_spec=pltpu.PrefetchScalarGridSpec(
+            num_scalar_prefetch=1,
+            grid=(slots,),
+            in_specs=[stat] * 3
+            + [pl.BlockSpec((1, strip, block), lambda s, meta: (s, 0, 0))] * groups,
+            out_specs=[stat] * 3,
+            scratch_shapes=[pltpu.VMEM((block, block), jnp.bfloat16)],
+        ),
+        out_shape=[jax.ShapeDtypeStruct(left_stat.shape, jnp.float32)] * 3,
+        compiler_params=pltpu.CompilerParams(vmem_limit_bytes=32 * MIB),
+        cost_estimate=pl.CostEstimate(
+            flops=4 * slots * block**3,
+            bytes_accessed=26 * slots * block * block,
+            transcendentals=0,
+        ),
+        name="statistics",
+    )(meta, left_stat, right_stat, second, *grads)
+
+
+def regroup_kernel(groups, slots, bands, halves, meta, *refs):
+    pieces, outs, placed = refs[:groups], refs[groups : 2 * groups], refs[-1]
+    block = pieces[0].shape[-1]
+    position = meta[0]
+
+    def place(s, carry):
+        for k in range(groups):
+            block_id = meta[2 + (position ^ k) * slots + s]
+            row_band, col_band = lax.div(block_id, bands), lax.rem(block_id, bands)
+            columns = pl.ds(pl.multiple_of(col_band * block, block), block)
+            for h in range(halves):
+                placed[(row_band * halves + h) ^ position, :, columns] = pieces[k][s, h]
+        return carry
+
+    lax.fori_loop(0, slots, place, 0)
+    for k in range(groups):
+        outs[k][...] = placed[k]
+
+
+def regroup(meta, pieces, bands):
+    groups = len(pieces)
+    slots, halves, sub, block = pieces[0].shape
+    return pl.pallas_call(
+        functools.partial(regroup_kernel, groups, slots, bands, halves),
+        grid_spec=pltpu.PrefetchScalarGridSpec(
+            num_scalar_prefetch=1,
+            grid=(),
+            in_specs=[pl.BlockSpec(memory_space=pltpu.VMEM)] * groups,
+            out_specs=[pl.BlockSpec(memory_space=pltpu.VMEM)] * groups,
+            scratch_shapes=[pltpu.VMEM((groups, sub, bands * block), jnp.bfloat16)],
+        ),
+        out_shape=[jax.ShapeDtypeStruct((sub, bands * block), jnp.bfloat16)] * groups,
+        compiler_params=pltpu.CompilerParams(vmem_limit_bytes=32 * MIB),
+        cost_estimate=pl.CostEstimate(
+            flops=0,
+            bytes_accessed=4 * groups * sub * bands * block,
+            transcendentals=0,
+        ),
+        name="regroup",
+    )(meta, *pieces)
+
+
+def stack_kernel(groups, meta, *refs):
+    pieces, out, sems = refs[:groups], refs[groups], refs[groups + 1]
+    sub = pieces[0].shape[0]
+    copies = []
+    for k in range(groups):
+        start = pl.multiple_of((meta[0] ^ k) * sub, sub)
+        copies.append(
+            pltpu.make_async_copy(pieces[k], out.at[0, pl.ds(start, sub), :], sems.at[k])
+        )
+    for copy in copies:
+        copy.start()
+    for copy in copies:
+        copy.wait()
+
+
+def stack_rows(meta, pieces):
+    groups = len(pieces)
+    sub, width = pieces[0].shape
+    return pl.pallas_call(
+        functools.partial(stack_kernel, groups),
+        grid_spec=pltpu.PrefetchScalarGridSpec(
+            num_scalar_prefetch=1,
+            grid=(),
+            in_specs=[pl.BlockSpec(memory_space=pl.ANY)] * groups,
+            out_specs=pl.BlockSpec(memory_space=pl.ANY),
+            scratch_shapes=[pltpu.SemaphoreType.DMA((groups,))],
+        ),
+        out_shape=jax.ShapeDtypeStruct((1, groups * sub, width), jnp.bfloat16),
+        cost_estimate=pl.CostEstimate(
+            flops=0, bytes_accessed=4 * groups * sub * width, transcendentals=0
+        ),
+        name="stack_rows",
+    )(meta, *pieces)
+
+
+def exchange(pieces):
+    return [pieces[0]] + [swap(pieces[k], "fsdp", k) for k in range(1, len(pieces))]
+
+
+def strip_plan(
+    context, cotangent, block_table, left_stat, right_stat, root_left, root_right, second_moment
+):
+    groups, ranks = lax.axis_size("fsdp"), lax.axis_size("tensor")
+    band_rows = context.shape[1]
+    block, slots = left_stat.shape[-1], left_stat.shape[1]
+    bands = cotangent.shape[1] * ranks // block
+    strip_rows = band_rows // groups
+    place = jnp.stack([lax.axis_index("fsdp"), lax.axis_index("tensor")]).astype(jnp.int32)
+    meta = jnp.concatenate([place, block_table[0]])
+
+    strips = exchange(cot_strips(meta, cotangent, groups, block))
+    ctxs = [context] + [None] * (groups - 1)
+    for k in range(groups):
+        if k % 2:
+            ctxs[k] = swap(ctxs[k - 1], "fsdp", 1)
+        elif k:
+            ctxs[k] = swap(context, "fsdp", k)
+    tokens = context.shape[0]
+    cots = [jnp.stack(strips).reshape(groups, -1, tokens)]
+    offset = ranks // 2
+    by_offset = {0: cots[0]}
+    while offset:
+        for known in list(by_offset):
+            by_offset[known ^ offset] = swap(by_offset[known], "tensor", offset)
+        offset //= 2
+    cots = [by_offset[t] for t in range(ranks)]
+
+    grads = exchange(gradient_strips(meta, cots, ctxs, slots, bands, block))
+    halves, sub = block // strip_rows, strip_rows // groups
+    pieces = exchange(
+        directions(meta, grads, second_moment, root_left, root_right, halves, sub)
+    )
+    left_new, right_new, second_new = statistics(
+        meta, grads, left_stat, right_stat, second_moment
+    )
+    rows = exchange(regroup(meta, pieces, bands))
+    return (left_new, right_new, second_new, stack_rows(meta, rows))
+
+
+def per_device(context, cotangent, block_table, left_stat, *rest):
+    groups, ranks = lax.axis_size("fsdp"), lax.axis_size("tensor")
+    block = left_stat.shape[-1]
+    strip_rows = context.shape[1] // groups
+    powers = groups & (groups - 1) == 0 and ranks & (ranks - 1) == 0
+    even = block % (16 * groups) == 0 and strip_rows % (16 * groups) == 0
+    whole = block % strip_rows == 0 and cotangent.shape[1] % block == 0
+    plan = strip_plan if powers and even and whole else general_plan
+    return plan(context, cotangent, block_table, left_stat, *rest)
+
+
 def solution(mesh):
     return jax.shard_map(
         per_device,

time: 612 us -> 350 us (0.57)
  waiting for transfers between devices: 480 us -> 183 us
  Pallas kernels: 0 us -> 99.6 us
  starting transfers between devices: 6.93 us -> 55.5 us
  matrix products: 38.8 us -> 0 us
  local copies, waits for them, and re-layouts: 45.1 us -> 6.39 us
  other arithmetic: 22.3 us -> 0.73 us
  between operations: 14.2 us -> 0.83 us
    reduce_scatter x1 -> x0, waiting for transfers between devices: 281 us -> none  [per_device(): lax.psum_scatter(blocks.reshape(slot_count * block_size * lax.axis_size('...]
    ppermute x0 -> x38, waiting for transfers between devices: none -> 183 us  [swap(): return lax.ppermute(value, axis, [(i, i ^ offset) for i in range(count)])]
    all_to_all x1 -> x0, waiting for transfers between devices: 172 us -> none  [per_device(): lax.all_to_all(outgoing_rows, 'fsdp', split_axis=0, concat_axis=0, tiled=...]
    pallas_call x0 -> x6, Pallas kernels: none -> 99.6 us  [the longest x1 65.4 us: stack_rows(): pl.pallas_call(functools.partial(stack_kernel, groups), grid_spec=pltpu.P...]
    ppermute x0 -> x38, starting transfers between devices: none -> 55.5 us  [swap(): return lax.ppermute(value, axis, [(i, i ^ offset) for i in range(count)])]
    dot_general x5 -> x0, matrix products: 38.8 us -> none  [the longest x1 19.8 us: per_device(): jnp.einsum('tnb,tnc->nbc', left_part, right_part, preferred_element_type=...]
    gather x4 -> x0, local copies, waits for them, and re-layouts: 28.8 us -> none  [the longest x1 10.6 us: per_device(): right_part = jnp.take(cot_bands, owner_table % col_bands, axis=1)]
    all_gather x1 -> x0, waiting for transfers between devices: 26.6 us -> none  [per_device(): full_cot = lax.all_gather(cotangent, 'tensor', axis=1, tiled=True)]
  transfers between devices with their start and end apart: 3 -> 38, of which waited for: 3 -> 30; matrix products, arithmetic and copies ran while one was open for 3% -> 0% of each run, Pallas kernels for 0% -> 3%
where the time goes in v1:
time: 350 us; the launch traced here: 346 us
  waiting for transfers between devices  183 us (52%)
  Pallas kernels  99.6 us (28%)
  starting transfers between devices  55.5 us (16%)
  local copies, waits for them, and re-layouts  6.39 us (2%)
    ppermute x38, waiting for transfers between devices, swap(): return lax.ppermute(value, axis, [(i, i ^ offset) for i in range(count)])  183 us
    pallas_call x1, Pallas kernels, stack_rows(): pl.pallas_call(functools.partial(stack_kernel, groups), grid_spec=pltpu.P...  65.4 us
    ppermute x38, starting transfers between devices, swap(): return lax.ppermute(value, axis, [(i, i ^ offset) for i in range(count)])  55.5 us
    pallas_call x1, Pallas kernels, directions(): pl.pallas_call(functools.partial(direction_kernel, groups, strip, sub), g...  11.4 us
    pallas_call x1, Pallas kernels, statistics(): pl.pallas_call(functools.partial(statistics_kernel, groups, strip), grid_...  9.96 us
    pallas_call x1, Pallas kernels, gradient_strips(): pl.pallas_call(functools.partial(gradient_kernel, groups, ranks, slots, b...  9.19 us
  transfers between devices with their start and end apart: 38, of which 30 were waited for; matrix products, arithmetic and copies ran while one was open for 0% of the time, Pallas kernels for 3%

profile of v1, /device:TPU:8, one launch (start us, length us, event | category | flops | bytes accessed | tf_op | source)
XLA Modules:
  0.0 345.9 jit_solution(17797919203841003140)
XLA Ops:
  2.6 1.6 cot_strips.1
  4.2 1.6 collective-permute-start
  7.8 2.6 collective-permute-start.3
  11.7 1.6 collective-permute-start.5
  14.5 1.6 collective-permute-done.2
  16.1 9.3 %collective-permute-done.3 = bf16[8,32,256]{2,1,0:T(8,128)(2,1)S(1)} collective-permute-done((bf16[8,32,256]{2,1,0:T(8,128)(2,1)S(1)}, bf16[8,32,256]{2,1,0:T(8,128)(2,1)S(1)}, u32[]{:S(2)}, u32[]{:S(2)}) %collective-permute-start.3) | collective-permute-done | bytes 131104 | tf_op jit(solution)/shard_map/ppermute | solution.py:77
  25.4 2.8 collective-permute-done.4
  28.2 2.6 collective-permute-done.5
  30.8 2.5 collective-permute-done.6
  34.9 3.6 %collective-permute-start.11 = (bf16[256,1024]{1,0:T(8,128)(2,1)}, bf16[256,1024]{1,0:T(8,128)(2,1)S(1)}, u32[]{:S(2)}, u32[]{:S(2)}) collective-permute-start(bf16[256,1024]{1,0:T(8,128)(2,1)} %refs_4_.1), channel_id=1, source_target_pairs={{0,8},{4,12},{8,0},{12,4},{16,24},{20,28},{24,16},{28,20},{1,9},{5... | collective-permute-start | bytes 1572872 | tf_op jit(solution)/shard_map/ppermute | solution.py:77
  39.0 21.4 %collective-permute-done.13.refs_8_ = bf16[256,1024]{1,0:T(8,128)(2,1)S(1)} collective-permute-done((bf16[256,1024]{1,0:T(8,128)(2,1)}, bf16[256,1024]{1,0:T(8,128)(2,1)S(1)}, u32[]{:S(2)}, u32[]{:S(2)}) %collective-permute-start.13) | collective-permute-done | bytes 524320 | tf_op jit(solution)/shard_map/ppermute | solution.py:77
  60.9 1.9 collective-permute-done.11.refs_6_
  64.8 16.7 %collective-permute-done.15.refs_10_ = bf16[256,1024]{1,0:T(8,128)(2,1)S(1)} collective-permute-done((bf16[256,1024]{1,0:T(8,128)(2,1)}, bf16[256,1024]{1,0:T(8,128)(2,1)S(1)}, u32[]{:S(2)}, u32[]{:S(2)}) %collective-permute-start.15) | collective-permute-done | bytes 524320 | tf_op jit(solution)/shard_map/ppermute | solution.py:77
  81.5 7.2 %collective-permute-done.12.refs_7_ = bf16[256,1024]{1,0:T(8,128)(2,1)S(1)} collective-permute-done((bf16[256,1024]{1,0:T(8,128)(2,1)S(1)}, bf16[256,1024]{1,0:T(8,128)(2,1)S(1)}, u32[]{:S(2)}, u32[]{:S(2)}) %collective-permute-start.12) | collective-permute-done | bytes 524320 | tf_op jit(solution)/shard_map/ppermute | solution.py:77
  88.7 8.6 %collective-permute-done.16.refs_11_ = bf16[256,1024]{1,0:T(8,128)(2,1)S(1)} collective-permute-done((bf16[256,1024]{1,0:T(8,128)(2,1)S(1)}, bf16[256,1024]{1,0:T(8,128)(2,1)S(1)}, u32[]{:S(2)}, u32[]{:S(2)}) %collective-permute-start.16) | collective-permute-done | bytes 524320 | tf_op jit(solution)/shard_map/ppermute | solution.py:77
  99.4 9.2 %gradient_strips.1 = (bf16[16,32,256]{2,1,0:T(8,128)(2,1)S(1)}, bf16[16,32,256]{2,1,0:T(8,128)(2,1)S(1)}, bf16[16,32,256]{2,1,0:T(8,128)(2,1)S(1)}, bf16[16,32,2...) custom-call(s32[130]{0:T(256)S(1)} %pad_add_fusion.meta, ...), custom_call_target="tpu_custom_call" | custom-call | flops 4294967296 | bytes 10485760 | tf_op jit(solution)/shard_map/gradient_strips/pallas_call | solution.py:163
  108.6 1.8 collective-permute-start.17
  110.4 10.9 %collective-permute-start.18 = (bf16[16,32,256]{2,1,0:T(8,128)(2,1)S(1)}, bf16[16,32,256]{2,1,0:T(8,128)(2,1)S(1)}, u32[]{:S(2)}, u32[]{:S(2)}) collective-permute-start(bf16[16,32,256]{2,1,0:T(8,128)(2,1)S(1)} %get-tuple-element.49), channel_id=1, source_target_pairs={{0,8},{4,12},{8,0},{12,4},{16,24},{20,28},{24,16},{28,20},{1,9},{5... | collective-permute-start | bytes 786440 | tf_op jit(solution)/shard_map/ppermute | solution.py:77
  123.8 1.6 collective-permute-start.21
  126.4 9.8 %collective-permute-done.18.refs_2_ = bf16[16,32,256]{2,1,0:T(8,128)(2,1)S(1)} collective-permute-done((bf16[16,32,256]{2,1,0:T(8,128)(2,1)S(1)}, bf16[16,32,256]{2,1,0:T(8,128)(2,1)S(1)}, u32[]{:S(2)}, u32[]{:S(2)}) %collective-permute-start.18) | collective-permute-done | bytes 262176 | tf_op jit(solution)/shard_map/ppermute | solution.py:77
  136.3 1.7 collective-permute-start.23
  138.0 1.9 collective-permute-done.19.refs_3_
  140.6 18.0 %collective-permute-done.21.refs_5_ = bf16[16,32,256]{2,1,0:T(8,128)(2,1)S(1)} collective-permute-done((bf16[16,32,256]{2,1,0:T(8,128)(2,1)S(1)}, bf16[16,32,256]{2,1,0:T(8,128)(2,1)S(1)}, u32[]{:S(2)}, u32[]{:S(2)}) %collective-permute-start.21) | collective-permute-done | bytes 262176 | tf_op jit(solution)/shard_map/ppermute | solution.py:77
  158.7 8.2 %collective-permute-done.22.refs_6_ = bf16[16,32,256]{2,1,0:T(8,128)(2,1)S(1)} collective-permute-done((bf16[16,32,256]{2,1,0:T(8,128)(2,1)S(1)}, bf16[16,32,256]{2,1,0:T(8,128)(2,1)S(1)}, u32[]{:S(2)}, u32[]{:S(2)}) %collective-permute-start.22) | collective-permute-done | bytes 262176 | tf_op jit(solution)/shard_map/ppermute | solution.py:77
  166.9 2.8 collective-permute-done.23.refs_7_
  169.7 2.2 copy-done.2
  171.9 11.4 %directions.1 = (bf16[16,2,16,256]{3,2,1,0:T(8,128)(2,1)S(1)}, bf16[16,2,16,256]{3,2,1,0:T(8,128)(2,1)S(1)}, bf16[16,2,16,256]{3,2,1,0:T(8,128)(2,1)S(1)}, bf16[...) custom-call(s32[130]{0:T(256)S(1)} %pad_add_fusion.meta, ...), custom_call_target="tpu_custom_call" | custom-call | flops 1073741824 | bytes 16777216 | tf_op jit(solution)/shard_map/directions/pallas_call | solution.py:225
  183.4 1.7 collective-permute-start.24
  185.1 1.8 collective-permute-start.26
  187.6 3.4 collective-permute-start.28
  190.9 1.7 collective-permute-done.24.refs_1_
  193.8 5.7 %collective-permute-done.25.refs_2_ = bf16[16,2,16,256]{3,2,1,0:T(8,128)(2,1)S(1)} collective-permute-done((bf16[16,2,16,256]{3,2,1,0:T(8,128)(2,1)S(1)}, bf16[16,2,16,256]{3,2,1,0:T(8,128)(2,1)S(1)}, u32[]{:S(2)}, u32[]{:S(2)}) %collective-permute-start.25) | collective-permute-done | bytes 262176 | tf_op jit(solution)/shard_map/ppermute | solution.py:77
  200.8 1.8 collective-permute-done.26.refs_3_
  202.6 2.7 collective-permute-done.27.refs_4_
  205.3 17.2 %collective-permute-done.28.refs_5_ = bf16[16,2,16,256]{3,2,1,0:T(8,128)(2,1)S(1)} collective-permute-done((bf16[16,2,16,256]{3,2,1,0:T(8,128)(2,1)S(1)}, bf16[16,2,16,256]{3,2,1,0:T(8,128)(2,1)S(1)}, u32[]{:S(2)}, u32[]{:S(2)}) %collective-permute-start.28) | collective-permute-done | bytes 262176 | tf_op jit(solution)/shard_map/ppermute | solution.py:77
  222.4 5.9 %collective-permute-done.29.refs_6_ = bf16[16,2,16,256]{3,2,1,0:T(8,128)(2,1)S(1)} collective-permute-done((bf16[16,2,16,256]{3,2,1,0:T(8,128)(2,1)S(1)}, bf16[16,2,16,256]{3,2,1,0:T(8,128)(2,1)S(1)}, u32[]{:S(2)}, u32[]{:S(2)}) %collective-permute-start.29) | collective-permute-done | bytes 262176 | tf_op jit(solution)/shard_map/ppermute | solution.py:77
  228.3 3.7 %collective-permute-done.30.refs_7_ = bf16[16,2,16,256]{3,2,1,0:T(8,128)(2,1)S(1)} collective-permute-done((bf16[16,2,16,256]{3,2,1,0:T(8,128)(2,1)S(1)}, bf16[16,2,16,256]{3,2,1,0:T(8,128)(2,1)S(1)}, u32[]{:S(2)}, u32[]{:S(2)}) %collective-permute-start.30) | collective-permute-done | bytes 262176 | tf_op jit(solution)/shard_map/ppermute | solution.py:77
  232.0 2.0 regroup.1
  234.6 2.9 collective-permute-start.33
  237.6 2.9 collective-permute-start.35
  242.6 3.6 %collective-permute-done.32.refs_2_ = bf16[16,8192]{1,0:T(8,128)(2,1)S(1)} collective-permute-done((bf16[16,8192]{1,0:T(8,128)(2,1)S(1)}, bf16[16,8192]{1,0:T(8,128)(2,1)S(1)}, u32[]{:S(2)}, u32[]{:S(2)}) %collective-permute-start.32) | collective-permute-done | bytes 262176 | tf_op jit(solution)/shard_map/ppermute | solution.py:77
  246.2 1.6 collective-permute-start.37
  247.8 10.0 %statistics.1 = (f32[1,16,256,256]{3,2,1,0:T(8,128)}, f32[1,16,256,256]{3,2,1,0:T(8,128)}, f32[1,16,256,256]{3,2,1,0:T(8,128)}) custom-call(s32[130]{0:T(256)S(1)} %pad_add_fusion.meta, f32[1,16,256,256]{3,2,1,0:T(8,128)S(1)} %copy-done.3, f32[1,16,256,256]{3,2,1,0:T(8,128)S(1)} %copy-done.4, f32[1,16,256,256]{3,2,1,0:T(8,128)S(1)} %copy-done, ...), custom_call_target="tpu_custom_call" | custom-call | flops 1073741824 | bytes 27262976 | tf_op jit(solution)/shard_map/statistics/pallas_call | solution.py:269
  257.8 8.2 %collective-permute-done.34.refs_4_ = bf16[16,8192]{1,0:T(8,128)(2,1)S(1)} collective-permute-done((bf16[16,8192]{1,0:T(8,128)(2,1)S(1)}, bf16[16,8192]{1,0:T(8,128)(2,1)S(1)}, u32[]{:S(2)}, u32[]{:S(2)}) %collective-permute-start.34) | collective-permute-done | bytes 262176 | tf_op jit(solution)/shard_map/ppermute | solution.py:77
  266.1 5.8 %collective-permute-done.35.refs_5_ = bf16[16,8192]{1,0:T(8,128)(2,1)S(1)} collective-permute-done((bf16[16,8192]{1,0:T(8,128)(2,1)S(1)}, bf16[16,8192]{1,0:T(8,128)(2,1)S(1)}, u32[]{:S(2)}, u32[]{:S(2)}) %collective-permute-start.35) | collective-permute-done | bytes 262176 | tf_op jit(solution)/shard_map/ppermute | solution.py:77
  271.8 5.2 %collective-permute-done.36.refs_6_ = bf16[16,8192]{1,0:T(8,128)(2,1)S(1)} collective-permute-done((bf16[16,8192]{1,0:T(8,128)(2,1)S(1)}, bf16[16,8192]{1,0:T(8,128)(2,1)S(1)}, u32[]{:S(2)}, u32[]{:S(2)}) %collective-permute-start.36) | collective-permute-done | bytes 262176 | tf_op jit(solution)/shard_map/ppermute | solution.py:77
  277.0 2.8 collective-permute-done.37.refs_7_
  280.5 65.4 %stack_rows.1 = bf16[1,128,8192]{2,1,0:T(8,128)(2,1)} custom-call(s32[130]{0:T(256)} %copy-done.7, bf16[16,8192]{1,0:T(8,128)(2,1)} %copy-done.6, bf16[16,8192]{1,0:T(8,128)(2,1)} %copy-done.9, bf16[16,8192]{1,0:T(8,128)(2,1)} %copy-done.10, bf16[16,8192]{1,0:T(8,128)(2,1)} %copy-done.11, bf16[16,8192]{1,0:T(8,128)(2,1)} %copy-done.12, ...), custom_call_target="tpu_custom_call" | custom-call | bytes 4194304 | tf_op jit(solution)/shard_map/stack_rows/pallas_call | solution.py:350
  (83 shorter events, 24.2 us)
Async XLA Ops:
  2.6 245.2 %copy-start.7 = (s32[130]{0:T(256)}, s32[130]{0:T(256)S(1)}, u32[]{:S(2)}) copy-start(s32[130]{0:T(256)S(1)} %pad_add_fusion.meta) | copy-start | bytes 1564
  4.2 7.5 %collective-permute-start = (bf16[8,32,256]{2,1,0:T(8,128)(2,1)S(1)}, bf16[8,32,256]{2,1,0:T(8,128)(2,1)S(1)}, u32[]{:S(2)}, u32[]{:S(2)}) collective-permute-start(bf16[8,32,256]{2,1,0:T(8,128)(2,1)S(1)} %get-tuple-element.40), channel_id=1, source_target_pairs={{0,4},{4,0},{8,12},{12,8},{16,20},{20,16},{24,28},{28,24},{1,5},{5... | collective-permute-start | bytes 393224 | tf_op jit(solution)/shard_map/ppermute | solution.py:77
  5.8 8.6 %collective-permute-start.1 = (bf16[8,32,256]{2,1,0:T(8,128)(2,1)S(1)}, bf16[8,32,256]{2,1,0:T(8,128)(2,1)S(1)}, u32[]{:S(2)}, u32[]{:S(2)}) collective-permute-start(bf16[8,32,256]{2,1,0:T(8,128)(2,1)S(1)} %get-tuple-element.41), channel_id=1, source_target_pairs={{0,8},{4,12},{8,0},{12,4},{16,24},{20,28},{24,16},{28,20},{1,9},{5... | collective-permute-start | bytes 393224 | tf_op jit(solution)/shard_map/ppermute | solution.py:77
  6.2 9.8 %collective-permute-start.2 = (bf16[8,32,256]{2,1,0:T(8,128)(2,1)S(1)}, bf16[8,32,256]{2,1,0:T(8,128)(2,1)S(1)}, u32[]{:S(2)}, u32[]{:S(2)}) collective-permute-start(bf16[8,32,256]{2,1,0:T(8,128)(2,1)S(1)} %get-tuple-element.42), channel_id=1, source_target_pairs={{0,12},{4,8},{8,4},{12,0},{16,28},{20,24},{24,20},{28,16},{1,13},{... | collective-permute-start | bytes 393224 | tf_op jit(solution)/shard_map/ppermute | solution.py:77
  7.8 17.6 %collective-permute-start.3 = (bf16[8,32,256]{2,1,0:T(8,128)(2,1)S(1)}, bf16[8,32,256]{2,1,0:T(8,128)(2,1)S(1)}, u32[]{:S(2)}, u32[]{:S(2)}) collective-permute-start(bf16[8,32,256]{2,1,0:T(8,128)(2,1)S(1)} %get-tuple-element.43), channel_id=1, source_target_pairs={{0,16},{4,20},{8,24},{12,28},{16,0},{20,4},{24,8},{28,12},{1,17},{... | collective-permute-start | bytes 393224 | tf_op jit(solution)/shard_map/ppermute | solution.py:77
  10.3 17.8 %collective-permute-start.4 = (bf16[8,32,256]{2,1,0:T(8,128)(2,1)S(1)}, bf16[8,32,256]{2,1,0:T(8,128)(2,1)S(1)}, u32[]{:S(2)}, u32[]{:S(2)}) collective-permute-start(bf16[8,32,256]{2,1,0:T(8,128)(2,1)S(1)} %get-tuple-element.44), channel_id=1, source_target_pairs={{0,20},{4,16},{8,28},{12,24},{16,4},{20,0},{24,12},{28,8},{1,21},{... | collective-permute-start | bytes 393224 | tf_op jit(solution)/shard_map/ppermute | solution.py:77
  11.7 19.1 %collective-permute-start.5 = (bf16[8,32,256]{2,1,0:T(8,128)(2,1)S(1)}, bf16[8,32,256]{2,1,0:T(8,128)(2,1)S(1)}, u32[]{:S(2)}, u32[]{:S(2)}) collective-permute-start(bf16[8,32,256]{2,1,0:T(8,128)(2,1)S(1)} %get-tuple-element.45), channel_id=1, source_target_pairs={{0,24},{4,28},{8,16},{12,20},{16,8},{20,12},{24,0},{28,4},{1,25},{... | collective-permute-start | bytes 393224 | tf_op jit(solution)/shard_map/ppermute | solution.py:77
  14.5 18.8 %collective-permute-start.6 = (bf16[8,32,256]{2,1,0:T(8,128)(2,1)S(1)}, bf16[8,32,256]{2,1,0:T(8,128)(2,1)S(1)}, u32[]{:S(2)}, u32[]{:S(2)}) collective-permute-start(bf16[8,32,256]{2,1,0:T(8,128)(2,1)S(1)} %get-tuple-element.46), channel_id=1, source_target_pairs={{0,28},{4,24},{8,20},{12,16},{16,12},{20,8},{24,4},{28,0},{1,29},{... | collective-permute-start | bytes 393224 | tf_op jit(solution)/shard_map/ppermute | solution.py:77
  33.3 65.0 %copy-start.16 = (bf16[8,256,256]{2,1,0:T(8,128)(2,1)}, bf16[8,256,256]{2,1,0:T(8,128)(2,1)S(1)}, u32[]{:S(2)}) copy-start(bf16[8,256,256]{2,1,0:T(8,128)(2,1)S(1)} %bitcast_dynamic-update-slice_fusion.refs_0_) | copy-start | bytes 3145732
  33.3 136.4 %copy-start = (f32[1,16,256,256]{3,2,1,0:T(8,128)S(1)}, f32[1,16,256,256]{3,2,1,0:T(8,128)}, u32[]{:S(2)}) copy-start(f32[1,16,256,256]{3,2,1,0:T(8,128)} %second_ref.3) | copy-start | bytes 12582916
  33.3 136.4 %copy-start.1 = (f32[1,16,256,256]{3,2,1,0:T(8,128)S(1)}, f32[1,16,256,256]{3,2,1,0:T(8,128)}, u32[]{:S(2)}) copy-start(f32[1,16,256,256]{3,2,1,0:T(8,128)} %left_ref.3) | copy-start | bytes 12582916
  33.3 27.0 %collective-permute-start.8 = (bf16[8,256,256]{2,1,0:T(8,128)(2,1)S(1)}, bf16[8,256,256]{2,1,0:T(8,128)(2,1)S(1)}, u32[]{:S(2)}, u32[]{:S(2)}) collective-permute-start(bf16[8,256,256]{2,1,0:T(8,128)(2,1)S(1)} %bitcast_dynamic-update-slice_fusion.refs_0_), channel_id=1, source_target_pairs={{0,2},{1,3},{2,0},{3,1},{4,6},{5,7},{6,4},{7,5},{8,10},{9,11},{10,... | collective-permute-start | bytes 3145736 | tf_op jit(solution)/shard_map/ppermute | solution.py:77
  34.9 25.5 %collective-permute-start.13 = (bf16[256,1024]{1,0:T(8,128)(2,1)}, bf16[256,1024]{1,0:T(8,128)(2,1)S(1)}, u32[]{:S(2)}, u32[]{:S(2)}) collective-permute-start(bf16[256,1024]{1,0:T(8,128)(2,1)} %refs_4_.1), channel_id=1, source_target_pairs={{0,16},{4,20},{8,24},{12,28},{16,0},{20,4},{24,8},{28,12},{1,17},{... | collective-permute-start | bytes 1572872 | tf_op jit(solution)/shard_map/ppermute | solution.py:77
  34.9 27.9 %collective-permute-start.11 = (bf16[256,1024]{1,0:T(8,128)(2,1)}, bf16[256,1024]{1,0:T(8,128)(2,1)S(1)}, u32[]{:S(2)}, u32[]{:S(2)}) collective-permute-start(bf16[256,1024]{1,0:T(8,128)(2,1)} %refs_4_.1), channel_id=1, source_target_pairs={{0,8},{4,12},{8,0},{12,4},{16,24},{20,28},{24,16},{28,20},{1,9},{5... | collective-permute-start | bytes 1572872 | tf_op jit(solution)/shard_map/ppermute | solution.py:77
  38.5 24.8 %collective-permute-start.10 = (bf16[256,1024]{1,0:T(8,128)(2,1)}, bf16[256,1024]{1,0:T(8,128)(2,1)S(1)}, u32[]{:S(2)}, u32[]{:S(2)}) collective-permute-start(bf16[256,1024]{1,0:T(8,128)(2,1)} %refs_4_.1), channel_id=1, source_target_pairs={{0,4},{4,0},{8,12},{12,8},{16,20},{20,16},{24,28},{28,24},{1,5},{5... | collective-permute-start | bytes 1572872 | tf_op jit(solution)/shard_map/ppermute | solution.py:77
  39.0 42.5 %collective-permute-start.15 = (bf16[256,1024]{1,0:T(8,128)(2,1)}, bf16[256,1024]{1,0:T(8,128)(2,1)S(1)}, u32[]{:S(2)}, u32[]{:S(2)}) collective-permute-start(bf16[256,1024]{1,0:T(8,128)(2,1)} %refs_4_.1), channel_id=1, source_target_pairs={{0,24},{4,28},{8,16},{12,20},{16,8},{20,12},{24,0},{28,4},{1,25},{... | collective-permute-start | bytes 1572872 | tf_op jit(solution)/shard_map/ppermute | solution.py:77
  60.4 36.9 %collective-permute-start.7 = (bf16[8,256,256]{2,1,0:T(8,128)(2,1)S(1)}, bf16[8,256,256]{2,1,0:T(8,128)(2,1)S(1)}, u32[]{:S(2)}, u32[]{:S(2)}) collective-permute-start(bf16[8,256,256]{2,1,0:T(8,128)(2,1)S(1)} %bitcast_dynamic-update-slice_fusion.refs_0_), channel_id=1, source_target_pairs={{0,1},{1,0},{2,3},{3,2},{4,5},{5,4},{6,7},{7,6},{8,9},{9,8},{10,11... | collective-permute-start | bytes 3145736 | tf_op jit(solution)/shard_map/ppermute | solution.py:77
  60.4 36.9 %copy-start.17 = (bf16[8,256,256]{2,1,0:T(8,128)(2,1)}, bf16[8,256,256]{2,1,0:T(8,128)(2,1)S(1)}, u32[]{:S(2)}) copy-start(bf16[8,256,256]{2,1,0:T(8,128)(2,1)S(1)} %collective-permute-done.8.refs_2_) | copy-start | bytes 3145732
  60.4 37.9 %collective-permute-start.9 = (bf16[8,256,256]{2,1,0:T(8,128)(2,1)S(1)}, bf16[8,256,256]{2,1,0:T(8,128)(2,1)}, u32[]{:S(2)}, u32[]{:S(2)}) collective-permute-start(bf16[8,256,256]{2,1,0:T(8,128)(2,1)S(1)} %collective-permute-done.8.refs_2_), channel_id=1, source_target_pairs={{0,1},{1,0},{2,3},{3,2},{4,5},{5,4},{6,7},{7,6},{8,9},{9,8},{10,11... | collective-permute-start | bytes 3145736 | tf_op jit(solution)/shard_map/ppermute | solution.py:77
  62.8 18.8 %collective-permute-start.14 = (bf16[256,1024]{1,0:T(8,128)(2,1)S(1)}, bf16[256,1024]{1,0:T(8,128)(2,1)S(1)}, u32[]{:S(2)}, u32[]{:S(2)}) collective-permute-start(bf16[256,1024]{1,0:T(8,128)(2,1)S(1)} %collective-permute-done.13.refs_8_), channel_id=1, source_target_pairs={{0,4},{4,0},{8,12},{12,8},{16,20},{20,16},{24,28},{28,24},{1,5},{5... | collective-permute-start | bytes 1572872 | tf_op jit(solution)/shard_map/ppermute | solution.py:77
  63.3 25.4 %collective-permute-start.12 = (bf16[256,1024]{1,0:T(8,128)(2,1)S(1)}, bf16[256,1024]{1,0:T(8,128)(2,1)S(1)}, u32[]{:S(2)}, u32[]{:S(2)}) collective-permute-start(bf16[256,1024]{1,0:T(8,128)(2,1)S(1)} %collective-permute-done.11.refs_6_), channel_id=1, source_target_pairs={{0,4},{4,0},{8,12},{12,8},{16,20},{20,16},{24,28},{28,24},{1,5},{5... | collective-permute-start | bytes 1572872 | tf_op jit(solution)/shard_map/ppermute | solution.py:77
  81.5 15.7 %collective-permute-start.16 = (bf16[256,1024]{1,0:T(8,128)(2,1)S(1)}, bf16[256,1024]{1,0:T(8,128)(2,1)S(1)}, u32[]{:S(2)}, u32[]{:S(2)}) collective-permute-start(bf16[256,1024]{1,0:T(8,128)(2,1)S(1)} %collective-permute-done.15.refs_10_), channel_id=1, source_target_pairs={{0,4},{4,0},{8,12},{12,8},{16,20},{20,16},{24,28},{28,24},{1,5},{5... | collective-permute-start | bytes 1572872 | tf_op jit(solution)/shard_map/ppermute | solution.py:77
  108.6 16.8 %collective-permute-start.17 = (bf16[16,32,256]{2,1,0:T(8,128)(2,1)S(1)}, bf16[16,32,256]{2,1,0:T(8,128)(2,1)S(1)}, u32[]{:S(2)}, u32[]{:S(2)}) collective-permute-start(bf16[16,32,256]{2,1,0:T(8,128)(2,1)S(1)} %get-tuple-element.48), channel_id=1, source_target_pairs={{0,4},{4,0},{8,12},{12,8},{16,20},{20,16},{24,28},{28,24},{1,5},{5... | collective-permute-start | bytes 786440 | tf_op jit(solution)/shard_map/ppermute | solution.py:77
  110.4 25.9 %collective-permute-start.18 = (bf16[16,32,256]{2,1,0:T(8,128)(2,1)S(1)}, bf16[16,32,256]{2,1,0:T(8,128)(2,1)S(1)}, u32[]{:S(2)}, u32[]{:S(2)}) collective-permute-start(bf16[16,32,256]{2,1,0:T(8,128)(2,1)S(1)} %get-tuple-element.49), channel_id=1, source_target_pairs={{0,8},{4,12},{8,0},{12,4},{16,24},{20,28},{24,16},{28,20},{1,9},{5... | collective-permute-start | bytes 786440 | tf_op jit(solution)/shard_map/ppermute | solution.py:77
  121.3 18.6 %collective-permute-start.19 = (bf16[16,32,256]{2,1,0:T(8,128)(2,1)S(1)}, bf16[16,32,256]{2,1,0:T(8,128)(2,1)S(1)}, u32[]{:S(2)}, u32[]{:S(2)}) collective-permute-start(bf16[16,32,256]{2,1,0:T(8,128)(2,1)S(1)} %get-tuple-element.50), channel_id=1, source_target_pairs={{0,12},{4,8},{8,4},{12,0},{16,28},{20,24},{24,20},{28,16},{1,13},{... | collective-permute-start | bytes 786440 | tf_op jit(solution)/shard_map/ppermute | solution.py:77
  122.5 18.1 %collective-permute-start.20 = (bf16[16,32,256]{2,1,0:T(8,128)(2,1)S(1)}, bf16[16,32,256]{2,1,0:T(8,128)(2,1)S(1)}, u32[]{:S(2)}, u32[]{:S(2)}) collective-permute-start(bf16[16,32,256]{2,1,0:T(8,128)(2,1)S(1)} %get-tuple-element.51), channel_id=1, source_target_pairs={{0,16},{4,20},{8,24},{12,28},{16,0},{20,4},{24,8},{28,12},{1,17},{... | collective-permute-start | bytes 786440 | tf_op jit(solution)/shard_map/ppermute | solution.py:77
  123.8 34.8 %collective-permute-start.21 = (bf16[16,32,256]{2,1,0:T(8,128)(2,1)S(1)}, bf16[16,32,256]{2,1,0:T(8,128)(2,1)S(1)}, u32[]{:S(2)}, u32[]{:S(2)}) collective-permute-start(bf16[16,32,256]{2,1,0:T(8,128)(2,1)S(1)} %get-tuple-element.52), channel_id=1, source_target_pairs={{0,20},{4,16},{8,28},{12,24},{16,4},{20,0},{24,12},{28,8},{1,21},{... | collective-permute-start | bytes 786440 | tf_op jit(solution)/shard_map/ppermute | solution.py:77
  125.4 41.5 %collective-permute-start.22 = (bf16[16,32,256]{2,1,0:T(8,128)(2,1)S(1)}, bf16[16,32,256]{2,1,0:T(8,128)(2,1)S(1)}, u32[]{:S(2)}, u32[]{:S(2)}) collective-permute-start(bf16[16,32,256]{2,1,0:T(8,128)(2,1)S(1)} %get-tuple-element.53), channel_id=1, source_target_pairs={{0,24},{4,28},{8,16},{12,20},{16,8},{20,12},{24,0},{28,4},{1,25},{... | collective-permute-start | bytes 786440 | tf_op jit(solution)/shard_map/ppermute | solution.py:77
  136.3 33.4 %collective-permute-start.23 = (bf16[16,32,256]{2,1,0:T(8,128)(2,1)S(1)}, bf16[16,32,256]{2,1,0:T(8,128)(2,1)S(1)}, u32[]{:S(2)}, u32[]{:S(2)}) collective-permute-start(bf16[16,32,256]{2,1,0:T(8,128)(2,1)S(1)} %get-tuple-element.54), channel_id=1, source_target_pairs={{0,28},{4,24},{8,20},{12,16},{16,12},{20,8},{24,4},{28,0},{1,29},{... | collective-permute-start | bytes 786440 | tf_op jit(solution)/shard_map/ppermute | solution.py:77
  171.9 75.9 %copy-start.3 = (f32[1,16,256,256]{3,2,1,0:T(8,128)S(1)}, f32[1,16,256,256]{3,2,1,0:T(8,128)}, u32[]{:S(2)}) copy-start(f32[1,16,256,256]{3,2,1,0:T(8,128)} %left_ref.2) | copy-start | bytes 12582916
  171.9 75.9 %copy-start.4 = (f32[1,16,256,256]{3,2,1,0:T(8,128)S(1)}, f32[1,16,256,256]{3,2,1,0:T(8,128)}, u32[]{:S(2)}) copy-start(f32[1,16,256,256]{3,2,1,0:T(8,128)} %right_ref.2) | copy-start | bytes 12582916
  183.4 9.2 %collective-permute-start.24 = (bf16[16,2,16,256]{3,2,1,0:T(8,128)(2,1)S(1)}, bf16[16,2,16,256]{3,2,1,0:T(8,128)(2,1)S(1)}, u32[]{:S(2)}, u32[]{:S(2)}) collective-permute-start(bf16[16,2,16,256]{3,2,1,0:T(8,128)(2,1)S(1)} %get-tuple-element.59), channel_id=1, source_target_pairs={{0,4},{4,0},{8,12},{12,8},{16,20},{20,16},{24,28},{28,24},{1,5},{5... | collective-permute-start | bytes 786440 | tf_op jit(solution)/shard_map/ppermute | solution.py:77
  185.1 14.4 %collective-permute-start.25 = (bf16[16,2,16,256]{3,2,1,0:T(8,128)(2,1)S(1)}, bf16[16,2,16,256]{3,2,1,0:T(8,128)(2,1)S(1)}, u32[]{:S(2)}, u32[]{:S(2)}) collective-permute-start(bf16[16,2,16,256]{3,2,1,0:T(8,128)(2,1)S(1)} %get-tuple-element.60), channel_id=1, source_target_pairs={{0,8},{4,12},{8,0},{12,4},{16,24},{20,28},{24,16},{28,20},{1,9},{5... | collective-permute-start | bytes 786440 | tf_op jit(solution)/shard_map/ppermute | solution.py:77
  185.1 17.5 %collective-permute-start.26 = (bf16[16,2,16,256]{3,2,1,0:T(8,128)(2,1)S(1)}, bf16[16,2,16,256]{3,2,1,0:T(8,128)(2,1)S(1)}, u32[]{:S(2)}, u32[]{:S(2)}) collective-permute-start(bf16[16,2,16,256]{3,2,1,0:T(8,128)(2,1)S(1)} %get-tuple-element.61), channel_id=1, source_target_pairs={{0,12},{4,8},{8,4},{12,0},{16,28},{20,24},{24,20},{28,16},{1,13},{... | collective-permute-start | bytes 786440 | tf_op jit(solution)/shard_map/ppermute | solution.py:77
  186.9 18.4 %collective-permute-start.27 = (bf16[16,2,16,256]{3,2,1,0:T(8,128)(2,1)S(1)}, bf16[16,2,16,256]{3,2,1,0:T(8,128)(2,1)S(1)}, u32[]{:S(2)}, u32[]{:S(2)}) collective-permute-start(bf16[16,2,16,256]{3,2,1,0:T(8,128)(2,1)S(1)} %get-tuple-element.62), channel_id=1, source_target_pairs={{0,16},{4,20},{8,24},{12,28},{16,0},{20,4},{24,8},{28,12},{1,17},{... | collective-permute-start | bytes 786440 | tf_op jit(solution)/shard_map/ppermute | solution.py:77
  187.6 34.9 %collective-permute-start.28 = (bf16[16,2,16,256]{3,2,1,0:T(8,128)(2,1)S(1)}, bf16[16,2,16,256]{3,2,1,0:T(8,128)(2,1)S(1)}, u32[]{:S(2)}, u32[]{:S(2)}) collective-permute-start(bf16[16,2,16,256]{3,2,1,0:T(8,128)(2,1)S(1)} %get-tuple-element.63), channel_id=1, source_target_pairs={{0,20},{4,16},{8,28},{12,24},{16,4},{20,0},{24,12},{28,8},{1,21},{... | collective-permute-start | bytes 786440 | tf_op jit(solution)/shard_map/ppermute | solution.py:77
  192.6 35.7 %collective-permute-start.29 = (bf16[16,2,16,256]{3,2,1,0:T(8,128)(2,1)S(1)}, bf16[16,2,16,256]{3,2,1,0:T(8,128)(2,1)S(1)}, u32[]{:S(2)}, u32[]{:S(2)}) collective-permute-start(bf16[16,2,16,256]{3,2,1,0:T(8,128)(2,1)S(1)} %get-tuple-element.64), channel_id=1, source_target_pairs={{0,24},{4,28},{8,16},{12,20},{16,8},{20,12},{24,0},{28,4},{1,25},{... | collective-permute-start | bytes 786440 | tf_op jit(solution)/shard_map/ppermute | solution.py:77
  199.5 32.5 %collective-permute-start.30 = (bf16[16,2,16,256]{3,2,1,0:T(8,128)(2,1)S(1)}, bf16[16,2,16,256]{3,2,1,0:T(8,128)(2,1)S(1)}, u32[]{:S(2)}, u32[]{:S(2)}) collective-permute-start(bf16[16,2,16,256]{3,2,1,0:T(8,128)(2,1)S(1)} %get-tuple-element.65), channel_id=1, source_target_pairs={{0,28},{4,24},{8,20},{12,16},{16,12},{20,8},{24,4},{28,0},{1,29},{... | collective-permute-start | bytes 786440 | tf_op jit(solution)/shard_map/ppermute | solution.py:77
  234.0 23.8 %copy-start.6 = (bf16[16,8192]{1,0:T(8,128)(2,1)}, bf16[16,8192]{1,0:T(8,128)(2,1)S(1)}, u32[]{:S(2)}) copy-start(bf16[16,8192]{1,0:T(8,128)(2,1)S(1)} %get-tuple-element.66.refs_0_) | copy-start | bytes 786436
  234.0 8.1 %collective-permute-start.31 = (bf16[16,8192]{1,0:T(8,128)(2,1)S(1)}, bf16[16,8192]{1,0:T(8,128)(2,1)S(1)}, u32[]{:S(2)}, u32[]{:S(2)}) collective-permute-start(bf16[16,8192]{1,0:T(8,128)(2,1)S(1)} %get-tuple-element.67), channel_id=1, source_target_pairs={{0,4},{4,0},{8,12},{12,8},{16,20},{20,16},{24,28},{28,24},{1,5},{5... | collective-permute-start | bytes 786440 | tf_op jit(solution)/shard_map/ppermute | solution.py:77
  234.6 11.6 %collective-permute-start.32 = (bf16[16,8192]{1,0:T(8,128)(2,1)S(1)}, bf16[16,8192]{1,0:T(8,128)(2,1)S(1)}, u32[]{:S(2)}, u32[]{:S(2)}) collective-permute-start(bf16[16,8192]{1,0:T(8,128)(2,1)S(1)} %get-tuple-element.68), channel_id=1, source_target_pairs={{0,8},{4,12},{8,0},{12,4},{16,24},{20,28},{24,16},{28,20},{1,9},{5... | collective-permute-start | bytes 786440 | tf_op jit(solution)/shard_map/ppermute | solution.py:77
  234.6 23.2 %collective-permute-start.33 = (bf16[16,8192]{1,0:T(8,128)(2,1)S(1)}, bf16[16,8192]{1,0:T(8,128)(2,1)S(1)}, u32[]{:S(2)}, u32[]{:S(2)}) collective-permute-start(bf16[16,8192]{1,0:T(8,128)(2,1)S(1)} %get-tuple-element.69), channel_id=1, source_target_pairs={{0,12},{4,8},{8,4},{12,0},{16,28},{20,24},{24,20},{28,16},{1,13},{... | collective-permute-start | bytes 786440 | tf_op jit(solution)/shard_map/ppermute | solution.py:77
  237.6 28.5 %collective-permute-start.34 = (bf16[16,8192]{1,0:T(8,128)(2,1)S(1)}, bf16[16,8192]{1,0:T(8,128)(2,1)S(1)}, u32[]{:S(2)}, u32[]{:S(2)}) collective-permute-start(bf16[16,8192]{1,0:T(8,128)(2,1)S(1)} %get-tuple-element.70), channel_id=1, source_target_pairs={{0,16},{4,20},{8,24},{12,28},{16,0},{20,4},{24,8},{28,12},{1,17},{... | collective-permute-start | bytes 786440 | tf_op jit(solution)/shard_map/ppermute | solution.py:77
  237.6 34.2 %collective-permute-start.35 = (bf16[16,8192]{1,0:T(8,128)(2,1)S(1)}, bf16[16,8192]{1,0:T(8,128)(2,1)S(1)}, u32[]{:S(2)}, u32[]{:S(2)}) collective-permute-start(bf16[16,8192]{1,0:T(8,128)(2,1)S(1)} %get-tuple-element.71), channel_id=1, source_target_pairs={{0,20},{4,16},{8,28},{12,24},{16,4},{20,0},{24,12},{28,8},{1,21},{... | collective-permute-start | bytes 786440 | tf_op jit(solution)/shard_map/ppermute | solution.py:77
  242.1 15.7 %copy-start.9 = (bf16[16,8192]{1,0:T(8,128)(2,1)}, bf16[16,8192]{1,0:T(8,128)(2,1)S(1)}, u32[]{:S(2)}) copy-start(bf16[16,8192]{1,0:T(8,128)(2,1)S(1)} %collective-permute-done.31.refs_1_) | copy-start | bytes 786436
  242.1 34.9 %collective-permute-start.36 = (bf16[16,8192]{1,0:T(8,128)(2,1)S(1)}, bf16[16,8192]{1,0:T(8,128)(2,1)S(1)}, u32[]{:S(2)}, u32[]{:S(2)}) collective-permute-start(bf16[16,8192]{1,0:T(8,128)(2,1)S(1)} %get-tuple-element.72), channel_id=1, source_target_pairs={{0,24},{4,28},{8,16},{12,20},{16,8},{20,12},{24,0},{28,4},{1,25},{... | collective-permute-start | bytes 786440 | tf_op jit(solution)/shard_map/ppermute | solution.py:77
  246.2 33.6 %collective-permute-start.37 = (bf16[16,8192]{1,0:T(8,128)(2,1)S(1)}, bf16[16,8192]{1,0:T(8,128)(2,1)S(1)}, u32[]{:S(2)}, u32[]{:S(2)}) collective-permute-start(bf16[16,8192]{1,0:T(8,128)(2,1)S(1)} %get-tuple-element.73), channel_id=1, source_target_pairs={{0,28},{4,24},{8,20},{12,16},{16,12},{20,8},{24,4},{28,0},{1,29},{... | collective-permute-start | bytes 786440 | tf_op jit(solution)/shard_map/ppermute | solution.py:77
  257.8 22.0 %copy-start.11 = (bf16[16,8192]{1,0:T(8,128)(2,1)}, bf16[16,8192]{1,0:T(8,128)(2,1)S(1)}, u32[]{:S(2)}) copy-start(bf16[16,8192]{1,0:T(8,128)(2,1)S(1)} %collective-permute-done.33.refs_3_) | copy-start | bytes 786436
  (10 other events, 43.5 us)

commit v2 on v1

--- a/solution.py
+++ b/solution.py
@@ -191,7 +191,7 @@
         turned[pl.ds(start, strip), :] = grads[k][0]
 
 
-def direction_kernel(groups, strip, sub, meta, second_ref, left_ref, right_ref, *refs):
+def direction_kernel(groups, strip, halves, meta, second_ref, left_ref, right_ref, *refs):
     grads, outs, turned, rows = refs[:groups], refs[groups : 2 * groups], refs[-2], refs[-1]
     position = meta[0]
     gather_block(groups, strip, position, grads, turned)
@@ -211,11 +211,12 @@
     shaped_sum = jnp.sum(shaped * shaped, keepdims=True)
     ratio = jnp.sqrt(adam_sum) / jnp.sqrt(shaped_sum + 1e-06)
     rows[...] = (shaped * ratio).astype(jnp.bfloat16)
-    halves = outs[0].shape[1]
+    sub = outs[0].shape[1]
     for k in range(groups):
-        for h in range(halves):
-            start = pl.multiple_of(h * groups * sub + (position ^ k) * sub, sub)
-            outs[k][0, h] = rows[pl.ds(start, sub), :]
+        middle = position ^ k
+        half, quarter = lax.rem(middle, halves), lax.div(middle, halves)
+        start = (half * (groups // halves) + quarter) * sub
+        outs[k][0] = rows[pl.ds(pl.multiple_of(start, sub), sub), :]
 
 
 def directions(meta, grads, second, root_left, root_right, halves, sub):
@@ -223,20 +224,19 @@
     slots, strip, block = grads[0].shape
     stat = pl.BlockSpec((1, 1, block, block), lambda s, meta: (0, s, 0, 0))
     return pl.pallas_call(
-        functools.partial(direction_kernel, groups, strip, sub),
+        functools.partial(direction_kernel, groups, strip, halves),
         grid_spec=pltpu.PrefetchScalarGridSpec(
             num_scalar_prefetch=1,
             grid=(slots,),
             in_specs=[stat] * 3
             + [pl.BlockSpec((1, strip, block), lambda s, meta: (s, 0, 0))] * groups,
-            out_specs=[pl.BlockSpec((1, halves, sub, block), lambda s, meta: (s, 0, 0, 0))]
-            * groups,
+            out_specs=[pl.BlockSpec((1, sub, block), lambda s, meta: (s, 0, 0))] * groups,
             scratch_shapes=[
                 pltpu.VMEM((block, block), jnp.bfloat16),
                 pltpu.VMEM((block, block), jnp.bfloat16),
             ],
         ),
-        out_shape=[jax.ShapeDtypeStruct((slots, halves, sub, block), jnp.bfloat16)] * groups,
+        out_shape=[jax.ShapeDtypeStruct((slots, sub, block), jnp.bfloat16)] * groups,
         compiler_params=pltpu.CompilerParams(vmem_limit_bytes=32 * MIB),
         cost_estimate=pl.CostEstimate(
             flops=4 * slots * block**3,
@@ -288,84 +288,99 @@
 
 
 def regroup_kernel(groups, slots, bands, halves, meta, *refs):
-    pieces, outs, placed = refs[:groups], refs[groups : 2 * groups], refs[-1]
+    pieces, outs, placed = refs[:groups], refs[groups:-1], refs[-1]
     block = pieces[0].shape[-1]
     position = meta[0]
+    own_band = lax.div(position, halves)
 
     def place(s, carry):
         for k in range(groups):
             block_id = meta[2 + (position ^ k) * slots + s]
             row_band, col_band = lax.div(block_id, bands), lax.rem(block_id, bands)
             columns = pl.ds(pl.multiple_of(col_band * block, block), block)
-            for h in range(halves):
-                placed[(row_band * halves + h) ^ position, :, columns] = pieces[k][s, h]
+            placed[row_band ^ own_band, :, columns] = pieces[k][s]
         return carry
 
     lax.fori_loop(0, slots, place, 0)
-    for k in range(groups):
+    for k in range(len(outs)):
         outs[k][...] = placed[k]
 
 
-def regroup(meta, pieces, bands):
+def regroup(meta, pieces, bands, halves):
     groups = len(pieces)
-    slots, halves, sub, block = pieces[0].shape
+    slots, sub, block = pieces[0].shape
+    row_bands = groups // halves
     return pl.pallas_call(
         functools.partial(regroup_kernel, groups, slots, bands, halves),
         grid_spec=pltpu.PrefetchScalarGridSpec(
             num_scalar_prefetch=1,
             grid=(),
             in_specs=[pl.BlockSpec(memory_space=pltpu.VMEM)] * groups,
-            out_specs=[pl.BlockSpec(memory_space=pltpu.VMEM)] * groups,
-            scratch_shapes=[pltpu.VMEM((groups, sub, bands * block), jnp.bfloat16)],
-        ),
-        out_shape=[jax.ShapeDtypeStruct((sub, bands * block), jnp.bfloat16)] * groups,
+            out_specs=[pl.BlockSpec(memory_space=pltpu.VMEM)] * row_bands,
+            scratch_shapes=[pltpu.VMEM((row_bands, sub, bands * block), jnp.bfloat16)],
+        ),
+        out_shape=[jax.ShapeDtypeStruct((sub, bands * block), jnp.bfloat16)] * row_bands,
         compiler_params=pltpu.CompilerParams(vmem_limit_bytes=32 * MIB),
         cost_estimate=pl.CostEstimate(
             flops=0,
-            bytes_accessed=4 * groups * sub * bands * block,
+            bytes_accessed=4 * row_bands * sub * bands * block,
             transcendentals=0,
         ),
         name="regroup",
     )(meta, *pieces)
 
 
-def stack_kernel(groups, meta, *refs):
-    pieces, out, sems = refs[:groups], refs[groups], refs[groups + 1]
+def stack_kernel(halves, meta, *refs):
+    pieces, out = refs[:-1], refs[-1]
     sub = pieces[0].shape[0]
-    copies = []
-    for k in range(groups):
-        start = pl.multiple_of((meta[0] ^ k) * sub, sub)
-        copies.append(
-            pltpu.make_async_copy(pieces[k], out.at[0, pl.ds(start, sub), :], sems.at[k])
-        )
-    for copy in copies:
-        copy.start()
-    for copy in copies:
-        copy.wait()
-
-
-def stack_rows(meta, pieces):
-    groups = len(pieces)
+    own_band = lax.div(meta[0], halves)
+    for k in range(len(pieces)):
+        start = pl.multiple_of((own_band ^ k) * sub, sub)
+        out[0, pl.ds(start, sub), :] = pieces[k][...]
+
+
+def stack_rows(meta, pieces, halves):
+    count = len(pieces)
     sub, width = pieces[0].shape
-    return pl.pallas_call(
-        functools.partial(stack_kernel, groups),
-        grid_spec=pltpu.PrefetchScalarGridSpec(
-            num_scalar_prefetch=1,
-            grid=(),
-            in_specs=[pl.BlockSpec(memory_space=pl.ANY)] * groups,
-            out_specs=pl.BlockSpec(memory_space=pl.ANY),
-            scratch_shapes=[pltpu.SemaphoreType.DMA((groups,))],
-        ),
-        out_shape=jax.ShapeDtypeStruct((1, groups * sub, width), jnp.bfloat16),
-        cost_estimate=pl.CostEstimate(
-            flops=0, bytes_accessed=4 * groups * sub * width, transcendentals=0
+    part = width // count
+    return pl.pallas_call(
+        functools.partial(stack_kernel, halves),
+        grid_spec=pltpu.PrefetchScalarGridSpec(
+            num_scalar_prefetch=1,
+            grid=(count,),
+            in_specs=[pl.BlockSpec((sub, part), lambda c, meta: (0, c))] * count,
+            out_specs=pl.BlockSpec((1, count * sub, part), lambda c, meta: (0, 0, c)),
+        ),
+        out_shape=jax.ShapeDtypeStruct((1, count * sub, width), jnp.bfloat16),
+        compiler_params=pltpu.CompilerParams(vmem_limit_bytes=16 * MIB),
+        cost_estimate=pl.CostEstimate(
+            flops=0, bytes_accessed=4 * count * sub * width, transcendentals=0
         ),
         name="stack_rows",
     )(meta, *pieces)
 
 
-def exchange(pieces):
-    return [pieces[0]] + [swap(pieces[k], "fsdp", k) for k in range(1, len(pieces))]
+def exchange(pieces, stride=1):
+    return [pieces[0]] + [swap(pieces[k], "fsdp", k * stride) for k in range(1, len(pieces))]
+
+
+def gather_relayed(value):
+    groups = lax.axis_size("fsdp")
+    found = [value] + [None] * (groups - 1)
+    far = groups // 2
+    found[far] = swap(value, "fsdp", far)
+    step = 1
+    while step < far:
+        found[step] = swap(value, "fsdp", step)
+        for k in range(1, step):
+            found[step + k] = swap(found[step], "fsdp", k)
+        step *= 2
+    step = 1
+    while step < far:
+        for k in range(step):
+            found[far + step + k] = swap(found[far + k], "fsdp", step)
+        step *= 2
+    return found
 
 
 def strip_plan(
@@ -380,12 +395,7 @@
     meta = jnp.concatenate([place, block_table[0]])
 
     strips = exchange(cot_strips(meta, cotangent, groups, block))
-    ctxs = [context] + [None] * (groups - 1)
-    for k in range(groups):
-        if k % 2:
-            ctxs[k] = swap(ctxs[k - 1], "fsdp", 1)
-        elif k:
-            ctxs[k] = swap(context, "fsdp", k)
+    ctxs = gather_relayed(context)
     tokens = context.shape[0]
     cots = [jnp.stack(strips).reshape(groups, -1, tokens)]
     offset = ranks // 2
@@ -397,15 +407,16 @@
     cots = [by_offset[t] for t in range(ranks)]
 
     grads = exchange(gradient_strips(meta, cots, ctxs, slots, bands, block))
-    halves, sub = block // strip_rows, strip_rows // groups
+    halves = block // strip_rows
+    sub = strip_rows * halves // groups
     pieces = exchange(
         directions(meta, grads, second_moment, root_left, root_right, halves, sub)
     )
     left_new, right_new, second_new = statistics(
         meta, grads, left_stat, right_stat, second_moment
     )
-    rows = exchange(regroup(meta, pieces, bands))
-    return (left_new, right_new, second_new, stack_rows(meta, rows))
+    rows = exchange(regroup(meta, pieces, bands, halves), halves)
+    return (left_new, right_new, second_new, stack_rows(meta, rows, halves))
 
 
 def per_device(context, cotangent, block_table, left_stat, *rest):
@@ -413,8 +424,8 @@
     block = left_stat.shape[-1]
     strip_rows = context.shape[1] // groups
     powers = groups & (groups - 1) == 0 and ranks & (ranks - 1) == 0
-    even = block % (16 * groups) == 0 and strip_rows % (16 * groups) == 0
     whole = block % strip_rows == 0 and cotangent.shape[1] % block == 0
+    even = block % (16 * groups) == 0
     plan = strip_plan if powers and even and whole else general_plan
     return plan(context, cotangent, block_table, left_stat, *rest)
 

time: 350 us -> 255 us (0.73); the launches traced: 346 us -> 255 us
  Pallas kernels: 99.6 us -> 36.4 us
  starting transfers between devices: 55.5 us -> 40.4 us
  waiting for transfers between devices: 183 us -> 172 us
    pallas_call x2, Pallas kernels: 76.8 us -> 14 us  [the longest x1 11.5 us: directions(): pl.pallas_call(functools.partial(direction_kernel, groups, strip, halves)...]
    ppermute x38 -> x34, starting transfers between devices: 55.5 us -> 40.4 us  [swap(): return lax.ppermute(value, axis, [(i, i ^ offset) for i in range(count)])]
    ppermute x38 -> x34, waiting for transfers between devices: 183 us -> 172 us  [swap(): return lax.ppermute(value, axis, [(i, i ^ offset) for i in range(count)])]
  transfers between devices with their start and end apart: 38 -> 34, of which waited for: 30 -> 29; matrix products, arithmetic and copies ran while one was open for 0% -> 0% of each run, Pallas kernels for 3% -> 4%
where the time goes in v2:
time: 255 us
  waiting for transfers between devices  172 us (67%)
  starting transfers between devices  40.4 us (16%)
  Pallas kernels  36.4 us (14%)
  local copies, waits for them, and re-layouts  5.34 us (2%)
    ppermute x34, waiting for transfers between devices, swap(): return lax.ppermute(value, axis, [(i, i ^ offset) for i in range(count)])  172 us
    ppermute x34, starting transfers between devices, swap(): return lax.ppermute(value, axis, [(i, i ^ offset) for i in range(count)])  40.4 us
    pallas_call x1, Pallas kernels, directions(): pl.pallas_call(functools.partial(direction_kernel, groups, strip, halves)...  11.5 us
    pallas_call x1, Pallas kernels, statistics(): pl.pallas_call(functools.partial(statistics_kernel, groups, strip), grid_...  9.96 us
    pallas_call x1, Pallas kernels, gradient_strips(): pl.pallas_call(functools.partial(gradient_kernel, groups, ranks, slots, b...  9.19 us
    unnamed x29, local copies, waits for them, and re-layouts  5.33 us
  transfers between devices with their start and end apart: 34, of which 29 were waited for; matrix products, arithmetic and copies ran while one was open for 0% of the time, Pallas kernels for 4%

profile of v2, /device:TPU:8, one launch (start us, length us, event | category | flops | bytes accessed | tf_op | source)
XLA Modules:
  0.0 255.2 jit_solution(14808371777290884209)
XLA Ops:
  2.6 1.6 cot_strips.1
  4.2 1.6 collective-permute-start
  6.2 1.5 collective-permute-start.2
  7.8 2.6 %collective-permute-start.3 = (bf16[8,32,256]{2,1,0:T(8,128)(2,1)S(1)}, bf16[8,32,256]{2,1,0:T(8,128)(2,1)S(1)}, u32[]{:S(2)}, u32[]{:S(2)}) collective-permute-start(bf16[8,32,256]{2,1,0:T(8,128)(2,1)S(1)} %get-tuple-element.39), channel_id=1, source_target_pairs={{0,16},{4,20},{8,24},{12,28},{16,0},{20,4},{24,8},{28,12},{1,17},{... | collective-permute-start | bytes 393224 | tf_op jit(solution)/shard_map/ppermute | solution.py:77
  11.7 1.6 collective-permute-start.5
  14.5 1.6 collective-permute-done.2
  16.1 9.3 %collective-permute-done.3 = bf16[8,32,256]{2,1,0:T(8,128)(2,1)S(1)} collective-permute-done((bf16[8,32,256]{2,1,0:T(8,128)(2,1)S(1)}, bf16[8,32,256]{2,1,0:T(8,128)(2,1)S(1)}, u32[]{:S(2)}, u32[]{:S(2)}) %collective-permute-start.3) | collective-permute-done | bytes 131104 | tf_op jit(solution)/shard_map/ppermute | solution.py:77
  25.4 2.8 %collective-permute-done.4 = bf16[8,32,256]{2,1,0:T(8,128)(2,1)S(1)} collective-permute-done((bf16[8,32,256]{2,1,0:T(8,128)(2,1)S(1)}, bf16[8,32,256]{2,1,0:T(8,128)(2,1)S(1)}, u32[]{:S(2)}, u32[]{:S(2)}) %collective-permute-start.4) | collective-permute-done | bytes 131104 | tf_op jit(solution)/shard_map/ppermute | solution.py:77
  28.2 2.6 %collective-permute-done.5 = bf16[8,32,256]{2,1,0:T(8,128)(2,1)S(1)} collective-permute-done((bf16[8,32,256]{2,1,0:T(8,128)(2,1)S(1)}, bf16[8,32,256]{2,1,0:T(8,128)(2,1)S(1)}, u32[]{:S(2)}, u32[]{:S(2)}) %collective-permute-start.5) | collective-permute-done | bytes 131104 | tf_op jit(solution)/shard_map/ppermute | solution.py:77
  30.8 2.5 collective-permute-done.6
  33.3 1.6 collective-permute-start.8
  34.9 3.6 %collective-permute-start.11 = (bf16[256,1024]{1,0:T(8,128)(2,1)}, bf16[256,1024]{1,0:T(8,128)(2,1)S(1)}, u32[]{:S(2)}, u32[]{:S(2)}) collective-permute-start(bf16[256,1024]{1,0:T(8,128)(2,1)} %refs_4_.1), channel_id=1, source_target_pairs={{0,8},{4,12},{8,0},{12,4},{16,24},{20,28},{24,16},{28,20},{1,9},{5... | collective-permute-start | bytes 1572872 | tf_op jit(solution)/shard_map/ppermute | solution.py:77
  39.0 17.8 %collective-permute-done.13.refs_8_ = bf16[256,1024]{1,0:T(8,128)(2,1)S(1)} collective-permute-done((bf16[256,1024]{1,0:T(8,128)(2,1)}, bf16[256,1024]{1,0:T(8,128)(2,1)S(1)}, u32[]{:S(2)}, u32[]{:S(2)}) %collective-permute-start.13) | collective-permute-done | bytes 524320 | tf_op jit(solution)/shard_map/ppermute | solution.py:77
  57.4 2.8 %collective-permute-done.11.refs_6_ = bf16[256,1024]{1,0:T(8,128)(2,1)S(1)} collective-permute-done((bf16[256,1024]{1,0:T(8,128)(2,1)}, bf16[256,1024]{1,0:T(8,128)(2,1)S(1)}, u32[]{:S(2)}, u32[]{:S(2)}) %collective-permute-start.11) | collective-permute-done | bytes 524320 | tf_op jit(solution)/shard_map/ppermute | solution.py:77
  60.2 2.5 collective-permute-start.15
  62.7 8.9 %collective-permute-done.14.refs_9_ = bf16[256,1024]{1,0:T(8,128)(2,1)S(1)} collective-permute-done((bf16[256,1024]{1,0:T(8,128)(2,1)S(1)}, bf16[256,1024]{1,0:T(8,128)(2,1)S(1)}, u32[]{:S(2)}, u32[]{:S(2)}) %collective-permute-start.14) | collective-permute-done | bytes 524320 | tf_op jit(solution)/shard_map/ppermute | solution.py:77
  71.6 3.8 %collective-permute-start.16 = (bf16[256,1024]{1,0:T(8,128)(2,1)S(1)}, bf16[256,1024]{1,0:T(8,128)(2,1)S(1)}, u32[]{:S(2)}, u32[]{:S(2)}) collective-permute-start(bf16[256,1024]{1,0:T(8,128)(2,1)S(1)} %collective-permute-done.14.refs_9_), channel_id=1, source_target_pairs={{0,8},{4,12},{8,0},{12,4},{16,24},{20,28},{24,16},{28,20},{1,9},{5... | collective-permute-start | bytes 1572872 | tf_op jit(solution)/shard_map/ppermute | solution.py:77
  75.4 4.5 %collective-permute-done.12.refs_7_ = bf16[256,1024]{1,0:T(8,128)(2,1)S(1)} collective-permute-done((bf16[256,1024]{1,0:T(8,128)(2,1)S(1)}, bf16[256,1024]{1,0:T(8,128)(2,1)S(1)}, u32[]{:S(2)}, u32[]{:S(2)}) %collective-permute-start.12) | collective-permute-done | bytes 524320 | tf_op jit(solution)/shard_map/ppermute | solution.py:77
  79.9 6.3 %collective-permute-done.16.refs_11_ = bf16[256,1024]{1,0:T(8,128)(2,1)S(1)} collective-permute-done((bf16[256,1024]{1,0:T(8,128)(2,1)S(1)}, bf16[256,1024]{1,0:T(8,128)(2,1)S(1)}, u32[]{:S(2)}, u32[]{:S(2)}) %collective-permute-start.16) | collective-permute-done | bytes 524320 | tf_op jit(solution)/shard_map/ppermute | solution.py:77
  88.0 9.2 %gradient_strips.1 = (bf16[16,32,256]{2,1,0:T(8,128)(2,1)S(1)}, bf16[16,32,256]{2,1,0:T(8,128)(2,1)S(1)}, bf16[16,32,256]{2,1,0:T(8,128)(2,1)S(1)}, bf16[16,32,2...) custom-call(s32[130]{0:T(256)S(1)} %pad_add_fusion.meta, ...), custom_call_target="tpu_custom_call" | custom-call | flops 4294967296 | bytes 10485760 | tf_op jit(solution)/shard_map/gradient_strips/pallas_call | solution.py:163
  97.6 1.7 collective-permute-start.18
  102.0 1.5 collective-permute-start.21
  103.5 2.4 collective-permute-done.17.refs_1_
  106.2 6.8 %collective-permute-done.18.refs_2_ = bf16[16,32,256]{2,1,0:T(8,128)(2,1)S(1)} collective-permute-done((bf16[16,32,256]{2,1,0:T(8,128)(2,1)S(1)}, bf16[16,32,256]{2,1,0:T(8,128)(2,1)S(1)}, u32[]{:S(2)}, u32[]{:S(2)}) %collective-permute-start.18) | collective-permute-done | bytes 262176 | tf_op jit(solution)/shard_map/ppermute | solution.py:77
  113.0 1.8 collective-permute-start.23
  115.8 2.0 collective-permute-done.20.refs_4_
  117.8 19.1 %collective-permute-done.21.refs_5_ = bf16[16,32,256]{2,1,0:T(8,128)(2,1)S(1)} collective-permute-done((bf16[16,32,256]{2,1,0:T(8,128)(2,1)S(1)}, bf16[16,32,256]{2,1,0:T(8,128)(2,1)S(1)}, u32[]{:S(2)}, u32[]{:S(2)}) %collective-permute-start.21) | collective-permute-done | bytes 262176 | tf_op jit(solution)/shard_map/ppermute | solution.py:77
  136.8 6.8 %collective-permute-done.22.refs_6_ = bf16[16,32,256]{2,1,0:T(8,128)(2,1)S(1)} collective-permute-done((bf16[16,32,256]{2,1,0:T(8,128)(2,1)S(1)}, bf16[16,32,256]{2,1,0:T(8,128)(2,1)S(1)}, u32[]{:S(2)}, u32[]{:S(2)}) %collective-permute-start.22) | collective-permute-done | bytes 262176 | tf_op jit(solution)/shard_map/ppermute | solution.py:77
  143.6 2.9 %collective-permute-done.23.refs_7_ = bf16[16,32,256]{2,1,0:T(8,128)(2,1)S(1)} collective-permute-done((bf16[16,32,256]{2,1,0:T(8,128)(2,1)S(1)}, bf16[16,32,256]{2,1,0:T(8,128)(2,1)S(1)}, u32[]{:S(2)}, u32[]{:S(2)}) %collective-permute-start.23) | collective-permute-done | bytes 262176 | tf_op jit(solution)/shard_map/ppermute | solution.py:77
  146.5 2.2 copy-done.2
  148.7 11.5 %directions.1 = (bf16[16,32,256]{2,1,0:T(8,128)(2,1)S(1)}, bf16[16,32,256]{2,1,0:T(8,128)(2,1)S(1)}, bf16[16,32,256]{2,1,0:T(8,128)(2,1)S(1)}, bf16[16,32,256]{2...) custom-call(s32[130]{0:T(256)S(1)} %pad_add_fusion.meta, ...), custom_call_target="tpu_custom_call" | custom-call | flops 1073741824 | bytes 16777216 | tf_op jit(solution)/shard_map/directions/pallas_call | solution.py:226
  160.2 1.4 collective-permute-start.24
  161.7 2.1 collective-permute-start.26
  163.8 3.7 %collective-permute-start.28 = (bf16[16,32,256]{2,1,0:T(8,128)(2,1)S(1)}, bf16[16,32,256]{2,1,0:T(8,128)(2,1)S(1)}, u32[]{:S(2)}, u32[]{:S(2)}) collective-permute-start(bf16[16,32,256]{2,1,0:T(8,128)(2,1)S(1)} %get-tuple-element.59), channel_id=1, source_target_pairs={{0,20},{4,16},{8,28},{12,24},{16,4},{20,0},{24,12},{28,8},{1,21},{... | collective-permute-start | bytes 786440 | tf_op jit(solution)/shard_map/ppermute | solution.py:77
  168.6 4.8 %collective-permute-done.25.refs_2_ = bf16[16,32,256]{2,1,0:T(8,128)(2,1)S(1)} collective-permute-done((bf16[16,32,256]{2,1,0:T(8,128)(2,1)S(1)}, bf16[16,32,256]{2,1,0:T(8,128)(2,1)S(1)}, u32[]{:S(2)}, u32[]{:S(2)}) %collective-permute-start.25) | collective-permute-done | bytes 262176 | tf_op jit(solution)/shard_map/ppermute | solution.py:77
  173.4 4.7 %collective-permute-done.26.refs_3_ = bf16[16,32,256]{2,1,0:T(8,128)(2,1)S(1)} collective-permute-done((bf16[16,32,256]{2,1,0:T(8,128)(2,1)S(1)}, bf16[16,32,256]{2,1,0:T(8,128)(2,1)S(1)}, u32[]{:S(2)}, u32[]{:S(2)}) %collective-permute-start.26) | collective-permute-done | bytes 262176 | tf_op jit(solution)/shard_map/ppermute | solution.py:77
  178.1 3.6 %collective-permute-done.27.refs_4_ = bf16[16,32,256]{2,1,0:T(8,128)(2,1)S(1)} collective-permute-done((bf16[16,32,256]{2,1,0:T(8,128)(2,1)S(1)}, bf16[16,32,256]{2,1,0:T(8,128)(2,1)S(1)}, u32[]{:S(2)}, u32[]{:S(2)}) %collective-permute-start.27) | collective-permute-done | bytes 262176 | tf_op jit(solution)/shard_map/ppermute | solution.py:77
  181.7 16.7 %collective-permute-done.28.refs_5_ = bf16[16,32,256]{2,1,0:T(8,128)(2,1)S(1)} collective-permute-done((bf16[16,32,256]{2,1,0:T(8,128)(2,1)S(1)}, bf16[16,32,256]{2,1,0:T(8,128)(2,1)S(1)}, u32[]{:S(2)}, u32[]{:S(2)}) %collective-permute-start.28) | collective-permute-done | bytes 262176 | tf_op jit(solution)/shard_map/ppermute | solution.py:77
  198.4 5.1 %collective-permute-done.29.refs_6_ = bf16[16,32,256]{2,1,0:T(8,128)(2,1)S(1)} collective-permute-done((bf16[16,32,256]{2,1,0:T(8,128)(2,1)S(1)}, bf16[16,32,256]{2,1,0:T(8,128)(2,1)S(1)}, u32[]{:S(2)}, u32[]{:S(2)}) %collective-permute-start.29) | collective-permute-done | bytes 262176 | tf_op jit(solution)/shard_map/ppermute | solution.py:77
  203.5 3.3 %collective-permute-done.30.refs_7_ = bf16[16,32,256]{2,1,0:T(8,128)(2,1)S(1)} collective-permute-done((bf16[16,32,256]{2,1,0:T(8,128)(2,1)S(1)}, bf16[16,32,256]{2,1,0:T(8,128)(2,1)S(1)}, u32[]{:S(2)}, u32[]{:S(2)}) %collective-permute-start.30) | collective-permute-done | bytes 262176 | tf_op jit(solution)/shard_map/ppermute | solution.py:77
  206.8 1.6 regroup.1
  208.5 2.0 collective-permute-start.32
  210.5 1.5 collective-permute-start.33
  212.0 10.0 %statistics.1 = (f32[1,16,256,256]{3,2,1,0:T(8,128)}, f32[1,16,256,256]{3,2,1,0:T(8,128)}, f32[1,16,256,256]{3,2,1,0:T(8,128)}) custom-call(s32[130]{0:T(256)S(1)} %pad_add_fusion.meta, f32[1,16,256,256]{3,2,1,0:T(8,128)S(1)} %copy-done.3, f32[1,16,256,256]{3,2,1,0:T(8,128)S(1)} %copy-done.4, f32[1,16,256,256]{3,2,1,0:T(8,128)S(1)} %copy-done, ...), custom_call_target="tpu_custom_call" | custom-call | flops 1073741824 | bytes 27262976 | tf_op jit(solution)/shard_map/statistics/pallas_call | solution.py:269
  221.9 5.0 %collective-permute-done.31.refs_1_ = bf16[32,8192]{1,0:T(8,128)(2,1)S(1)} collective-permute-done((bf16[32,8192]{1,0:T(8,128)(2,1)S(1)}, bf16[32,8192]{1,0:T(8,128)(2,1)S(1)}, u32[]{:S(2)}, u32[]{:S(2)}) %collective-permute-start.31) | collective-permute-done | bytes 524320 | tf_op jit(solution)/shard_map/ppermute | solution.py:77
  226.9 17.1 %collective-permute-done.32.refs_2_ = bf16[32,8192]{1,0:T(8,128)(2,1)S(1)} collective-permute-done((bf16[32,8192]{1,0:T(8,128)(2,1)S(1)}, bf16[32,8192]{1,0:T(8,128)(2,1)S(1)}, u32[]{:S(2)}, u32[]{:S(2)}) %collective-permute-start.32) | collective-permute-done | bytes 524320 | tf_op jit(solution)/shard_map/ppermute | solution.py:77
  244.0 8.7 %collective-permute-done.33.refs_3_ = bf16[32,8192]{1,0:T(8,128)(2,1)S(1)} collective-permute-done((bf16[32,8192]{1,0:T(8,128)(2,1)S(1)}, bf16[32,8192]{1,0:T(8,128)(2,1)S(1)}, u32[]{:S(2)}, u32[]{:S(2)}) %collective-permute-start.33) | collective-permute-done | bytes 524320 | tf_op jit(solution)/shard_map/ppermute | solution.py:77
  252.7 2.5 stack_rows.1
  (57 shorter events, 13.4 us)
Async XLA Ops:
  1.4 1.2 copy-start.5
  4.2 7.5 %collective-permute-start = (bf16[8,32,256]{2,1,0:T(8,128)(2,1)S(1)}, bf16[8,32,256]{2,1,0:T(8,128)(2,1)S(1)}, u32[]{:S(2)}, u32[]{:S(2)}) collective-permute-start(bf16[8,32,256]{2,1,0:T(8,128)(2,1)S(1)} %get-tuple-element.36), channel_id=1, source_target_pairs={{0,4},{4,0},{8,12},{12,8},{16,20},{20,16},{24,28},{28,24},{1,5},{5... | collective-permute-start | bytes 393224 | tf_op jit(solution)/shard_map/ppermute | solution.py:77
  5.8 8.6 %collective-permute-start.1 = (bf16[8,32,256]{2,1,0:T(8,128)(2,1)S(1)}, bf16[8,32,256]{2,1,0:T(8,128)(2,1)S(1)}, u32[]{:S(2)}, u32[]{:S(2)}) collective-permute-start(bf16[8,32,256]{2,1,0:T(8,128)(2,1)S(1)} %get-tuple-element.37), channel_id=1, source_target_pairs={{0,8},{4,12},{8,0},{12,4},{16,24},{20,28},{24,16},{28,20},{1,9},{5... | collective-permute-start | bytes 393224 | tf_op jit(solution)/shard_map/ppermute | solution.py:77
  6.2 9.8 %collective-permute-start.2 = (bf16[8,32,256]{2,1,0:T(8,128)(2,1)S(1)}, bf16[8,32,256]{2,1,0:T(8,128)(2,1)S(1)}, u32[]{:S(2)}, u32[]{:S(2)}) collective-permute-start(bf16[8,32,256]{2,1,0:T(8,128)(2,1)S(1)} %get-tuple-element.38), channel_id=1, source_target_pairs={{0,12},{4,8},{8,4},{12,0},{16,28},{20,24},{24,20},{28,16},{1,13},{... | collective-permute-start | bytes 393224 | tf_op jit(solution)/shard_map/ppermute | solution.py:77
  7.8 17.6 %collective-permute-start.3 = (bf16[8,32,256]{2,1,0:T(8,128)(2,1)S(1)}, bf16[8,32,256]{2,1,0:T(8,128)(2,1)S(1)}, u32[]{:S(2)}, u32[]{:S(2)}) collective-permute-start(bf16[8,32,256]{2,1,0:T(8,128)(2,1)S(1)} %get-tuple-element.39), channel_id=1, source_target_pairs={{0,16},{4,20},{8,24},{12,28},{16,0},{20,4},{24,8},{28,12},{1,17},{... | collective-permute-start | bytes 393224 | tf_op jit(solution)/shard_map/ppermute | solution.py:77
  10.3 17.8 %collective-permute-start.4 = (bf16[8,32,256]{2,1,0:T(8,128)(2,1)S(1)}, bf16[8,32,256]{2,1,0:T(8,128)(2,1)S(1)}, u32[]{:S(2)}, u32[]{:S(2)}) collective-permute-start(bf16[8,32,256]{2,1,0:T(8,128)(2,1)S(1)} %get-tuple-element.40), channel_id=1, source_target_pairs={{0,20},{4,16},{8,28},{12,24},{16,4},{20,0},{24,12},{28,8},{1,21},{... | collective-permute-start | bytes 393224 | tf_op jit(solution)/shard_map/ppermute | solution.py:77
  11.7 19.1 %collective-permute-start.5 = (bf16[8,32,256]{2,1,0:T(8,128)(2,1)S(1)}, bf16[8,32,256]{2,1,0:T(8,128)(2,1)S(1)}, u32[]{:S(2)}, u32[]{:S(2)}) collective-permute-start(bf16[8,32,256]{2,1,0:T(8,128)(2,1)S(1)} %get-tuple-element.41), channel_id=1, source_target_pairs={{0,24},{4,28},{8,16},{12,20},{16,8},{20,12},{24,0},{28,4},{1,25},{... | collective-permute-start | bytes 393224 | tf_op jit(solution)/shard_map/ppermute | solution.py:77
  14.4 18.8 %collective-permute-start.6 = (bf16[8,32,256]{2,1,0:T(8,128)(2,1)S(1)}, bf16[8,32,256]{2,1,0:T(8,128)(2,1)S(1)}, u32[]{:S(2)}, u32[]{:S(2)}) collective-permute-start(bf16[8,32,256]{2,1,0:T(8,128)(2,1)S(1)} %get-tuple-element.42), channel_id=1, source_target_pairs={{0,28},{4,24},{8,20},{12,16},{16,12},{20,8},{24,4},{28,0},{1,29},{... | collective-permute-start | bytes 393224 | tf_op jit(solution)/shard_map/ppermute | solution.py:77
  33.3 52.9 %copy-start.7 = (bf16[8,256,256]{2,1,0:T(8,128)(2,1)}, bf16[8,256,256]{2,1,0:T(8,128)(2,1)S(1)}, u32[]{:S(2)}) copy-start(bf16[8,256,256]{2,1,0:T(8,128)(2,1)S(1)} %bitcast_dynamic-update-slice_fusion.refs_0_) | copy-start | bytes 3145732
  33.3 113.2 %copy-start = (f32[1,16,256,256]{3,2,1,0:T(8,128)S(1)}, f32[1,16,256,256]{3,2,1,0:T(8,128)}, u32[]{:S(2)}) copy-start(f32[1,16,256,256]{3,2,1,0:T(8,128)} %second_ref.3) | copy-start | bytes 12582916
  33.3 113.2 %copy-start.1 = (f32[1,16,256,256]{3,2,1,0:T(8,128)S(1)}, f32[1,16,256,256]{3,2,1,0:T(8,128)}, u32[]{:S(2)}) copy-start(f32[1,16,256,256]{3,2,1,0:T(8,128)} %left_ref.3) | copy-start | bytes 12582916
  33.3 24.1 %collective-permute-start.8 = (bf16[8,256,256]{2,1,0:T(8,128)(2,1)S(1)}, bf16[8,256,256]{2,1,0:T(8,128)(2,1)S(1)}, u32[]{:S(2)}, u32[]{:S(2)}) collective-permute-start(bf16[8,256,256]{2,1,0:T(8,128)(2,1)S(1)} %bitcast_dynamic-update-slice_fusion.refs_0_), channel_id=1, source_target_pairs={{0,2},{1,3},{2,0},{3,1},{4,6},{5,7},{6,4},{7,5},{8,10},{9,11},{10,... | collective-permute-start | bytes 3145736 | tf_op jit(solution)/shard_map/ppermute | solution.py:77
  34.9 21.9 %collective-permute-start.13 = (bf16[256,1024]{1,0:T(8,128)(2,1)}, bf16[256,1024]{1,0:T(8,128)(2,1)S(1)}, u32[]{:S(2)}, u32[]{:S(2)}) collective-permute-start(bf16[256,1024]{1,0:T(8,128)(2,1)} %refs_4_.1), channel_id=1, source_target_pairs={{0,16},{4,20},{8,24},{12,28},{16,0},{20,4},{24,8},{28,12},{1,17},{... | collective-permute-start | bytes 1572872 | tf_op jit(solution)/shard_map/ppermute | solution.py:77
  34.9 25.3 %collective-permute-start.11 = (bf16[256,1024]{1,0:T(8,128)(2,1)}, bf16[256,1024]{1,0:T(8,128)(2,1)S(1)}, u32[]{:S(2)}, u32[]{:S(2)}) collective-permute-start(bf16[256,1024]{1,0:T(8,128)(2,1)} %refs_4_.1), channel_id=1, source_target_pairs={{0,8},{4,12},{8,0},{12,4},{16,24},{20,28},{24,16},{28,20},{1,9},{5... | collective-permute-start | bytes 1572872 | tf_op jit(solution)/shard_map/ppermute | solution.py:77
  38.5 21.7 %collective-permute-start.10 = (bf16[256,1024]{1,0:T(8,128)(2,1)}, bf16[256,1024]{1,0:T(8,128)(2,1)S(1)}, u32[]{:S(2)}, u32[]{:S(2)}) collective-permute-start(bf16[256,1024]{1,0:T(8,128)(2,1)} %refs_4_.1), channel_id=1, source_target_pairs={{0,4},{4,0},{8,12},{12,8},{16,20},{20,16},{24,28},{28,24},{1,5},{5... | collective-permute-start | bytes 1572872 | tf_op jit(solution)/shard_map/ppermute | solution.py:77
  39.0 40.9 %collective-permute-start.7 = (bf16[8,256,256]{2,1,0:T(8,128)(2,1)S(1)}, bf16[8,256,256]{2,1,0:T(8,128)(2,1)S(1)}, u32[]{:S(2)}, u32[]{:S(2)}) collective-permute-start(bf16[8,256,256]{2,1,0:T(8,128)(2,1)S(1)} %bitcast_dynamic-update-slice_fusion.refs_0_), channel_id=1, source_target_pairs={{0,1},{1,0},{2,3},{3,2},{4,5},{5,4},{6,7},{7,6},{8,9},{9,8},{10,11... | collective-permute-start | bytes 3145736 | tf_op jit(solution)/shard_map/ppermute | solution.py:77
  56.8 14.9 %collective-permute-start.14 = (bf16[256,1024]{1,0:T(8,128)(2,1)S(1)}, bf16[256,1024]{1,0:T(8,128)(2,1)S(1)}, u32[]{:S(2)}, u32[]{:S(2)}) collective-permute-start(bf16[256,1024]{1,0:T(8,128)(2,1)S(1)} %collective-permute-done.13.refs_8_), channel_id=1, source_target_pairs={{0,4},{4,0},{8,12},{12,8},{16,20},{20,16},{24,28},{28,24},{1,5},{5... | collective-permute-start | bytes 1572872 | tf_op jit(solution)/shard_map/ppermute | solution.py:77
  57.4 28.7 %copy-start.8 = (bf16[8,256,256]{2,1,0:T(8,128)(2,1)}, bf16[8,256,256]{2,1,0:T(8,128)(2,1)S(1)}, u32[]{:S(2)}) copy-start(bf16[8,256,256]{2,1,0:T(8,128)(2,1)S(1)} %collective-permute-done.8.refs_2_) | copy-start | bytes 3145732
  57.4 28.7 %collective-permute-start.9 = (bf16[8,256,256]{2,1,0:T(8,128)(2,1)S(1)}, bf16[8,256,256]{2,1,0:T(8,128)(2,1)}, u32[]{:S(2)}, u32[]{:S(2)}) collective-permute-start(bf16[8,256,256]{2,1,0:T(8,128)(2,1)S(1)} %collective-permute-done.8.refs_2_), channel_id=1, source_target_pairs={{0,1},{1,0},{2,3},{3,2},{4,5},{5,4},{6,7},{7,6},{8,9},{9,8},{10,11... | collective-permute-start | bytes 3145736 | tf_op jit(solution)/shard_map/ppermute | solution.py:77
  60.2 19.7 %collective-permute-start.12 = (bf16[256,1024]{1,0:T(8,128)(2,1)S(1)}, bf16[256,1024]{1,0:T(8,128)(2,1)S(1)}, u32[]{:S(2)}, u32[]{:S(2)}) collective-permute-start(bf16[256,1024]{1,0:T(8,128)(2,1)S(1)} %collective-permute-done.11.refs_6_), channel_id=1, source_target_pairs={{0,4},{4,0},{8,12},{12,8},{16,20},{20,16},{24,28},{28,24},{1,5},{5... | collective-permute-start | bytes 1572872 | tf_op jit(solution)/shard_map/ppermute | solution.py:77
  60.2 19.7 %collective-permute-start.15 = (bf16[256,1024]{1,0:T(8,128)(2,1)S(1)}, bf16[256,1024]{1,0:T(8,128)(2,1)S(1)}, u32[]{:S(2)}, u32[]{:S(2)}) collective-permute-start(bf16[256,1024]{1,0:T(8,128)(2,1)S(1)} %collective-permute-done.13.refs_8_), channel_id=1, source_target_pairs={{0,8},{4,12},{8,0},{12,4},{16,24},{20,28},{24,16},{28,20},{1,9},{5... | collective-permute-start | bytes 1572872 | tf_op jit(solution)/shard_map/ppermute | solution.py:77
  71.6 14.5 %collective-permute-start.16 = (bf16[256,1024]{1,0:T(8,128)(2,1)S(1)}, bf16[256,1024]{1,0:T(8,128)(2,1)S(1)}, u32[]{:S(2)}, u32[]{:S(2)}) collective-permute-start(bf16[256,1024]{1,0:T(8,128)(2,1)S(1)} %collective-permute-done.14.refs_9_), channel_id=1, source_target_pairs={{0,8},{4,12},{8,0},{12,4},{16,24},{20,28},{24,16},{28,20},{1,9},{5... | collective-permute-start | bytes 1572872 | tf_op jit(solution)/shard_map/ppermute | solution.py:77
  79.9 6.3 %copy-start.9 = (bf16[8,256,256]{2,1,0:T(8,128)(2,1)}, bf16[8,256,256]{2,1,0:T(8,128)(2,1)S(1)}, u32[]{:S(2)}) copy-start(bf16[8,256,256]{2,1,0:T(8,128)(2,1)S(1)} %collective-permute-done.7.refs_1_) | copy-start | bytes 3145732
  86.2 0.8 copy-start.10
  87.0 1.0 copy-start.6
  97.2 8.7 %collective-permute-start.17 = (bf16[16,32,256]{2,1,0:T(8,128)(2,1)S(1)}, bf16[16,32,256]{2,1,0:T(8,128)(2,1)S(1)}, u32[]{:S(2)}, u32[]{:S(2)}) collective-permute-start(bf16[16,32,256]{2,1,0:T(8,128)(2,1)S(1)} %get-tuple-element.44), channel_id=1, source_target_pairs={{0,4},{4,0},{8,12},{12,8},{16,20},{20,16},{24,28},{28,24},{1,5},{5... | collective-permute-start | bytes 786440 | tf_op jit(solution)/shard_map/ppermute | solution.py:77
  97.6 15.4 %collective-permute-start.18 = (bf16[16,32,256]{2,1,0:T(8,128)(2,1)S(1)}, bf16[16,32,256]{2,1,0:T(8,128)(2,1)S(1)}, u32[]{:S(2)}, u32[]{:S(2)}) collective-permute-start(bf16[16,32,256]{2,1,0:T(8,128)(2,1)S(1)} %get-tuple-element.45), channel_id=1, source_target_pairs={{0,8},{4,12},{8,0},{12,4},{16,24},{20,28},{24,16},{28,20},{1,9},{5... | collective-permute-start | bytes 786440 | tf_op jit(solution)/shard_map/ppermute | solution.py:77
  99.4 16.5 %collective-permute-start.19 = (bf16[16,32,256]{2,1,0:T(8,128)(2,1)S(1)}, bf16[16,32,256]{2,1,0:T(8,128)(2,1)S(1)}, u32[]{:S(2)}, u32[]{:S(2)}) collective-permute-start(bf16[16,32,256]{2,1,0:T(8,128)(2,1)S(1)} %get-tuple-element.46), channel_id=1, source_target_pairs={{0,12},{4,8},{8,4},{12,0},{16,28},{20,24},{24,20},{28,16},{1,13},{... | collective-permute-start | bytes 786440 | tf_op jit(solution)/shard_map/ppermute | solution.py:77
  100.8 17.0 %collective-permute-start.20 = (bf16[16,32,256]{2,1,0:T(8,128)(2,1)S(1)}, bf16[16,32,256]{2,1,0:T(8,128)(2,1)S(1)}, u32[]{:S(2)}, u32[]{:S(2)}) collective-permute-start(bf16[16,32,256]{2,1,0:T(8,128)(2,1)S(1)} %get-tuple-element.47), channel_id=1, source_target_pairs={{0,16},{4,20},{8,24},{12,28},{16,0},{20,4},{24,8},{28,12},{1,17},{... | collective-permute-start | bytes 786440 | tf_op jit(solution)/shard_map/ppermute | solution.py:77
  102.0 34.9 %collective-permute-start.21 = (bf16[16,32,256]{2,1,0:T(8,128)(2,1)S(1)}, bf16[16,32,256]{2,1,0:T(8,128)(2,1)S(1)}, u32[]{:S(2)}, u32[]{:S(2)}) collective-permute-start(bf16[16,32,256]{2,1,0:T(8,128)(2,1)S(1)} %get-tuple-element.48), channel_id=1, source_target_pairs={{0,20},{4,16},{8,28},{12,24},{16,4},{20,0},{24,12},{28,8},{1,21},{... | collective-permute-start | bytes 786440 | tf_op jit(solution)/shard_map/ppermute | solution.py:77
  105.9 37.7 %collective-permute-start.22 = (bf16[16,32,256]{2,1,0:T(8,128)(2,1)S(1)}, bf16[16,32,256]{2,1,0:T(8,128)(2,1)S(1)}, u32[]{:S(2)}, u32[]{:S(2)}) collective-permute-start(bf16[16,32,256]{2,1,0:T(8,128)(2,1)S(1)} %get-tuple-element.49), channel_id=1, source_target_pairs={{0,24},{4,28},{8,16},{12,20},{16,8},{20,12},{24,0},{28,4},{1,25},{... | collective-permute-start | bytes 786440 | tf_op jit(solution)/shard_map/ppermute | solution.py:77
  113.0 33.5 %collective-permute-start.23 = (bf16[16,32,256]{2,1,0:T(8,128)(2,1)S(1)}, bf16[16,32,256]{2,1,0:T(8,128)(2,1)S(1)}, u32[]{:S(2)}, u32[]{:S(2)}) collective-permute-start(bf16[16,32,256]{2,1,0:T(8,128)(2,1)S(1)} %get-tuple-element.50), channel_id=1, source_target_pairs={{0,28},{4,24},{8,20},{12,16},{16,12},{20,8},{24,4},{28,0},{1,29},{... | collective-permute-start | bytes 786440 | tf_op jit(solution)/shard_map/ppermute | solution.py:77
  146.5 2.2 copy-start.2
  148.7 63.2 %copy-start.3 = (f32[1,16,256,256]{3,2,1,0:T(8,128)S(1)}, f32[1,16,256,256]{3,2,1,0:T(8,128)}, u32[]{:S(2)}) copy-start(f32[1,16,256,256]{3,2,1,0:T(8,128)} %left_ref.2) | copy-start | bytes 12582916
  148.7 63.2 %copy-start.4 = (f32[1,16,256,256]{3,2,1,0:T(8,128)S(1)}, f32[1,16,256,256]{3,2,1,0:T(8,128)}, u32[]{:S(2)}) copy-start(f32[1,16,256,256]{3,2,1,0:T(8,128)} %right_ref.2) | copy-start | bytes 12582916
  160.2 8.3 %collective-permute-start.24 = (bf16[16,32,256]{2,1,0:T(8,128)(2,1)S(1)}, bf16[16,32,256]{2,1,0:T(8,128)(2,1)S(1)}, u32[]{:S(2)}, u32[]{:S(2)}) collective-permute-start(bf16[16,32,256]{2,1,0:T(8,128)(2,1)S(1)} %get-tuple-element.55), channel_id=1, source_target_pairs={{0,4},{4,0},{8,12},{12,8},{16,20},{20,16},{24,28},{28,24},{1,5},{5... | collective-permute-start | bytes 786440 | tf_op jit(solution)/shard_map/ppermute | solution.py:77
  161.7 11.7 %collective-permute-start.25 = (bf16[16,32,256]{2,1,0:T(8,128)(2,1)S(1)}, bf16[16,32,256]{2,1,0:T(8,128)(2,1)S(1)}, u32[]{:S(2)}, u32[]{:S(2)}) collective-permute-start(bf16[16,32,256]{2,1,0:T(8,128)(2,1)S(1)} %get-tuple-element.56), channel_id=1, source_target_pairs={{0,8},{4,12},{8,0},{12,4},{16,24},{20,28},{24,16},{28,20},{1,9},{5... | collective-permute-start | bytes 786440 | tf_op jit(solution)/shard_map/ppermute | solution.py:77
  161.7 16.4 %collective-permute-start.26 = (bf16[16,32,256]{2,1,0:T(8,128)(2,1)S(1)}, bf16[16,32,256]{2,1,0:T(8,128)(2,1)S(1)}, u32[]{:S(2)}, u32[]{:S(2)}) collective-permute-start(bf16[16,32,256]{2,1,0:T(8,128)(2,1)S(1)} %get-tuple-element.57), channel_id=1, source_target_pairs={{0,12},{4,8},{8,4},{12,0},{16,28},{20,24},{24,20},{28,16},{1,13},{... | collective-permute-start | bytes 786440 | tf_op jit(solution)/shard_map/ppermute | solution.py:77
  163.8 17.9 %collective-permute-start.27 = (bf16[16,32,256]{2,1,0:T(8,128)(2,1)S(1)}, bf16[16,32,256]{2,1,0:T(8,128)(2,1)S(1)}, u32[]{:S(2)}, u32[]{:S(2)}) collective-permute-start(bf16[16,32,256]{2,1,0:T(8,128)(2,1)S(1)} %get-tuple-element.58), channel_id=1, source_target_pairs={{0,16},{4,20},{8,24},{12,28},{16,0},{20,4},{24,8},{28,12},{1,17},{... | collective-permute-start | bytes 786440 | tf_op jit(solution)/shard_map/ppermute | solution.py:77
  163.8 34.6 %collective-permute-start.28 = (bf16[16,32,256]{2,1,0:T(8,128)(2,1)S(1)}, bf16[16,32,256]{2,1,0:T(8,128)(2,1)S(1)}, u32[]{:S(2)}, u32[]{:S(2)}) collective-permute-start(bf16[16,32,256]{2,1,0:T(8,128)(2,1)S(1)} %get-tuple-element.59), channel_id=1, source_target_pairs={{0,20},{4,16},{8,28},{12,24},{16,4},{20,0},{24,12},{28,8},{1,21},{... | collective-permute-start | bytes 786440 | tf_op jit(solution)/shard_map/ppermute | solution.py:77
  168.6 34.9 %collective-permute-start.29 = (bf16[16,32,256]{2,1,0:T(8,128)(2,1)S(1)}, bf16[16,32,256]{2,1,0:T(8,128)(2,1)S(1)}, u32[]{:S(2)}, u32[]{:S(2)}) collective-permute-start(bf16[16,32,256]{2,1,0:T(8,128)(2,1)S(1)} %get-tuple-element.60), channel_id=1, source_target_pairs={{0,24},{4,28},{8,16},{12,20},{16,8},{20,12},{24,0},{28,4},{1,25},{... | collective-permute-start | bytes 786440 | tf_op jit(solution)/shard_map/ppermute | solution.py:77
  173.4 33.4 %collective-permute-start.30 = (bf16[16,32,256]{2,1,0:T(8,128)(2,1)S(1)}, bf16[16,32,256]{2,1,0:T(8,128)(2,1)S(1)}, u32[]{:S(2)}, u32[]{:S(2)}) collective-permute-start(bf16[16,32,256]{2,1,0:T(8,128)(2,1)S(1)} %get-tuple-element.61), channel_id=1, source_target_pairs={{0,28},{4,24},{8,20},{12,16},{16,12},{20,8},{24,4},{28,0},{1,29},{... | collective-permute-start | bytes 786440 | tf_op jit(solution)/shard_map/ppermute | solution.py:77
  208.4 18.5 %collective-permute-start.31 = (bf16[32,8192]{1,0:T(8,128)(2,1)S(1)}, bf16[32,8192]{1,0:T(8,128)(2,1)S(1)}, u32[]{:S(2)}, u32[]{:S(2)}) collective-permute-start(bf16[32,8192]{1,0:T(8,128)(2,1)S(1)} %get-tuple-element.63), channel_id=1, source_target_pairs={{0,8},{4,12},{8,0},{12,4},{16,24},{20,28},{24,16},{28,20},{1,9},{5... | collective-permute-start | bytes 1572872 | tf_op jit(solution)/shard_map/ppermute | solution.py:77
  208.5 35.5 %collective-permute-start.32 = (bf16[32,8192]{1,0:T(8,128)(2,1)S(1)}, bf16[32,8192]{1,0:T(8,128)(2,1)S(1)}, u32[]{:S(2)}, u32[]{:S(2)}) collective-permute-start(bf16[32,8192]{1,0:T(8,128)(2,1)S(1)} %get-tuple-element.64), channel_id=1, source_target_pairs={{0,16},{4,20},{8,24},{12,28},{16,0},{20,4},{24,8},{28,12},{1,17},{... | collective-permute-start | bytes 1572872 | tf_op jit(solution)/shard_map/ppermute | solution.py:77
  210.5 42.2 %collective-permute-start.33 = (bf16[32,8192]{1,0:T(8,128)(2,1)S(1)}, bf16[32,8192]{1,0:T(8,128)(2,1)S(1)}, u32[]{:S(2)}, u32[]{:S(2)}) collective-permute-start(bf16[32,8192]{1,0:T(8,128)(2,1)S(1)} %get-tuple-element.65), channel_id=1, source_target_pairs={{0,24},{4,28},{8,16},{12,20},{16,8},{20,12},{24,0},{28,4},{1,25},{... | collective-permute-start | bytes 1572872 | tf_op jit(solution)/shard_map/ppermute | solution.py:77

commit v3 on v2

--- a/solution.py
+++ b/solution.py
@@ -107,10 +107,11 @@
     )(meta, cotangent)
 
 
-def gradient_kernel(groups, ranks, slots, bands, strip, block, meta, *refs):
+def gradient_kernel(groups, ranks, chunks, bands, strip, block, meta, *refs):
     cots, ctxs = refs[:ranks], refs[ranks : ranks + groups]
-    outs = refs[ranks + groups : ranks + 2 * groups]
-    lhs, rhs, strips, sems = refs[ranks + 2 * groups :]
+    outs = refs[ranks + groups : -4]
+    lhs, rhs, strips, sems = refs[-4:]
+    slots = sum(chunks)
     tokens = ctxs[0].shape[0]
     rows = lhs.shape[1]
     position, rank = meta[0], meta[1]
@@ -140,33 +141,36 @@
         ).astype(jnp.bfloat16)
     own_bands = bands // ranks
 
-    def place(s, carry):
+    def place(first, pieces, s, carry):
         for k in range(groups):
-            block_id = meta[2 + (position ^ k) * slots + s]
+            block_id = meta[2 + (position ^ k) * slots + first + s]
             row_band, col_band = lax.div(block_id, bands), lax.rem(block_id, bands)
             piece = lax.div(col_band, own_bands) ^ rank
             start = piece * rows + lax.rem(col_band, own_bands) * strip
-            outs[k][s] = strips[
+            pieces[k][s] = strips[
                 pl.ds(pl.multiple_of(start, strip), strip),
                 pl.ds(pl.multiple_of(row_band * block, block), block),
             ]
         return carry
 
-    lax.fori_loop(0, slots, place, 0)
-
-
-def gradient_strips(meta, cots, ctxs, slots, bands, block):
+    for i, count in enumerate(chunks):
+        pieces = outs[i * groups : (i + 1) * groups]
+        lax.fori_loop(0, count, functools.partial(place, sum(chunks[:i]), pieces), 0)
+
+
+def gradient_strips(meta, cots, ctxs, chunks, bands, block):
     groups, ranks = len(ctxs), len(cots)
     tokens, band_rows = ctxs[0].shape
     rows, strip = cots[0].shape[1], block // groups
     flops = 2 * ranks * rows * groups * tokens * band_rows
-    return pl.pallas_call(
-        functools.partial(gradient_kernel, groups, ranks, slots, bands, strip, block),
+    slots = sum(chunks)
+    outs = pl.pallas_call(
+        functools.partial(gradient_kernel, groups, ranks, chunks, bands, strip, block),
         grid_spec=pltpu.PrefetchScalarGridSpec(
             num_scalar_prefetch=1,
             grid=(),
             in_specs=[pl.BlockSpec(memory_space=pl.ANY)] * (ranks + groups),
-            out_specs=[pl.BlockSpec(memory_space=pltpu.VMEM)] * groups,
+            out_specs=[pl.BlockSpec(memory_space=pltpu.VMEM)] * (groups * len(chunks)),
             scratch_shapes=[
                 pltpu.VMEM((ranks, rows, groups * tokens), jnp.bfloat16),
                 pltpu.VMEM((groups * tokens, band_rows), jnp.bfloat16),
@@ -174,7 +178,11 @@
                 pltpu.SemaphoreType.DMA(((ranks + 1) * groups,)),
             ],
         ),
-        out_shape=[jax.ShapeDtypeStruct((slots, strip, block), jnp.bfloat16)] * groups,
+        out_shape=[
+            jax.ShapeDtypeStruct((count, strip, block), jnp.bfloat16)
+            for count in chunks
+            for _ in range(groups)
+        ],
         compiler_params=pltpu.CompilerParams(vmem_limit_bytes=48 * MIB),
         cost_estimate=pl.CostEstimate(
             flops=flops,
@@ -183,6 +191,7 @@
         ),
         name="gradient_strips",
     )(meta, *cots, *ctxs)
+    return [outs[i * groups : (i + 1) * groups] for i in range(len(chunks))]
 
 
 def gather_block(groups, strip, position, grads, turned):
@@ -219,10 +228,10 @@
         outs[k][0] = rows[pl.ds(pl.multiple_of(start, sub), sub), :]
 
 
-def directions(meta, grads, second, root_left, root_right, halves, sub):
+def directions(meta, grads, first, second, root_left, root_right, halves, sub):
     groups = len(grads)
     slots, strip, block = grads[0].shape
-    stat = pl.BlockSpec((1, 1, block, block), lambda s, meta: (0, s, 0, 0))
+    stat = pl.BlockSpec((1, 1, block, block), lambda s, meta: (0, first + s, 0, 0))
     return pl.pallas_call(
         functools.partial(direction_kernel, groups, strip, halves),
         grid_spec=pltpu.PrefetchScalarGridSpec(
@@ -247,10 +256,17 @@
     )(meta, second, root_left, root_right, *grads)
 
 
-def statistics_kernel(groups, strip, meta, left_ref, right_ref, second_ref, *refs):
-    grads = refs[:groups]
-    left_out, right_out, second_out, turned = refs[groups:]
-    gather_block(groups, strip, meta[0], grads, turned)
+def statistics_kernel(groups, strip, chunks, meta, left_ref, right_ref, second_ref, *refs):
+    grads = refs[: groups * len(chunks)]
+    left_out, right_out, second_out, turned = refs[groups * len(chunks) :]
+    slot = pl.program_id(0)
+    for i, count in enumerate(chunks):
+        first = sum(chunks[:i])
+
+        @pl.when(jnp.logical_and(slot >= first, slot < first + count))
+        def _():
+            gather_block(groups, strip, meta[0], grads[i * groups : (i + 1) * groups], turned)
+
     block = turned.shape[0]
     grad_t = turned[...]
     grad_bf16 = grad_t.T
@@ -263,16 +279,25 @@
 
 
 def statistics(meta, grads, left_stat, right_stat, second):
-    groups = len(grads)
-    slots, strip, block = grads[0].shape
+    groups, chunks = len(grads[0]), [chunk[0].shape[0] for chunk in grads]
+    _, strip, block = grads[0][0].shape
+    slots = sum(chunks)
     stat = pl.BlockSpec((1, 1, block, block), lambda s, meta: (0, s, 0, 0))
+
+    def strip_spec(first, count):
+        return pl.BlockSpec(
+            (1, strip, block), lambda s, meta: (jnp.clip(s - first, 0, count - 1), 0, 0)
+        )
+
+    strip_specs = [
+        strip_spec(sum(chunks[:i]), count) for i, count in enumerate(chunks) for _ in range(groups)
+    ]
     return pl.pallas_call(
-        functools.partial(statistics_kernel, groups, strip),
+        functools.partial(statistics_kernel, groups, strip, chunks),
         grid_spec=pltpu.PrefetchScalarGridSpec(
             num_scalar_prefetch=1,
             grid=(slots,),
-            in_specs=[stat] * 3
-            + [pl.BlockSpec((1, strip, block), lambda s, meta: (s, 0, 0))] * groups,
+            in_specs=[stat] * 3 + strip_specs,
             out_specs=[stat] * 3,
             scratch_shapes=[pltpu.VMEM((block, block), jnp.bfloat16)],
         ),
@@ -284,38 +309,41 @@
             transcendentals=0,
         ),
         name="statistics",
-    )(meta, left_stat, right_stat, second, *grads)
-
-
-def regroup_kernel(groups, slots, bands, halves, meta, *refs):
-    pieces, outs, placed = refs[:groups], refs[groups:-1], refs[-1]
-    block = pieces[0].shape[-1]
+    )(meta, left_stat, right_stat, second, *[piece for chunk in grads for piece in chunk])
+
+
+def regroup_kernel(groups, chunks, bands, halves, meta, *refs):
+    inputs, outs, placed = refs[: groups * len(chunks)], refs[groups * len(chunks) : -1], refs[-1]
+    block = inputs[0].shape[-1]
     position = meta[0]
     own_band = lax.div(position, halves)
-
-    def place(s, carry):
+    slots = sum(chunks)
+
+    def place(first, pieces, s, carry):
         for k in range(groups):
-            block_id = meta[2 + (position ^ k) * slots + s]
+            block_id = meta[2 + (position ^ k) * slots + first + s]
             row_band, col_band = lax.div(block_id, bands), lax.rem(block_id, bands)
             columns = pl.ds(pl.multiple_of(col_band * block, block), block)
             placed[row_band ^ own_band, :, columns] = pieces[k][s]
         return carry
 
-    lax.fori_loop(0, slots, place, 0)
+    for i, count in enumerate(chunks):
+        pieces = inputs[i * groups : (i + 1) * groups]
+        lax.fori_loop(0, count, functools.partial(place, sum(chunks[:i]), pieces), 0)
     for k in range(len(outs)):
         outs[k][...] = placed[k]
 
 
 def regroup(meta, pieces, bands, halves):
-    groups = len(pieces)
-    slots, sub, block = pieces[0].shape
+    groups, chunks = len(pieces[0]), [chunk[0].shape[0] for chunk in pieces]
+    _, sub, block = pieces[0][0].shape
     row_bands = groups // halves
     return pl.pallas_call(
-        functools.partial(regroup_kernel, groups, slots, bands, halves),
+        functools.partial(regroup_kernel, groups, chunks, bands, halves),
         grid_spec=pltpu.PrefetchScalarGridSpec(
             num_scalar_prefetch=1,
             grid=(),
-            in_specs=[pl.BlockSpec(memory_space=pltpu.VMEM)] * groups,
+            in_specs=[pl.BlockSpec(memory_space=pltpu.VMEM)] * (groups * len(chunks)),
             out_specs=[pl.BlockSpec(memory_space=pltpu.VMEM)] * row_bands,
             scratch_shapes=[pltpu.VMEM((row_bands, sub, bands * block), jnp.bfloat16)],
         ),
@@ -327,7 +355,7 @@
             transcendentals=0,
         ),
         name="regroup",
-    )(meta, *pieces)
+    )(meta, *[piece for chunk in pieces for piece in chunk])
 
 
 def stack_kernel(halves, meta, *refs):
@@ -406,12 +434,16 @@
         offset //= 2
     cots = [by_offset[t] for t in range(ranks)]
 
-    grads = exchange(gradient_strips(meta, cots, ctxs, slots, bands, block))
+    chunks = [slots - slots // 2, slots // 2]
+    grads = [
+        exchange(chunk) for chunk in gradient_strips(meta, cots, ctxs, chunks, bands, block)
+    ]
     halves = block // strip_rows
     sub = strip_rows * halves // groups
-    pieces = exchange(
-        directions(meta, grads, second_moment, root_left, root_right, halves, sub)
-    )
+    pieces = []
+    for i, chunk in enumerate(grads):
+        stale = (second_moment, root_left, root_right)
+        pieces.append(exchange(directions(meta, chunk, sum(chunks[:i]), *stale, halves, sub)))
     left_new, right_new, second_new = statistics(
         meta, grads, left_stat, right_stat, second_moment
     )

time: 255 us -> 242 us (0.949)
  waiting for transfers between devices: 172 us -> 127 us
  starting transfers between devices: 40.4 us -> 70.2 us
    ppermute x34 -> x48, waiting for transfers between devices: 172 us -> 127 us  [swap(): return lax.ppermute(value, axis, [(i, i ^ offset) for i in range(count)])]
    ppermute x34 -> x48, starting transfers between devices: 40.4 us -> 70.2 us  [swap(): return lax.ppermute(value, axis, [(i, i ^ offset) for i in range(count)])]
    pallas_call x1 -> x2, Pallas kernels: 11.5 us -> 12.1 us  [directions(): pl.pallas_call(functools.partial(direction_kernel, groups, strip, halves)...]
  transfers between devices with their start and end apart: 34 -> 48, of which waited for: 29 -> 27; matrix products, arithmetic and copies ran while one was open for 0% -> 0% of each run, Pallas kernels for 4% -> 9%
where the time goes in v3:
time: 242 us; the launch traced here: 241 us
  waiting for transfers between devices  127 us (52%)
  starting transfers between devices  70.2 us (29%)
  Pallas kernels  37.1 us (15%)
  local copies, waits for them, and re-layouts  5.34 us (2%)
    ppermute x48, waiting for transfers between devices, swap(): return lax.ppermute(value, axis, [(i, i ^ offset) for i in range(count)])  127 us
    ppermute x48, starting transfers between devices, swap(): return lax.ppermute(value, axis, [(i, i ^ offset) for i in range(count)])  70.2 us
    pallas_call x2, Pallas kernels, directions(): pl.pallas_call(functools.partial(direction_kernel, groups, strip, halves)...  12.1 us
    pallas_call x1, Pallas kernels, statistics(): pl.pallas_call(functools.partial(statistics_kernel, groups, strip, chunks...  10 us
    pallas_call x1, Pallas kernels, gradient_strips(): pl.pallas_call(functools.partial(gradient_kernel, groups, ranks, chunks,...  9.19 us
    unnamed x29, local copies, waits for them, and re-layouts  5.33 us
  transfers between devices with their start and end apart: 48, of which 27 were waited for; matrix products, arithmetic and copies ran while one was open for 0% of the time, Pallas kernels for 9%

profile of v3, /device:TPU:8, one launch (start us, length us, event | category | flops | bytes accessed | tf_op | source)
XLA Modules:
  0.0 241.3 jit_solution(16366424728952348104)
XLA Ops:
  7.8 2.6 %collective-permute-start.3 = (bf16[8,32,256]{2,1,0:T(8,128)(2,1)S(1)}, bf16[8,32,256]{2,1,0:T(8,128)(2,1)S(1)}, u32[]{:S(2)}, u32[]{:S(2)}) collective-permute-start(bf16[8,32,256]{2,1,0:T(8,128)(2,1)S(1)} %get-tuple-element.55), channel_id=1, source_target_pairs={{0,16},{4,20},{8,24},{12,28},{16,0},{20,4},{24,8},{28,12},{1,17},{... | collective-permute-start | bytes 393224 | tf_op jit(solution)/shard_map/ppermute | solution.py:77
  11.7 1.6 collective-permute-start.5
  16.1 9.3 %collective-permute-done.3 = bf16[8,32,256]{2,1,0:T(8,128)(2,1)S(1)} collective-permute-done((bf16[8,32,256]{2,1,0:T(8,128)(2,1)S(1)}, bf16[8,32,256]{2,1,0:T(8,128)(2,1)S(1)}, u32[]{:S(2)}, u32[]{:S(2)}) %collective-permute-start.3) | collective-permute-done | bytes 131104 | tf_op jit(solution)/shard_map/ppermute | solution.py:77
  25.4 2.8 %collective-permute-done.4 = bf16[8,32,256]{2,1,0:T(8,128)(2,1)S(1)} collective-permute-done((bf16[8,32,256]{2,1,0:T(8,128)(2,1)S(1)}, bf16[8,32,256]{2,1,0:T(8,128)(2,1)S(1)}, u32[]{:S(2)}, u32[]{:S(2)}) %collective-permute-start.4) | collective-permute-done | bytes 131104 | tf_op jit(solution)/shard_map/ppermute | solution.py:77
  28.2 2.6 %collective-permute-done.5 = bf16[8,32,256]{2,1,0:T(8,128)(2,1)S(1)} collective-permute-done((bf16[8,32,256]{2,1,0:T(8,128)(2,1)S(1)}, bf16[8,32,256]{2,1,0:T(8,128)(2,1)S(1)}, u32[]{:S(2)}, u32[]{:S(2)}) %collective-permute-start.5) | collective-permute-done | bytes 131104 | tf_op jit(solution)/shard_map/ppermute | solution.py:77
  30.8 2.5 %collective-permute-done.6 = bf16[8,32,256]{2,1,0:T(8,128)(2,1)S(1)} collective-permute-done((bf16[8,32,256]{2,1,0:T(8,128)(2,1)S(1)}, bf16[8,32,256]{2,1,0:T(8,128)(2,1)S(1)}, u32[]{:S(2)}, u32[]{:S(2)}) %collective-permute-start.6) | collective-permute-done | bytes 131104 | tf_op jit(solution)/shard_map/ppermute | solution.py:77
  34.9 3.6 %collective-permute-start.11 = (bf16[256,1024]{1,0:T(8,128)(2,1)}, bf16[256,1024]{1,0:T(8,128)(2,1)S(1)}, u32[]{:S(2)}, u32[]{:S(2)}) collective-permute-start(bf16[256,1024]{1,0:T(8,128)(2,1)} %refs_4_.1), channel_id=1, source_target_pairs={{0,8},{4,12},{8,0},{12,4},{16,24},{20,28},{24,16},{28,20},{1,9},{5... | collective-permute-start | bytes 1572872 | tf_op jit(solution)/shard_map/ppermute | solution.py:77
  39.0 17.8 %collective-permute-done.13.refs_8_ = bf16[256,1024]{1,0:T(8,128)(2,1)S(1)} collective-permute-done((bf16[256,1024]{1,0:T(8,128)(2,1)}, bf16[256,1024]{1,0:T(8,128)(2,1)S(1)}, u32[]{:S(2)}, u32[]{:S(2)}) %collective-permute-start.13) | collective-permute-done | bytes 524320 | tf_op jit(solution)/shard_map/ppermute | solution.py:77
  57.4 2.8 %collective-permute-done.11.refs_6_ = bf16[256,1024]{1,0:T(8,128)(2,1)S(1)} collective-permute-done((bf16[256,1024]{1,0:T(8,128)(2,1)}, bf16[256,1024]{1,0:T(8,128)(2,1)S(1)}, u32[]{:S(2)}, u32[]{:S(2)}) %collective-permute-start.11) | collective-permute-done | bytes 524320 | tf_op jit(solution)/shard_map/ppermute | solution.py:77
  60.2 2.5 %collective-permute-start.15 = (bf16[256,1024]{1,0:T(8,128)(2,1)S(1)}, bf16[256,1024]{1,0:T(8,128)(2,1)S(1)}, u32[]{:S(2)}, u32[]{:S(2)}) collective-permute-start(bf16[256,1024]{1,0:T(8,128)(2,1)S(1)} %collective-permute-done.13.refs_8_), channel_id=1, source_target_pairs={{0,8},{4,12},{8,0},{12,4},{16,24},{20,28},{24,16},{28,20},{1,9},{5... | collective-permute-start | bytes 1572872 | tf_op jit(solution)/shard_map/ppermute | solution.py:77
  62.7 8.9 %collective-permute-done.14.refs_9_ = bf16[256,1024]{1,0:T(8,128)(2,1)S(1)} collective-permute-done((bf16[256,1024]{1,0:T(8,128)(2,1)S(1)}, bf16[256,1024]{1,0:T(8,128)(2,1)S(1)}, u32[]{:S(2)}, u32[]{:S(2)}) %collective-permute-start.14) | collective-permute-done | bytes 524320 | tf_op jit(solution)/shard_map/ppermute | solution.py:77
  71.6 3.8 %collective-permute-start.16 = (bf16[256,1024]{1,0:T(8,128)(2,1)S(1)}, bf16[256,1024]{1,0:T(8,128)(2,1)S(1)}, u32[]{:S(2)}, u32[]{:S(2)}) collective-permute-start(bf16[256,1024]{1,0:T(8,128)(2,1)S(1)} %collective-permute-done.14.refs_9_), channel_id=1, source_target_pairs={{0,8},{4,12},{8,0},{12,4},{16,24},{20,28},{24,16},{28,20},{1,9},{5... | collective-permute-start | bytes 1572872 | tf_op jit(solution)/shard_map/ppermute | solution.py:77
  75.4 4.5 %collective-permute-done.12.refs_7_ = bf16[256,1024]{1,0:T(8,128)(2,1)S(1)} collective-permute-done((bf16[256,1024]{1,0:T(8,128)(2,1)S(1)}, bf16[256,1024]{1,0:T(8,128)(2,1)S(1)}, u32[]{:S(2)}, u32[]{:S(2)}) %collective-permute-start.12) | collective-permute-done | bytes 524320 | tf_op jit(solution)/shard_map/ppermute | solution.py:77
  79.9 6.3 %collective-permute-done.16.refs_11_ = bf16[256,1024]{1,0:T(8,128)(2,1)S(1)} collective-permute-done((bf16[256,1024]{1,0:T(8,128)(2,1)S(1)}, bf16[256,1024]{1,0:T(8,128)(2,1)S(1)}, u32[]{:S(2)}, u32[]{:S(2)}) %collective-permute-start.16) | collective-permute-done | bytes 524320 | tf_op jit(solution)/shard_map/ppermute | solution.py:77
  88.0 9.2 %gradient_strips.1 = (bf16[8,32,256]{2,1,0:T(8,128)(2,1)S(1)}, bf16[8,32,256]{2,1,0:T(8,128)(2,1)S(1)}, bf16[8,32,256]{2,1,0:T(8,128)(2,1)S(1)}, bf16[8,32,256]{...) custom-call(s32[130]{0:T(256)S(1)} %pad_add_fusion.meta, ...), custom_call_target="tpu_custom_call" | custom-call | flops 4294967296 | bytes 10485760 | tf_op jit(solution)/shard_map/gradient_strips/pallas_call | solution.py:167
  97.6 1.7 collective-permute-start.18
  99.3 1.7 collective-permute-start.24
  102.8 1.7 collective-permute-start.27
  105.6 2.2 collective-permute-start.28
  107.8 2.5 %collective-permute-start.29 = (bf16[8,32,256]{2,1,0:T(8,128)(2,1)S(1)}, bf16[8,32,256]{2,1,0:T(8,128)(2,1)S(1)}, u32[]{:S(2)}, u32[]{:S(2)}) collective-permute-start(bf16[8,32,256]{2,1,0:T(8,128)(2,1)S(1)} %get-tuple-element.73), channel_id=1, source_target_pairs={{0,24},{4,28},{8,16},{12,20},{16,8},{20,12},{24,0},{28,4},{1,25},{... | collective-permute-start | bytes 393224 | tf_op jit(solution)/shard_map/ppermute | solution.py:77
  110.8 2.5 %collective-permute-start.19 = (bf16[8,32,256]{2,1,0:T(8,128)(2,1)S(1)}, bf16[8,32,256]{2,1,0:T(8,128)(2,1)S(1)}, u32[]{:S(2)}, u32[]{:S(2)}) collective-permute-start(bf16[8,32,256]{2,1,0:T(8,128)(2,1)S(1)} %get-tuple-element.62), channel_id=1, source_target_pairs={{0,12},{4,8},{8,4},{12,0},{16,28},{20,24},{24,20},{28,16},{1,13},{... | collective-permute-start | bytes 393224 | tf_op jit(solution)/shard_map/ppermute | solution.py:77
  113.3 3.2 %collective-permute-done.27.refs_12_.refs_4_ = bf16[8,32,256]{2,1,0:T(8,128)(2,1)S(1)} collective-permute-done((bf16[8,32,256]{2,1,0:T(8,128)(2,1)S(1)}, bf16[8,32,256]{2,1,0:T(8,128)(2,1)S(1)}, u32[]{:S(2)}, u32[]{:S(2)}) %collective-permute-start.27) | collective-permute-done | bytes 131104 | tf_op jit(solution)/shard_map/ppermute | solution.py:77
  116.6 3.9 %collective-permute-start.20 = (bf16[8,32,256]{2,1,0:T(8,128)(2,1)S(1)}, bf16[8,32,256]{2,1,0:T(8,128)(2,1)S(1)}, u32[]{:S(2)}, u32[]{:S(2)}) collective-permute-start(bf16[8,32,256]{2,1,0:T(8,128)(2,1)S(1)} %get-tuple-element.63), channel_id=1, source_target_pairs={{0,16},{4,20},{8,24},{12,28},{16,0},{20,4},{24,8},{28,12},{1,17},{... | collective-permute-start | bytes 393224 | tf_op jit(solution)/shard_map/ppermute | solution.py:77
  120.5 8.2 %collective-permute-done.28.refs_13_.refs_5_ = bf16[8,32,256]{2,1,0:T(8,128)(2,1)S(1)} collective-permute-done((bf16[8,32,256]{2,1,0:T(8,128)(2,1)S(1)}, bf16[8,32,256]{2,1,0:T(8,128)(2,1)S(1)}, u32[]{:S(2)}, u32[]{:S(2)}) %collective-permute-start.28) | collective-permute-done | bytes 131104 | tf_op jit(solution)/shard_map/ppermute | solution.py:77
  128.6 4.3 %collective-permute-start.21 = (bf16[8,32,256]{2,1,0:T(8,128)(2,1)S(1)}, bf16[8,32,256]{2,1,0:T(8,128)(2,1)S(1)}, u32[]{:S(2)}, u32[]{:S(2)}) collective-permute-start(bf16[8,32,256]{2,1,0:T(8,128)(2,1)S(1)} %get-tuple-element.64), channel_id=1, source_target_pairs={{0,20},{4,16},{8,28},{12,24},{16,4},{20,0},{24,12},{28,8},{1,21},{... | collective-permute-start | bytes 393224 | tf_op jit(solution)/shard_map/ppermute | solution.py:77
  133.9 5.5 %collective-permute-done.30.refs_15_.refs_7_ = bf16[8,32,256]{2,1,0:T(8,128)(2,1)S(1)} collective-permute-done((bf16[8,32,256]{2,1,0:T(8,128)(2,1)S(1)}, bf16[8,32,256]{2,1,0:T(8,128)(2,1)S(1)}, u32[]{:S(2)}, u32[]{:S(2)}) %collective-permute-start.30) | collective-permute-done | bytes 131104 | tf_op jit(solution)/shard_map/ppermute | solution.py:77
  139.4 2.4 collective-permute-start.23
  141.9 2.2 copy-done.2
  144.0 6.0 %directions.3 = (bf16[8,32,256]{2,1,0:T(8,128)(2,1)S(1)}, bf16[8,32,256]{2,1,0:T(8,128)(2,1)S(1)}, bf16[8,32,256]{2,1,0:T(8,128)(2,1)S(1)}, bf16[8,32,256]{2,1,0...) custom-call(s32[130]{0:T(256)S(1)} %pad_add_fusion.meta, ...), custom_call_target="tpu_custom_call" | custom-call | flops 536870912 | bytes 8388608 | tf_op jit(solution)/shard_map/directions/pallas_call | solution.py:235
  150.5 3.2 %collective-permute-start.40 = (bf16[8,32,256]{2,1,0:T(8,128)(2,1)S(1)}, bf16[8,32,256]{2,1,0:T(8,128)(2,1)S(1)}, u32[]{:S(2)}, u32[]{:S(2)}) collective-permute-start(bf16[8,32,256]{2,1,0:T(8,128)(2,1)S(1)} %get-tuple-element.89), channel_id=1, source_target_pairs={{0,12},{4,8},{8,4},{12,0},{16,28},{20,24},{24,20},{28,16},{1,13},{... | collective-permute-start | bytes 393224 | tf_op jit(solution)/shard_map/ppermute | solution.py:77
  154.1 2.2 collective-permute-start.42
  156.3 6.0 %directions.2 = (bf16[8,32,256]{2,1,0:T(8,128)(2,1)S(1)}, bf16[8,32,256]{2,1,0:T(8,128)(2,1)S(1)}, bf16[8,32,256]{2,1,0:T(8,128)(2,1)S(1)}, bf16[8,32,256]{2,1,0...) custom-call(s32[130]{0:T(256)S(1)} %pad_add_fusion.meta, ...), custom_call_target="tpu_custom_call" | custom-call | flops 536870912 | bytes 8388608 | tf_op jit(solution)/shard_map/directions/pallas_call | solution.py:235
  163.2 2.4 %collective-permute-start.44 = (bf16[8,32,256]{2,1,0:T(8,128)(2,1)S(1)}, bf16[8,32,256]{2,1,0:T(8,128)(2,1)S(1)}, u32[]{:S(2)}, u32[]{:S(2)}) collective-permute-start(bf16[8,32,256]{2,1,0:T(8,128)(2,1)S(1)} %get-tuple-element.93), channel_id=1, source_target_pairs={{0,28},{4,24},{8,20},{12,16},{16,12},{20,8},{24,4},{28,0},{1,29},{... | collective-permute-start | bytes 393224 | tf_op jit(solution)/shard_map/ppermute | solution.py:77
  165.9 2.6 %collective-permute-start.32 = (bf16[8,32,256]{2,1,0:T(8,128)(2,1)S(1)}, bf16[8,32,256]{2,1,0:T(8,128)(2,1)S(1)}, u32[]{:S(2)}, u32[]{:S(2)}) collective-permute-start(bf16[8,32,256]{2,1,0:T(8,128)(2,1)S(1)} %get-tuple-element.80), channel_id=1, source_target_pairs={{0,8},{4,12},{8,0},{12,4},{16,24},{20,28},{24,16},{28,20},{1,9},{5... | collective-permute-start | bytes 393224 | tf_op jit(solution)/shard_map/ppermute | solution.py:77
  168.6 6.0 %collective-permute-done.42.refs_13_ = bf16[8,32,256]{2,1,0:T(8,128)(2,1)S(1)} collective-permute-done((bf16[8,32,256]{2,1,0:T(8,128)(2,1)S(1)}, bf16[8,32,256]{2,1,0:T(8,128)(2,1)S(1)}, u32[]{:S(2)}, u32[]{:S(2)}) %collective-permute-start.42) | collective-permute-done | bytes 131104 | tf_op jit(solution)/shard_map/ppermute | solution.py:77
  174.5 4.0 %collective-permute-start.33 = (bf16[8,32,256]{2,1,0:T(8,128)(2,1)S(1)}, bf16[8,32,256]{2,1,0:T(8,128)(2,1)S(1)}, u32[]{:S(2)}, u32[]{:S(2)}) collective-permute-start(bf16[8,32,256]{2,1,0:T(8,128)(2,1)S(1)} %get-tuple-element.81), channel_id=1, source_target_pairs={{0,12},{4,8},{8,4},{12,0},{16,28},{20,24},{24,20},{28,16},{1,13},{... | collective-permute-start | bytes 393224 | tf_op jit(solution)/shard_map/ppermute | solution.py:77
  178.9 3.3 %collective-permute-done.44.refs_15_ = bf16[8,32,256]{2,1,0:T(8,128)(2,1)S(1)} collective-permute-done((bf16[8,32,256]{2,1,0:T(8,128)(2,1)S(1)}, bf16[8,32,256]{2,1,0:T(8,128)(2,1)S(1)}, u32[]{:S(2)}, u32[]{:S(2)}) %collective-permute-start.44) | collective-permute-done | bytes 131104 | tf_op jit(solution)/shard_map/ppermute | solution.py:77
  182.2 1.6 collective-permute-start.36
  184.9 4.2 %collective-permute-done.35.refs_5_ = bf16[8,32,256]{2,1,0:T(8,128)(2,1)S(1)} collective-permute-done((bf16[8,32,256]{2,1,0:T(8,128)(2,1)S(1)}, bf16[8,32,256]{2,1,0:T(8,128)(2,1)S(1)}, u32[]{:S(2)}, u32[]{:S(2)}) %collective-permute-start.35) | collective-permute-done | bytes 131104 | tf_op jit(solution)/shard_map/ppermute | solution.py:77
  189.1 2.3 collective-permute-done.36.refs_6_
  191.3 4.2 %collective-permute-done.37.refs_7_ = bf16[8,32,256]{2,1,0:T(8,128)(2,1)S(1)} collective-permute-done((bf16[8,32,256]{2,1,0:T(8,128)(2,1)S(1)}, bf16[8,32,256]{2,1,0:T(8,128)(2,1)S(1)}, u32[]{:S(2)}, u32[]{:S(2)}) %collective-permute-start.37) | collective-permute-done | bytes 131104 | tf_op jit(solution)/shard_map/ppermute | solution.py:77
  195.6 1.6 regroup.1
  197.2 1.7 collective-permute-start.45
  200.8 10.0 %statistics.1 = (f32[1,16,256,256]{3,2,1,0:T(8,128)}, f32[1,16,256,256]{3,2,1,0:T(8,128)}, f32[1,16,256,256]{3,2,1,0:T(8,128)}) custom-call(s32[130]{0:T(256)S(1)} %pad_add_fusion.meta, f32[1,16,256,256]{3,2,1,0:T(8,128)S(1)} %copy-done.3, f32[1,16,256,256]{3,2,1,0:T(8,128)S(1)} %copy-done.4, f32[1,16,256,256]{3,2,1,0:T(8,128)S(1)} %copy-done, ...), custom_call_target="tpu_custom_call" | custom-call | flops 1073741824 | bytes 27262976 | tf_op jit(solution)/shard_map/statistics/pallas_call | solution.py:295
  210.8 4.9 %collective-permute-done.45.refs_1_ = bf16[32,8192]{1,0:T(8,128)(2,1)S(1)} collective-permute-done((bf16[32,8192]{1,0:T(8,128)(2,1)S(1)}, bf16[32,8192]{1,0:T(8,128)(2,1)S(1)}, u32[]{:S(2)}, u32[]{:S(2)}) %collective-permute-start.45) | collective-permute-done | bytes 524320 | tf_op jit(solution)/shard_map/ppermute | solution.py:77
  215.7 15.0 %collective-permute-done.46.refs_2_ = bf16[32,8192]{1,0:T(8,128)(2,1)S(1)} collective-permute-done((bf16[32,8192]{1,0:T(8,128)(2,1)S(1)}, bf16[32,8192]{1,0:T(8,128)(2,1)S(1)}, u32[]{:S(2)}, u32[]{:S(2)}) %collective-permute-start.46) | collective-permute-done | bytes 524320 | tf_op jit(solution)/shard_map/ppermute | solution.py:77
  230.6 8.1 %collective-permute-done.47.refs_3_ = bf16[32,8192]{1,0:T(8,128)(2,1)S(1)} collective-permute-done((bf16[32,8192]{1,0:T(8,128)(2,1)S(1)}, bf16[32,8192]{1,0:T(8,128)(2,1)S(1)}, u32[]{:S(2)}, u32[]{:S(2)}) %collective-permute-start.47) | collective-permute-done | bytes 524320 | tf_op jit(solution)/shard_map/ppermute | solution.py:77
  238.8 2.5 %stack_rows.1 = bf16[1,128,8192]{2,1,0:T(8,128)(2,1)} custom-call(s32[130]{0:T(256)S(1)} %pad_add_fusion.meta, bf16[32,8192]{1,0:T(8,128)(2,1)S(1)} %get-tuple-element.94.refs_0_, bf16[32,8192]{1,0:T(8,128)(2,1)S(1)} %collective-permute-done.45.refs_1_, bf16[32,8192]{1,0:T(8,128)(2,1)S(1)} %collective-permute-done.46.refs_2_, ...), custom_call_target="tpu_custom_call" | custom-call | bytes 4194304 | tf_op jit(solution)/shard_map/stack_rows/pallas_call | solution.py:374
  (86 shorter events, 25.9 us)
Async XLA Ops:
  4.2 7.5 %collective-permute-start = (bf16[8,32,256]{2,1,0:T(8,128)(2,1)S(1)}, bf16[8,32,256]{2,1,0:T(8,128)(2,1)S(1)}, u32[]{:S(2)}, u32[]{:S(2)}) collective-permute-start(bf16[8,32,256]{2,1,0:T(8,128)(2,1)S(1)} %get-tuple-element.52), channel_id=1, source_target_pairs={{0,4},{4,0},{8,12},{12,8},{16,20},{20,16},{24,28},{28,24},{1,5},{5... | collective-permute-start | bytes 393224 | tf_op jit(solution)/shard_map/ppermute | solution.py:77
  5.8 8.6 %collective-permute-start.1 = (bf16[8,32,256]{2,1,0:T(8,128)(2,1)S(1)}, bf16[8,32,256]{2,1,0:T(8,128)(2,1)S(1)}, u32[]{:S(2)}, u32[]{:S(2)}) collective-permute-start(bf16[8,32,256]{2,1,0:T(8,128)(2,1)S(1)} %get-tuple-element.53), channel_id=1, source_target_pairs={{0,8},{4,12},{8,0},{12,4},{16,24},{20,28},{24,16},{28,20},{1,9},{5... | collective-permute-start | bytes 393224 | tf_op jit(solution)/shard_map/ppermute | solution.py:77
  6.2 9.8 %collective-permute-start.2 = (bf16[8,32,256]{2,1,0:T(8,128)(2,1)S(1)}, bf16[8,32,256]{2,1,0:T(8,128)(2,1)S(1)}, u32[]{:S(2)}, u32[]{:S(2)}) collective-permute-start(bf16[8,32,256]{2,1,0:T(8,128)(2,1)S(1)} %get-tuple-element.54), channel_id=1, source_target_pairs={{0,12},{4,8},{8,4},{12,0},{16,28},{20,24},{24,20},{28,16},{1,13},{... | collective-permute-start | bytes 393224 | tf_op jit(solution)/shard_map/ppermute | solution.py:77
  7.8 17.6 %collective-permute-start.3 = (bf16[8,32,256]{2,1,0:T(8,128)(2,1)S(1)}, bf16[8,32,256]{2,1,0:T(8,128)(2,1)S(1)}, u32[]{:S(2)}, u32[]{:S(2)}) collective-permute-start(bf16[8,32,256]{2,1,0:T(8,128)(2,1)S(1)} %get-tuple-element.55), channel_id=1, source_target_pairs={{0,16},{4,20},{8,24},{12,28},{16,0},{20,4},{24,8},{28,12},{1,17},{... | collective-permute-start | bytes 393224 | tf_op jit(solution)/shard_map/ppermute | solution.py:77
  10.3 17.8 %collective-permute-start.4 = (bf16[8,32,256]{2,1,0:T(8,128)(2,1)S(1)}, bf16[8,32,256]{2,1,0:T(8,128)(2,1)S(1)}, u32[]{:S(2)}, u32[]{:S(2)}) collective-permute-start(bf16[8,32,256]{2,1,0:T(8,128)(2,1)S(1)} %get-tuple-element.56), channel_id=1, source_target_pairs={{0,20},{4,16},{8,28},{12,24},{16,4},{20,0},{24,12},{28,8},{1,21},{... | collective-permute-start | bytes 393224 | tf_op jit(solution)/shard_map/ppermute | solution.py:77
  11.7 19.1 %collective-permute-start.5 = (bf16[8,32,256]{2,1,0:T(8,128)(2,1)S(1)}, bf16[8,32,256]{2,1,0:T(8,128)(2,1)S(1)}, u32[]{:S(2)}, u32[]{:S(2)}) collective-permute-start(bf16[8,32,256]{2,1,0:T(8,128)(2,1)S(1)} %get-tuple-element.57), channel_id=1, source_target_pairs={{0,24},{4,28},{8,16},{12,20},{16,8},{20,12},{24,0},{28,4},{1,25},{... | collective-permute-start | bytes 393224 | tf_op jit(solution)/shard_map/ppermute | solution.py:77
  14.4 18.8 %collective-permute-start.6 = (bf16[8,32,256]{2,1,0:T(8,128)(2,1)S(1)}, bf16[8,32,256]{2,1,0:T(8,128)(2,1)S(1)}, u32[]{:S(2)}, u32[]{:S(2)}) collective-permute-start(bf16[8,32,256]{2,1,0:T(8,128)(2,1)S(1)} %get-tuple-element.58), channel_id=1, source_target_pairs={{0,28},{4,24},{8,20},{12,16},{16,12},{20,8},{24,4},{28,0},{1,29},{... | collective-permute-start | bytes 393224 | tf_op jit(solution)/shard_map/ppermute | solution.py:77
  33.3 24.1 %collective-permute-start.8 = (bf16[8,256,256]{2,1,0:T(8,128)(2,1)S(1)}, bf16[8,256,256]{2,1,0:T(8,128)(2,1)S(1)}, u32[]{:S(2)}, u32[]{:S(2)}) collective-permute-start(bf16[8,256,256]{2,1,0:T(8,128)(2,1)S(1)} %bitcast_dynamic-update-slice_fusion.refs_0_), channel_id=1, source_target_pairs={{0,2},{1,3},{2,0},{3,1},{4,6},{5,7},{6,4},{7,5},{8,10},{9,11},{10,... | collective-permute-start | bytes 3145736 | tf_op jit(solution)/shard_map/ppermute | solution.py:77
  34.9 21.9 %collective-permute-start.13 = (bf16[256,1024]{1,0:T(8,128)(2,1)}, bf16[256,1024]{1,0:T(8,128)(2,1)S(1)}, u32[]{:S(2)}, u32[]{:S(2)}) collective-permute-start(bf16[256,1024]{1,0:T(8,128)(2,1)} %refs_4_.1), channel_id=1, source_target_pairs={{0,16},{4,20},{8,24},{12,28},{16,0},{20,4},{24,8},{28,12},{1,17},{... | collective-permute-start | bytes 1572872 | tf_op jit(solution)/shard_map/ppermute | solution.py:77
  34.9 25.3 %collective-permute-start.11 = (bf16[256,1024]{1,0:T(8,128)(2,1)}, bf16[256,1024]{1,0:T(8,128)(2,1)S(1)}, u32[]{:S(2)}, u32[]{:S(2)}) collective-permute-start(bf16[256,1024]{1,0:T(8,128)(2,1)} %refs_4_.1), channel_id=1, source_target_pairs={{0,8},{4,12},{8,0},{12,4},{16,24},{20,28},{24,16},{28,20},{1,9},{5... | collective-permute-start | bytes 1572872 | tf_op jit(solution)/shard_map/ppermute | solution.py:77
  38.5 21.7 %collective-permute-start.10 = (bf16[256,1024]{1,0:T(8,128)(2,1)}, bf16[256,1024]{1,0:T(8,128)(2,1)S(1)}, u32[]{:S(2)}, u32[]{:S(2)}) collective-permute-start(bf16[256,1024]{1,0:T(8,128)(2,1)} %refs_4_.1), channel_id=1, source_target_pairs={{0,4},{4,0},{8,12},{12,8},{16,20},{20,16},{24,28},{28,24},{1,5},{5... | collective-permute-start | bytes 1572872 | tf_op jit(solution)/shard_map/ppermute | solution.py:77
  39.0 40.9 %collective-permute-start.7 = (bf16[8,256,256]{2,1,0:T(8,128)(2,1)S(1)}, bf16[8,256,256]{2,1,0:T(8,128)(2,1)S(1)}, u32[]{:S(2)}, u32[]{:S(2)}) collective-permute-start(bf16[8,256,256]{2,1,0:T(8,128)(2,1)S(1)} %bitcast_dynamic-update-slice_fusion.refs_0_), channel_id=1, source_target_pairs={{0,1},{1,0},{2,3},{3,2},{4,5},{5,4},{6,7},{7,6},{8,9},{9,8},{10,11... | collective-permute-start | bytes 3145736 | tf_op jit(solution)/shard_map/ppermute | solution.py:77
  56.8 14.9 %collective-permute-start.14 = (bf16[256,1024]{1,0:T(8,128)(2,1)S(1)}, bf16[256,1024]{1,0:T(8,128)(2,1)S(1)}, u32[]{:S(2)}, u32[]{:S(2)}) collective-permute-start(bf16[256,1024]{1,0:T(8,128)(2,1)S(1)} %collective-permute-done.13.refs_8_), channel_id=1, source_target_pairs={{0,4},{4,0},{8,12},{12,8},{16,20},{20,16},{24,28},{28,24},{1,5},{5... | collective-permute-start | bytes 1572872 | tf_op jit(solution)/shard_map/ppermute | solution.py:77
  57.4 28.7 %collective-permute-start.9 = (bf16[8,256,256]{2,1,0:T(8,128)(2,1)S(1)}, bf16[8,256,256]{2,1,0:T(8,128)(2,1)}, u32[]{:S(2)}, u32[]{:S(2)}) collective-permute-start(bf16[8,256,256]{2,1,0:T(8,128)(2,1)S(1)} %collective-permute-done.8.refs_2_), channel_id=1, source_target_pairs={{0,1},{1,0},{2,3},{3,2},{4,5},{5,4},{6,7},{7,6},{8,9},{9,8},{10,11... | collective-permute-start | bytes 3145736 | tf_op jit(solution)/shard_map/ppermute | solution.py:77
  60.2 19.7 %collective-permute-start.12 = (bf16[256,1024]{1,0:T(8,128)(2,1)S(1)}, bf16[256,1024]{1,0:T(8,128)(2,1)S(1)}, u32[]{:S(2)}, u32[]{:S(2)}) collective-permute-start(bf16[256,1024]{1,0:T(8,128)(2,1)S(1)} %collective-permute-done.11.refs_6_), channel_id=1, source_target_pairs={{0,4},{4,0},{8,12},{12,8},{16,20},{20,16},{24,28},{28,24},{1,5},{5... | collective-permute-start | bytes 1572872 | tf_op jit(solution)/shard_map/ppermute | solution.py:77
  60.2 19.7 %collective-permute-start.15 = (bf16[256,1024]{1,0:T(8,128)(2,1)S(1)}, bf16[256,1024]{1,0:T(8,128)(2,1)S(1)}, u32[]{:S(2)}, u32[]{:S(2)}) collective-permute-start(bf16[256,1024]{1,0:T(8,128)(2,1)S(1)} %collective-permute-done.13.refs_8_), channel_id=1, source_target_pairs={{0,8},{4,12},{8,0},{12,4},{16,24},{20,28},{24,16},{28,20},{1,9},{5... | collective-permute-start | bytes 1572872 | tf_op jit(solution)/shard_map/ppermute | solution.py:77
  71.6 14.5 %collective-permute-start.16 = (bf16[256,1024]{1,0:T(8,128)(2,1)S(1)}, bf16[256,1024]{1,0:T(8,128)(2,1)S(1)}, u32[]{:S(2)}, u32[]{:S(2)}) collective-permute-start(bf16[256,1024]{1,0:T(8,128)(2,1)S(1)} %collective-permute-done.14.refs_9_), channel_id=1, source_target_pairs={{0,8},{4,12},{8,0},{12,4},{16,24},{20,28},{24,16},{28,20},{1,9},{5... | collective-permute-start | bytes 1572872 | tf_op jit(solution)/shard_map/ppermute | solution.py:77
  97.2 5.6 %collective-permute-start.17 = (bf16[8,32,256]{2,1,0:T(8,128)(2,1)S(1)}, bf16[8,32,256]{2,1,0:T(8,128)(2,1)S(1)}, u32[]{:S(2)}, u32[]{:S(2)}) collective-permute-start(bf16[8,32,256]{2,1,0:T(8,128)(2,1)S(1)} %get-tuple-element.60), channel_id=1, source_target_pairs={{0,4},{4,0},{8,12},{12,8},{16,20},{20,16},{24,28},{28,24},{1,5},{5... | collective-permute-start | bytes 393224 | tf_op jit(solution)/shard_map/ppermute | solution.py:77
  97.6 8.0 %collective-permute-start.18 = (bf16[8,32,256]{2,1,0:T(8,128)(2,1)S(1)}, bf16[8,32,256]{2,1,0:T(8,128)(2,1)S(1)}, u32[]{:S(2)}, u32[]{:S(2)}) collective-permute-start(bf16[8,32,256]{2,1,0:T(8,128)(2,1)S(1)} %get-tuple-element.61), channel_id=1, source_target_pairs={{0,8},{4,12},{8,0},{12,4},{16,24},{20,28},{24,16},{28,20},{1,9},{5... | collective-permute-start | bytes 393224 | tf_op jit(solution)/shard_map/ppermute | solution.py:77
  99.3 8.5 %collective-permute-start.24 = (bf16[8,32,256]{2,1,0:T(8,128)(2,1)S(1)}, bf16[8,32,256]{2,1,0:T(8,128)(2,1)S(1)}, u32[]{:S(2)}, u32[]{:S(2)}) collective-permute-start(bf16[8,32,256]{2,1,0:T(8,128)(2,1)S(1)} %get-tuple-element.68), channel_id=1, source_target_pairs={{0,4},{4,0},{8,12},{12,8},{16,20},{20,16},{24,28},{28,24},{1,5},{5... | collective-permute-start | bytes 393224 | tf_op jit(solution)/shard_map/ppermute | solution.py:77
  101.0 9.3 %collective-permute-start.25 = (bf16[8,32,256]{2,1,0:T(8,128)(2,1)S(1)}, bf16[8,32,256]{2,1,0:T(8,128)(2,1)S(1)}, u32[]{:S(2)}, u32[]{:S(2)}) collective-permute-start(bf16[8,32,256]{2,1,0:T(8,128)(2,1)S(1)} %get-tuple-element.69), channel_id=1, source_target_pairs={{0,8},{4,12},{8,0},{12,4},{16,24},{20,28},{24,16},{28,20},{1,9},{5... | collective-permute-start | bytes 393224 | tf_op jit(solution)/shard_map/ppermute | solution.py:77
  101.3 9.5 %collective-permute-start.26 = (bf16[8,32,256]{2,1,0:T(8,128)(2,1)S(1)}, bf16[8,32,256]{2,1,0:T(8,128)(2,1)S(1)}, u32[]{:S(2)}, u32[]{:S(2)}) collective-permute-start(bf16[8,32,256]{2,1,0:T(8,128)(2,1)S(1)} %get-tuple-element.70), channel_id=1, source_target_pairs={{0,12},{4,8},{8,4},{12,0},{16,28},{20,24},{24,20},{28,16},{1,13},{... | collective-permute-start | bytes 393224 | tf_op jit(solution)/shard_map/ppermute | solution.py:77
  102.8 13.7 %collective-permute-start.27 = (bf16[8,32,256]{2,1,0:T(8,128)(2,1)S(1)}, bf16[8,32,256]{2,1,0:T(8,128)(2,1)S(1)}, u32[]{:S(2)}, u32[]{:S(2)}) collective-permute-start(bf16[8,32,256]{2,1,0:T(8,128)(2,1)S(1)} %get-tuple-element.71), channel_id=1, source_target_pairs={{0,16},{4,20},{8,24},{12,28},{16,0},{20,4},{24,8},{28,12},{1,17},{... | collective-permute-start | bytes 393224 | tf_op jit(solution)/shard_map/ppermute | solution.py:77
  105.6 23.0 %collective-permute-start.28 = (bf16[8,32,256]{2,1,0:T(8,128)(2,1)S(1)}, bf16[8,32,256]{2,1,0:T(8,128)(2,1)S(1)}, u32[]{:S(2)}, u32[]{:S(2)}) collective-permute-start(bf16[8,32,256]{2,1,0:T(8,128)(2,1)S(1)} %get-tuple-element.72), channel_id=1, source_target_pairs={{0,20},{4,16},{8,28},{12,24},{16,4},{20,0},{24,12},{28,8},{1,21},{... | collective-permute-start | bytes 393224 | tf_op jit(solution)/shard_map/ppermute | solution.py:77
  107.8 25.1 %collective-permute-start.29 = (bf16[8,32,256]{2,1,0:T(8,128)(2,1)S(1)}, bf16[8,32,256]{2,1,0:T(8,128)(2,1)S(1)}, u32[]{:S(2)}, u32[]{:S(2)}) collective-permute-start(bf16[8,32,256]{2,1,0:T(8,128)(2,1)S(1)} %get-tuple-element.73), channel_id=1, source_target_pairs={{0,24},{4,28},{8,16},{12,20},{16,8},{20,12},{24,0},{28,4},{1,25},{... | collective-permute-start | bytes 393224 | tf_op jit(solution)/shard_map/ppermute | solution.py:77
  110.3 29.1 %collective-permute-start.30 = (bf16[8,32,256]{2,1,0:T(8,128)(2,1)S(1)}, bf16[8,32,256]{2,1,0:T(8,128)(2,1)S(1)}, u32[]{:S(2)}, u32[]{:S(2)}) collective-permute-start(bf16[8,32,256]{2,1,0:T(8,128)(2,1)S(1)} %get-tuple-element.74), channel_id=1, source_target_pairs={{0,28},{4,24},{8,20},{12,16},{16,12},{20,8},{24,4},{28,0},{1,29},{... | collective-permute-start | bytes 393224 | tf_op jit(solution)/shard_map/ppermute | solution.py:77
  110.8 39.3 %collective-permute-start.19 = (bf16[8,32,256]{2,1,0:T(8,128)(2,1)S(1)}, bf16[8,32,256]{2,1,0:T(8,128)(2,1)S(1)}, u32[]{:S(2)}, u32[]{:S(2)}) collective-permute-start(bf16[8,32,256]{2,1,0:T(8,128)(2,1)S(1)} %get-tuple-element.62), channel_id=1, source_target_pairs={{0,12},{4,8},{8,4},{12,0},{16,28},{20,24},{24,20},{28,16},{1,13},{... | collective-permute-start | bytes 393224 | tf_op jit(solution)/shard_map/ppermute | solution.py:77
  116.6 33.9 %collective-permute-start.20 = (bf16[8,32,256]{2,1,0:T(8,128)(2,1)S(1)}, bf16[8,32,256]{2,1,0:T(8,128)(2,1)S(1)}, u32[]{:S(2)}, u32[]{:S(2)}) collective-permute-start(bf16[8,32,256]{2,1,0:T(8,128)(2,1)S(1)} %get-tuple-element.63), channel_id=1, source_target_pairs={{0,16},{4,20},{8,24},{12,28},{16,0},{20,4},{24,8},{28,12},{1,17},{... | collective-permute-start | bytes 393224 | tf_op jit(solution)/shard_map/ppermute | solution.py:77
  128.6 21.8 %collective-permute-start.21 = (bf16[8,32,256]{2,1,0:T(8,128)(2,1)S(1)}, bf16[8,32,256]{2,1,0:T(8,128)(2,1)S(1)}, u32[]{:S(2)}, u32[]{:S(2)}) collective-permute-start(bf16[8,32,256]{2,1,0:T(8,128)(2,1)S(1)} %get-tuple-element.64), channel_id=1, source_target_pairs={{0,20},{4,16},{8,28},{12,24},{16,4},{20,0},{24,12},{28,8},{1,21},{... | collective-permute-start | bytes 393224 | tf_op jit(solution)/shard_map/ppermute | solution.py:77
  132.9 20.7 %collective-permute-start.22 = (bf16[8,32,256]{2,1,0:T(8,128)(2,1)S(1)}, bf16[8,32,256]{2,1,0:T(8,128)(2,1)S(1)}, u32[]{:S(2)}, u32[]{:S(2)}) collective-permute-start(bf16[8,32,256]{2,1,0:T(8,128)(2,1)S(1)} %get-tuple-element.65), channel_id=1, source_target_pairs={{0,24},{4,28},{8,16},{12,20},{16,8},{20,12},{24,0},{28,4},{1,25},{... | collective-permute-start | bytes 393224 | tf_op jit(solution)/shard_map/ppermute | solution.py:77
  139.4 14.7 %collective-permute-start.23 = (bf16[8,32,256]{2,1,0:T(8,128)(2,1)S(1)}, bf16[8,32,256]{2,1,0:T(8,128)(2,1)S(1)}, u32[]{:S(2)}, u32[]{:S(2)}) collective-permute-start(bf16[8,32,256]{2,1,0:T(8,128)(2,1)S(1)} %get-tuple-element.66), channel_id=1, source_target_pairs={{0,28},{4,24},{8,20},{12,16},{16,12},{20,8},{24,4},{28,0},{1,29},{... | collective-permute-start | bytes 393224 | tf_op jit(solution)/shard_map/ppermute | solution.py:77
  150.1 12.3 %collective-permute-start.38 = (bf16[8,32,256]{2,1,0:T(8,128)(2,1)S(1)}, bf16[8,32,256]{2,1,0:T(8,128)(2,1)S(1)}, u32[]{:S(2)}, u32[]{:S(2)}) collective-permute-start(bf16[8,32,256]{2,1,0:T(8,128)(2,1)S(1)} %get-tuple-element.87), channel_id=1, source_target_pairs={{0,4},{4,0},{8,12},{12,8},{16,20},{20,16},{24,28},{28,24},{1,5},{5... | collective-permute-start | bytes 393224 | tf_op jit(solution)/shard_map/ppermute | solution.py:77
  150.5 12.8 %collective-permute-start.39 = (bf16[8,32,256]{2,1,0:T(8,128)(2,1)S(1)}, bf16[8,32,256]{2,1,0:T(8,128)(2,1)S(1)}, u32[]{:S(2)}, u32[]{:S(2)}) collective-permute-start(bf16[8,32,256]{2,1,0:T(8,128)(2,1)S(1)} %get-tuple-element.88), channel_id=1, source_target_pairs={{0,8},{4,12},{8,0},{12,4},{16,24},{20,28},{24,16},{28,20},{1,9},{5... | collective-permute-start | bytes 393224 | tf_op jit(solution)/shard_map/ppermute | solution.py:77
  150.5 15.2 %collective-permute-start.40 = (bf16[8,32,256]{2,1,0:T(8,128)(2,1)S(1)}, bf16[8,32,256]{2,1,0:T(8,128)(2,1)S(1)}, u32[]{:S(2)}, u32[]{:S(2)}) collective-permute-start(bf16[8,32,256]{2,1,0:T(8,128)(2,1)S(1)} %get-tuple-element.89), channel_id=1, source_target_pairs={{0,12},{4,8},{8,4},{12,0},{16,28},{20,24},{24,20},{28,16},{1,13},{... | collective-permute-start | bytes 393224 | tf_op jit(solution)/shard_map/ppermute | solution.py:77
  153.7 12.3 %collective-permute-start.41 = (bf16[8,32,256]{2,1,0:T(8,128)(2,1)S(1)}, bf16[8,32,256]{2,1,0:T(8,128)(2,1)S(1)}, u32[]{:S(2)}, u32[]{:S(2)}) collective-permute-start(bf16[8,32,256]{2,1,0:T(8,128)(2,1)S(1)} %get-tuple-element.90), channel_id=1, source_target_pairs={{0,16},{4,20},{8,24},{12,28},{16,0},{20,4},{24,8},{28,12},{1,17},{... | collective-permute-start | bytes 393224 | tf_op jit(solution)/shard_map/ppermute | solution.py:77
  154.1 20.4 %collective-permute-start.42 = (bf16[8,32,256]{2,1,0:T(8,128)(2,1)S(1)}, bf16[8,32,256]{2,1,0:T(8,128)(2,1)S(1)}, u32[]{:S(2)}, u32[]{:S(2)}) collective-permute-start(bf16[8,32,256]{2,1,0:T(8,128)(2,1)S(1)} %get-tuple-element.91), channel_id=1, source_target_pairs={{0,20},{4,16},{8,28},{12,24},{16,4},{20,0},{24,12},{28,8},{1,21},{... | collective-permute-start | bytes 393224 | tf_op jit(solution)/shard_map/ppermute | solution.py:77
  162.4 16.5 %collective-permute-start.43 = (bf16[8,32,256]{2,1,0:T(8,128)(2,1)S(1)}, bf16[8,32,256]{2,1,0:T(8,128)(2,1)S(1)}, u32[]{:S(2)}, u32[]{:S(2)}) collective-permute-start(bf16[8,32,256]{2,1,0:T(8,128)(2,1)S(1)} %get-tuple-element.92), channel_id=1, source_target_pairs={{0,24},{4,28},{8,16},{12,20},{16,8},{20,12},{24,0},{28,4},{1,25},{... | collective-permute-start | bytes 393224 | tf_op jit(solution)/shard_map/ppermute | solution.py:77
  163.2 19.0 %collective-permute-start.44 = (bf16[8,32,256]{2,1,0:T(8,128)(2,1)S(1)}, bf16[8,32,256]{2,1,0:T(8,128)(2,1)S(1)}, u32[]{:S(2)}, u32[]{:S(2)}) collective-permute-start(bf16[8,32,256]{2,1,0:T(8,128)(2,1)S(1)} %get-tuple-element.93), channel_id=1, source_target_pairs={{0,28},{4,24},{8,20},{12,16},{16,12},{20,8},{24,4},{28,0},{1,29},{... | collective-permute-start | bytes 393224 | tf_op jit(solution)/shard_map/ppermute | solution.py:77
  165.6 16.6 %collective-permute-start.31 = (bf16[8,32,256]{2,1,0:T(8,128)(2,1)S(1)}, bf16[8,32,256]{2,1,0:T(8,128)(2,1)S(1)}, u32[]{:S(2)}, u32[]{:S(2)}) collective-permute-start(bf16[8,32,256]{2,1,0:T(8,128)(2,1)S(1)} %get-tuple-element.79), channel_id=1, source_target_pairs={{0,4},{4,0},{8,12},{12,8},{16,20},{20,16},{24,28},{28,24},{1,5},{5... | collective-permute-start | bytes 393224 | tf_op jit(solution)/shard_map/ppermute | solution.py:77
  165.9 17.9 %collective-permute-start.32 = (bf16[8,32,256]{2,1,0:T(8,128)(2,1)S(1)}, bf16[8,32,256]{2,1,0:T(8,128)(2,1)S(1)}, u32[]{:S(2)}, u32[]{:S(2)}) collective-permute-start(bf16[8,32,256]{2,1,0:T(8,128)(2,1)S(1)} %get-tuple-element.80), channel_id=1, source_target_pairs={{0,8},{4,12},{8,0},{12,4},{16,24},{20,28},{24,16},{28,20},{1,9},{5... | collective-permute-start | bytes 393224 | tf_op jit(solution)/shard_map/ppermute | solution.py:77
  174.5 10.2 %collective-permute-start.33 = (bf16[8,32,256]{2,1,0:T(8,128)(2,1)S(1)}, bf16[8,32,256]{2,1,0:T(8,128)(2,1)S(1)}, u32[]{:S(2)}, u32[]{:S(2)}) collective-permute-start(bf16[8,32,256]{2,1,0:T(8,128)(2,1)S(1)} %get-tuple-element.81), channel_id=1, source_target_pairs={{0,12},{4,8},{8,4},{12,0},{16,28},{20,24},{24,20},{28,16},{1,13},{... | collective-permute-start | bytes 393224 | tf_op jit(solution)/shard_map/ppermute | solution.py:77
  178.9 6.0 %collective-permute-start.34 = (bf16[8,32,256]{2,1,0:T(8,128)(2,1)S(1)}, bf16[8,32,256]{2,1,0:T(8,128)(2,1)S(1)}, u32[]{:S(2)}, u32[]{:S(2)}) collective-permute-start(bf16[8,32,256]{2,1,0:T(8,128)(2,1)S(1)} %get-tuple-element.82), channel_id=1, source_target_pairs={{0,16},{4,20},{8,24},{12,28},{16,0},{20,4},{24,8},{28,12},{1,17},{... | collective-permute-start | bytes 393224 | tf_op jit(solution)/shard_map/ppermute | solution.py:77
  182.2 6.9 %collective-permute-start.35 = (bf16[8,32,256]{2,1,0:T(8,128)(2,1)S(1)}, bf16[8,32,256]{2,1,0:T(8,128)(2,1)S(1)}, u32[]{:S(2)}, u32[]{:S(2)}) collective-permute-start(bf16[8,32,256]{2,1,0:T(8,128)(2,1)S(1)} %get-tuple-element.83), channel_id=1, source_target_pairs={{0,20},{4,16},{8,28},{12,24},{16,4},{20,0},{24,12},{28,8},{1,21},{... | collective-permute-start | bytes 393224 | tf_op jit(solution)/shard_map/ppermute | solution.py:77
  182.2 9.1 %collective-permute-start.36 = (bf16[8,32,256]{2,1,0:T(8,128)(2,1)S(1)}, bf16[8,32,256]{2,1,0:T(8,128)(2,1)S(1)}, u32[]{:S(2)}, u32[]{:S(2)}) collective-permute-start(bf16[8,32,256]{2,1,0:T(8,128)(2,1)S(1)} %get-tuple-element.84), channel_id=1, source_target_pairs={{0,24},{4,28},{8,16},{12,20},{16,8},{20,12},{24,0},{28,4},{1,25},{... | collective-permute-start | bytes 393224 | tf_op jit(solution)/shard_map/ppermute | solution.py:77
  183.9 11.7 %collective-permute-start.37 = (bf16[8,32,256]{2,1,0:T(8,128)(2,1)S(1)}, bf16[8,32,256]{2,1,0:T(8,128)(2,1)S(1)}, u32[]{:S(2)}, u32[]{:S(2)}) collective-permute-start(bf16[8,32,256]{2,1,0:T(8,128)(2,1)S(1)} %get-tuple-element.85), channel_id=1, source_target_pairs={{0,28},{4,24},{8,20},{12,16},{16,12},{20,8},{24,4},{28,0},{1,29},{... | collective-permute-start | bytes 393224 | tf_op jit(solution)/shard_map/ppermute | solution.py:77
  197.2 18.5 %collective-permute-start.45 = (bf16[32,8192]{1,0:T(8,128)(2,1)S(1)}, bf16[32,8192]{1,0:T(8,128)(2,1)S(1)}, u32[]{:S(2)}, u32[]{:S(2)}) collective-permute-start(bf16[32,8192]{1,0:T(8,128)(2,1)S(1)} %get-tuple-element.95), channel_id=1, source_target_pairs={{0,8},{4,12},{8,0},{12,4},{16,24},{20,28},{24,16},{28,20},{1,9},{5... | collective-permute-start | bytes 1572872 | tf_op jit(solution)/shard_map/ppermute | solution.py:77
  198.9 31.8 %collective-permute-start.46 = (bf16[32,8192]{1,0:T(8,128)(2,1)S(1)}, bf16[32,8192]{1,0:T(8,128)(2,1)S(1)}, u32[]{:S(2)}, u32[]{:S(2)}) collective-permute-start(bf16[32,8192]{1,0:T(8,128)(2,1)S(1)} %get-tuple-element.96), channel_id=1, source_target_pairs={{0,16},{4,20},{8,24},{12,28},{16,0},{20,4},{24,8},{28,12},{1,17},{... | collective-permute-start | bytes 1572872 | tf_op jit(solution)/shard_map/ppermute | solution.py:77
  200.5 38.3 %collective-permute-start.47 = (bf16[32,8192]{1,0:T(8,128)(2,1)S(1)}, bf16[32,8192]{1,0:T(8,128)(2,1)S(1)}, u32[]{:S(2)}, u32[]{:S(2)}) collective-permute-start(bf16[32,8192]{1,0:T(8,128)(2,1)S(1)} %get-tuple-element.97), channel_id=1, source_target_pairs={{0,24},{4,28},{8,16},{12,20},{16,8},{20,12},{24,0},{28,4},{1,25},{... | collective-permute-start | bytes 1572872 | tf_op jit(solution)/shard_map/ppermute | solution.py:77
  (11 other events, 399.2 us)

commit v4 on v3

--- a/solution.py
+++ b/solution.py
@@ -77,67 +77,66 @@
     return lax.ppermute(value, axis, [(i, i ^ offset) for i in range(count)])
 
 
-def strip_kernel(groups, strip, meta, cot_ref, *refs):
-    outs, turned = refs[:groups], refs[groups]
-    position = meta[0]
+def prepare_kernel(pairs, block, meta, cot_ref, context_ref, *refs):
+    outs, (own, other, turned) = refs[:pairs], refs[pairs:]
+    strip, half = block // pairs, block // 2
+    pair, side = lax.div(meta[0], 2), lax.rem(meta[0], 2)
     turned[...] = cot_ref[...].T
-    for k in range(groups):
-        start = pl.multiple_of((position ^ k) * strip, strip)
+    for k in range(pairs):
+        start = pl.multiple_of((pair ^ k) * strip, strip)
         outs[k][0] = turned[pl.ds(start, strip), :]
 
-
-def cot_strips(meta, cotangent, groups, block):
+    @pl.when(pl.program_id(0) == 0)
+    def _():
+        for out, place in ((own, side), (other, side ^ 1)):
+            for r in range(out.shape[1] // half):
+                start = pl.multiple_of(r * block + place * half, half)
+                out[:, r * half : (r + 1) * half] = context_ref[:, pl.ds(start, half)]
+
+
+def prepare(meta, cotangent, context, pairs, block):
     tokens, width = cotangent.shape
-    bands, strip = width // block, block // groups
-    return pl.pallas_call(
-        functools.partial(strip_kernel, groups, strip),
+    band_rows = context.shape[1]
+    bands, strip = width // block, block // pairs
+    outs = pl.pallas_call(
+        functools.partial(prepare_kernel, pairs, block),
         grid_spec=pltpu.PrefetchScalarGridSpec(
             num_scalar_prefetch=1,
             grid=(bands,),
-            in_specs=[pl.BlockSpec((tokens, block), lambda c, meta: (0, c))],
-            out_specs=[pl.BlockSpec((1, strip, tokens), lambda c, meta: (c, 0, 0))] * groups,
+            in_specs=[
+                pl.BlockSpec((tokens, block), lambda c, meta: (0, c)),
+                pl.BlockSpec((tokens, band_rows), lambda c, meta: (0, 0)),
+            ],
+            out_specs=[pl.BlockSpec((1, strip, tokens), lambda c, meta: (c, 0, 0))] * pairs
+            + [pl.BlockSpec((tokens, band_rows // 2), lambda c, meta: (0, 0))] * 2,
             scratch_shapes=[pltpu.VMEM((block, tokens), jnp.bfloat16)],
         ),
-        out_shape=[jax.ShapeDtypeStruct((bands, strip, tokens), jnp.bfloat16)] * groups,
+        out_shape=[jax.ShapeDtypeStruct((bands, strip, tokens), jnp.bfloat16)] * pairs
+        + [jax.ShapeDtypeStruct((tokens, band_rows // 2), jnp.bfloat16)] * 2,
         compiler_params=pltpu.CompilerParams(vmem_limit_bytes=16 * MIB),
         cost_estimate=pl.CostEstimate(
-            flops=0, bytes_accessed=4 * tokens * width, transcendentals=0
-        ),
-        name="cot_strips",
-    )(meta, cotangent)
-
-
-def gradient_kernel(groups, ranks, chunks, bands, strip, block, meta, *refs):
-    cots, ctxs = refs[:ranks], refs[ranks : ranks + groups]
-    outs = refs[ranks + groups : -4]
-    lhs, rhs, strips, sems = refs[-4:]
+            flops=0, bytes_accessed=4 * tokens * (width + band_rows), transcendentals=0
+        ),
+        name="prepare",
+    )(meta, cotangent, context)
+    return outs[:pairs], outs[pairs], outs[pairs + 1]
+
+
+def gradient_kernel(groups, ranks, sources, chunks, bands, meta, *refs):
+    pairs = groups // 2
+    count = 1 + max(source for source, _ in sources)
+    cots, ctxs = refs[:count], refs[count : count + pairs]
+    outs, strips = refs[count + pairs : -1], refs[-1]
     slots = sum(chunks)
-    tokens = ctxs[0].shape[0]
-    rows = lhs.shape[1]
+    rows = cots[0].shape[1]
+    strip, part = outs[0].shape[1:]
     position, rank = meta[0], meta[1]
-    copies = []
-    for k in range(groups):
-        copies.append(
-            pltpu.make_async_copy(
-                ctxs[k], rhs.at[pl.ds(k * tokens, tokens), :], sems.at[ranks * groups + k]
-            )
-        )
+    rhs = jnp.concatenate([ctxs[k // 2][k % 2] for k in range(groups)], axis=0)
     for t in range(ranks):
-        for k in range(groups):
-            copies.append(
-                pltpu.make_async_copy(
-                    cots[t].at[k],
-                    lhs.at[t, :, pl.ds(k * tokens, tokens)],
-                    sems.at[t * groups + k],
-                )
-            )
-    for copy in copies:
-        copy.start()
-    for copy in copies:
-        copy.wait()
-    for t in range(ranks):
+        found = sources[t * groups : (t + 1) * groups]
+        lhs = jnp.concatenate([cots[source][place] for source, place in found], axis=1)
         strips[pl.ds(t * rows, rows), :] = jnp.dot(
-            lhs[t], rhs[...], preferred_element_type=jnp.float32
+            lhs, rhs, preferred_element_type=jnp.float32
         ).astype(jnp.bfloat16)
     own_bands = bands // ranks
 
@@ -149,7 +148,7 @@
             start = piece * rows + lax.rem(col_band, own_bands) * strip
             pieces[k][s] = strips[
                 pl.ds(pl.multiple_of(start, strip), strip),
-                pl.ds(pl.multiple_of(row_band * block, block), block),
+                pl.ds(pl.multiple_of(row_band * part, part), part),
             ]
         return carry
 
@@ -159,51 +158,58 @@
 
 
 def gradient_strips(meta, cots, ctxs, chunks, bands, block):
-    groups, ranks = len(ctxs), len(cots)
-    tokens, band_rows = ctxs[0].shape
-    rows, strip = cots[0].shape[1], block // groups
-    flops = 2 * ranks * rows * groups * tokens * band_rows
+    ranks, pairs = len(cots), len(ctxs)
+    groups = 2 * pairs
+    sources, first = [], 0
+    for own, *other in cots:
+        places = [(first + 1 + i, n) for i, piece in enumerate(other) for n in range(piece.shape[0])]
+        for pair in range(pairs):
+            sources += [(first, pair), places[pair]]
+        first += 1 + len(other)
+    _, tokens, band_rows = ctxs[0].shape
+    rows = cots[0][0].shape[1]
+    strip, part = block // pairs, block // 2
     slots = sum(chunks)
     outs = pl.pallas_call(
-        functools.partial(gradient_kernel, groups, ranks, chunks, bands, strip, block),
+        functools.partial(gradient_kernel, groups, ranks, sources, chunks, bands),
         grid_spec=pltpu.PrefetchScalarGridSpec(
             num_scalar_prefetch=1,
             grid=(),
-            in_specs=[pl.BlockSpec(memory_space=pl.ANY)] * (ranks + groups),
+            in_specs=[pl.BlockSpec(memory_space=pltpu.VMEM)] * (first + pairs),
             out_specs=[pl.BlockSpec(memory_space=pltpu.VMEM)] * (groups * len(chunks)),
-            scratch_shapes=[
-                pltpu.VMEM((ranks, rows, groups * tokens), jnp.bfloat16),
-                pltpu.VMEM((groups * tokens, band_rows), jnp.bfloat16),
-                pltpu.VMEM((ranks * rows, band_rows), jnp.bfloat16),
-                pltpu.SemaphoreType.DMA(((ranks + 1) * groups,)),
-            ],
+            scratch_shapes=[pltpu.VMEM((ranks * rows, band_rows), jnp.bfloat16)],
         ),
         out_shape=[
-            jax.ShapeDtypeStruct((count, strip, block), jnp.bfloat16)
+            jax.ShapeDtypeStruct((count, strip, part), jnp.bfloat16)
             for count in chunks
             for _ in range(groups)
         ],
-        compiler_params=pltpu.CompilerParams(vmem_limit_bytes=48 * MIB),
-        cost_estimate=pl.CostEstimate(
-            flops=flops,
-            bytes_accessed=2 * groups * (ranks * rows * tokens + tokens * band_rows + slots * strip * block),
+        compiler_params=pltpu.CompilerParams(vmem_limit_bytes=32 * MIB),
+        cost_estimate=pl.CostEstimate(
+            flops=2 * ranks * rows * groups * tokens * band_rows,
+            bytes_accessed=2
+            * groups
+            * (ranks * rows * tokens + tokens * band_rows + slots * strip * part),
             transcendentals=0,
         ),
         name="gradient_strips",
-    )(meta, *cots, *ctxs)
+    )(meta, *[piece for rank in cots for piece in rank], *ctxs)
     return [outs[i * groups : (i + 1) * groups] for i in range(len(chunks))]
 
 
-def gather_block(groups, strip, position, grads, turned):
-    for k in range(groups):
-        start = pl.multiple_of((position ^ k) * strip, strip)
-        turned[pl.ds(start, strip), :] = grads[k][0]
-
-
-def direction_kernel(groups, strip, halves, meta, second_ref, left_ref, right_ref, *refs):
+def gather_block(position, grads, turned):
+    for k, piece in enumerate(grads):
+        _, strip, part = piece.shape
+        middle = position ^ k
+        rows = pl.ds(pl.multiple_of(lax.div(middle, 2) * strip, strip), strip)
+        columns = pl.ds(pl.multiple_of(lax.rem(middle, 2) * part, part), part)
+        turned[rows, columns] = piece[0]
+
+
+def direction_kernel(groups, halves, meta, second_ref, left_ref, right_ref, *refs):
     grads, outs, turned, rows = refs[:groups], refs[groups : 2 * groups], refs[-2], refs[-1]
     position = meta[0]
-    gather_block(groups, strip, position, grads, turned)
+    gather_block(position, grads, turned)
     grad_bf16 = turned[...].T
     grad = grad_bf16.astype(jnp.float32)
     second = decay_rate * second_ref[0, 0] + (1.0 - decay_rate) * grad * grad
@@ -230,15 +236,16 @@
 
 def directions(meta, grads, first, second, root_left, root_right, halves, sub):
     groups = len(grads)
-    slots, strip, block = grads[0].shape
+    slots, strip, part = grads[0].shape
+    block = second.shape[-1]
     stat = pl.BlockSpec((1, 1, block, block), lambda s, meta: (0, first + s, 0, 0))
     return pl.pallas_call(
-        functools.partial(direction_kernel, groups, strip, halves),
+        functools.partial(direction_kernel, groups, halves),
         grid_spec=pltpu.PrefetchScalarGridSpec(
             num_scalar_prefetch=1,
             grid=(slots,),
             in_specs=[stat] * 3
-            + [pl.BlockSpec((1, strip, block), lambda s, meta: (s, 0, 0))] * groups,
+            + [pl.BlockSpec((1, strip, part), lambda s, meta: (s, 0, 0))] * groups,
             out_specs=[pl.BlockSpec((1, sub, block), lambda s, meta: (s, 0, 0))] * groups,
             scratch_shapes=[
                 pltpu.VMEM((block, block), jnp.bfloat16),
@@ -256,7 +263,7 @@
     )(meta, second, root_left, root_right, *grads)
 
 
-def statistics_kernel(groups, strip, chunks, meta, left_ref, right_ref, second_ref, *refs):
+def statistics_kernel(groups, chunks, meta, left_ref, right_ref, second_ref, *refs):
     grads = refs[: groups * len(chunks)]
     left_out, right_out, second_out, turned = refs[groups * len(chunks) :]
     slot = pl.program_id(0)
@@ -265,7 +272,7 @@
 
         @pl.when(jnp.logical_and(slot >= first, slot < first + count))
         def _():
-            gather_block(groups, strip, meta[0], grads[i * groups : (i + 1) * groups], turned)
+            gather_block(meta[0], grads[i * groups : (i + 1) * groups], turned)
 
     block = turned.shape[0]
     grad_t = turned[...]
@@ -280,20 +287,21 @@
 
 def statistics(meta, grads, left_stat, right_stat, second):
     groups, chunks = len(grads[0]), [chunk[0].shape[0] for chunk in grads]
-    _, strip, block = grads[0][0].shape
+    _, strip, part = grads[0][0].shape
+    block = second.shape[-1]
     slots = sum(chunks)
     stat = pl.BlockSpec((1, 1, block, block), lambda s, meta: (0, s, 0, 0))
 
     def strip_spec(first, count):
         return pl.BlockSpec(
-            (1, strip, block), lambda s, meta: (jnp.clip(s - first, 0, count - 1), 0, 0)
+            (1, strip, part), lambda s, meta: (jnp.clip(s - first, 0, count - 1), 0, 0)
         )
 
     strip_specs = [
         strip_spec(sum(chunks[:i]), count) for i, count in enumerate(chunks) for _ in range(groups)
     ]
     return pl.pallas_call(
-        functools.partial(statistics_kernel, groups, strip, chunks),
+        functools.partial(statistics_kernel, groups, chunks),
         grid_spec=pltpu.PrefetchScalarGridSpec(
             num_scalar_prefetch=1,
             grid=(slots,),
@@ -390,25 +398,6 @@
 
 def exchange(pieces, stride=1):
     return [pieces[0]] + [swap(pieces[k], "fsdp", k * stride) for k in range(1, len(pieces))]
-
-
-def gather_relayed(value):
-    groups = lax.axis_size("fsdp")
-    found = [value] + [None] * (groups - 1)
-    far = groups // 2
-    found[far] = swap(value, "fsdp", far)
-    step = 1
-    while step < far:
-        found[step] = swap(value, "fsdp", step)
-        for k in range(1, step):
-            found[step + k] = swap(found[step], "fsdp", k)
-        step *= 2
-    step = 1
-    while step < far:
-        for k in range(step):
-            found[far + step + k] = swap(found[far + k], "fsdp", step)
-        step *= 2
-    return found
 
 
 def strip_plan(
@@ -422,17 +411,39 @@
     place = jnp.stack([lax.axis_index("fsdp"), lax.axis_index("tensor")]).astype(jnp.int32)
     meta = jnp.concatenate([place, block_table[0]])
 
-    strips = exchange(cot_strips(meta, cotangent, groups, block))
-    ctxs = gather_relayed(context)
-    tokens = context.shape[0]
-    cots = [jnp.stack(strips).reshape(groups, -1, tokens)]
+    pairs, tokens = groups // 2, context.shape[0]
+    pairs, tokens = groups // 2, context.shape[0]
+    strips, own, other = prepare(meta, cotangent, context, pairs, block)
+    strips = exchange(strips, 2)
+    other = swap(other, "fsdp", 1)
+    strips, other = lax.optimization_barrier((strips, other))
+    strips = jnp.stack(strips).reshape(pairs, -1, tokens)
+    ctxs = [jnp.stack([own, other])] + [None] * (pairs - 1)
+    far = pairs // 2
+    ctxs[far] = swap(ctxs[0], "fsdp", 2 * far)
+    step = 1
+    while step < far:
+        for k in range(step):
+            ctxs[step + k] = swap(ctxs[k], "fsdp", 2 * step)
+            ctxs[far + step + k] = swap(ctxs[far + k], "fsdp", 2 * step)
+        step *= 2
+    by_pair = swap(strips, "fsdp", 1)
+    cots = {0: [strips, by_pair]}
     offset = ranks // 2
-    by_offset = {0: cots[0]}
     while offset:
-        for known in list(by_offset):
-            by_offset[known ^ offset] = swap(by_offset[known], "tensor", offset)
+        for known in list(cots):
+            here = cots[known]
+            if known == 0 and offset == ranks // 2:
+                there = [swap(strips, "tensor", offset)]
+                there.append(swap(by_pair[:far], "tensor", offset))
+                there.append(swap(there[0][far:], "fsdp", 1))
+            else:
+                if known:
+                    here[0], _ = lax.optimization_barrier((here[0], here[1]))
+                there = [swap(piece, "tensor", offset) for piece in here]
+            cots[known ^ offset] = there
         offset //= 2
-    cots = [by_offset[t] for t in range(ranks)]
+    cots = [cots[t] for t in range(ranks)]
 
     chunks = [slots - slots // 2, slots // 2]
     grads = [
@@ -457,7 +468,7 @@
     strip_rows = context.shape[1] // groups
     powers = groups & (groups - 1) == 0 and ranks & (ranks - 1) == 0
     whole = block % strip_rows == 0 and cotangent.shape[1] % block == 0
-    even = block % (16 * groups) == 0
+    even = block % (16 * groups) == 0 and block == 2 * strip_rows and groups >= 8
     plan = strip_plan if powers and even and whole else general_plan
     return plan(context, cotangent, block_table, left_stat, *rest)
 

time: 242 us -> 236 us (0.975)
  starting transfers between devices: 70.2 us -> 59.5 us
  waiting for transfers between devices: 127 us -> 136 us
  local copies, waits for them, and re-layouts: 5.34 us -> 2.36 us
    ppermute x48 -> x47, starting transfers between devices: 70.2 us -> 59.5 us  [swap(): return lax.ppermute(value, axis, [(i, i ^ offset) for i in range(count)])]
    ppermute x48 -> x47, waiting for transfers between devices: 127 us -> 136 us  [swap(): return lax.ppermute(value, axis, [(i, i ^ offset) for i in range(count)])]
    unnamed x29 -> x14, local copies, waits for them, and re-layouts: 5.33 us -> 2.29 us
  transfers between devices with their start and end apart: 48 -> 47, of which waited for: 27 -> 24; matrix products, arithmetic and copies ran while one was open for 0% -> 0% of each run, Pallas kernels for 9% -> 10%
where the time goes in v4:
time: 236 us; the launch traced here: 235 us
  waiting for transfers between devices  136 us (58%)
  starting transfers between devices  59.5 us (25%)
  Pallas kernels  35.4 us (15%)
  local copies, waits for them, and re-layouts  2.36 us (1%)
    ppermute x47, waiting for transfers between devices, swap(): return lax.ppermute(value, axis, [(i, i ^ offset) for i in range(count)])  136 us
    ppermute x47, starting transfers between devices, swap(): return lax.ppermute(value, axis, [(i, i ^ offset) for i in range(count)])  59.5 us
    pallas_call x2, Pallas kernels, directions(): pl.pallas_call(functools.partial(direction_kernel, groups, halves), grid_...  12.6 us
    pallas_call x1, Pallas kernels, statistics(): pl.pallas_call(functools.partial(statistics_kernel, groups, chunks), grid...  10.4 us
    pallas_call x1, Pallas kernels, gradient_strips(): pl.pallas_call(functools.partial(gradient_kernel, groups, ranks, sources,...  6.51 us
  transfers between devices with their start and end apart: 47, of which 24 were waited for; matrix products, arithmetic and copies ran while one was open for 0% of the time, Pallas kernels for 10%

profile of v4, /device:TPU:8, one launch (start us, length us, event | category | flops | bytes accessed | tf_op | source)
XLA Modules:
  0.0 235.4 jit_solution(18334263537569628793)
XLA Ops:
  3.6 1.7 prepare.1
  5.5 3.0 %collective-permute-start.1 = (bf16[8,64,256]{2,1,0:T(8,128)(2,1)S(1)}, bf16[8,64,256]{2,1,0:T(8,128)(2,1)S(1)}, u32[]{:S(2)}, u32[]{:S(2)}) collective-permute-start(bf16[8,64,256]{2,1,0:T(8,128)(2,1)S(1)} %get-tuple-element.57), channel_id=1, source_target_pairs={{0,16},{4,20},{8,24},{12,28},{16,0},{20,4},{24,8},{28,12},{1,17},{... | collective-permute-start | bytes 786440 | tf_op jit(solution)/shard_map/ppermute | solution.py:77
  8.9 1.5 collective-permute-start.3
  10.4 5.7 %collective-permute-done = bf16[8,64,256]{2,1,0:T(8,128)(2,1)S(1)} collective-permute-done((bf16[8,64,256]{2,1,0:T(8,128)(2,1)S(1)}, bf16[8,64,256]{2,1,0:T(8,128)(2,1)S(1)}, u32[]{:S(2)}, u32[]{:S(2)}) %collective-permute-start) | collective-permute-done | bytes 262176 | tf_op jit(solution)/shard_map/ppermute | solution.py:77
  16.1 10.3 %collective-permute-done.1 = bf16[8,64,256]{2,1,0:T(8,128)(2,1)S(1)} collective-permute-done((bf16[8,64,256]{2,1,0:T(8,128)(2,1)S(1)}, bf16[8,64,256]{2,1,0:T(8,128)(2,1)S(1)}, u32[]{:S(2)}, u32[]{:S(2)}) %collective-permute-start.1) | collective-permute-done | bytes 262176 | tf_op jit(solution)/shard_map/ppermute | solution.py:77
  26.4 5.1 %collective-permute-done.2 = bf16[8,64,256]{2,1,0:T(8,128)(2,1)S(1)} collective-permute-done((bf16[8,64,256]{2,1,0:T(8,128)(2,1)S(1)}, bf16[8,64,256]{2,1,0:T(8,128)(2,1)S(1)}, u32[]{:S(2)}, u32[]{:S(2)}) %collective-permute-start.2) | collective-permute-done | bytes 262176 | tf_op jit(solution)/shard_map/ppermute | solution.py:77
  31.7 1.6 collective-permute-start.4
  33.3 1.5 collective-permute-start.7
  34.9 20.6 %collective-permute-done.4.refs_1_ = bf16[4,512,256]{2,1,0:T(8,128)(2,1)S(1)} collective-permute-done((bf16[4,512,256]{2,1,0:T(8,128)(2,1)S(1)}, bf16[4,512,256]{2,1,0:T(8,128)(2,1)S(1)}, u32[]{:S(2)}, u32[]{:S(2)}) %collective-permute-start.4) | collective-permute-done | bytes 1048608 | tf_op jit(solution)/shard_map/ppermute | solution.py:77
  55.6 1.6 collective-permute-start.8
  57.1 2.3 collective-permute-start.15
  60.8 7.2 %collective-permute-done.8.refs_5_ = bf16[2,512,256]{2,1,0:T(8,128)(2,1)S(1)} collective-permute-done((bf16[2,512,256]{2,1,0:T(8,128)(2,1)S(1)}, bf16[2,512,256]{2,1,0:T(8,128)(2,1)S(1)}, u32[]{:S(2)}, u32[]{:S(2)}) %collective-permute-start.8) | collective-permute-done | bytes 524320 | tf_op jit(solution)/shard_map/ppermute | solution.py:77
  68.0 4.0 %collective-permute-done.13.refs_11_ = bf16[2,256,512]{2,1,0:T(8,128)(2,1)S(1)} collective-permute-done((bf16[2,256,512]{2,1,0:T(8,128)(2,1)S(1)}, bf16[2,256,512]{2,1,0:T(8,128)(2,1)S(1)}, u32[]{:S(2)}, u32[]{:S(2)}) %collective-permute-start.13) | collective-permute-done | bytes 524320 | tf_op jit(solution)/shard_map/ppermute | solution.py:77
  73.4 6.3 %collective-permute-done.15.refs_13_ = bf16[2,256,512]{2,1,0:T(8,128)(2,1)S(1)} collective-permute-done((bf16[2,256,512]{2,1,0:T(8,128)(2,1)S(1)}, bf16[2,256,512]{2,1,0:T(8,128)(2,1)S(1)}, u32[]{:S(2)}, u32[]{:S(2)}) %collective-permute-start.15) | collective-permute-done | bytes 524320 | tf_op jit(solution)/shard_map/ppermute | solution.py:77
  79.7 1.9 collective-permute-done.11.refs_8_
  81.6 6.5 %gradient_strips.1 = (bf16[8,64,128]{2,1,0:T(8,128)(2,1)S(1)}, bf16[8,64,128]{2,1,0:T(8,128)(2,1)S(1)}, bf16[8,64,128]{2,1,0:T(8,128)(2,1)S(1)}, bf16[8,64,128]{...) custom-call(s32[130]{0:T(256)S(1)} %pad_add_fusion.meta, ...), custom_call_target="tpu_custom_call" | custom-call | flops 4294967296 | bytes 12582912 | tf_op jit(solution)/shard_map/gradient_strips/pallas_call | solution.py:173
  88.1 1.6 collective-permute-start.16
  90.9 1.5 collective-permute-start.23
  92.4 2.0 collective-permute-start.25
  94.4 2.2 collective-permute-start.26
  96.6 1.6 collective-permute-start.27
  98.2 1.7 collective-permute-start.28
  100.9 1.6 collective-permute-start.29
  103.0 3.4 %collective-permute-start.18 = (bf16[8,64,128]{2,1,0:T(8,128)(2,1)S(1)}, bf16[8,64,128]{2,1,0:T(8,128)(2,1)S(1)}, u32[]{:S(2)}, u32[]{:S(2)}) collective-permute-start(bf16[8,64,128]{2,1,0:T(8,128)(2,1)S(1)} %get-tuple-element.70), channel_id=1, source_target_pairs={{0,12},{4,8},{8,4},{12,0},{16,28},{20,24},{24,20},{28,16},{1,13},{... | collective-permute-start | bytes 393224 | tf_op jit(solution)/shard_map/ppermute | solution.py:77
  106.4 4.6 %collective-permute-done.26.refs_12_.refs_4_ = bf16[8,64,128]{2,1,0:T(8,128)(2,1)S(1)} collective-permute-done((bf16[8,64,128]{2,1,0:T(8,128)(2,1)S(1)}, bf16[8,64,128]{2,1,0:T(8,128)(2,1)S(1)}, u32[]{:S(2)}, u32[]{:S(2)}) %collective-permute-start.26) | collective-permute-done | bytes 131104 | tf_op jit(solution)/shard_map/ppermute | solution.py:77
  111.0 3.9 %collective-permute-start.19 = (bf16[8,64,128]{2,1,0:T(8,128)(2,1)S(1)}, bf16[8,64,128]{2,1,0:T(8,128)(2,1)S(1)}, u32[]{:S(2)}, u32[]{:S(2)}) collective-permute-start(bf16[8,64,128]{2,1,0:T(8,128)(2,1)S(1)} %get-tuple-element.71), channel_id=1, source_target_pairs={{0,16},{4,20},{8,24},{12,28},{16,0},{20,4},{24,8},{28,12},{1,17},{... | collective-permute-start | bytes 393224 | tf_op jit(solution)/shard_map/ppermute | solution.py:77
  114.9 6.5 %collective-permute-done.27.refs_13_.refs_5_ = bf16[8,64,128]{2,1,0:T(8,128)(2,1)S(1)} collective-permute-done((bf16[8,64,128]{2,1,0:T(8,128)(2,1)S(1)}, bf16[8,64,128]{2,1,0:T(8,128)(2,1)S(1)}, u32[]{:S(2)}, u32[]{:S(2)}) %collective-permute-start.27) | collective-permute-done | bytes 131104 | tf_op jit(solution)/shard_map/ppermute | solution.py:77
  121.4 4.4 %collective-permute-start.20 = (bf16[8,64,128]{2,1,0:T(8,128)(2,1)S(1)}, bf16[8,64,128]{2,1,0:T(8,128)(2,1)S(1)}, u32[]{:S(2)}, u32[]{:S(2)}) collective-permute-start(bf16[8,64,128]{2,1,0:T(8,128)(2,1)S(1)} %get-tuple-element.72), channel_id=1, source_target_pairs={{0,20},{4,16},{8,28},{12,24},{16,4},{20,0},{24,12},{28,8},{1,21},{... | collective-permute-start | bytes 393224 | tf_op jit(solution)/shard_map/ppermute | solution.py:77
  127.4 5.9 %collective-permute-done.29.refs_15_.refs_7_ = bf16[8,64,128]{2,1,0:T(8,128)(2,1)S(1)} collective-permute-done((bf16[8,64,128]{2,1,0:T(8,128)(2,1)S(1)}, bf16[8,64,128]{2,1,0:T(8,128)(2,1)S(1)}, u32[]{:S(2)}, u32[]{:S(2)}) %collective-permute-start.29) | collective-permute-done | bytes 131104 | tf_op jit(solution)/shard_map/ppermute | solution.py:77
  133.4 6.3 %directions.3 = (bf16[8,32,256]{2,1,0:T(8,128)(2,1)S(1)}, bf16[8,32,256]{2,1,0:T(8,128)(2,1)S(1)}, bf16[8,32,256]{2,1,0:T(8,128)(2,1)S(1)}, bf16[8,32,256]{2,1,0...) custom-call(s32[130]{0:T(256)S(1)} %pad_add_fusion.meta, ...), custom_call_target="tpu_custom_call" | custom-call | flops 536870912 | bytes 8388608 | tf_op jit(solution)/shard_map/directions/pallas_call | solution.py:242
  139.7 1.6 collective-permute-start.37
  141.3 2.0 collective-permute-start.39
  143.3 2.5 %collective-permute-start.40 = (bf16[8,32,256]{2,1,0:T(8,128)(2,1)S(1)}, bf16[8,32,256]{2,1,0:T(8,128)(2,1)S(1)}, u32[]{:S(2)}, u32[]{:S(2)}) collective-permute-start(bf16[8,32,256]{2,1,0:T(8,128)(2,1)S(1)} %get-tuple-element.98), channel_id=1, source_target_pairs={{0,16},{4,20},{8,24},{12,28},{16,0},{20,4},{24,8},{28,12},{1,17},{... | collective-permute-start | bytes 393224 | tf_op jit(solution)/shard_map/ppermute | solution.py:77
  145.8 2.1 collective-permute-done.22.refs_7_
  147.9 6.3 %directions.2 = (bf16[8,32,256]{2,1,0:T(8,128)(2,1)S(1)}, bf16[8,32,256]{2,1,0:T(8,128)(2,1)S(1)}, bf16[8,32,256]{2,1,0:T(8,128)(2,1)S(1)}, bf16[8,32,256]{2,1,0...) custom-call(s32[130]{0:T(256)S(1)} %pad_add_fusion.meta, ...), custom_call_target="tpu_custom_call" | custom-call | flops 536870912 | bytes 8388608 | tf_op jit(solution)/shard_map/directions/pallas_call | solution.py:242
  155.5 1.8 collective-permute-start.43
  157.8 4.2 %collective-permute-start.31 = (bf16[8,32,256]{2,1,0:T(8,128)(2,1)S(1)}, bf16[8,32,256]{2,1,0:T(8,128)(2,1)S(1)}, u32[]{:S(2)}, u32[]{:S(2)}) collective-permute-start(bf16[8,32,256]{2,1,0:T(8,128)(2,1)S(1)} %get-tuple-element.88), channel_id=1, source_target_pairs={{0,8},{4,12},{8,0},{12,4},{16,24},{20,28},{24,16},{28,20},{1,9},{5... | collective-permute-start | bytes 393224 | tf_op jit(solution)/shard_map/ppermute | solution.py:77
  162.3 4.1 %collective-permute-done.42.refs_14_ = bf16[8,32,256]{2,1,0:T(8,128)(2,1)S(1)} collective-permute-done((bf16[8,32,256]{2,1,0:T(8,128)(2,1)S(1)}, bf16[8,32,256]{2,1,0:T(8,128)(2,1)S(1)}, u32[]{:S(2)}, u32[]{:S(2)}) %collective-permute-start.42) | collective-permute-done | bytes 131104 | tf_op jit(solution)/shard_map/ppermute | solution.py:77
  166.4 8.0 %collective-permute-done.43.refs_15_ = bf16[8,32,256]{2,1,0:T(8,128)(2,1)S(1)} collective-permute-done((bf16[8,32,256]{2,1,0:T(8,128)(2,1)S(1)}, bf16[8,32,256]{2,1,0:T(8,128)(2,1)S(1)}, u32[]{:S(2)}, u32[]{:S(2)}) %collective-permute-start.43) | collective-permute-done | bytes 131104 | tf_op jit(solution)/shard_map/ppermute | solution.py:77
  176.7 4.5 %collective-permute-done.34.refs_5_ = bf16[8,32,256]{2,1,0:T(8,128)(2,1)S(1)} collective-permute-done((bf16[8,32,256]{2,1,0:T(8,128)(2,1)S(1)}, bf16[8,32,256]{2,1,0:T(8,128)(2,1)S(1)}, u32[]{:S(2)}, u32[]{:S(2)}) %collective-permute-start.34) | collective-permute-done | bytes 131104 | tf_op jit(solution)/shard_map/ppermute | solution.py:77
  181.3 4.6 %collective-permute-done.35.refs_6_ = bf16[8,32,256]{2,1,0:T(8,128)(2,1)S(1)} collective-permute-done((bf16[8,32,256]{2,1,0:T(8,128)(2,1)S(1)}, bf16[8,32,256]{2,1,0:T(8,128)(2,1)S(1)}, u32[]{:S(2)}, u32[]{:S(2)}) %collective-permute-start.35) | collective-permute-done | bytes 131104 | tf_op jit(solution)/shard_map/ppermute | solution.py:77
  185.9 1.8 collective-permute-done.36.refs_7_
  187.7 1.6 regroup.1
  189.4 2.5 %collective-permute-start.45 = (bf16[32,8192]{1,0:T(8,128)(2,1)S(1)}, bf16[32,8192]{1,0:T(8,128)(2,1)S(1)}, u32[]{:S(2)}, u32[]{:S(2)}) collective-permute-start(bf16[32,8192]{1,0:T(8,128)(2,1)S(1)} %get-tuple-element.104), channel_id=1, source_target_pairs={{0,16},{4,20},{8,24},{12,28},{16,0},{20,4},{24,8},{28,12},{1,17},{... | collective-permute-start | bytes 1572872 | tf_op jit(solution)/shard_map/ppermute | solution.py:77
  192.9 10.4 %statistics.1 = (f32[1,16,256,256]{3,2,1,0:T(8,128)}, f32[1,16,256,256]{3,2,1,0:T(8,128)}, f32[1,16,256,256]{3,2,1,0:T(8,128)}) custom-call(s32[130]{0:T(256)S(1)} %pad_add_fusion.meta, f32[1,16,256,256]{3,2,1,0:T(8,128)S(1)} %copy-done.3, f32[1,16,256,256]{3,2,1,0:T(8,128)S(1)} %copy-done.4, f32[1,16,256,256]{3,2,1,0:T(8,128)S(1)} %copy-done, ...), custom_call_target="tpu_custom_call" | custom-call | flops 1073741824 | bytes 27262976 | tf_op jit(solution)/shard_map/statistics/pallas_call | solution.py:303
  204.2 21.2 %collective-permute-done.45.refs_2_ = bf16[32,8192]{1,0:T(8,128)(2,1)S(1)} collective-permute-done((bf16[32,8192]{1,0:T(8,128)(2,1)S(1)}, bf16[32,8192]{1,0:T(8,128)(2,1)S(1)}, u32[]{:S(2)}, u32[]{:S(2)}) %collective-permute-start.45) | collective-permute-done | bytes 524320 | tf_op jit(solution)/shard_map/ppermute | solution.py:77
  225.4 7.4 %collective-permute-done.46.refs_3_ = bf16[32,8192]{1,0:T(8,128)(2,1)S(1)} collective-permute-done((bf16[32,8192]{1,0:T(8,128)(2,1)S(1)}, bf16[32,8192]{1,0:T(8,128)(2,1)S(1)}, u32[]{:S(2)}, u32[]{:S(2)}) %collective-permute-start.46) | collective-permute-done | bytes 524320 | tf_op jit(solution)/shard_map/ppermute | solution.py:77
  232.8 2.5 %stack_rows.1 = bf16[1,128,8192]{2,1,0:T(8,128)(2,1)} custom-call(s32[130]{0:T(256)S(1)} %pad_add_fusion.meta, bf16[32,8192]{1,0:T(8,128)(2,1)S(1)} %get-tuple-element.102.refs_0_, bf16[32,8192]{1,0:T(8,128)(2,1)S(1)} %collective-permute-done.44.refs_1_, bf16[32,8192]{1,0:T(8,128)(2,1)S(1)} %collective-permute-done.45.refs_2_, ...), custom_call_target="tpu_custom_call" | custom-call | bytes 4194304 | tf_op jit(solution)/shard_map/stack_rows/pallas_call | solution.py:382
  (72 shorter events, 17.2 us)
Async XLA Ops:
  5.4 10.8 %collective-permute-start = (bf16[8,64,256]{2,1,0:T(8,128)(2,1)S(1)}, bf16[8,64,256]{2,1,0:T(8,128)(2,1)S(1)}, u32[]{:S(2)}, u32[]{:S(2)}) collective-permute-start(bf16[8,64,256]{2,1,0:T(8,128)(2,1)S(1)} %get-tuple-element.56), channel_id=1, source_target_pairs={{0,8},{4,12},{8,0},{12,4},{16,24},{20,28},{24,16},{28,20},{1,9},{5... | collective-permute-start | bytes 786440 | tf_op jit(solution)/shard_map/ppermute | solution.py:77
  5.5 21.0 %collective-permute-start.1 = (bf16[8,64,256]{2,1,0:T(8,128)(2,1)S(1)}, bf16[8,64,256]{2,1,0:T(8,128)(2,1)S(1)}, u32[]{:S(2)}, u32[]{:S(2)}) collective-permute-start(bf16[8,64,256]{2,1,0:T(8,128)(2,1)S(1)} %get-tuple-element.57), channel_id=1, source_target_pairs={{0,16},{4,20},{8,24},{12,28},{16,0},{20,4},{24,8},{28,12},{1,17},{... | collective-permute-start | bytes 786440 | tf_op jit(solution)/shard_map/ppermute | solution.py:77
  8.5 23.1 %collective-permute-start.2 = (bf16[8,64,256]{2,1,0:T(8,128)(2,1)S(1)}, bf16[8,64,256]{2,1,0:T(8,128)(2,1)S(1)}, u32[]{:S(2)}, u32[]{:S(2)}) collective-permute-start(bf16[8,64,256]{2,1,0:T(8,128)(2,1)S(1)} %get-tuple-element.58), channel_id=1, source_target_pairs={{0,24},{4,28},{8,16},{12,20},{16,8},{20,12},{24,0},{28,4},{1,25},{... | collective-permute-start | bytes 786440 | tf_op jit(solution)/shard_map/ppermute | solution.py:77
  8.9 22.6 %collective-permute-start.3 = (bf16[256,512]{1,0:T(8,128)(2,1)S(1)}, bf16[256,512]{1,0:T(8,128)(2,1)S(1)}, u32[]{:S(2)}, u32[]{:S(2)}) collective-permute-start(bf16[256,512]{1,0:T(8,128)(2,1)S(1)} %get-tuple-element.59), channel_id=1, source_target_pairs={{0,4},{4,0},{8,12},{12,8},{16,20},{20,16},{24,28},{28,24},{1,5},{5... | collective-permute-start | bytes 786440 | tf_op jit(solution)/shard_map/ppermute | solution.py:77
  31.7 23.8 %collective-permute-start.4 = (bf16[4,512,256]{2,1,0:T(8,128)(2,1)S(1)}, bf16[4,512,256]{2,1,0:T(8,128)(2,1)S(1)}, u32[]{:S(2)}, u32[]{:S(2)}) collective-permute-start(bf16[4,512,256]{2,1,0:T(8,128)(2,1)S(1)} %pad_maximum_fusion.refs_0_), channel_id=1, source_target_pairs={{0,4},{4,0},{8,12},{12,8},{16,20},{20,16},{24,28},{28,24},{1,5},{5... | collective-permute-start | bytes 3145736 | tf_op jit(solution)/shard_map/ppermute | solution.py:77
  33.3 26.2 %collective-permute-start.7 = (bf16[4,512,256]{2,1,0:T(8,128)(2,1)S(1)}, bf16[4,512,256]{2,1,0:T(8,128)(2,1)S(1)}, u32[]{:S(2)}, u32[]{:S(2)}) collective-permute-start(bf16[4,512,256]{2,1,0:T(8,128)(2,1)S(1)} %pad_maximum_fusion.refs_0_), channel_id=1, source_target_pairs={{0,2},{1,3},{2,0},{3,1},{4,6},{5,7},{6,4},{7,5},{8,10},{9,11},{10,... | collective-permute-start | bytes 3145736 | tf_op jit(solution)/shard_map/ppermute | solution.py:77
  34.8 22.3 %collective-permute-start.14 = (bf16[2,256,512]{2,1,0:T(8,128)(2,1)S(1)}, bf16[2,256,512]{2,1,0:T(8,128)(2,1)S(1)}, u32[]{:S(2)}, u32[]{:S(2)}) collective-permute-start(bf16[2,256,512]{2,1,0:T(8,128)(2,1)S(1)} %pad_maximum_fusion.1.refs_10_), channel_id=1, source_target_pairs={{0,16},{4,20},{8,24},{12,28},{16,0},{20,4},{24,8},{28,12},{1,17},{... | collective-permute-start | bytes 1572872 | tf_op jit(solution)/shard_map/ppermute | solution.py:77
  55.6 12.4 %collective-permute-start.8 = (bf16[2,512,256]{2,1,0:T(8,128)(2,1)S(1)}, bf16[2,512,256]{2,1,0:T(8,128)(2,1)S(1)}, u32[]{:S(2)}, u32[]{:S(2)}) collective-permute-start(bf16[2,512,256]{2,1,0:T(8,128)(2,1)S(1)} %slice.8), channel_id=1, source_target_pairs={{0,2},{1,3},{2,0},{3,1},{4,6},{5,7},{6,4},{7,5},{8,10},{9,11},{10,... | collective-permute-start | bytes 1572872 | tf_op jit(solution)/shard_map/ppermute | solution.py:77
  57.1 14.9 %collective-permute-start.13 = (bf16[2,256,512]{2,1,0:T(8,128)(2,1)S(1)}, bf16[2,256,512]{2,1,0:T(8,128)(2,1)S(1)}, u32[]{:S(2)}, u32[]{:S(2)}) collective-permute-start(bf16[2,256,512]{2,1,0:T(8,128)(2,1)S(1)} %pad_maximum_fusion.1.refs_10_), channel_id=1, source_target_pairs={{0,8},{4,12},{8,0},{12,4},{16,24},{20,28},{24,16},{28,20},{1,9},{5... | collective-permute-start | bytes 1572872 | tf_op jit(solution)/shard_map/ppermute | solution.py:77
  57.1 22.6 %collective-permute-start.5 = (bf16[4,512,256]{2,1,0:T(8,128)(2,1)S(1)}, bf16[4,512,256]{2,1,0:T(8,128)(2,1)S(1)}, u32[]{:S(2)}, u32[]{:S(2)}) collective-permute-start(bf16[4,512,256]{2,1,0:T(8,128)(2,1)S(1)} %pad_maximum_fusion.refs_0_), channel_id=1, source_target_pairs={{0,1},{1,0},{2,3},{3,2},{4,5},{5,4},{6,7},{7,6},{8,9},{9,8},{10,11... | collective-permute-start | bytes 3145736 | tf_op jit(solution)/shard_map/ppermute | solution.py:77
  57.1 22.5 %collective-permute-start.15 = (bf16[2,256,512]{2,1,0:T(8,128)(2,1)S(1)}, bf16[2,256,512]{2,1,0:T(8,128)(2,1)S(1)}, u32[]{:S(2)}, u32[]{:S(2)}) collective-permute-start(bf16[2,256,512]{2,1,0:T(8,128)(2,1)S(1)} %collective-permute-done.14.refs_12_), channel_id=1, source_target_pairs={{0,8},{4,12},{8,0},{12,4},{16,24},{20,28},{24,16},{28,20},{1,9},{5... | collective-permute-start | bytes 1572872 | tf_op jit(solution)/shard_map/ppermute | solution.py:77
  59.5 73.9 %copy-start = (f32[1,16,256,256]{3,2,1,0:T(8,128)S(1)}, f32[1,16,256,256]{3,2,1,0:T(8,128)}, u32[]{:S(2)}) copy-start(f32[1,16,256,256]{3,2,1,0:T(8,128)} %second_ref.5) | copy-start | bytes 12582916
  59.6 13.8 %collective-permute-start.9 = (bf16[2,512,256]{2,1,0:T(8,128)(2,1)S(1)}, bf16[2,512,256]{2,1,0:T(8,128)(2,1)S(1)}, u32[]{:S(2)}, u32[]{:S(2)}) collective-permute-start(bf16[2,512,256]{2,1,0:T(8,128)(2,1)S(1)} %slice.9), channel_id=1, source_target_pairs={{0,4},{4,0},{8,12},{12,8},{16,20},{20,16},{24,28},{28,24},{1,5},{5... | collective-permute-start | bytes 1572872 | tf_op jit(solution)/shard_map/ppermute | solution.py:77
  68.0 11.7 %collective-permute-start.6 = (bf16[4,512,256]{2,1,0:T(8,128)(2,1)S(1)}, bf16[4,512,256]{2,1,0:T(8,128)(2,1)S(1)}, u32[]{:S(2)}, u32[]{:S(2)}) collective-permute-start(bf16[4,512,256]{2,1,0:T(8,128)(2,1)S(1)} %collective-permute-done.4.refs_1_), channel_id=1, source_target_pairs={{0,1},{1,0},{2,3},{3,2},{4,5},{5,4},{6,7},{7,6},{8,9},{9,8},{10,11... | collective-permute-start | bytes 3145736 | tf_op jit(solution)/shard_map/ppermute | solution.py:77
  72.0 9.6 %collective-permute-start.10 = (bf16[4,512,256]{2,1,0:T(8,128)(2,1)S(1)}, bf16[4,512,256]{2,1,0:T(8,128)(2,1)S(1)}, u32[]{:S(2)}, u32[]{:S(2)}) collective-permute-start(bf16[4,512,256]{2,1,0:T(8,128)(2,1)S(1)} %collective-permute-done.7.refs_4_), channel_id=1, source_target_pairs={{0,1},{1,0},{2,3},{3,2},{4,5},{5,4},{6,7},{7,6},{8,9},{9,8},{10,11... | collective-permute-start | bytes 3145736 | tf_op jit(solution)/shard_map/ppermute | solution.py:77
  73.4 6.3 %collective-permute-start.12 = (bf16[2,512,256]{2,1,0:T(8,128)(2,1)S(1)}, bf16[2,512,256]{2,1,0:T(8,128)(2,1)S(1)}, u32[]{:S(2)}, u32[]{:S(2)}) collective-permute-start(bf16[2,512,256]{2,1,0:T(8,128)(2,1)S(1)} %collective-permute-done.9.refs_6_), channel_id=1, source_target_pairs={{0,1},{1,0},{2,3},{3,2},{4,5},{5,4},{6,7},{7,6},{8,9},{9,8},{10,11... | collective-permute-start | bytes 1572872 | tf_op jit(solution)/shard_map/ppermute | solution.py:77
  79.7 1.9 collective-permute-start.11
  88.1 6.3 %collective-permute-start.16 = (bf16[8,64,128]{2,1,0:T(8,128)(2,1)S(1)}, bf16[8,64,128]{2,1,0:T(8,128)(2,1)S(1)}, u32[]{:S(2)}, u32[]{:S(2)}) collective-permute-start(bf16[8,64,128]{2,1,0:T(8,128)(2,1)S(1)} %get-tuple-element.68), channel_id=1, source_target_pairs={{0,4},{4,0},{8,12},{12,8},{16,20},{20,16},{24,28},{28,24},{1,5},{5... | collective-permute-start | bytes 393224 | tf_op jit(solution)/shard_map/ppermute | solution.py:77
  89.7 6.9 %collective-permute-start.17 = (bf16[8,64,128]{2,1,0:T(8,128)(2,1)S(1)}, bf16[8,64,128]{2,1,0:T(8,128)(2,1)S(1)}, u32[]{:S(2)}, u32[]{:S(2)}) collective-permute-start(bf16[8,64,128]{2,1,0:T(8,128)(2,1)S(1)} %get-tuple-element.69), channel_id=1, source_target_pairs={{0,8},{4,12},{8,0},{12,4},{16,24},{20,28},{24,16},{28,20},{1,9},{5... | collective-permute-start | bytes 393224 | tf_op jit(solution)/shard_map/ppermute | solution.py:77
  90.9 7.4 %collective-permute-start.23 = (bf16[8,64,128]{2,1,0:T(8,128)(2,1)S(1)}, bf16[8,64,128]{2,1,0:T(8,128)(2,1)S(1)}, u32[]{:S(2)}, u32[]{:S(2)}) collective-permute-start(bf16[8,64,128]{2,1,0:T(8,128)(2,1)S(1)} %get-tuple-element.76), channel_id=1, source_target_pairs={{0,4},{4,0},{8,12},{12,8},{16,20},{20,16},{24,28},{28,24},{1,5},{5... | collective-permute-start | bytes 393224 | tf_op jit(solution)/shard_map/ppermute | solution.py:77
  92.4 8.6 %collective-permute-start.24 = (bf16[8,64,128]{2,1,0:T(8,128)(2,1)S(1)}, bf16[8,64,128]{2,1,0:T(8,128)(2,1)S(1)}, u32[]{:S(2)}, u32[]{:S(2)}) collective-permute-start(bf16[8,64,128]{2,1,0:T(8,128)(2,1)S(1)} %get-tuple-element.77), channel_id=1, source_target_pairs={{0,8},{4,12},{8,0},{12,4},{16,24},{20,28},{24,16},{28,20},{1,9},{5... | collective-permute-start | bytes 393224 | tf_op jit(solution)/shard_map/ppermute | solution.py:77
  92.4 10.7 %collective-permute-start.25 = (bf16[8,64,128]{2,1,0:T(8,128)(2,1)S(1)}, bf16[8,64,128]{2,1,0:T(8,128)(2,1)S(1)}, u32[]{:S(2)}, u32[]{:S(2)}) collective-permute-start(bf16[8,64,128]{2,1,0:T(8,128)(2,1)S(1)} %get-tuple-element.78), channel_id=1, source_target_pairs={{0,12},{4,8},{8,4},{12,0},{16,28},{20,24},{24,20},{28,16},{1,13},{... | collective-permute-start | bytes 393224 | tf_op jit(solution)/shard_map/ppermute | solution.py:77
  94.4 16.7 %collective-permute-start.26 = (bf16[8,64,128]{2,1,0:T(8,128)(2,1)S(1)}, bf16[8,64,128]{2,1,0:T(8,128)(2,1)S(1)}, u32[]{:S(2)}, u32[]{:S(2)}) collective-permute-start(bf16[8,64,128]{2,1,0:T(8,128)(2,1)S(1)} %get-tuple-element.79), channel_id=1, source_target_pairs={{0,16},{4,20},{8,24},{12,28},{16,0},{20,4},{24,8},{28,12},{1,17},{... | collective-permute-start | bytes 393224 | tf_op jit(solution)/shard_map/ppermute | solution.py:77
  96.6 24.8 %collective-permute-start.27 = (bf16[8,64,128]{2,1,0:T(8,128)(2,1)S(1)}, bf16[8,64,128]{2,1,0:T(8,128)(2,1)S(1)}, u32[]{:S(2)}, u32[]{:S(2)}) collective-permute-start(bf16[8,64,128]{2,1,0:T(8,128)(2,1)S(1)} %get-tuple-element.80), channel_id=1, source_target_pairs={{0,20},{4,16},{8,28},{12,24},{16,4},{20,0},{24,12},{28,8},{1,21},{... | collective-permute-start | bytes 393224 | tf_op jit(solution)/shard_map/ppermute | solution.py:77
  98.2 28.2 %collective-permute-start.28 = (bf16[8,64,128]{2,1,0:T(8,128)(2,1)S(1)}, bf16[8,64,128]{2,1,0:T(8,128)(2,1)S(1)}, u32[]{:S(2)}, u32[]{:S(2)}) collective-permute-start(bf16[8,64,128]{2,1,0:T(8,128)(2,1)S(1)} %get-tuple-element.81), channel_id=1, source_target_pairs={{0,24},{4,28},{8,16},{12,20},{16,8},{20,12},{24,0},{28,4},{1,25},{... | collective-permute-start | bytes 393224 | tf_op jit(solution)/shard_map/ppermute | solution.py:77
  100.9 32.4 %collective-permute-start.29 = (bf16[8,64,128]{2,1,0:T(8,128)(2,1)S(1)}, bf16[8,64,128]{2,1,0:T(8,128)(2,1)S(1)}, u32[]{:S(2)}, u32[]{:S(2)}) collective-permute-start(bf16[8,64,128]{2,1,0:T(8,128)(2,1)S(1)} %get-tuple-element.82), channel_id=1, source_target_pairs={{0,28},{4,24},{8,20},{12,16},{16,12},{20,8},{24,4},{28,0},{1,29},{... | collective-permute-start | bytes 393224 | tf_op jit(solution)/shard_map/ppermute | solution.py:77
  103.0 36.7 %collective-permute-start.18 = (bf16[8,64,128]{2,1,0:T(8,128)(2,1)S(1)}, bf16[8,64,128]{2,1,0:T(8,128)(2,1)S(1)}, u32[]{:S(2)}, u32[]{:S(2)}) collective-permute-start(bf16[8,64,128]{2,1,0:T(8,128)(2,1)S(1)} %get-tuple-element.70), channel_id=1, source_target_pairs={{0,12},{4,8},{8,4},{12,0},{16,28},{20,24},{24,20},{28,16},{1,13},{... | collective-permute-start | bytes 393224 | tf_op jit(solution)/shard_map/ppermute | solution.py:77
  111.0 30.3 %collective-permute-start.19 = (bf16[8,64,128]{2,1,0:T(8,128)(2,1)S(1)}, bf16[8,64,128]{2,1,0:T(8,128)(2,1)S(1)}, u32[]{:S(2)}, u32[]{:S(2)}) collective-permute-start(bf16[8,64,128]{2,1,0:T(8,128)(2,1)S(1)} %get-tuple-element.71), channel_id=1, source_target_pairs={{0,16},{4,20},{8,24},{12,28},{16,0},{20,4},{24,8},{28,12},{1,17},{... | collective-permute-start | bytes 393224 | tf_op jit(solution)/shard_map/ppermute | solution.py:77
  121.4 19.9 %collective-permute-start.20 = (bf16[8,64,128]{2,1,0:T(8,128)(2,1)S(1)}, bf16[8,64,128]{2,1,0:T(8,128)(2,1)S(1)}, u32[]{:S(2)}, u32[]{:S(2)}) collective-permute-start(bf16[8,64,128]{2,1,0:T(8,128)(2,1)S(1)} %get-tuple-element.72), channel_id=1, source_target_pairs={{0,20},{4,16},{8,28},{12,24},{16,4},{20,0},{24,12},{28,8},{1,21},{... | collective-permute-start | bytes 393224 | tf_op jit(solution)/shard_map/ppermute | solution.py:77
  126.4 16.9 %collective-permute-start.21 = (bf16[8,64,128]{2,1,0:T(8,128)(2,1)S(1)}, bf16[8,64,128]{2,1,0:T(8,128)(2,1)S(1)}, u32[]{:S(2)}, u32[]{:S(2)}) collective-permute-start(bf16[8,64,128]{2,1,0:T(8,128)(2,1)S(1)} %get-tuple-element.73), channel_id=1, source_target_pairs={{0,24},{4,28},{8,16},{12,20},{16,8},{20,12},{24,0},{28,4},{1,25},{... | collective-permute-start | bytes 393224 | tf_op jit(solution)/shard_map/ppermute | solution.py:77
  133.4 14.5 %collective-permute-start.22 = (bf16[8,64,128]{2,1,0:T(8,128)(2,1)S(1)}, bf16[8,64,128]{2,1,0:T(8,128)(2,1)S(1)}, u32[]{:S(2)}, u32[]{:S(2)}) collective-permute-start(bf16[8,64,128]{2,1,0:T(8,128)(2,1)S(1)} %get-tuple-element.74), channel_id=1, source_target_pairs={{0,28},{4,24},{8,20},{12,16},{16,12},{20,8},{24,4},{28,0},{1,29},{... | collective-permute-start | bytes 393224 | tf_op jit(solution)/shard_map/ppermute | solution.py:77
  139.7 14.5 %collective-permute-start.37 = (bf16[8,32,256]{2,1,0:T(8,128)(2,1)S(1)}, bf16[8,32,256]{2,1,0:T(8,128)(2,1)S(1)}, u32[]{:S(2)}, u32[]{:S(2)}) collective-permute-start(bf16[8,32,256]{2,1,0:T(8,128)(2,1)S(1)} %get-tuple-element.95), channel_id=1, source_target_pairs={{0,4},{4,0},{8,12},{12,8},{16,20},{20,16},{24,28},{28,24},{1,5},{5... | collective-permute-start | bytes 393224 | tf_op jit(solution)/shard_map/ppermute | solution.py:77
  141.3 14.2 %collective-permute-start.38 = (bf16[8,32,256]{2,1,0:T(8,128)(2,1)S(1)}, bf16[8,32,256]{2,1,0:T(8,128)(2,1)S(1)}, u32[]{:S(2)}, u32[]{:S(2)}) collective-permute-start(bf16[8,32,256]{2,1,0:T(8,128)(2,1)S(1)} %get-tuple-element.96), channel_id=1, source_target_pairs={{0,8},{4,12},{8,0},{12,4},{16,24},{20,28},{24,16},{28,20},{1,9},{5... | collective-permute-start | bytes 393224 | tf_op jit(solution)/shard_map/ppermute | solution.py:77
  141.3 16.0 %collective-permute-start.39 = (bf16[8,32,256]{2,1,0:T(8,128)(2,1)S(1)}, bf16[8,32,256]{2,1,0:T(8,128)(2,1)S(1)}, u32[]{:S(2)}, u32[]{:S(2)}) collective-permute-start(bf16[8,32,256]{2,1,0:T(8,128)(2,1)S(1)} %get-tuple-element.97), channel_id=1, source_target_pairs={{0,12},{4,8},{8,4},{12,0},{16,28},{20,24},{24,20},{28,16},{1,13},{... | collective-permute-start | bytes 393224 | tf_op jit(solution)/shard_map/ppermute | solution.py:77
  143.3 14.5 %collective-permute-start.40 = (bf16[8,32,256]{2,1,0:T(8,128)(2,1)S(1)}, bf16[8,32,256]{2,1,0:T(8,128)(2,1)S(1)}, u32[]{:S(2)}, u32[]{:S(2)}) collective-permute-start(bf16[8,32,256]{2,1,0:T(8,128)(2,1)S(1)} %get-tuple-element.98), channel_id=1, source_target_pairs={{0,16},{4,20},{8,24},{12,28},{16,0},{20,4},{24,8},{28,12},{1,17},{... | collective-permute-start | bytes 393224 | tf_op jit(solution)/shard_map/ppermute | solution.py:77
  147.9 14.1 %collective-permute-start.41 = (bf16[8,32,256]{2,1,0:T(8,128)(2,1)S(1)}, bf16[8,32,256]{2,1,0:T(8,128)(2,1)S(1)}, u32[]{:S(2)}, u32[]{:S(2)}) collective-permute-start(bf16[8,32,256]{2,1,0:T(8,128)(2,1)S(1)} %get-tuple-element.99), channel_id=1, source_target_pairs={{0,20},{4,16},{8,28},{12,24},{16,4},{20,0},{24,12},{28,8},{1,21},{... | collective-permute-start | bytes 393224 | tf_op jit(solution)/shard_map/ppermute | solution.py:77
  154.2 12.2 %collective-permute-start.42 = (bf16[8,32,256]{2,1,0:T(8,128)(2,1)S(1)}, bf16[8,32,256]{2,1,0:T(8,128)(2,1)S(1)}, u32[]{:S(2)}, u32[]{:S(2)}) collective-permute-start(bf16[8,32,256]{2,1,0:T(8,128)(2,1)S(1)} %get-tuple-element.100), channel_id=1, source_target_pairs={{0,24},{4,28},{8,16},{12,20},{16,8},{20,12},{24,0},{28,4},{1,25},{... | collective-permute-start | bytes 393224 | tf_op jit(solution)/shard_map/ppermute | solution.py:77
  155.5 18.9 %collective-permute-start.43 = (bf16[8,32,256]{2,1,0:T(8,128)(2,1)S(1)}, bf16[8,32,256]{2,1,0:T(8,128)(2,1)S(1)}, u32[]{:S(2)}, u32[]{:S(2)}) collective-permute-start(bf16[8,32,256]{2,1,0:T(8,128)(2,1)S(1)} %get-tuple-element.101), channel_id=1, source_target_pairs={{0,28},{4,24},{8,20},{12,16},{16,12},{20,8},{24,4},{28,0},{1,29},{... | collective-permute-start | bytes 393224 | tf_op jit(solution)/shard_map/ppermute | solution.py:77
  157.4 17.0 %collective-permute-start.30 = (bf16[8,32,256]{2,1,0:T(8,128)(2,1)S(1)}, bf16[8,32,256]{2,1,0:T(8,128)(2,1)S(1)}, u32[]{:S(2)}, u32[]{:S(2)}) collective-permute-start(bf16[8,32,256]{2,1,0:T(8,128)(2,1)S(1)} %get-tuple-element.87), channel_id=1, source_target_pairs={{0,4},{4,0},{8,12},{12,8},{16,20},{20,16},{24,28},{28,24},{1,5},{5... | collective-permute-start | bytes 393224 | tf_op jit(solution)/shard_map/ppermute | solution.py:77
  157.8 17.8 %collective-permute-start.31 = (bf16[8,32,256]{2,1,0:T(8,128)(2,1)S(1)}, bf16[8,32,256]{2,1,0:T(8,128)(2,1)S(1)}, u32[]{:S(2)}, u32[]{:S(2)}) collective-permute-start(bf16[8,32,256]{2,1,0:T(8,128)(2,1)S(1)} %get-tuple-element.88), channel_id=1, source_target_pairs={{0,8},{4,12},{8,0},{12,4},{16,24},{20,28},{24,16},{28,20},{1,9},{5... | collective-permute-start | bytes 393224 | tf_op jit(solution)/shard_map/ppermute | solution.py:77
  162.0 14.8 %collective-permute-start.32 = (bf16[8,32,256]{2,1,0:T(8,128)(2,1)S(1)}, bf16[8,32,256]{2,1,0:T(8,128)(2,1)S(1)}, u32[]{:S(2)}, u32[]{:S(2)}) collective-permute-start(bf16[8,32,256]{2,1,0:T(8,128)(2,1)S(1)} %get-tuple-element.89), channel_id=1, source_target_pairs={{0,12},{4,8},{8,4},{12,0},{16,28},{20,24},{24,20},{28,16},{1,13},{... | collective-permute-start | bytes 393224 | tf_op jit(solution)/shard_map/ppermute | solution.py:77
  166.4 10.3 %collective-permute-start.33 = (bf16[8,32,256]{2,1,0:T(8,128)(2,1)S(1)}, bf16[8,32,256]{2,1,0:T(8,128)(2,1)S(1)}, u32[]{:S(2)}, u32[]{:S(2)}) collective-permute-start(bf16[8,32,256]{2,1,0:T(8,128)(2,1)S(1)} %get-tuple-element.90), channel_id=1, source_target_pairs={{0,16},{4,20},{8,24},{12,28},{16,0},{20,4},{24,8},{28,12},{1,17},{... | collective-permute-start | bytes 393224 | tf_op jit(solution)/shard_map/ppermute | solution.py:77
  174.4 6.9 %collective-permute-start.34 = (bf16[8,32,256]{2,1,0:T(8,128)(2,1)S(1)}, bf16[8,32,256]{2,1,0:T(8,128)(2,1)S(1)}, u32[]{:S(2)}, u32[]{:S(2)}) collective-permute-start(bf16[8,32,256]{2,1,0:T(8,128)(2,1)S(1)} %get-tuple-element.91), channel_id=1, source_target_pairs={{0,20},{4,16},{8,28},{12,24},{16,4},{20,0},{24,12},{28,8},{1,21},{... | collective-permute-start | bytes 393224 | tf_op jit(solution)/shard_map/ppermute | solution.py:77
  174.4 11.5 %collective-permute-start.35 = (bf16[8,32,256]{2,1,0:T(8,128)(2,1)S(1)}, bf16[8,32,256]{2,1,0:T(8,128)(2,1)S(1)}, u32[]{:S(2)}, u32[]{:S(2)}) collective-permute-start(bf16[8,32,256]{2,1,0:T(8,128)(2,1)S(1)} %get-tuple-element.92), channel_id=1, source_target_pairs={{0,24},{4,28},{8,16},{12,20},{16,8},{20,12},{24,0},{28,4},{1,25},{... | collective-permute-start | bytes 393224 | tf_op jit(solution)/shard_map/ppermute | solution.py:77
  175.5 12.1 %collective-permute-start.36 = (bf16[8,32,256]{2,1,0:T(8,128)(2,1)S(1)}, bf16[8,32,256]{2,1,0:T(8,128)(2,1)S(1)}, u32[]{:S(2)}, u32[]{:S(2)}) collective-permute-start(bf16[8,32,256]{2,1,0:T(8,128)(2,1)S(1)} %get-tuple-element.93), channel_id=1, source_target_pairs={{0,28},{4,24},{8,20},{12,16},{16,12},{20,8},{24,4},{28,0},{1,29},{... | collective-permute-start | bytes 393224 | tf_op jit(solution)/shard_map/ppermute | solution.py:77
  189.3 14.9 %collective-permute-start.44 = (bf16[32,8192]{1,0:T(8,128)(2,1)S(1)}, bf16[32,8192]{1,0:T(8,128)(2,1)S(1)}, u32[]{:S(2)}, u32[]{:S(2)}) collective-permute-start(bf16[32,8192]{1,0:T(8,128)(2,1)S(1)} %get-tuple-element.103), channel_id=1, source_target_pairs={{0,8},{4,12},{8,0},{12,4},{16,24},{20,28},{24,16},{28,20},{1,9},{5... | collective-permute-start | bytes 1572872 | tf_op jit(solution)/shard_map/ppermute | solution.py:77
  189.4 36.0 %collective-permute-start.45 = (bf16[32,8192]{1,0:T(8,128)(2,1)S(1)}, bf16[32,8192]{1,0:T(8,128)(2,1)S(1)}, u32[]{:S(2)}, u32[]{:S(2)}) collective-permute-start(bf16[32,8192]{1,0:T(8,128)(2,1)S(1)} %get-tuple-element.104), channel_id=1, source_target_pairs={{0,16},{4,20},{8,24},{12,28},{16,0},{20,4},{24,8},{28,12},{1,17},{... | collective-permute-start | bytes 1572872 | tf_op jit(solution)/shard_map/ppermute | solution.py:77
  191.9 41.0 %collective-permute-start.46 = (bf16[32,8192]{1,0:T(8,128)(2,1)S(1)}, bf16[32,8192]{1,0:T(8,128)(2,1)S(1)}, u32[]{:S(2)}, u32[]{:S(2)}) collective-permute-start(bf16[32,8192]{1,0:T(8,128)(2,1)S(1)} %get-tuple-element.105), channel_id=1, source_target_pairs={{0,24},{4,28},{8,16},{12,20},{16,8},{20,12},{24,0},{28,4},{1,25},{... | collective-permute-start | bytes 1572872 | tf_op jit(solution)/shard_map/ppermute | solution.py:77
  (6 other events, 239.9 us)

commit v5 on v4

--- a/solution.py
+++ b/solution.py
@@ -113,7 +113,7 @@
         ),
         out_shape=[jax.ShapeDtypeStruct((bands, strip, tokens), jnp.bfloat16)] * pairs
         + [jax.ShapeDtypeStruct((tokens, band_rows // 2), jnp.bfloat16)] * 2,
-        compiler_params=pltpu.CompilerParams(vmem_limit_bytes=16 * MIB),
+        compiler_params=pltpu.CompilerParams(vmem_limit_bytes=8 * MIB),
         cost_estimate=pl.CostEstimate(
             flops=0, bytes_accessed=4 * tokens * (width + band_rows), transcendentals=0
         ),
@@ -184,7 +184,7 @@
             for count in chunks
             for _ in range(groups)
         ],
-        compiler_params=pltpu.CompilerParams(vmem_limit_bytes=32 * MIB),
+        compiler_params=pltpu.CompilerParams(vmem_limit_bytes=16 * MIB),
         cost_estimate=pl.CostEstimate(
             flops=2 * ranks * rows * groups * tokens * band_rows,
             bytes_accessed=2
@@ -253,7 +253,7 @@
             ],
         ),
         out_shape=[jax.ShapeDtypeStruct((slots, sub, block), jnp.bfloat16)] * groups,
-        compiler_params=pltpu.CompilerParams(vmem_limit_bytes=32 * MIB),
+        compiler_params=pltpu.CompilerParams(vmem_limit_bytes=8 * MIB),
         cost_estimate=pl.CostEstimate(
             flops=4 * slots * block**3,
             bytes_accessed=16 * slots * block * block,
@@ -310,7 +310,7 @@
             scratch_shapes=[pltpu.VMEM((block, block), jnp.bfloat16)],
         ),
         out_shape=[jax.ShapeDtypeStruct(left_stat.shape, jnp.float32)] * 3,
-        compiler_params=pltpu.CompilerParams(vmem_limit_bytes=32 * MIB),
+        compiler_params=pltpu.CompilerParams(vmem_limit_bytes=8 * MIB),
         cost_estimate=pl.CostEstimate(
             flops=4 * slots * block**3,
             bytes_accessed=26 * slots * block * block,
@@ -356,7 +356,7 @@
             scratch_shapes=[pltpu.VMEM((row_bands, sub, bands * block), jnp.bfloat16)],
         ),
         out_shape=[jax.ShapeDtypeStruct((sub, bands * block), jnp.bfloat16)] * row_bands,
-        compiler_params=pltpu.CompilerParams(vmem_limit_bytes=32 * MIB),
+        compiler_params=pltpu.CompilerParams(vmem_limit_bytes=8 * MIB),
         cost_estimate=pl.CostEstimate(
             flops=0,
             bytes_accessed=4 * row_bands * sub * bands * block,
@@ -367,28 +367,33 @@
 
 
 def stack_kernel(halves, meta, *refs):
-    pieces, out = refs[:-1], refs[-1]
+    pieces, out, sems = refs[:-2], refs[-2], refs[-1]
     sub = pieces[0].shape[0]
     own_band = lax.div(meta[0], halves)
-    for k in range(len(pieces)):
+    copies = []
+    for k, piece in enumerate(pieces):
         start = pl.multiple_of((own_band ^ k) * sub, sub)
-        out[0, pl.ds(start, sub), :] = pieces[k][...]
+        copies.append(pltpu.make_async_copy(piece, out.at[0, pl.ds(start, sub), :], sems.at[k]))
+    for copy in copies:
+        copy.start()
+    for copy in copies:
+        copy.wait()
 
 
 def stack_rows(meta, pieces, halves):
     count = len(pieces)
     sub, width = pieces[0].shape
-    part = width // count
     return pl.pallas_call(
         functools.partial(stack_kernel, halves),
         grid_spec=pltpu.PrefetchScalarGridSpec(
             num_scalar_prefetch=1,
-            grid=(count,),
-            in_specs=[pl.BlockSpec((sub, part), lambda c, meta: (0, c))] * count,
-            out_specs=pl.BlockSpec((1, count * sub, part), lambda c, meta: (0, 0, c)),
+            grid=(),
+            in_specs=[pl.BlockSpec(memory_space=pltpu.VMEM)] * count,
+            out_specs=pl.BlockSpec(memory_space=pl.ANY),
+            scratch_shapes=[pltpu.SemaphoreType.DMA((count,))],
         ),
         out_shape=jax.ShapeDtypeStruct((1, count * sub, width), jnp.bfloat16),
-        compiler_params=pltpu.CompilerParams(vmem_limit_bytes=16 * MIB),
+        compiler_params=pltpu.CompilerParams(vmem_limit_bytes=4 * MIB),
         cost_estimate=pl.CostEstimate(
             flops=0, bytes_accessed=4 * count * sub * width, transcendentals=0
         ),
@@ -428,20 +433,23 @@
             ctxs[far + step + k] = swap(ctxs[far + k], "fsdp", 2 * step)
         step *= 2
     by_pair = swap(strips, "fsdp", 1)
-    cots = {0: [strips, by_pair]}
-    offset = ranks // 2
+    by_rank = swap(strips, "tensor", ranks // 2)
+    to_rank, to_pair = by_pair[:far], by_rank[far:]
+    to_rank, _ = lax.optimization_barrier((to_rank, ctxs[1]))
+    across = [
+        by_rank,
+        swap(to_rank, "tensor", ranks // 2),
+        swap(to_pair, "fsdp", 1),
+    ]
+    cots = {0: [strips, by_pair], ranks // 2: across}
+    offset = ranks // 4
     while offset:
         for known in list(cots):
-            here = cots[known]
-            if known == 0 and offset == ranks // 2:
-                there = [swap(strips, "tensor", offset)]
-                there.append(swap(by_pair[:far], "tensor", offset))
-                there.append(swap(there[0][far:], "fsdp", 1))
-            else:
-                if known:
-                    here[0], _ = lax.optimization_barrier((here[0], here[1]))
-                there = [swap(piece, "tensor", offset) for piece in here]
-            cots[known ^ offset] = there
+            here = list(cots[known])
+            if known:
+                here[0], _ = lax.optimization_barrier((here[0], here[1]))
+
+            cots[known ^ offset] = [swap(piece, "tensor", offset) for piece in here]
         offset //= 2
     cots = [cots[t] for t in range(ranks)]
 

time: 236 us -> 232 us (0.983)
  waiting for transfers between devices: 136 us -> 132 us
    ppermute x47, waiting for transfers between devices: 136 us -> 132 us  [swap(): return lax.ppermute(value, axis, [(i, i ^ offset) for i in range(count)])]
  transfers between devices with their start and end apart: 47 -> 47, of which waited for: 24 -> 25; matrix products, arithmetic and copies ran while one was open for 0% -> 0% of each run, Pallas kernels for 10% -> 10%
where the time goes in v5:
time: 232 us
  waiting for transfers between devices  132 us (57%)
  starting transfers between devices  60.8 us (26%)
  Pallas kernels  34.8 us (15%)
  local copies, waits for them, and re-layouts  2.36 us (1%)
    ppermute x47, waiting for transfers between devices, swap(): return lax.ppermute(value, axis, [(i, i ^ offset) for i in range(count)])  132 us
    ppermute x47, starting transfers between devices, swap(): return lax.ppermute(value, axis, [(i, i ^ offset) for i in range(count)])  60.8 us
    pallas_call x2, Pallas kernels, directions(): pl.pallas_call(functools.partial(direction_kernel, groups, halves), grid_...  12.6 us
    pallas_call x1, Pallas kernels, statistics(): pl.pallas_call(functools.partial(statistics_kernel, groups, chunks), grid...  10.4 us
    pallas_call x1, Pallas kernels, gradient_strips(): pl.pallas_call(functools.partial(gradient_kernel, groups, ranks, sources,...  6.51 us
  transfers between devices with their start and end apart: 47, of which 25 were waited for; matrix products, arithmetic and copies ran while one was open for 0% of the time, Pallas kernels for 10%

profile of v5, /device:TPU:8, one launch (start us, length us, event | category | flops | bytes accessed | tf_op | source)
XLA Modules:
  0.0 231.7 jit_solution(2434796424411720456)
XLA Ops:
  3.6 1.7 prepare.1
  5.5 3.0 %collective-permute-start.1 = (bf16[8,64,256]{2,1,0:T(8,128)(2,1)S(1)}, bf16[8,64,256]{2,1,0:T(8,128)(2,1)S(1)}, u32[]{:S(2)}, u32[]{:S(2)}) collective-permute-start(bf16[8,64,256]{2,1,0:T(8,128)(2,1)S(1)} %get-tuple-element.58), channel_id=1, source_target_pairs={{0,16},{4,20},{8,24},{12,28},{16,0},{20,4},{24,8},{28,12},{1,17},{... | collective-permute-start | bytes 786440 | tf_op jit(solution)/shard_map/ppermute | solution.py:77
  8.9 1.5 collective-permute-start.3
  10.4 5.7 %collective-permute-done = bf16[8,64,256]{2,1,0:T(8,128)(2,1)S(1)} collective-permute-done((bf16[8,64,256]{2,1,0:T(8,128)(2,1)S(1)}, bf16[8,64,256]{2,1,0:T(8,128)(2,1)S(1)}, u32[]{:S(2)}, u32[]{:S(2)}) %collective-permute-start) | collective-permute-done | bytes 262176 | tf_op jit(solution)/shard_map/ppermute | solution.py:77
  16.1 10.3 %collective-permute-done.1 = bf16[8,64,256]{2,1,0:T(8,128)(2,1)S(1)} collective-permute-done((bf16[8,64,256]{2,1,0:T(8,128)(2,1)S(1)}, bf16[8,64,256]{2,1,0:T(8,128)(2,1)S(1)}, u32[]{:S(2)}, u32[]{:S(2)}) %collective-permute-start.1) | collective-permute-done | bytes 262176 | tf_op jit(solution)/shard_map/ppermute | solution.py:77
  26.4 5.1 %collective-permute-done.2 = bf16[8,64,256]{2,1,0:T(8,128)(2,1)S(1)} collective-permute-done((bf16[8,64,256]{2,1,0:T(8,128)(2,1)S(1)}, bf16[8,64,256]{2,1,0:T(8,128)(2,1)S(1)}, u32[]{:S(2)}, u32[]{:S(2)}) %collective-permute-start.2) | collective-permute-done | bytes 262176 | tf_op jit(solution)/shard_map/ppermute | solution.py:77
  31.7 1.6 collective-permute-start.4
  33.3 1.5 collective-permute-start.7
  34.9 3.0 %collective-permute-start.14 = (bf16[2,256,512]{2,1,0:T(8,128)(2,1)S(1)}, bf16[2,256,512]{2,1,0:T(8,128)(2,1)S(1)}, u32[]{:S(2)}, u32[]{:S(2)}) collective-permute-start(bf16[2,256,512]{2,1,0:T(8,128)(2,1)S(1)} %pad_maximum_fusion.1.refs_10_), channel_id=1, source_target_pairs={{0,16},{4,20},{8,24},{12,28},{16,0},{20,4},{24,8},{28,12},{1,17},{... | collective-permute-start | bytes 1572872 | tf_op jit(solution)/shard_map/ppermute | solution.py:77
  37.9 17.6 %collective-permute-done.4.refs_1_ = bf16[4,512,256]{2,1,0:T(8,128)(2,1)S(1)} collective-permute-done((bf16[4,512,256]{2,1,0:T(8,128)(2,1)S(1)}, bf16[4,512,256]{2,1,0:T(8,128)(2,1)S(1)}, u32[]{:S(2)}, u32[]{:S(2)}) %collective-permute-start.4) | collective-permute-done | bytes 1048608 | tf_op jit(solution)/shard_map/ppermute | solution.py:77
  57.1 2.1 collective-permute-done.14.refs_12_
  59.2 1.6 collective-permute-start.15
  61.4 6.6 %collective-permute-done.9.refs_5_ = bf16[2,512,256]{2,1,0:T(8,128)(2,1)S(1)} collective-permute-done((bf16[2,512,256]{2,1,0:T(8,128)(2,1)S(1)}, bf16[2,512,256]{2,1,0:T(8,128)(2,1)S(1)}, u32[]{:S(2)}, u32[]{:S(2)}) %collective-permute-start.9) | collective-permute-done | bytes 524320 | tf_op jit(solution)/shard_map/ppermute | solution.py:77
  68.0 5.0 %collective-permute-done.10.refs_6_ = bf16[2,512,256]{2,1,0:T(8,128)(2,1)S(1)} collective-permute-done((bf16[2,512,256]{2,1,0:T(8,128)(2,1)S(1)}, bf16[2,512,256]{2,1,0:T(8,128)(2,1)S(1)}, u32[]{:S(2)}, u32[]{:S(2)}) %collective-permute-start.10) | collective-permute-done | bytes 524320 | tf_op jit(solution)/shard_map/ppermute | solution.py:77
  73.5 1.4 collective-permute-done.13.refs_9_
  75.7 6.5 %gradient_strips.1 = (bf16[8,64,128]{2,1,0:T(8,128)(2,1)S(1)}, bf16[8,64,128]{2,1,0:T(8,128)(2,1)S(1)}, bf16[8,64,128]{2,1,0:T(8,128)(2,1)S(1)}, bf16[8,64,128]{...) custom-call(s32[130]{0:T(256)S(1)} %pad_add_fusion.meta, ...), custom_call_target="tpu_custom_call" | custom-call | flops 4294967296 | bytes 12582912 | tf_op jit(solution)/shard_map/gradient_strips/pallas_call | solution.py:173
  82.7 1.4 collective-permute-start.17
  84.6 1.6 collective-permute-start.24
  90.0 1.5 collective-permute-start.27
  92.7 2.1 collective-permute-done.24.refs_10_.refs_2_
  96.6 3.8 %collective-permute-start.18 = (bf16[8,64,128]{2,1,0:T(8,128)(2,1)S(1)}, bf16[8,64,128]{2,1,0:T(8,128)(2,1)S(1)}, u32[]{:S(2)}, u32[]{:S(2)}) collective-permute-start(bf16[8,64,128]{2,1,0:T(8,128)(2,1)S(1)} %get-tuple-element.72), channel_id=1, source_target_pairs={{0,12},{4,8},{8,4},{12,0},{16,28},{20,24},{24,20},{28,16},{1,13},{... | collective-permute-start | bytes 393224 | tf_op jit(solution)/shard_map/ppermute | solution.py:77
  100.3 4.5 %collective-permute-done.26.refs_12_.refs_4_ = bf16[8,64,128]{2,1,0:T(8,128)(2,1)S(1)} collective-permute-done((bf16[8,64,128]{2,1,0:T(8,128)(2,1)S(1)}, bf16[8,64,128]{2,1,0:T(8,128)(2,1)S(1)}, u32[]{:S(2)}, u32[]{:S(2)}) %collective-permute-start.26) | collective-permute-done | bytes 131104 | tf_op jit(solution)/shard_map/ppermute | solution.py:77
  104.8 3.8 %collective-permute-start.19 = (bf16[8,64,128]{2,1,0:T(8,128)(2,1)S(1)}, bf16[8,64,128]{2,1,0:T(8,128)(2,1)S(1)}, u32[]{:S(2)}, u32[]{:S(2)}) collective-permute-start(bf16[8,64,128]{2,1,0:T(8,128)(2,1)S(1)} %get-tuple-element.73), channel_id=1, source_target_pairs={{0,16},{4,20},{8,24},{12,28},{16,0},{20,4},{24,8},{28,12},{1,17},{... | collective-permute-start | bytes 393224 | tf_op jit(solution)/shard_map/ppermute | solution.py:77
  108.6 6.4 %collective-permute-done.27.refs_13_.refs_5_ = bf16[8,64,128]{2,1,0:T(8,128)(2,1)S(1)} collective-permute-done((bf16[8,64,128]{2,1,0:T(8,128)(2,1)S(1)}, bf16[8,64,128]{2,1,0:T(8,128)(2,1)S(1)}, u32[]{:S(2)}, u32[]{:S(2)}) %collective-permute-start.27) | collective-permute-done | bytes 131104 | tf_op jit(solution)/shard_map/ppermute | solution.py:77
  115.0 4.3 %collective-permute-start.20 = (bf16[8,64,128]{2,1,0:T(8,128)(2,1)S(1)}, bf16[8,64,128]{2,1,0:T(8,128)(2,1)S(1)}, u32[]{:S(2)}, u32[]{:S(2)}) collective-permute-start(bf16[8,64,128]{2,1,0:T(8,128)(2,1)S(1)} %get-tuple-element.74), channel_id=1, source_target_pairs={{0,20},{4,16},{8,28},{12,24},{16,4},{20,0},{24,12},{28,8},{1,21},{... | collective-permute-start | bytes 393224 | tf_op jit(solution)/shard_map/ppermute | solution.py:77
  120.3 4.9 %collective-permute-done.29.refs_15_.refs_7_ = bf16[8,64,128]{2,1,0:T(8,128)(2,1)S(1)} collective-permute-done((bf16[8,64,128]{2,1,0:T(8,128)(2,1)S(1)}, bf16[8,64,128]{2,1,0:T(8,128)(2,1)S(1)}, u32[]{:S(2)}, u32[]{:S(2)}) %collective-permute-start.29) | collective-permute-done | bytes 131104 | tf_op jit(solution)/shard_map/ppermute | solution.py:77
  125.2 3.0 %collective-permute-start.22 = (bf16[8,64,128]{2,1,0:T(8,128)(2,1)S(1)}, bf16[8,64,128]{2,1,0:T(8,128)(2,1)S(1)}, u32[]{:S(2)}, u32[]{:S(2)}) collective-permute-start(bf16[8,64,128]{2,1,0:T(8,128)(2,1)S(1)} %get-tuple-element.76), channel_id=1, source_target_pairs={{0,28},{4,24},{8,20},{12,16},{16,12},{20,8},{24,4},{28,0},{1,29},{... | collective-permute-start | bytes 393224 | tf_op jit(solution)/shard_map/ppermute | solution.py:77
  128.2 6.3 %directions.3 = (bf16[8,32,256]{2,1,0:T(8,128)(2,1)S(1)}, bf16[8,32,256]{2,1,0:T(8,128)(2,1)S(1)}, bf16[8,32,256]{2,1,0:T(8,128)(2,1)S(1)}, bf16[8,32,256]{2,1,0...) custom-call(s32[130]{0:T(256)S(1)} %pad_add_fusion.meta, ...), custom_call_target="tpu_custom_call" | custom-call | flops 536870912 | bytes 8388608 | tf_op jit(solution)/shard_map/directions/pallas_call | solution.py:242
  134.5 1.6 collective-permute-start.37
  136.2 1.9 collective-permute-start.39
  138.1 2.6 %collective-permute-done.22.refs_7_ = bf16[8,64,128]{2,1,0:T(8,128)(2,1)S(1)} collective-permute-done((bf16[8,64,128]{2,1,0:T(8,128)(2,1)S(1)}, bf16[8,64,128]{2,1,0:T(8,128)(2,1)S(1)}, u32[]{:S(2)}, u32[]{:S(2)}) %collective-permute-start.22) | collective-permute-done | bytes 131104 | tf_op jit(solution)/shard_map/ppermute | solution.py:77
  142.0 6.3 %directions.2 = (bf16[8,32,256]{2,1,0:T(8,128)(2,1)S(1)}, bf16[8,32,256]{2,1,0:T(8,128)(2,1)S(1)}, bf16[8,32,256]{2,1,0:T(8,128)(2,1)S(1)}, bf16[8,32,256]{2,1,0...) custom-call(s32[130]{0:T(256)S(1)} %pad_add_fusion.meta, ...), custom_call_target="tpu_custom_call" | custom-call | flops 536870912 | bytes 8388608 | tf_op jit(solution)/shard_map/directions/pallas_call | solution.py:242
  150.4 1.5 collective-permute-start.30
  151.9 3.8 %collective-permute-start.31 = (bf16[8,32,256]{2,1,0:T(8,128)(2,1)S(1)}, bf16[8,32,256]{2,1,0:T(8,128)(2,1)S(1)}, u32[]{:S(2)}, u32[]{:S(2)}) collective-permute-start(bf16[8,32,256]{2,1,0:T(8,128)(2,1)S(1)} %get-tuple-element.90), channel_id=1, source_target_pairs={{0,8},{4,12},{8,0},{12,4},{16,24},{20,28},{24,16},{28,20},{1,9},{5... | collective-permute-start | bytes 393224 | tf_op jit(solution)/shard_map/ppermute | solution.py:77
  157.0 3.3 %collective-permute-done.42.refs_14_ = bf16[8,32,256]{2,1,0:T(8,128)(2,1)S(1)} collective-permute-done((bf16[8,32,256]{2,1,0:T(8,128)(2,1)S(1)}, bf16[8,32,256]{2,1,0:T(8,128)(2,1)S(1)}, u32[]{:S(2)}, u32[]{:S(2)}) %collective-permute-start.42) | collective-permute-done | bytes 131104 | tf_op jit(solution)/shard_map/ppermute | solution.py:77
  160.3 7.8 %collective-permute-done.43.refs_15_ = bf16[8,32,256]{2,1,0:T(8,128)(2,1)S(1)} collective-permute-done((bf16[8,32,256]{2,1,0:T(8,128)(2,1)S(1)}, bf16[8,32,256]{2,1,0:T(8,128)(2,1)S(1)}, u32[]{:S(2)}, u32[]{:S(2)}) %collective-permute-start.43) | collective-permute-done | bytes 131104 | tf_op jit(solution)/shard_map/ppermute | solution.py:77
  168.7 1.7 collective-permute-start.36
  170.4 4.6 %collective-permute-done.34.refs_5_ = bf16[8,32,256]{2,1,0:T(8,128)(2,1)S(1)} collective-permute-done((bf16[8,32,256]{2,1,0:T(8,128)(2,1)S(1)}, bf16[8,32,256]{2,1,0:T(8,128)(2,1)S(1)}, u32[]{:S(2)}, u32[]{:S(2)}) %collective-permute-start.34) | collective-permute-done | bytes 131104 | tf_op jit(solution)/shard_map/ppermute | solution.py:77
  175.0 4.3 %collective-permute-done.35.refs_6_ = bf16[8,32,256]{2,1,0:T(8,128)(2,1)S(1)} collective-permute-done((bf16[8,32,256]{2,1,0:T(8,128)(2,1)S(1)}, bf16[8,32,256]{2,1,0:T(8,128)(2,1)S(1)}, u32[]{:S(2)}, u32[]{:S(2)}) %collective-permute-start.35) | collective-permute-done | bytes 131104 | tf_op jit(solution)/shard_map/ppermute | solution.py:77
  179.3 2.3 collective-permute-done.36.refs_7_
  181.5 1.6 regroup.1
  183.2 1.9 collective-permute-start.45
  185.2 1.5 collective-permute-start.46
  186.7 10.4 %statistics.1 = (f32[1,16,256,256]{3,2,1,0:T(8,128)}, f32[1,16,256,256]{3,2,1,0:T(8,128)}, f32[1,16,256,256]{3,2,1,0:T(8,128)}) custom-call(s32[130]{0:T(256)S(1)} %pad_add_fusion.meta, f32[1,16,256,256]{3,2,1,0:T(8,128)S(1)} %copy-done.3, f32[1,16,256,256]{3,2,1,0:T(8,128)S(1)} %copy-done.4, f32[1,16,256,256]{3,2,1,0:T(8,128)S(1)} %copy-done, ...), custom_call_target="tpu_custom_call" | custom-call | flops 1073741824 | bytes 27262976 | tf_op jit(solution)/shard_map/statistics/pallas_call | solution.py:303
  197.1 6.3 %collective-permute-done.44.refs_1_ = bf16[32,8192]{1,0:T(8,128)(2,1)S(1)} collective-permute-done((bf16[32,8192]{1,0:T(8,128)(2,1)S(1)}, bf16[32,8192]{1,0:T(8,128)(2,1)S(1)}, u32[]{:S(2)}, u32[]{:S(2)}) %collective-permute-start.44) | collective-permute-done | bytes 524320 | tf_op jit(solution)/shard_map/ppermute | solution.py:77
  203.4 16.7 %collective-permute-done.45.refs_2_ = bf16[32,8192]{1,0:T(8,128)(2,1)S(1)} collective-permute-done((bf16[32,8192]{1,0:T(8,128)(2,1)S(1)}, bf16[32,8192]{1,0:T(8,128)(2,1)S(1)}, u32[]{:S(2)}, u32[]{:S(2)}) %collective-permute-start.45) | collective-permute-done | bytes 524320 | tf_op jit(solution)/shard_map/ppermute | solution.py:77
  220.0 9.7 %collective-permute-done.46.refs_3_ = bf16[32,8192]{1,0:T(8,128)(2,1)S(1)} collective-permute-done((bf16[32,8192]{1,0:T(8,128)(2,1)S(1)}, bf16[32,8192]{1,0:T(8,128)(2,1)S(1)}, u32[]{:S(2)}, u32[]{:S(2)}) %collective-permute-start.46) | collective-permute-done | bytes 524320 | tf_op jit(solution)/shard_map/ppermute | solution.py:77
  229.8 1.9 stack_rows.1
  (72 shorter events, 21.4 us)
Async XLA Ops:
  5.4 10.8 %collective-permute-start = (bf16[8,64,256]{2,1,0:T(8,128)(2,1)S(1)}, bf16[8,64,256]{2,1,0:T(8,128)(2,1)S(1)}, u32[]{:S(2)}, u32[]{:S(2)}) collective-permute-start(bf16[8,64,256]{2,1,0:T(8,128)(2,1)S(1)} %get-tuple-element.57), channel_id=1, source_target_pairs={{0,8},{4,12},{8,0},{12,4},{16,24},{20,28},{24,16},{28,20},{1,9},{5... | collective-permute-start | bytes 786440 | tf_op jit(solution)/shard_map/ppermute | solution.py:77
  5.5 21.0 %collective-permute-start.1 = (bf16[8,64,256]{2,1,0:T(8,128)(2,1)S(1)}, bf16[8,64,256]{2,1,0:T(8,128)(2,1)S(1)}, u32[]{:S(2)}, u32[]{:S(2)}) collective-permute-start(bf16[8,64,256]{2,1,0:T(8,128)(2,1)S(1)} %get-tuple-element.58), channel_id=1, source_target_pairs={{0,16},{4,20},{8,24},{12,28},{16,0},{20,4},{24,8},{28,12},{1,17},{... | collective-permute-start | bytes 786440 | tf_op jit(solution)/shard_map/ppermute | solution.py:77
  8.5 23.1 %collective-permute-start.2 = (bf16[8,64,256]{2,1,0:T(8,128)(2,1)S(1)}, bf16[8,64,256]{2,1,0:T(8,128)(2,1)S(1)}, u32[]{:S(2)}, u32[]{:S(2)}) collective-permute-start(bf16[8,64,256]{2,1,0:T(8,128)(2,1)S(1)} %get-tuple-element.59), channel_id=1, source_target_pairs={{0,24},{4,28},{8,16},{12,20},{16,8},{20,12},{24,0},{28,4},{1,25},{... | collective-permute-start | bytes 786440 | tf_op jit(solution)/shard_map/ppermute | solution.py:77
  8.9 22.6 %collective-permute-start.3 = (bf16[256,512]{1,0:T(8,128)(2,1)S(1)}, bf16[256,512]{1,0:T(8,128)(2,1)S(1)}, u32[]{:S(2)}, u32[]{:S(2)}) collective-permute-start(bf16[256,512]{1,0:T(8,128)(2,1)S(1)} %get-tuple-element.60), channel_id=1, source_target_pairs={{0,4},{4,0},{8,12},{12,8},{16,20},{20,16},{24,28},{28,24},{1,5},{5... | collective-permute-start | bytes 786440 | tf_op jit(solution)/shard_map/ppermute | solution.py:77
  31.7 23.8 %collective-permute-start.4 = (bf16[4,512,256]{2,1,0:T(8,128)(2,1)S(1)}, bf16[4,512,256]{2,1,0:T(8,128)(2,1)S(1)}, u32[]{:S(2)}, u32[]{:S(2)}) collective-permute-start(bf16[4,512,256]{2,1,0:T(8,128)(2,1)S(1)} %pad_maximum_fusion.refs_0_), channel_id=1, source_target_pairs={{0,4},{4,0},{8,12},{12,8},{16,20},{20,16},{24,28},{28,24},{1,5},{5... | collective-permute-start | bytes 3145736 | tf_op jit(solution)/shard_map/ppermute | solution.py:77
  33.3 27.5 %collective-permute-start.7 = (bf16[4,512,256]{2,1,0:T(8,128)(2,1)S(1)}, bf16[4,512,256]{2,1,0:T(8,128)(2,1)S(1)}, u32[]{:S(2)}, u32[]{:S(2)}) collective-permute-start(bf16[4,512,256]{2,1,0:T(8,128)(2,1)S(1)} %pad_maximum_fusion.refs_0_), channel_id=1, source_target_pairs={{0,2},{1,3},{2,0},{3,1},{4,6},{5,7},{6,4},{7,5},{8,10},{9,11},{10,... | collective-permute-start | bytes 3145736 | tf_op jit(solution)/shard_map/ppermute | solution.py:77
  34.8 20.9 %collective-permute-start.8 = (bf16[2,256,512]{2,1,0:T(8,128)(2,1)S(1)}, bf16[2,256,512]{2,1,0:T(8,128)(2,1)S(1)}, u32[]{:S(2)}, u32[]{:S(2)}) collective-permute-start(bf16[2,256,512]{2,1,0:T(8,128)(2,1)S(1)} %pad_maximum_fusion.1.refs_10_), channel_id=1, source_target_pairs={{0,8},{4,12},{8,0},{12,4},{16,24},{20,28},{24,16},{28,20},{1,9},{5... | collective-permute-start | bytes 1572872 | tf_op jit(solution)/shard_map/ppermute | solution.py:77
  34.9 24.3 %collective-permute-start.14 = (bf16[2,256,512]{2,1,0:T(8,128)(2,1)S(1)}, bf16[2,256,512]{2,1,0:T(8,128)(2,1)S(1)}, u32[]{:S(2)}, u32[]{:S(2)}) collective-permute-start(bf16[2,256,512]{2,1,0:T(8,128)(2,1)S(1)} %pad_maximum_fusion.1.refs_10_), channel_id=1, source_target_pairs={{0,16},{4,20},{8,24},{12,28},{16,0},{20,4},{24,8},{28,12},{1,17},{... | collective-permute-start | bytes 1572872 | tf_op jit(solution)/shard_map/ppermute | solution.py:77
  55.8 12.2 %collective-permute-start.9 = (bf16[2,512,256]{2,1,0:T(8,128)(2,1)S(1)}, bf16[2,512,256]{2,1,0:T(8,128)(2,1)S(1)}, u32[]{:S(2)}, u32[]{:S(2)}) collective-permute-start(bf16[2,512,256]{2,1,0:T(8,128)(2,1)S(1)} %slice.8), channel_id=1, source_target_pairs={{0,2},{1,3},{2,0},{3,1},{4,6},{5,7},{6,4},{7,5},{8,10},{9,11},{10,... | collective-permute-start | bytes 1572872 | tf_op jit(solution)/shard_map/ppermute | solution.py:77
  57.1 16.4 %collective-permute-start.5 = (bf16[4,512,256]{2,1,0:T(8,128)(2,1)S(1)}, bf16[4,512,256]{2,1,0:T(8,128)(2,1)S(1)}, u32[]{:S(2)}, u32[]{:S(2)}) collective-permute-start(bf16[4,512,256]{2,1,0:T(8,128)(2,1)S(1)} %pad_maximum_fusion.refs_0_), channel_id=1, source_target_pairs={{0,1},{1,0},{2,3},{3,2},{4,5},{5,4},{6,7},{7,6},{8,9},{9,8},{10,11... | collective-permute-start | bytes 3145736 | tf_op jit(solution)/shard_map/ppermute | solution.py:77
  59.2 13.8 %collective-permute-start.15 = (bf16[2,256,512]{2,1,0:T(8,128)(2,1)S(1)}, bf16[2,256,512]{2,1,0:T(8,128)(2,1)S(1)}, u32[]{:S(2)}, u32[]{:S(2)}) collective-permute-start(bf16[2,256,512]{2,1,0:T(8,128)(2,1)S(1)} %collective-permute-done.14.refs_12_), channel_id=1, source_target_pairs={{0,8},{4,12},{8,0},{12,4},{16,24},{20,28},{24,16},{28,20},{1,9},{5... | collective-permute-start | bytes 1572872 | tf_op jit(solution)/shard_map/ppermute | solution.py:77
  60.8 67.4 %copy-start = (f32[1,16,256,256]{3,2,1,0:T(8,128)S(1)}, f32[1,16,256,256]{3,2,1,0:T(8,128)}, u32[]{:S(2)}) copy-start(f32[1,16,256,256]{3,2,1,0:T(8,128)} %second_ref.5) | copy-start | bytes 12582916
  60.9 12.1 %collective-permute-start.10 = (bf16[2,512,256]{2,1,0:T(8,128)(2,1)S(1)}, bf16[2,512,256]{2,1,0:T(8,128)(2,1)S(1)}, u32[]{:S(2)}, u32[]{:S(2)}) collective-permute-start(bf16[2,512,256]{2,1,0:T(8,128)(2,1)S(1)} %slice.9), channel_id=1, source_target_pairs={{0,4},{4,0},{8,12},{12,8},{16,20},{20,16},{24,28},{28,24},{1,5},{5... | collective-permute-start | bytes 1572872 | tf_op jit(solution)/shard_map/ppermute | solution.py:77
  61.4 12.1 %collective-permute-start.6 = (bf16[4,512,256]{2,1,0:T(8,128)(2,1)S(1)}, bf16[4,512,256]{2,1,0:T(8,128)(2,1)S(1)}, u32[]{:S(2)}, u32[]{:S(2)}) collective-permute-start(bf16[4,512,256]{2,1,0:T(8,128)(2,1)S(1)} %collective-permute-done.4.refs_1_), channel_id=1, source_target_pairs={{0,1},{1,0},{2,3},{3,2},{4,5},{5,4},{6,7},{7,6},{8,9},{9,8},{10,11... | collective-permute-start | bytes 3145736 | tf_op jit(solution)/shard_map/ppermute | solution.py:77
  68.0 7.6 %collective-permute-start.11 = (bf16[4,512,256]{2,1,0:T(8,128)(2,1)S(1)}, bf16[4,512,256]{2,1,0:T(8,128)(2,1)S(1)}, u32[]{:S(2)}, u32[]{:S(2)}) collective-permute-start(bf16[4,512,256]{2,1,0:T(8,128)(2,1)S(1)} %collective-permute-done.7.refs_4_), channel_id=1, source_target_pairs={{0,1},{1,0},{2,3},{3,2},{4,5},{5,4},{6,7},{7,6},{8,9},{9,8},{10,11... | collective-permute-start | bytes 3145736 | tf_op jit(solution)/shard_map/ppermute | solution.py:77
  73.0 1.9 collective-permute-start.13
  73.0 2.7 %collective-permute-start.12 = (bf16[2,512,256]{2,1,0:T(8,128)(2,1)S(1)}, bf16[2,512,256]{2,1,0:T(8,128)(2,1)S(1)}, u32[]{:S(2)}, u32[]{:S(2)}) collective-permute-start(bf16[2,512,256]{2,1,0:T(8,128)(2,1)S(1)} %collective-permute-done.9.refs_5_), channel_id=1, source_target_pairs={{0,1},{1,0},{2,3},{3,2},{4,5},{5,4},{6,7},{7,6},{8,9},{9,8},{10,11... | collective-permute-start | bytes 1572872 | tf_op jit(solution)/shard_map/ppermute | solution.py:77
  82.2 6.4 %collective-permute-start.16 = (bf16[8,64,128]{2,1,0:T(8,128)(2,1)S(1)}, bf16[8,64,128]{2,1,0:T(8,128)(2,1)S(1)}, u32[]{:S(2)}, u32[]{:S(2)}) collective-permute-start(bf16[8,64,128]{2,1,0:T(8,128)(2,1)S(1)} %get-tuple-element.70), channel_id=1, source_target_pairs={{0,4},{4,0},{8,12},{12,8},{16,20},{20,16},{24,28},{28,24},{1,5},{5... | collective-permute-start | bytes 393224 | tf_op jit(solution)/shard_map/ppermute | solution.py:77
  82.7 7.2 %collective-permute-start.17 = (bf16[8,64,128]{2,1,0:T(8,128)(2,1)S(1)}, bf16[8,64,128]{2,1,0:T(8,128)(2,1)S(1)}, u32[]{:S(2)}, u32[]{:S(2)}) collective-permute-start(bf16[8,64,128]{2,1,0:T(8,128)(2,1)S(1)} %get-tuple-element.71), channel_id=1, source_target_pairs={{0,8},{4,12},{8,0},{12,4},{16,24},{20,28},{24,16},{28,20},{1,9},{5... | collective-permute-start | bytes 393224 | tf_op jit(solution)/shard_map/ppermute | solution.py:77
  84.1 7.3 %collective-permute-start.23 = (bf16[8,64,128]{2,1,0:T(8,128)(2,1)S(1)}, bf16[8,64,128]{2,1,0:T(8,128)(2,1)S(1)}, u32[]{:S(2)}, u32[]{:S(2)}) collective-permute-start(bf16[8,64,128]{2,1,0:T(8,128)(2,1)S(1)} %get-tuple-element.78), channel_id=1, source_target_pairs={{0,4},{4,0},{8,12},{12,8},{16,20},{20,16},{24,28},{28,24},{1,5},{5... | collective-permute-start | bytes 393224 | tf_op jit(solution)/shard_map/ppermute | solution.py:77
  84.6 10.1 %collective-permute-start.24 = (bf16[8,64,128]{2,1,0:T(8,128)(2,1)S(1)}, bf16[8,64,128]{2,1,0:T(8,128)(2,1)S(1)}, u32[]{:S(2)}, u32[]{:S(2)}) collective-permute-start(bf16[8,64,128]{2,1,0:T(8,128)(2,1)S(1)} %get-tuple-element.79), channel_id=1, source_target_pairs={{0,8},{4,12},{8,0},{12,4},{16,24},{20,28},{24,16},{28,20},{1,9},{5... | collective-permute-start | bytes 393224 | tf_op jit(solution)/shard_map/ppermute | solution.py:77
  86.3 10.3 %collective-permute-start.25 = (bf16[8,64,128]{2,1,0:T(8,128)(2,1)S(1)}, bf16[8,64,128]{2,1,0:T(8,128)(2,1)S(1)}, u32[]{:S(2)}, u32[]{:S(2)}) collective-permute-start(bf16[8,64,128]{2,1,0:T(8,128)(2,1)S(1)} %get-tuple-element.80), channel_id=1, source_target_pairs={{0,12},{4,8},{8,4},{12,0},{16,28},{20,24},{24,20},{28,16},{1,13},{... | collective-permute-start | bytes 393224 | tf_op jit(solution)/shard_map/ppermute | solution.py:77
  88.6 16.2 %collective-permute-start.26 = (bf16[8,64,128]{2,1,0:T(8,128)(2,1)S(1)}, bf16[8,64,128]{2,1,0:T(8,128)(2,1)S(1)}, u32[]{:S(2)}, u32[]{:S(2)}) collective-permute-start(bf16[8,64,128]{2,1,0:T(8,128)(2,1)S(1)} %get-tuple-element.81), channel_id=1, source_target_pairs={{0,16},{4,20},{8,24},{12,28},{16,0},{20,4},{24,8},{28,12},{1,17},{... | collective-permute-start | bytes 393224 | tf_op jit(solution)/shard_map/ppermute | solution.py:77
  90.0 25.1 %collective-permute-start.27 = (bf16[8,64,128]{2,1,0:T(8,128)(2,1)S(1)}, bf16[8,64,128]{2,1,0:T(8,128)(2,1)S(1)}, u32[]{:S(2)}, u32[]{:S(2)}) collective-permute-start(bf16[8,64,128]{2,1,0:T(8,128)(2,1)S(1)} %get-tuple-element.82), channel_id=1, source_target_pairs={{0,20},{4,16},{8,28},{12,24},{16,4},{20,0},{24,12},{28,8},{1,21},{... | collective-permute-start | bytes 393224 | tf_op jit(solution)/shard_map/ppermute | solution.py:77
  91.5 27.8 %collective-permute-start.28 = (bf16[8,64,128]{2,1,0:T(8,128)(2,1)S(1)}, bf16[8,64,128]{2,1,0:T(8,128)(2,1)S(1)}, u32[]{:S(2)}, u32[]{:S(2)}) collective-permute-start(bf16[8,64,128]{2,1,0:T(8,128)(2,1)S(1)} %get-tuple-element.83), channel_id=1, source_target_pairs={{0,24},{4,28},{8,16},{12,20},{16,8},{20,12},{24,0},{28,4},{1,25},{... | collective-permute-start | bytes 393224 | tf_op jit(solution)/shard_map/ppermute | solution.py:77
  94.7 30.5 %collective-permute-start.29 = (bf16[8,64,128]{2,1,0:T(8,128)(2,1)S(1)}, bf16[8,64,128]{2,1,0:T(8,128)(2,1)S(1)}, u32[]{:S(2)}, u32[]{:S(2)}) collective-permute-start(bf16[8,64,128]{2,1,0:T(8,128)(2,1)S(1)} %get-tuple-element.84), channel_id=1, source_target_pairs={{0,28},{4,24},{8,20},{12,16},{16,12},{20,8},{24,4},{28,0},{1,29},{... | collective-permute-start | bytes 393224 | tf_op jit(solution)/shard_map/ppermute | solution.py:77
  96.6 38.0 %collective-permute-start.18 = (bf16[8,64,128]{2,1,0:T(8,128)(2,1)S(1)}, bf16[8,64,128]{2,1,0:T(8,128)(2,1)S(1)}, u32[]{:S(2)}, u32[]{:S(2)}) collective-permute-start(bf16[8,64,128]{2,1,0:T(8,128)(2,1)S(1)} %get-tuple-element.72), channel_id=1, source_target_pairs={{0,12},{4,8},{8,4},{12,0},{16,28},{20,24},{24,20},{28,16},{1,13},{... | collective-permute-start | bytes 393224 | tf_op jit(solution)/shard_map/ppermute | solution.py:77
  104.8 31.4 %collective-permute-start.19 = (bf16[8,64,128]{2,1,0:T(8,128)(2,1)S(1)}, bf16[8,64,128]{2,1,0:T(8,128)(2,1)S(1)}, u32[]{:S(2)}, u32[]{:S(2)}) collective-permute-start(bf16[8,64,128]{2,1,0:T(8,128)(2,1)S(1)} %get-tuple-element.73), channel_id=1, source_target_pairs={{0,16},{4,20},{8,24},{12,28},{16,0},{20,4},{24,8},{28,12},{1,17},{... | collective-permute-start | bytes 393224 | tf_op jit(solution)/shard_map/ppermute | solution.py:77
  115.0 21.2 %collective-permute-start.20 = (bf16[8,64,128]{2,1,0:T(8,128)(2,1)S(1)}, bf16[8,64,128]{2,1,0:T(8,128)(2,1)S(1)}, u32[]{:S(2)}, u32[]{:S(2)}) collective-permute-start(bf16[8,64,128]{2,1,0:T(8,128)(2,1)S(1)} %get-tuple-element.74), channel_id=1, source_target_pairs={{0,20},{4,16},{8,28},{12,24},{16,4},{20,0},{24,12},{28,8},{1,21},{... | collective-permute-start | bytes 393224 | tf_op jit(solution)/shard_map/ppermute | solution.py:77
  119.3 18.8 %collective-permute-start.21 = (bf16[8,64,128]{2,1,0:T(8,128)(2,1)S(1)}, bf16[8,64,128]{2,1,0:T(8,128)(2,1)S(1)}, u32[]{:S(2)}, u32[]{:S(2)}) collective-permute-start(bf16[8,64,128]{2,1,0:T(8,128)(2,1)S(1)} %get-tuple-element.75), channel_id=1, source_target_pairs={{0,24},{4,28},{8,16},{12,20},{16,8},{20,12},{24,0},{28,4},{1,25},{... | collective-permute-start | bytes 393224 | tf_op jit(solution)/shard_map/ppermute | solution.py:77
  125.2 15.4 %collective-permute-start.22 = (bf16[8,64,128]{2,1,0:T(8,128)(2,1)S(1)}, bf16[8,64,128]{2,1,0:T(8,128)(2,1)S(1)}, u32[]{:S(2)}, u32[]{:S(2)}) collective-permute-start(bf16[8,64,128]{2,1,0:T(8,128)(2,1)S(1)} %get-tuple-element.76), channel_id=1, source_target_pairs={{0,28},{4,24},{8,20},{12,16},{16,12},{20,8},{24,4},{28,0},{1,29},{... | collective-permute-start | bytes 393224 | tf_op jit(solution)/shard_map/ppermute | solution.py:77
  134.5 13.8 %collective-permute-start.37 = (bf16[8,32,256]{2,1,0:T(8,128)(2,1)S(1)}, bf16[8,32,256]{2,1,0:T(8,128)(2,1)S(1)}, u32[]{:S(2)}, u32[]{:S(2)}) collective-permute-start(bf16[8,32,256]{2,1,0:T(8,128)(2,1)S(1)} %get-tuple-element.97), channel_id=1, source_target_pairs={{0,4},{4,0},{8,12},{12,8},{16,20},{20,16},{24,28},{28,24},{1,5},{5... | collective-permute-start | bytes 393224 | tf_op jit(solution)/shard_map/ppermute | solution.py:77
  136.2 13.1 %collective-permute-start.38 = (bf16[8,32,256]{2,1,0:T(8,128)(2,1)S(1)}, bf16[8,32,256]{2,1,0:T(8,128)(2,1)S(1)}, u32[]{:S(2)}, u32[]{:S(2)}) collective-permute-start(bf16[8,32,256]{2,1,0:T(8,128)(2,1)S(1)} %get-tuple-element.98), channel_id=1, source_target_pairs={{0,8},{4,12},{8,0},{12,4},{16,24},{20,28},{24,16},{28,20},{1,9},{5... | collective-permute-start | bytes 393224 | tf_op jit(solution)/shard_map/ppermute | solution.py:77
  136.2 14.2 %collective-permute-start.39 = (bf16[8,32,256]{2,1,0:T(8,128)(2,1)S(1)}, bf16[8,32,256]{2,1,0:T(8,128)(2,1)S(1)}, u32[]{:S(2)}, u32[]{:S(2)}) collective-permute-start(bf16[8,32,256]{2,1,0:T(8,128)(2,1)S(1)} %get-tuple-element.99), channel_id=1, source_target_pairs={{0,12},{4,8},{8,4},{12,0},{16,28},{20,24},{24,20},{28,16},{1,13},{... | collective-permute-start | bytes 393224 | tf_op jit(solution)/shard_map/ppermute | solution.py:77
  138.1 13.8 %collective-permute-start.40 = (bf16[8,32,256]{2,1,0:T(8,128)(2,1)S(1)}, bf16[8,32,256]{2,1,0:T(8,128)(2,1)S(1)}, u32[]{:S(2)}, u32[]{:S(2)}) collective-permute-start(bf16[8,32,256]{2,1,0:T(8,128)(2,1)S(1)} %get-tuple-element.100), channel_id=1, source_target_pairs={{0,16},{4,20},{8,24},{12,28},{16,0},{20,4},{24,8},{28,12},{1,17},{... | collective-permute-start | bytes 393224 | tf_op jit(solution)/shard_map/ppermute | solution.py:77
  140.7 15.0 %collective-permute-start.41 = (bf16[8,32,256]{2,1,0:T(8,128)(2,1)S(1)}, bf16[8,32,256]{2,1,0:T(8,128)(2,1)S(1)}, u32[]{:S(2)}, u32[]{:S(2)}) collective-permute-start(bf16[8,32,256]{2,1,0:T(8,128)(2,1)S(1)} %get-tuple-element.101), channel_id=1, source_target_pairs={{0,20},{4,16},{8,28},{12,24},{16,4},{20,0},{24,12},{28,8},{1,21},{... | collective-permute-start | bytes 393224 | tf_op jit(solution)/shard_map/ppermute | solution.py:77
  148.3 12.0 %collective-permute-start.42 = (bf16[8,32,256]{2,1,0:T(8,128)(2,1)S(1)}, bf16[8,32,256]{2,1,0:T(8,128)(2,1)S(1)}, u32[]{:S(2)}, u32[]{:S(2)}) collective-permute-start(bf16[8,32,256]{2,1,0:T(8,128)(2,1)S(1)} %get-tuple-element.102), channel_id=1, source_target_pairs={{0,24},{4,28},{8,16},{12,20},{16,8},{20,12},{24,0},{28,4},{1,25},{... | collective-permute-start | bytes 393224 | tf_op jit(solution)/shard_map/ppermute | solution.py:77
  149.3 18.8 %collective-permute-start.43 = (bf16[8,32,256]{2,1,0:T(8,128)(2,1)S(1)}, bf16[8,32,256]{2,1,0:T(8,128)(2,1)S(1)}, u32[]{:S(2)}, u32[]{:S(2)}) collective-permute-start(bf16[8,32,256]{2,1,0:T(8,128)(2,1)S(1)} %get-tuple-element.103), channel_id=1, source_target_pairs={{0,28},{4,24},{8,20},{12,16},{16,12},{20,8},{24,4},{28,0},{1,29},{... | collective-permute-start | bytes 393224 | tf_op jit(solution)/shard_map/ppermute | solution.py:77
  150.4 17.8 %collective-permute-start.30 = (bf16[8,32,256]{2,1,0:T(8,128)(2,1)S(1)}, bf16[8,32,256]{2,1,0:T(8,128)(2,1)S(1)}, u32[]{:S(2)}, u32[]{:S(2)}) collective-permute-start(bf16[8,32,256]{2,1,0:T(8,128)(2,1)S(1)} %get-tuple-element.89), channel_id=1, source_target_pairs={{0,4},{4,0},{8,12},{12,8},{16,20},{20,16},{24,28},{28,24},{1,5},{5... | collective-permute-start | bytes 393224 | tf_op jit(solution)/shard_map/ppermute | solution.py:77
  151.9 16.8 %collective-permute-start.31 = (bf16[8,32,256]{2,1,0:T(8,128)(2,1)S(1)}, bf16[8,32,256]{2,1,0:T(8,128)(2,1)S(1)}, u32[]{:S(2)}, u32[]{:S(2)}) collective-permute-start(bf16[8,32,256]{2,1,0:T(8,128)(2,1)S(1)} %get-tuple-element.90), channel_id=1, source_target_pairs={{0,8},{4,12},{8,0},{12,4},{16,24},{20,28},{24,16},{28,20},{1,9},{5... | collective-permute-start | bytes 393224 | tf_op jit(solution)/shard_map/ppermute | solution.py:77
  155.7 14.7 %collective-permute-start.32 = (bf16[8,32,256]{2,1,0:T(8,128)(2,1)S(1)}, bf16[8,32,256]{2,1,0:T(8,128)(2,1)S(1)}, u32[]{:S(2)}, u32[]{:S(2)}) collective-permute-start(bf16[8,32,256]{2,1,0:T(8,128)(2,1)S(1)} %get-tuple-element.91), channel_id=1, source_target_pairs={{0,12},{4,8},{8,4},{12,0},{16,28},{20,24},{24,20},{28,16},{1,13},{... | collective-permute-start | bytes 393224 | tf_op jit(solution)/shard_map/ppermute | solution.py:77
  160.3 10.1 %collective-permute-start.33 = (bf16[8,32,256]{2,1,0:T(8,128)(2,1)S(1)}, bf16[8,32,256]{2,1,0:T(8,128)(2,1)S(1)}, u32[]{:S(2)}, u32[]{:S(2)}) collective-permute-start(bf16[8,32,256]{2,1,0:T(8,128)(2,1)S(1)} %get-tuple-element.92), channel_id=1, source_target_pairs={{0,16},{4,20},{8,24},{12,28},{16,0},{20,4},{24,8},{28,12},{1,17},{... | collective-permute-start | bytes 393224 | tf_op jit(solution)/shard_map/ppermute | solution.py:77
  168.1 6.9 %collective-permute-start.34 = (bf16[8,32,256]{2,1,0:T(8,128)(2,1)S(1)}, bf16[8,32,256]{2,1,0:T(8,128)(2,1)S(1)}, u32[]{:S(2)}, u32[]{:S(2)}) collective-permute-start(bf16[8,32,256]{2,1,0:T(8,128)(2,1)S(1)} %get-tuple-element.93), channel_id=1, source_target_pairs={{0,20},{4,16},{8,28},{12,24},{16,4},{20,0},{24,12},{28,8},{1,21},{... | collective-permute-start | bytes 393224 | tf_op jit(solution)/shard_map/ppermute | solution.py:77
  168.1 11.1 %collective-permute-start.35 = (bf16[8,32,256]{2,1,0:T(8,128)(2,1)S(1)}, bf16[8,32,256]{2,1,0:T(8,128)(2,1)S(1)}, u32[]{:S(2)}, u32[]{:S(2)}) collective-permute-start(bf16[8,32,256]{2,1,0:T(8,128)(2,1)S(1)} %get-tuple-element.94), channel_id=1, source_target_pairs={{0,24},{4,28},{8,16},{12,20},{16,8},{20,12},{24,0},{28,4},{1,25},{... | collective-permute-start | bytes 393224 | tf_op jit(solution)/shard_map/ppermute | solution.py:77
  168.7 12.9 %collective-permute-start.36 = (bf16[8,32,256]{2,1,0:T(8,128)(2,1)S(1)}, bf16[8,32,256]{2,1,0:T(8,128)(2,1)S(1)}, u32[]{:S(2)}, u32[]{:S(2)}) collective-permute-start(bf16[8,32,256]{2,1,0:T(8,128)(2,1)S(1)} %get-tuple-element.95), channel_id=1, source_target_pairs={{0,28},{4,24},{8,20},{12,16},{16,12},{20,8},{24,4},{28,0},{1,29},{... | collective-permute-start | bytes 393224 | tf_op jit(solution)/shard_map/ppermute | solution.py:77
  183.2 20.2 %collective-permute-start.44 = (bf16[32,8192]{1,0:T(8,128)(2,1)S(1)}, bf16[32,8192]{1,0:T(8,128)(2,1)S(1)}, u32[]{:S(2)}, u32[]{:S(2)}) collective-permute-start(bf16[32,8192]{1,0:T(8,128)(2,1)S(1)} %get-tuple-element.105), channel_id=1, source_target_pairs={{0,8},{4,12},{8,0},{12,4},{16,24},{20,28},{24,16},{28,20},{1,9},{5... | collective-permute-start | bytes 1572872 | tf_op jit(solution)/shard_map/ppermute | solution.py:77
  183.2 36.8 %collective-permute-start.45 = (bf16[32,8192]{1,0:T(8,128)(2,1)S(1)}, bf16[32,8192]{1,0:T(8,128)(2,1)S(1)}, u32[]{:S(2)}, u32[]{:S(2)}) collective-permute-start(bf16[32,8192]{1,0:T(8,128)(2,1)S(1)} %get-tuple-element.106), channel_id=1, source_target_pairs={{0,16},{4,20},{8,24},{12,28},{16,0},{20,4},{24,8},{28,12},{1,17},{... | collective-permute-start | bytes 1572872 | tf_op jit(solution)/shard_map/ppermute | solution.py:77
  185.2 44.6 %collective-permute-start.46 = (bf16[32,8192]{1,0:T(8,128)(2,1)S(1)}, bf16[32,8192]{1,0:T(8,128)(2,1)S(1)}, u32[]{:S(2)}, u32[]{:S(2)}) collective-permute-start(bf16[32,8192]{1,0:T(8,128)(2,1)S(1)} %get-tuple-element.107), channel_id=1, source_target_pairs={{0,24},{4,28},{8,16},{12,20},{16,8},{20,12},{24,0},{28,4},{1,25},{... | collective-permute-start | bytes 1572872 | tf_op jit(solution)/shard_map/ppermute | solution.py:77
  (6 other events, 226.4 us)

commit v6 on v5

--- a/solution.py
+++ b/solution.py
@@ -77,6 +77,16 @@
     return lax.ppermute(value, axis, [(i, i ^ offset) for i in range(count)])
 
 
+def offsets_of(groups):
+    far, near = range(groups // 2, groups), range(1, groups // 2)
+    order = [k for pair in zip(far, near) for k in pair]
+    return [*order, groups - 1, 0]
+
+
+def pair_order(pairs):
+    return [pairs // 2, 0, *[k for k in range(1, pairs) if k != pairs // 2]]
+
+
 def prepare_kernel(pairs, block, meta, cot_ref, context_ref, *refs):
     outs, (own, other, turned) = refs[:pairs], refs[pairs:]
     strip, half = block // pairs, block // 2
@@ -125,7 +135,8 @@
 def gradient_kernel(groups, ranks, sources, chunks, bands, meta, *refs):
     pairs = groups // 2
     count = 1 + max(source for source, _ in sources)
-    cots, ctxs = refs[:count], refs[count : count + pairs]
+    order = pair_order(pairs)
+    ctxs, cots = [refs[order.index(k)] for k in range(pairs)], refs[pairs : count + pairs]
     outs, strips = refs[count + pairs : -1], refs[-1]
     slots = sum(chunks)
     rows = cots[0].shape[1]
@@ -139,10 +150,11 @@
             lhs, rhs, preferred_element_type=jnp.float32
         ).astype(jnp.bfloat16)
     own_bands = bands // ranks
+    offsets = offsets_of(groups)
 
     def place(first, pieces, s, carry):
         for k in range(groups):
-            block_id = meta[2 + (position ^ k) * slots + first + s]
+            block_id = meta[2 + (position ^ offsets[k]) * slots + first + s]
             row_band, col_band = lax.div(block_id, bands), lax.rem(block_id, bands)
             piece = lax.div(col_band, own_bands) ^ rank
             start = piece * rows + lax.rem(col_band, own_bands) * strip
@@ -193,14 +205,14 @@
             transcendentals=0,
         ),
         name="gradient_strips",
-    )(meta, *[piece for rank in cots for piece in rank], *ctxs)
+    )(meta, *[ctxs[k] for k in pair_order(pairs)], *[piece for rank in cots for piece in rank])
     return [outs[i * groups : (i + 1) * groups] for i in range(len(chunks))]
 
 
 def gather_block(position, grads, turned):
-    for k, piece in enumerate(grads):
+    for offset, piece in zip(offsets_of(len(grads)), grads):
         _, strip, part = piece.shape
-        middle = position ^ k
+        middle = position ^ offset
         rows = pl.ds(pl.multiple_of(lax.div(middle, 2) * strip, strip), strip)
         columns = pl.ds(pl.multiple_of(lax.rem(middle, 2) * part, part), part)
         turned[rows, columns] = piece[0]
@@ -227,8 +239,8 @@
     ratio = jnp.sqrt(adam_sum) / jnp.sqrt(shaped_sum + 1e-06)
     rows[...] = (shaped * ratio).astype(jnp.bfloat16)
     sub = outs[0].shape[1]
-    for k in range(groups):
-        middle = position ^ k
+    for k, offset in enumerate(offsets_of(groups)):
+        middle = position ^ offset
         half, quarter = lax.rem(middle, halves), lax.div(middle, halves)
         start = (half * (groups // halves) + quarter) * sub
         outs[k][0] = rows[pl.ds(pl.multiple_of(start, sub), sub), :]
@@ -326,10 +338,11 @@
     position = meta[0]
     own_band = lax.div(position, halves)
     slots = sum(chunks)
+    offsets = offsets_of(groups)
 
     def place(first, pieces, s, carry):
         for k in range(groups):
-            block_id = meta[2 + (position ^ k) * slots + first + s]
+            block_id = meta[2 + (position ^ offsets[k]) * slots + first + s]
             row_band, col_band = lax.div(block_id, bands), lax.rem(block_id, bands)
             columns = pl.ds(pl.multiple_of(col_band * block, block), block)
             placed[row_band ^ own_band, :, columns] = pieces[k][s]
@@ -401,8 +414,8 @@
     )(meta, *pieces)
 
 
-def exchange(pieces, stride=1):
-    return [pieces[0]] + [swap(pieces[k], "fsdp", k * stride) for k in range(1, len(pieces))]
+def exchange(pieces, offsets):
+    return [swap(piece, "fsdp", k) if k else piece for piece, k in zip(pieces, offsets)]
 
 
 def strip_plan(
@@ -417,9 +430,9 @@
     meta = jnp.concatenate([place, block_table[0]])
 
     pairs, tokens = groups // 2, context.shape[0]
-    pairs, tokens = groups // 2, context.shape[0]
+    offsets = offsets_of(groups)
     strips, own, other = prepare(meta, cotangent, context, pairs, block)
-    strips = exchange(strips, 2)
+    strips = exchange(strips, range(0, groups, 2))
     other = swap(other, "fsdp", 1)
     strips, other = lax.optimization_barrier((strips, other))
     strips = jnp.stack(strips).reshape(pairs, -1, tokens)
@@ -448,25 +461,25 @@
             here = list(cots[known])
             if known:
                 here[0], _ = lax.optimization_barrier((here[0], here[1]))
-
             cots[known ^ offset] = [swap(piece, "tensor", offset) for piece in here]
         offset //= 2
     cots = [cots[t] for t in range(ranks)]
 
     chunks = [slots - slots // 2, slots // 2]
     grads = [
-        exchange(chunk) for chunk in gradient_strips(meta, cots, ctxs, chunks, bands, block)
+        exchange(chunk, offsets) for chunk in gradient_strips(meta, cots, ctxs, chunks, bands, block)
     ]
     halves = block // strip_rows
     sub = strip_rows * halves // groups
     pieces = []
     for i, chunk in enumerate(grads):
         stale = (second_moment, root_left, root_right)
-        pieces.append(exchange(directions(meta, chunk, sum(chunks[:i]), *stale, halves, sub)))
+        parts = directions(meta, chunk, sum(chunks[:i]), *stale, halves, sub)
+        pieces.append(exchange(parts, offsets))
     left_new, right_new, second_new = statistics(
         meta, grads, left_stat, right_stat, second_moment
     )
-    rows = exchange(regroup(meta, pieces, bands, halves), halves)
+    rows = exchange(regroup(meta, pieces, bands, halves), range(0, groups, halves))
     return (left_new, right_new, second_new, stack_rows(meta, rows, halves))
 
 

time: 232 us -> 228 us (0.983)
  waiting for transfers between devices: 132 us -> 124 us
  starting transfers between devices: 60.8 us -> 64 us
    ppermute x47, waiting for transfers between devices: 132 us -> 124 us  [swap(): return lax.ppermute(value, axis, [(i, i ^ offset) for i in range(count)])]
    ppermute x47, starting transfers between devices: 60.8 us -> 64 us  [swap(): return lax.ppermute(value, axis, [(i, i ^ offset) for i in range(count)])]
  transfers between devices with their start and end apart: 47 -> 47, of which waited for: 25 -> 23; matrix products, arithmetic and copies ran while one was open for 0% -> 0% of each run, Pallas kernels for 10% -> 10%
where the time goes in v6:
time: 228 us; the launch traced here: 227 us
  waiting for transfers between devices  124 us (54%)
  starting transfers between devices  64 us (28%)
  Pallas kernels  34.8 us (15%)
  local copies, waits for them, and re-layouts  2.36 us (1%)
    ppermute x47, waiting for transfers between devices, swap(): return lax.ppermute(value, axis, [(i, i ^ offset) for i in range(count)])  124 us
    ppermute x47, starting transfers between devices, swap(): return lax.ppermute(value, axis, [(i, i ^ offset) for i in range(count)])  64 us
    pallas_call x2, Pallas kernels, directions(): pl.pallas_call(functools.partial(direction_kernel, groups, halves), grid_...  12.6 us
    pallas_call x1, Pallas kernels, statistics(): pl.pallas_call(functools.partial(statistics_kernel, groups, chunks), grid...  10.4 us
    pallas_call x1, Pallas kernels, gradient_strips(): pl.pallas_call(functools.partial(gradient_kernel, groups, ranks, sources,...  6.53 us
  transfers between devices with their start and end apart: 47, of which 23 were waited for; matrix products, arithmetic and copies ran while one was open for 0% of the time, Pallas kernels for 10%

profile of v6, /device:TPU:8, one launch (start us, length us, event | category | flops | bytes accessed | tf_op | source)
XLA Modules:
  0.0 227.2 jit_solution(7566884730828318733)
XLA Ops:
  3.6 1.7 prepare.1
  5.5 3.0 %collective-permute-start.1 = (bf16[8,64,256]{2,1,0:T(8,128)(2,1)S(1)}, bf16[8,64,256]{2,1,0:T(8,128)(2,1)S(1)}, u32[]{:S(2)}, u32[]{:S(2)}) collective-permute-start(bf16[8,64,256]{2,1,0:T(8,128)(2,1)S(1)} %get-tuple-element.59), channel_id=1, source_target_pairs={{0,16},{4,20},{8,24},{12,28},{16,0},{20,4},{24,8},{28,12},{1,17},{... | collective-permute-start | bytes 786440 | tf_op jit(solution)/shard_map/ppermute | solution.py:77
  8.9 1.5 collective-permute-start.3
  10.4 5.7 %collective-permute-done = bf16[8,64,256]{2,1,0:T(8,128)(2,1)S(1)} collective-permute-done((bf16[8,64,256]{2,1,0:T(8,128)(2,1)S(1)}, bf16[8,64,256]{2,1,0:T(8,128)(2,1)S(1)}, u32[]{:S(2)}, u32[]{:S(2)}) %collective-permute-start) | collective-permute-done | bytes 262176 | tf_op jit(solution)/shard_map/ppermute | solution.py:77
  16.1 10.3 %collective-permute-done.1 = bf16[8,64,256]{2,1,0:T(8,128)(2,1)S(1)} collective-permute-done((bf16[8,64,256]{2,1,0:T(8,128)(2,1)S(1)}, bf16[8,64,256]{2,1,0:T(8,128)(2,1)S(1)}, u32[]{:S(2)}, u32[]{:S(2)}) %collective-permute-start.1) | collective-permute-done | bytes 262176 | tf_op jit(solution)/shard_map/ppermute | solution.py:77
  26.4 5.1 %collective-permute-done.2 = bf16[8,64,256]{2,1,0:T(8,128)(2,1)S(1)} collective-permute-done((bf16[8,64,256]{2,1,0:T(8,128)(2,1)S(1)}, bf16[8,64,256]{2,1,0:T(8,128)(2,1)S(1)}, u32[]{:S(2)}, u32[]{:S(2)}) %collective-permute-start.2) | collective-permute-done | bytes 262176 | tf_op jit(solution)/shard_map/ppermute | solution.py:77
  31.7 1.6 collective-permute-start.7
  33.3 1.5 collective-permute-start.10
  34.9 3.0 %collective-permute-start.4 = (bf16[2,256,512]{2,1,0:T(8,128)(2,1)S(1)}, bf16[2,256,512]{2,1,0:T(8,128)(2,1)S(1)}, u32[]{:S(2)}, u32[]{:S(2)}) collective-permute-start(bf16[2,256,512]{2,1,0:T(8,128)(2,1)S(1)} %pad_maximum_fusion.1.refs_1_), channel_id=1, source_target_pairs={{0,16},{4,20},{8,24},{12,28},{16,0},{20,4},{24,8},{28,12},{1,17},{... | collective-permute-start | bytes 1572872 | tf_op jit(solution)/shard_map/ppermute | solution.py:77
  37.9 17.6 %collective-permute-done.7.refs_5_ = bf16[4,512,256]{2,1,0:T(8,128)(2,1)S(1)} collective-permute-done((bf16[4,512,256]{2,1,0:T(8,128)(2,1)S(1)}, bf16[4,512,256]{2,1,0:T(8,128)(2,1)S(1)}, u32[]{:S(2)}, u32[]{:S(2)}) %collective-permute-start.7) | collective-permute-done | bytes 1048608 | tf_op jit(solution)/shard_map/ppermute | solution.py:77
  55.8 1.4 collective-permute-start.11
  57.1 2.1 collective-permute-done.4.refs_0_
  59.2 1.6 collective-permute-start.6
  61.4 6.6 %collective-permute-done.11.refs_9_ = bf16[2,512,256]{2,1,0:T(8,128)(2,1)S(1)} collective-permute-done((bf16[2,512,256]{2,1,0:T(8,128)(2,1)S(1)}, bf16[2,512,256]{2,1,0:T(8,128)(2,1)S(1)}, u32[]{:S(2)}, u32[]{:S(2)}) %collective-permute-start.11) | collective-permute-done | bytes 524320 | tf_op jit(solution)/shard_map/ppermute | solution.py:77
  68.0 5.0 %collective-permute-done.12.refs_10_ = bf16[2,512,256]{2,1,0:T(8,128)(2,1)S(1)} collective-permute-done((bf16[2,512,256]{2,1,0:T(8,128)(2,1)S(1)}, bf16[2,512,256]{2,1,0:T(8,128)(2,1)S(1)}, u32[]{:S(2)}, u32[]{:S(2)}) %collective-permute-start.12) | collective-permute-done | bytes 524320 | tf_op jit(solution)/shard_map/ppermute | solution.py:77
  73.5 1.4 collective-permute-done.15.refs_13_
  75.7 6.5 %gradient_strips.1 = (bf16[8,64,128]{2,1,0:T(8,128)(2,1)S(1)}, bf16[8,64,128]{2,1,0:T(8,128)(2,1)S(1)}, bf16[8,64,128]{2,1,0:T(8,128)(2,1)S(1)}, bf16[8,64,128]{...) custom-call(s32[130]{0:T(256)S(1)} %pad_add_fusion.meta, ...), custom_call_target="tpu_custom_call" | custom-call | flops 4294967296 | bytes 12582912 | tf_op jit(solution)/shard_map/gradient_strips/pallas_call | solution.py:185
  82.2 1.4 collective-permute-start.16
  83.6 1.5 collective-permute-start.17
  85.7 1.5 collective-permute-start.24
  87.2 2.3 %collective-permute-start.25 = (bf16[8,64,128]{2,1,0:T(8,128)(2,1)S(1)}, bf16[8,64,128]{2,1,0:T(8,128)(2,1)S(1)}, u32[]{:S(2)}, u32[]{:S(2)}) collective-permute-start(bf16[8,64,128]{2,1,0:T(8,128)(2,1)S(1)} %get-tuple-element.79), channel_id=1, source_target_pairs={{0,20},{4,16},{8,28},{12,24},{16,4},{20,0},{24,12},{28,8},{1,21},{... | collective-permute-start | bytes 393224 | tf_op jit(solution)/shard_map/ppermute | solution.py:77
  89.5 5.7 %collective-permute-done.16.refs_0_ = bf16[8,64,128]{2,1,0:T(8,128)(2,1)S(1)} collective-permute-done((bf16[8,64,128]{2,1,0:T(8,128)(2,1)S(1)}, bf16[8,64,128]{2,1,0:T(8,128)(2,1)S(1)}, u32[]{:S(2)}, u32[]{:S(2)}) %collective-permute-start.16) | collective-permute-done | bytes 131104 | tf_op jit(solution)/shard_map/ppermute | solution.py:77
  95.2 3.1 %collective-permute-start.26 = (bf16[8,64,128]{2,1,0:T(8,128)(2,1)S(1)}, bf16[8,64,128]{2,1,0:T(8,128)(2,1)S(1)}, u32[]{:S(2)}, u32[]{:S(2)}) collective-permute-start(bf16[8,64,128]{2,1,0:T(8,128)(2,1)S(1)} %get-tuple-element.80), channel_id=1, source_target_pairs={{0,8},{4,12},{8,0},{12,4},{16,24},{20,28},{24,16},{28,20},{1,9},{5... | collective-permute-start | bytes 393224 | tf_op jit(solution)/shard_map/ppermute | solution.py:77
  99.1 2.3 %collective-permute-start.28 = (bf16[8,64,128]{2,1,0:T(8,128)(2,1)S(1)}, bf16[8,64,128]{2,1,0:T(8,128)(2,1)S(1)}, u32[]{:S(2)}, u32[]{:S(2)}) collective-permute-start(bf16[8,64,128]{2,1,0:T(8,128)(2,1)S(1)} %get-tuple-element.82), channel_id=1, source_target_pairs={{0,12},{4,8},{8,4},{12,0},{16,28},{20,24},{24,20},{28,16},{1,13},{... | collective-permute-start | bytes 393224 | tf_op jit(solution)/shard_map/ppermute | solution.py:77
  101.5 1.4 collective-permute-start.29
  103.2 4.6 %collective-permute-start.18 = (bf16[8,64,128]{2,1,0:T(8,128)(2,1)S(1)}, bf16[8,64,128]{2,1,0:T(8,128)(2,1)S(1)}, u32[]{:S(2)}, u32[]{:S(2)}) collective-permute-start(bf16[8,64,128]{2,1,0:T(8,128)(2,1)S(1)} %get-tuple-element.71), channel_id=1, source_target_pairs={{0,20},{4,16},{8,28},{12,24},{16,4},{20,0},{24,12},{28,8},{1,21},{... | collective-permute-start | bytes 393224 | tf_op jit(solution)/shard_map/ppermute | solution.py:77
  109.0 4.5 %collective-permute-done.27.refs_12_.refs_4_ = bf16[8,64,128]{2,1,0:T(8,128)(2,1)S(1)} collective-permute-done((bf16[8,64,128]{2,1,0:T(8,128)(2,1)S(1)}, bf16[8,64,128]{2,1,0:T(8,128)(2,1)S(1)}, u32[]{:S(2)}, u32[]{:S(2)}) %collective-permute-start.27) | collective-permute-done | bytes 131104 | tf_op jit(solution)/shard_map/ppermute | solution.py:77
  115.3 2.1 collective-permute-done.29.refs_14_.refs_6_
  117.4 3.5 %collective-permute-start.22 = (bf16[8,64,128]{2,1,0:T(8,128)(2,1)S(1)}, bf16[8,64,128]{2,1,0:T(8,128)(2,1)S(1)}, u32[]{:S(2)}, u32[]{:S(2)}) collective-permute-start(bf16[8,64,128]{2,1,0:T(8,128)(2,1)S(1)} %get-tuple-element.75), channel_id=1, source_target_pairs={{0,28},{4,24},{8,20},{12,16},{16,12},{20,8},{24,4},{28,0},{1,29},{... | collective-permute-start | bytes 393224 | tf_op jit(solution)/shard_map/ppermute | solution.py:77
  120.9 6.3 %directions.3 = (bf16[8,32,256]{2,1,0:T(8,128)(2,1)S(1)}, bf16[8,32,256]{2,1,0:T(8,128)(2,1)S(1)}, bf16[8,32,256]{2,1,0:T(8,128)(2,1)S(1)}, bf16[8,32,256]{2,1,0...) custom-call(s32[130]{0:T(256)S(1)} %pad_add_fusion.meta, ...), custom_call_target="tpu_custom_call" | custom-call | flops 536870912 | bytes 8388608 | tf_op jit(solution)/shard_map/directions/pallas_call | solution.py:254
  128.4 3.2 %collective-permute-start.39 = (bf16[8,32,256]{2,1,0:T(8,128)(2,1)S(1)}, bf16[8,32,256]{2,1,0:T(8,128)(2,1)S(1)}, u32[]{:S(2)}, u32[]{:S(2)}) collective-permute-start(bf16[8,32,256]{2,1,0:T(8,128)(2,1)S(1)} %get-tuple-element.98), channel_id=1, source_target_pairs={{0,20},{4,16},{8,28},{12,24},{16,4},{20,0},{24,12},{28,8},{1,21},{... | collective-permute-start | bytes 393224 | tf_op jit(solution)/shard_map/ppermute | solution.py:77
  131.7 3.5 %collective-permute-done.22.refs_6_ = bf16[8,64,128]{2,1,0:T(8,128)(2,1)S(1)} collective-permute-done((bf16[8,64,128]{2,1,0:T(8,128)(2,1)S(1)}, bf16[8,64,128]{2,1,0:T(8,128)(2,1)S(1)}, u32[]{:S(2)}, u32[]{:S(2)}) %collective-permute-start.22) | collective-permute-done | bytes 131104 | tf_op jit(solution)/shard_map/ppermute | solution.py:77
  135.2 2.6 %collective-permute-start.41 = (bf16[8,32,256]{2,1,0:T(8,128)(2,1)S(1)}, bf16[8,32,256]{2,1,0:T(8,128)(2,1)S(1)}, u32[]{:S(2)}, u32[]{:S(2)}) collective-permute-start(bf16[8,32,256]{2,1,0:T(8,128)(2,1)S(1)} %get-tuple-element.100), channel_id=1, source_target_pairs={{0,24},{4,28},{8,16},{12,20},{16,8},{20,12},{24,0},{28,4},{1,25},{... | collective-permute-start | bytes 393224 | tf_op jit(solution)/shard_map/ppermute | solution.py:77
  137.7 6.3 %directions.2 = (bf16[8,32,256]{2,1,0:T(8,128)(2,1)S(1)}, bf16[8,32,256]{2,1,0:T(8,128)(2,1)S(1)}, bf16[8,32,256]{2,1,0:T(8,128)(2,1)S(1)}, bf16[8,32,256]{2,1,0...) custom-call(s32[130]{0:T(256)S(1)} %pad_add_fusion.meta, ...), custom_call_target="tpu_custom_call" | custom-call | flops 536870912 | bytes 8388608 | tf_op jit(solution)/shard_map/directions/pallas_call | solution.py:254
  145.1 4.3 %collective-permute-start.30 = (bf16[8,32,256]{2,1,0:T(8,128)(2,1)S(1)}, bf16[8,32,256]{2,1,0:T(8,128)(2,1)S(1)}, u32[]{:S(2)}, u32[]{:S(2)}) collective-permute-start(bf16[8,32,256]{2,1,0:T(8,128)(2,1)S(1)} %get-tuple-element.88), channel_id=1, source_target_pairs={{0,16},{4,20},{8,24},{12,28},{16,0},{20,4},{24,8},{28,12},{1,17},{... | collective-permute-start | bytes 393224 | tf_op jit(solution)/shard_map/ppermute | solution.py:77
  149.4 1.5 collective-permute-start.32
  152.3 7.7 %collective-permute-done.43.refs_14_ = bf16[8,32,256]{2,1,0:T(8,128)(2,1)S(1)} collective-permute-done((bf16[8,32,256]{2,1,0:T(8,128)(2,1)S(1)}, bf16[8,32,256]{2,1,0:T(8,128)(2,1)S(1)}, u32[]{:S(2)}, u32[]{:S(2)}) %collective-permute-start.43) | collective-permute-done | bytes 131104 | tf_op jit(solution)/shard_map/ppermute | solution.py:77
  160.1 3.2 %collective-permute-done.30.refs_0_ = bf16[8,32,256]{2,1,0:T(8,128)(2,1)S(1)} collective-permute-done((bf16[8,32,256]{2,1,0:T(8,128)(2,1)S(1)}, bf16[8,32,256]{2,1,0:T(8,128)(2,1)S(1)}, u32[]{:S(2)}, u32[]{:S(2)}) %collective-permute-start.30) | collective-permute-done | bytes 131104 | tf_op jit(solution)/shard_map/ppermute | solution.py:77
  163.3 3.8 %collective-permute-start.35 = (bf16[8,32,256]{2,1,0:T(8,128)(2,1)S(1)}, bf16[8,32,256]{2,1,0:T(8,128)(2,1)S(1)}, u32[]{:S(2)}, u32[]{:S(2)}) collective-permute-start(bf16[8,32,256]{2,1,0:T(8,128)(2,1)S(1)} %get-tuple-element.93), channel_id=1, source_target_pairs={{0,12},{4,8},{8,4},{12,0},{16,28},{20,24},{24,20},{28,16},{1,13},{... | collective-permute-start | bytes 393224 | tf_op jit(solution)/shard_map/ppermute | solution.py:77
  168.1 5.2 %collective-permute-done.34.refs_4_ = bf16[8,32,256]{2,1,0:T(8,128)(2,1)S(1)} collective-permute-done((bf16[8,32,256]{2,1,0:T(8,128)(2,1)S(1)}, bf16[8,32,256]{2,1,0:T(8,128)(2,1)S(1)}, u32[]{:S(2)}, u32[]{:S(2)}) %collective-permute-start.34) | collective-permute-done | bytes 131104 | tf_op jit(solution)/shard_map/ppermute | solution.py:77
  173.3 2.5 %collective-permute-done.36.refs_6_ = bf16[8,32,256]{2,1,0:T(8,128)(2,1)S(1)} collective-permute-done((bf16[8,32,256]{2,1,0:T(8,128)(2,1)S(1)}, bf16[8,32,256]{2,1,0:T(8,128)(2,1)S(1)}, u32[]{:S(2)}, u32[]{:S(2)}) %collective-permute-start.36) | collective-permute-done | bytes 131104 | tf_op jit(solution)/shard_map/ppermute | solution.py:77
  175.8 1.7 regroup.1
  177.5 2.8 %collective-permute-start.45 = (bf16[32,8192]{1,0:T(8,128)(2,1)S(1)}, bf16[32,8192]{1,0:T(8,128)(2,1)S(1)}, u32[]{:S(2)}, u32[]{:S(2)}) collective-permute-start(bf16[32,8192]{1,0:T(8,128)(2,1)S(1)} %get-tuple-element.106), channel_id=1, source_target_pairs={{0,16},{4,20},{8,24},{12,28},{16,0},{20,4},{24,8},{28,12},{1,17},{... | collective-permute-start | bytes 1572872 | tf_op jit(solution)/shard_map/ppermute | solution.py:77
  181.0 10.4 %statistics.1 = (f32[1,16,256,256]{3,2,1,0:T(8,128)}, f32[1,16,256,256]{3,2,1,0:T(8,128)}, f32[1,16,256,256]{3,2,1,0:T(8,128)}) custom-call(s32[130]{0:T(256)S(1)} %pad_add_fusion.meta, f32[1,16,256,256]{3,2,1,0:T(8,128)S(1)} %copy-done.3, f32[1,16,256,256]{3,2,1,0:T(8,128)S(1)} %copy-done.4, f32[1,16,256,256]{3,2,1,0:T(8,128)S(1)} %copy-done, ...), custom_call_target="tpu_custom_call" | custom-call | flops 1073741824 | bytes 27262976 | tf_op jit(solution)/shard_map/statistics/pallas_call | solution.py:315
  191.4 7.1 %collective-permute-done.44.refs_1_ = bf16[32,8192]{1,0:T(8,128)(2,1)S(1)} collective-permute-done((bf16[32,8192]{1,0:T(8,128)(2,1)S(1)}, bf16[32,8192]{1,0:T(8,128)(2,1)S(1)}, u32[]{:S(2)}, u32[]{:S(2)}) %collective-permute-start.44) | collective-permute-done | bytes 524320 | tf_op jit(solution)/shard_map/ppermute | solution.py:77
  198.5 16.8 %collective-permute-done.45.refs_2_ = bf16[32,8192]{1,0:T(8,128)(2,1)S(1)} collective-permute-done((bf16[32,8192]{1,0:T(8,128)(2,1)S(1)}, bf16[32,8192]{1,0:T(8,128)(2,1)S(1)}, u32[]{:S(2)}, u32[]{:S(2)}) %collective-permute-start.45) | collective-permute-done | bytes 524320 | tf_op jit(solution)/shard_map/ppermute | solution.py:77
  215.2 10.1 %collective-permute-done.46.refs_3_ = bf16[32,8192]{1,0:T(8,128)(2,1)S(1)} collective-permute-done((bf16[32,8192]{1,0:T(8,128)(2,1)S(1)}, bf16[32,8192]{1,0:T(8,128)(2,1)S(1)}, u32[]{:S(2)}, u32[]{:S(2)}) %collective-permute-start.46) | collective-permute-done | bytes 524320 | tf_op jit(solution)/shard_map/ppermute | solution.py:77
  225.3 1.9 stack_rows.1
  (72 shorter events, 16.2 us)
Async XLA Ops:
  5.4 10.8 %collective-permute-start = (bf16[8,64,256]{2,1,0:T(8,128)(2,1)S(1)}, bf16[8,64,256]{2,1,0:T(8,128)(2,1)S(1)}, u32[]{:S(2)}, u32[]{:S(2)}) collective-permute-start(bf16[8,64,256]{2,1,0:T(8,128)(2,1)S(1)} %get-tuple-element.58), channel_id=1, source_target_pairs={{0,8},{4,12},{8,0},{12,4},{16,24},{20,28},{24,16},{28,20},{1,9},{5... | collective-permute-start | bytes 786440 | tf_op jit(solution)/shard_map/ppermute | solution.py:77
  5.5 21.0 %collective-permute-start.1 = (bf16[8,64,256]{2,1,0:T(8,128)(2,1)S(1)}, bf16[8,64,256]{2,1,0:T(8,128)(2,1)S(1)}, u32[]{:S(2)}, u32[]{:S(2)}) collective-permute-start(bf16[8,64,256]{2,1,0:T(8,128)(2,1)S(1)} %get-tuple-element.59), channel_id=1, source_target_pairs={{0,16},{4,20},{8,24},{12,28},{16,0},{20,4},{24,8},{28,12},{1,17},{... | collective-permute-start | bytes 786440 | tf_op jit(solution)/shard_map/ppermute | solution.py:77
  8.5 23.1 %collective-permute-start.2 = (bf16[8,64,256]{2,1,0:T(8,128)(2,1)S(1)}, bf16[8,64,256]{2,1,0:T(8,128)(2,1)S(1)}, u32[]{:S(2)}, u32[]{:S(2)}) collective-permute-start(bf16[8,64,256]{2,1,0:T(8,128)(2,1)S(1)} %get-tuple-element.60), channel_id=1, source_target_pairs={{0,24},{4,28},{8,16},{12,20},{16,8},{20,12},{24,0},{28,4},{1,25},{... | collective-permute-start | bytes 786440 | tf_op jit(solution)/shard_map/ppermute | solution.py:77
  8.9 22.6 %collective-permute-start.3 = (bf16[256,512]{1,0:T(8,128)(2,1)S(1)}, bf16[256,512]{1,0:T(8,128)(2,1)S(1)}, u32[]{:S(2)}, u32[]{:S(2)}) collective-permute-start(bf16[256,512]{1,0:T(8,128)(2,1)S(1)} %get-tuple-element.61), channel_id=1, source_target_pairs={{0,4},{4,0},{8,12},{12,8},{16,20},{20,16},{24,28},{28,24},{1,5},{5... | collective-permute-start | bytes 786440 | tf_op jit(solution)/shard_map/ppermute | solution.py:77
  31.7 23.8 %collective-permute-start.7 = (bf16[4,512,256]{2,1,0:T(8,128)(2,1)S(1)}, bf16[4,512,256]{2,1,0:T(8,128)(2,1)S(1)}, u32[]{:S(2)}, u32[]{:S(2)}) collective-permute-start(bf16[4,512,256]{2,1,0:T(8,128)(2,1)S(1)} %pad_maximum_fusion.refs_4_), channel_id=1, source_target_pairs={{0,4},{4,0},{8,12},{12,8},{16,20},{20,16},{24,28},{28,24},{1,5},{5... | collective-permute-start | bytes 3145736 | tf_op jit(solution)/shard_map/ppermute | solution.py:77
  33.3 27.5 %collective-permute-start.10 = (bf16[4,512,256]{2,1,0:T(8,128)(2,1)S(1)}, bf16[4,512,256]{2,1,0:T(8,128)(2,1)S(1)}, u32[]{:S(2)}, u32[]{:S(2)}) collective-permute-start(bf16[4,512,256]{2,1,0:T(8,128)(2,1)S(1)} %pad_maximum_fusion.refs_4_), channel_id=1, source_target_pairs={{0,2},{1,3},{2,0},{3,1},{4,6},{5,7},{6,4},{7,5},{8,10},{9,11},{10,... | collective-permute-start | bytes 3145736 | tf_op jit(solution)/shard_map/ppermute | solution.py:77
  34.8 20.9 %collective-permute-start.5 = (bf16[2,256,512]{2,1,0:T(8,128)(2,1)S(1)}, bf16[2,256,512]{2,1,0:T(8,128)(2,1)S(1)}, u32[]{:S(2)}, u32[]{:S(2)}) collective-permute-start(bf16[2,256,512]{2,1,0:T(8,128)(2,1)S(1)} %pad_maximum_fusion.1.refs_1_), channel_id=1, source_target_pairs={{0,8},{4,12},{8,0},{12,4},{16,24},{20,28},{24,16},{28,20},{1,9},{5... | collective-permute-start | bytes 1572872 | tf_op jit(solution)/shard_map/ppermute | solution.py:77
  34.9 24.3 %collective-permute-start.4 = (bf16[2,256,512]{2,1,0:T(8,128)(2,1)S(1)}, bf16[2,256,512]{2,1,0:T(8,128)(2,1)S(1)}, u32[]{:S(2)}, u32[]{:S(2)}) collective-permute-start(bf16[2,256,512]{2,1,0:T(8,128)(2,1)S(1)} %pad_maximum_fusion.1.refs_1_), channel_id=1, source_target_pairs={{0,16},{4,20},{8,24},{12,28},{16,0},{20,4},{24,8},{28,12},{1,17},{... | collective-permute-start | bytes 1572872 | tf_op jit(solution)/shard_map/ppermute | solution.py:77
  55.8 12.2 %collective-permute-start.11 = (bf16[2,512,256]{2,1,0:T(8,128)(2,1)S(1)}, bf16[2,512,256]{2,1,0:T(8,128)(2,1)S(1)}, u32[]{:S(2)}, u32[]{:S(2)}) collective-permute-start(bf16[2,512,256]{2,1,0:T(8,128)(2,1)S(1)} %slice.8), channel_id=1, source_target_pairs={{0,2},{1,3},{2,0},{3,1},{4,6},{5,7},{6,4},{7,5},{8,10},{9,11},{10,... | collective-permute-start | bytes 1572872 | tf_op jit(solution)/shard_map/ppermute | solution.py:77
  57.1 16.4 %collective-permute-start.8 = (bf16[4,512,256]{2,1,0:T(8,128)(2,1)S(1)}, bf16[4,512,256]{2,1,0:T(8,128)(2,1)S(1)}, u32[]{:S(2)}, u32[]{:S(2)}) collective-permute-start(bf16[4,512,256]{2,1,0:T(8,128)(2,1)S(1)} %pad_maximum_fusion.refs_4_), channel_id=1, source_target_pairs={{0,1},{1,0},{2,3},{3,2},{4,5},{5,4},{6,7},{7,6},{8,9},{9,8},{10,11... | collective-permute-start | bytes 3145736 | tf_op jit(solution)/shard_map/ppermute | solution.py:77
  59.2 13.8 %collective-permute-start.6 = (bf16[2,256,512]{2,1,0:T(8,128)(2,1)S(1)}, bf16[2,256,512]{2,1,0:T(8,128)(2,1)S(1)}, u32[]{:S(2)}, u32[]{:S(2)}) collective-permute-start(bf16[2,256,512]{2,1,0:T(8,128)(2,1)S(1)} %collective-permute-done.4.refs_0_), channel_id=1, source_target_pairs={{0,8},{4,12},{8,0},{12,4},{16,24},{20,28},{24,16},{28,20},{1,9},{5... | collective-permute-start | bytes 1572872 | tf_op jit(solution)/shard_map/ppermute | solution.py:77
  60.8 60.0 %copy-start = (f32[1,16,256,256]{3,2,1,0:T(8,128)S(1)}, f32[1,16,256,256]{3,2,1,0:T(8,128)}, u32[]{:S(2)}) copy-start(f32[1,16,256,256]{3,2,1,0:T(8,128)} %second_ref.5) | copy-start | bytes 12582916
  60.9 12.1 %collective-permute-start.12 = (bf16[2,512,256]{2,1,0:T(8,128)(2,1)S(1)}, bf16[2,512,256]{2,1,0:T(8,128)(2,1)S(1)}, u32[]{:S(2)}, u32[]{:S(2)}) collective-permute-start(bf16[2,512,256]{2,1,0:T(8,128)(2,1)S(1)} %slice.9), channel_id=1, source_target_pairs={{0,4},{4,0},{8,12},{12,8},{16,20},{20,16},{24,28},{28,24},{1,5},{5... | collective-permute-start | bytes 1572872 | tf_op jit(solution)/shard_map/ppermute | solution.py:77
  61.4 12.1 %collective-permute-start.9 = (bf16[4,512,256]{2,1,0:T(8,128)(2,1)S(1)}, bf16[4,512,256]{2,1,0:T(8,128)(2,1)S(1)}, u32[]{:S(2)}, u32[]{:S(2)}) collective-permute-start(bf16[4,512,256]{2,1,0:T(8,128)(2,1)S(1)} %collective-permute-done.7.refs_5_), channel_id=1, source_target_pairs={{0,1},{1,0},{2,3},{3,2},{4,5},{5,4},{6,7},{7,6},{8,9},{9,8},{10,11... | collective-permute-start | bytes 3145736 | tf_op jit(solution)/shard_map/ppermute | solution.py:77
  68.0 7.6 %collective-permute-start.13 = (bf16[4,512,256]{2,1,0:T(8,128)(2,1)S(1)}, bf16[4,512,256]{2,1,0:T(8,128)(2,1)S(1)}, u32[]{:S(2)}, u32[]{:S(2)}) collective-permute-start(bf16[4,512,256]{2,1,0:T(8,128)(2,1)S(1)} %collective-permute-done.10.refs_8_), channel_id=1, source_target_pairs={{0,1},{1,0},{2,3},{3,2},{4,5},{5,4},{6,7},{7,6},{8,9},{9,8},{10,11... | collective-permute-start | bytes 3145736 | tf_op jit(solution)/shard_map/ppermute | solution.py:77
  73.0 1.9 collective-permute-start.15
  73.0 2.7 %collective-permute-start.14 = (bf16[2,512,256]{2,1,0:T(8,128)(2,1)S(1)}, bf16[2,512,256]{2,1,0:T(8,128)(2,1)S(1)}, u32[]{:S(2)}, u32[]{:S(2)}) collective-permute-start(bf16[2,512,256]{2,1,0:T(8,128)(2,1)S(1)} %collective-permute-done.11.refs_9_), channel_id=1, source_target_pairs={{0,1},{1,0},{2,3},{3,2},{4,5},{5,4},{6,7},{7,6},{8,9},{9,8},{10,11... | collective-permute-start | bytes 1572872 | tf_op jit(solution)/shard_map/ppermute | solution.py:77
  82.2 13.0 %collective-permute-start.16 = (bf16[8,64,128]{2,1,0:T(8,128)(2,1)S(1)}, bf16[8,64,128]{2,1,0:T(8,128)(2,1)S(1)}, u32[]{:S(2)}, u32[]{:S(2)}) collective-permute-start(bf16[8,64,128]{2,1,0:T(8,128)(2,1)S(1)} %get-tuple-element.69), channel_id=1, source_target_pairs={{0,16},{4,20},{8,24},{12,28},{16,0},{20,4},{24,8},{28,12},{1,17},{... | collective-permute-start | bytes 393224 | tf_op jit(solution)/shard_map/ppermute | solution.py:77
  83.6 14.7 %collective-permute-start.17 = (bf16[8,64,128]{2,1,0:T(8,128)(2,1)S(1)}, bf16[8,64,128]{2,1,0:T(8,128)(2,1)S(1)}, u32[]{:S(2)}, u32[]{:S(2)}) collective-permute-start(bf16[8,64,128]{2,1,0:T(8,128)(2,1)S(1)} %get-tuple-element.70), channel_id=1, source_target_pairs={{0,4},{4,0},{8,12},{12,8},{16,20},{20,16},{24,28},{28,24},{1,5},{5... | collective-permute-start | bytes 393224 | tf_op jit(solution)/shard_map/ppermute | solution.py:77
  85.1 14.0 %collective-permute-start.23 = (bf16[8,64,128]{2,1,0:T(8,128)(2,1)S(1)}, bf16[8,64,128]{2,1,0:T(8,128)(2,1)S(1)}, u32[]{:S(2)}, u32[]{:S(2)}) collective-permute-start(bf16[8,64,128]{2,1,0:T(8,128)(2,1)S(1)} %get-tuple-element.77), channel_id=1, source_target_pairs={{0,16},{4,20},{8,24},{12,28},{16,0},{20,4},{24,8},{28,12},{1,17},{... | collective-permute-start | bytes 393224 | tf_op jit(solution)/shard_map/ppermute | solution.py:77
  85.7 15.8 %collective-permute-start.24 = (bf16[8,64,128]{2,1,0:T(8,128)(2,1)S(1)}, bf16[8,64,128]{2,1,0:T(8,128)(2,1)S(1)}, u32[]{:S(2)}, u32[]{:S(2)}) collective-permute-start(bf16[8,64,128]{2,1,0:T(8,128)(2,1)S(1)} %get-tuple-element.78), channel_id=1, source_target_pairs={{0,4},{4,0},{8,12},{12,8},{16,20},{20,16},{24,28},{28,24},{1,5},{5... | collective-permute-start | bytes 393224 | tf_op jit(solution)/shard_map/ppermute | solution.py:77
  87.2 16.0 %collective-permute-start.25 = (bf16[8,64,128]{2,1,0:T(8,128)(2,1)S(1)}, bf16[8,64,128]{2,1,0:T(8,128)(2,1)S(1)}, u32[]{:S(2)}, u32[]{:S(2)}) collective-permute-start(bf16[8,64,128]{2,1,0:T(8,128)(2,1)S(1)} %get-tuple-element.79), channel_id=1, source_target_pairs={{0,20},{4,16},{8,28},{12,24},{16,4},{20,0},{24,12},{28,8},{1,21},{... | collective-permute-start | bytes 393224 | tf_op jit(solution)/shard_map/ppermute | solution.py:77
  95.2 12.6 %collective-permute-start.26 = (bf16[8,64,128]{2,1,0:T(8,128)(2,1)S(1)}, bf16[8,64,128]{2,1,0:T(8,128)(2,1)S(1)}, u32[]{:S(2)}, u32[]{:S(2)}) collective-permute-start(bf16[8,64,128]{2,1,0:T(8,128)(2,1)S(1)} %get-tuple-element.80), channel_id=1, source_target_pairs={{0,8},{4,12},{8,0},{12,4},{16,24},{20,28},{24,16},{28,20},{1,9},{5... | collective-permute-start | bytes 393224 | tf_op jit(solution)/shard_map/ppermute | solution.py:77
  98.3 15.2 %collective-permute-start.27 = (bf16[8,64,128]{2,1,0:T(8,128)(2,1)S(1)}, bf16[8,64,128]{2,1,0:T(8,128)(2,1)S(1)}, u32[]{:S(2)}, u32[]{:S(2)}) collective-permute-start(bf16[8,64,128]{2,1,0:T(8,128)(2,1)S(1)} %get-tuple-element.81), channel_id=1, source_target_pairs={{0,24},{4,28},{8,16},{12,20},{16,8},{20,12},{24,0},{28,4},{1,25},{... | collective-permute-start | bytes 393224 | tf_op jit(solution)/shard_map/ppermute | solution.py:77
  99.1 15.3 %collective-permute-start.28 = (bf16[8,64,128]{2,1,0:T(8,128)(2,1)S(1)}, bf16[8,64,128]{2,1,0:T(8,128)(2,1)S(1)}, u32[]{:S(2)}, u32[]{:S(2)}) collective-permute-start(bf16[8,64,128]{2,1,0:T(8,128)(2,1)S(1)} %get-tuple-element.82), channel_id=1, source_target_pairs={{0,12},{4,8},{8,4},{12,0},{16,28},{20,24},{24,20},{28,16},{1,13},{... | collective-permute-start | bytes 393224 | tf_op jit(solution)/shard_map/ppermute | solution.py:77
  101.5 15.9 %collective-permute-start.29 = (bf16[8,64,128]{2,1,0:T(8,128)(2,1)S(1)}, bf16[8,64,128]{2,1,0:T(8,128)(2,1)S(1)}, u32[]{:S(2)}, u32[]{:S(2)}) collective-permute-start(bf16[8,64,128]{2,1,0:T(8,128)(2,1)S(1)} %get-tuple-element.83), channel_id=1, source_target_pairs={{0,28},{4,24},{8,20},{12,16},{16,12},{20,8},{24,4},{28,0},{1,29},{... | collective-permute-start | bytes 393224 | tf_op jit(solution)/shard_map/ppermute | solution.py:77
  103.2 23.9 %collective-permute-start.18 = (bf16[8,64,128]{2,1,0:T(8,128)(2,1)S(1)}, bf16[8,64,128]{2,1,0:T(8,128)(2,1)S(1)}, u32[]{:S(2)}, u32[]{:S(2)}) collective-permute-start(bf16[8,64,128]{2,1,0:T(8,128)(2,1)S(1)} %get-tuple-element.71), channel_id=1, source_target_pairs={{0,20},{4,16},{8,28},{12,24},{16,4},{20,0},{24,12},{28,8},{1,21},{... | collective-permute-start | bytes 393224 | tf_op jit(solution)/shard_map/ppermute | solution.py:77
  107.8 19.6 %collective-permute-start.19 = (bf16[8,64,128]{2,1,0:T(8,128)(2,1)S(1)}, bf16[8,64,128]{2,1,0:T(8,128)(2,1)S(1)}, u32[]{:S(2)}, u32[]{:S(2)}) collective-permute-start(bf16[8,64,128]{2,1,0:T(8,128)(2,1)S(1)} %get-tuple-element.72), channel_id=1, source_target_pairs={{0,8},{4,12},{8,0},{12,4},{16,24},{20,28},{24,16},{28,20},{1,9},{5... | collective-permute-start | bytes 393224 | tf_op jit(solution)/shard_map/ppermute | solution.py:77
  113.5 14.9 %collective-permute-start.20 = (bf16[8,64,128]{2,1,0:T(8,128)(2,1)S(1)}, bf16[8,64,128]{2,1,0:T(8,128)(2,1)S(1)}, u32[]{:S(2)}, u32[]{:S(2)}) collective-permute-start(bf16[8,64,128]{2,1,0:T(8,128)(2,1)S(1)} %get-tuple-element.73), channel_id=1, source_target_pairs={{0,24},{4,28},{8,16},{12,20},{16,8},{20,12},{24,0},{28,4},{1,25},{... | collective-permute-start | bytes 393224 | tf_op jit(solution)/shard_map/ppermute | solution.py:77
  114.4 17.3 %collective-permute-start.21 = (bf16[8,64,128]{2,1,0:T(8,128)(2,1)S(1)}, bf16[8,64,128]{2,1,0:T(8,128)(2,1)S(1)}, u32[]{:S(2)}, u32[]{:S(2)}) collective-permute-start(bf16[8,64,128]{2,1,0:T(8,128)(2,1)S(1)} %get-tuple-element.74), channel_id=1, source_target_pairs={{0,12},{4,8},{8,4},{12,0},{16,28},{20,24},{24,20},{28,16},{1,13},{... | collective-permute-start | bytes 393224 | tf_op jit(solution)/shard_map/ppermute | solution.py:77
  117.4 17.7 %collective-permute-start.22 = (bf16[8,64,128]{2,1,0:T(8,128)(2,1)S(1)}, bf16[8,64,128]{2,1,0:T(8,128)(2,1)S(1)}, u32[]{:S(2)}, u32[]{:S(2)}) collective-permute-start(bf16[8,64,128]{2,1,0:T(8,128)(2,1)S(1)} %get-tuple-element.75), channel_id=1, source_target_pairs={{0,28},{4,24},{8,20},{12,16},{16,12},{20,8},{24,4},{28,0},{1,29},{... | collective-permute-start | bytes 393224 | tf_op jit(solution)/shard_map/ppermute | solution.py:77
  127.2 16.8 %collective-permute-start.37 = (bf16[8,32,256]{2,1,0:T(8,128)(2,1)S(1)}, bf16[8,32,256]{2,1,0:T(8,128)(2,1)S(1)}, u32[]{:S(2)}, u32[]{:S(2)}) collective-permute-start(bf16[8,32,256]{2,1,0:T(8,128)(2,1)S(1)} %get-tuple-element.96), channel_id=1, source_target_pairs={{0,16},{4,20},{8,24},{12,28},{16,0},{20,4},{24,8},{28,12},{1,17},{... | collective-permute-start | bytes 393224 | tf_op jit(solution)/shard_map/ppermute | solution.py:77
  127.4 16.7 %collective-permute-start.38 = (bf16[8,32,256]{2,1,0:T(8,128)(2,1)S(1)}, bf16[8,32,256]{2,1,0:T(8,128)(2,1)S(1)}, u32[]{:S(2)}, u32[]{:S(2)}) collective-permute-start(bf16[8,32,256]{2,1,0:T(8,128)(2,1)S(1)} %get-tuple-element.97), channel_id=1, source_target_pairs={{0,4},{4,0},{8,12},{12,8},{16,20},{20,16},{24,28},{28,24},{1,5},{5... | collective-permute-start | bytes 393224 | tf_op jit(solution)/shard_map/ppermute | solution.py:77
  128.4 16.6 %collective-permute-start.39 = (bf16[8,32,256]{2,1,0:T(8,128)(2,1)S(1)}, bf16[8,32,256]{2,1,0:T(8,128)(2,1)S(1)}, u32[]{:S(2)}, u32[]{:S(2)}) collective-permute-start(bf16[8,32,256]{2,1,0:T(8,128)(2,1)S(1)} %get-tuple-element.98), channel_id=1, source_target_pairs={{0,20},{4,16},{8,28},{12,24},{16,4},{20,0},{24,12},{28,8},{1,21},{... | collective-permute-start | bytes 393224 | tf_op jit(solution)/shard_map/ppermute | solution.py:77
  131.7 17.7 %collective-permute-start.40 = (bf16[8,32,256]{2,1,0:T(8,128)(2,1)S(1)}, bf16[8,32,256]{2,1,0:T(8,128)(2,1)S(1)}, u32[]{:S(2)}, u32[]{:S(2)}) collective-permute-start(bf16[8,32,256]{2,1,0:T(8,128)(2,1)S(1)} %get-tuple-element.99), channel_id=1, source_target_pairs={{0,8},{4,12},{8,0},{12,4},{16,24},{20,28},{24,16},{28,20},{1,9},{5... | collective-permute-start | bytes 393224 | tf_op jit(solution)/shard_map/ppermute | solution.py:77
  135.2 14.3 %collective-permute-start.41 = (bf16[8,32,256]{2,1,0:T(8,128)(2,1)S(1)}, bf16[8,32,256]{2,1,0:T(8,128)(2,1)S(1)}, u32[]{:S(2)}, u32[]{:S(2)}) collective-permute-start(bf16[8,32,256]{2,1,0:T(8,128)(2,1)S(1)} %get-tuple-element.100), channel_id=1, source_target_pairs={{0,24},{4,28},{8,16},{12,20},{16,8},{20,12},{24,0},{28,4},{1,25},{... | collective-permute-start | bytes 393224 | tf_op jit(solution)/shard_map/ppermute | solution.py:77
  144.0 8.1 %collective-permute-start.42 = (bf16[8,32,256]{2,1,0:T(8,128)(2,1)S(1)}, bf16[8,32,256]{2,1,0:T(8,128)(2,1)S(1)}, u32[]{:S(2)}, u32[]{:S(2)}) collective-permute-start(bf16[8,32,256]{2,1,0:T(8,128)(2,1)S(1)} %get-tuple-element.101), channel_id=1, source_target_pairs={{0,12},{4,8},{8,4},{12,0},{16,28},{20,24},{24,20},{28,16},{1,13},{... | collective-permute-start | bytes 393224 | tf_op jit(solution)/shard_map/ppermute | solution.py:77
  144.1 15.9 %collective-permute-start.43 = (bf16[8,32,256]{2,1,0:T(8,128)(2,1)S(1)}, bf16[8,32,256]{2,1,0:T(8,128)(2,1)S(1)}, u32[]{:S(2)}, u32[]{:S(2)}) collective-permute-start(bf16[8,32,256]{2,1,0:T(8,128)(2,1)S(1)} %get-tuple-element.102), channel_id=1, source_target_pairs={{0,28},{4,24},{8,20},{12,16},{16,12},{20,8},{24,4},{28,0},{1,29},{... | collective-permute-start | bytes 393224 | tf_op jit(solution)/shard_map/ppermute | solution.py:77
  145.1 18.2 %collective-permute-start.30 = (bf16[8,32,256]{2,1,0:T(8,128)(2,1)S(1)}, bf16[8,32,256]{2,1,0:T(8,128)(2,1)S(1)}, u32[]{:S(2)}, u32[]{:S(2)}) collective-permute-start(bf16[8,32,256]{2,1,0:T(8,128)(2,1)S(1)} %get-tuple-element.88), channel_id=1, source_target_pairs={{0,16},{4,20},{8,24},{12,28},{16,0},{20,4},{24,8},{28,12},{1,17},{... | collective-permute-start | bytes 393224 | tf_op jit(solution)/shard_map/ppermute | solution.py:77
  149.4 17.7 %collective-permute-start.31 = (bf16[8,32,256]{2,1,0:T(8,128)(2,1)S(1)}, bf16[8,32,256]{2,1,0:T(8,128)(2,1)S(1)}, u32[]{:S(2)}, u32[]{:S(2)}) collective-permute-start(bf16[8,32,256]{2,1,0:T(8,128)(2,1)S(1)} %get-tuple-element.89), channel_id=1, source_target_pairs={{0,4},{4,0},{8,12},{12,8},{16,20},{20,16},{24,28},{28,24},{1,5},{5... | collective-permute-start | bytes 393224 | tf_op jit(solution)/shard_map/ppermute | solution.py:77
  149.4 18.7 %collective-permute-start.32 = (bf16[8,32,256]{2,1,0:T(8,128)(2,1)S(1)}, bf16[8,32,256]{2,1,0:T(8,128)(2,1)S(1)}, u32[]{:S(2)}, u32[]{:S(2)}) collective-permute-start(bf16[8,32,256]{2,1,0:T(8,128)(2,1)S(1)} %get-tuple-element.90), channel_id=1, source_target_pairs={{0,20},{4,16},{8,28},{12,24},{16,4},{20,0},{24,12},{28,8},{1,21},{... | collective-permute-start | bytes 393224 | tf_op jit(solution)/shard_map/ppermute | solution.py:77
  152.1 16.0 %collective-permute-start.33 = (bf16[8,32,256]{2,1,0:T(8,128)(2,1)S(1)}, bf16[8,32,256]{2,1,0:T(8,128)(2,1)S(1)}, u32[]{:S(2)}, u32[]{:S(2)}) collective-permute-start(bf16[8,32,256]{2,1,0:T(8,128)(2,1)S(1)} %get-tuple-element.91), channel_id=1, source_target_pairs={{0,8},{4,12},{8,0},{12,4},{16,24},{20,28},{24,16},{28,20},{1,9},{5... | collective-permute-start | bytes 393224 | tf_op jit(solution)/shard_map/ppermute | solution.py:77
  160.0 13.3 %collective-permute-start.34 = (bf16[8,32,256]{2,1,0:T(8,128)(2,1)S(1)}, bf16[8,32,256]{2,1,0:T(8,128)(2,1)S(1)}, u32[]{:S(2)}, u32[]{:S(2)}) collective-permute-start(bf16[8,32,256]{2,1,0:T(8,128)(2,1)S(1)} %get-tuple-element.92), channel_id=1, source_target_pairs={{0,24},{4,28},{8,16},{12,20},{16,8},{20,12},{24,0},{28,4},{1,25},{... | collective-permute-start | bytes 393224 | tf_op jit(solution)/shard_map/ppermute | solution.py:77
  163.3 10.0 %collective-permute-start.35 = (bf16[8,32,256]{2,1,0:T(8,128)(2,1)S(1)}, bf16[8,32,256]{2,1,0:T(8,128)(2,1)S(1)}, u32[]{:S(2)}, u32[]{:S(2)}) collective-permute-start(bf16[8,32,256]{2,1,0:T(8,128)(2,1)S(1)} %get-tuple-element.93), channel_id=1, source_target_pairs={{0,12},{4,8},{8,4},{12,0},{16,28},{20,24},{24,20},{28,16},{1,13},{... | collective-permute-start | bytes 393224 | tf_op jit(solution)/shard_map/ppermute | solution.py:77
  167.1 8.7 %collective-permute-start.36 = (bf16[8,32,256]{2,1,0:T(8,128)(2,1)S(1)}, bf16[8,32,256]{2,1,0:T(8,128)(2,1)S(1)}, u32[]{:S(2)}, u32[]{:S(2)}) collective-permute-start(bf16[8,32,256]{2,1,0:T(8,128)(2,1)S(1)} %get-tuple-element.94), channel_id=1, source_target_pairs={{0,28},{4,24},{8,20},{12,16},{16,12},{20,8},{24,4},{28,0},{1,29},{... | collective-permute-start | bytes 393224 | tf_op jit(solution)/shard_map/ppermute | solution.py:77
  177.5 21.0 %collective-permute-start.44 = (bf16[32,8192]{1,0:T(8,128)(2,1)S(1)}, bf16[32,8192]{1,0:T(8,128)(2,1)S(1)}, u32[]{:S(2)}, u32[]{:S(2)}) collective-permute-start(bf16[32,8192]{1,0:T(8,128)(2,1)S(1)} %get-tuple-element.105), channel_id=1, source_target_pairs={{0,8},{4,12},{8,0},{12,4},{16,24},{20,28},{24,16},{28,20},{1,9},{5... | collective-permute-start | bytes 1572872 | tf_op jit(solution)/shard_map/ppermute | solution.py:77
  177.5 37.7 %collective-permute-start.45 = (bf16[32,8192]{1,0:T(8,128)(2,1)S(1)}, bf16[32,8192]{1,0:T(8,128)(2,1)S(1)}, u32[]{:S(2)}, u32[]{:S(2)}) collective-permute-start(bf16[32,8192]{1,0:T(8,128)(2,1)S(1)} %get-tuple-element.106), channel_id=1, source_target_pairs={{0,16},{4,20},{8,24},{12,28},{16,0},{20,4},{24,8},{28,12},{1,17},{... | collective-permute-start | bytes 1572872 | tf_op jit(solution)/shard_map/ppermute | solution.py:77
  180.4 45.0 %collective-permute-start.46 = (bf16[32,8192]{1,0:T(8,128)(2,1)S(1)}, bf16[32,8192]{1,0:T(8,128)(2,1)S(1)}, u32[]{:S(2)}, u32[]{:S(2)}) collective-permute-start(bf16[32,8192]{1,0:T(8,128)(2,1)S(1)} %get-tuple-element.107), channel_id=1, source_target_pairs={{0,24},{4,28},{8,16},{12,20},{16,8},{20,12},{24,0},{28,4},{1,25},{... | collective-permute-start | bytes 1572872 | tf_op jit(solution)/shard_map/ppermute | solution.py:77
  (6 other events, 208.9 us)

commit v7 on v6

--- a/solution.py
+++ b/solution.py
@@ -87,52 +87,59 @@
     return [pairs // 2, 0, *[k for k in range(1, pairs) if k != pairs // 2]]
 
 
-def prepare_kernel(pairs, block, meta, cot_ref, context_ref, *refs):
-    outs, (own, other, turned) = refs[:pairs], refs[pairs:]
-    strip, half = block // pairs, block // 2
-    pair, side = lax.div(meta[0], 2), lax.rem(meta[0], 2)
+def strip_kernel(pairs, cot_ref, *refs):
+    outs, turned = refs[:pairs], refs[pairs]
+    strip = turned.shape[0] // pairs
+    pair = lax.div(lax.axis_index("fsdp"), 2)
     turned[...] = cot_ref[...].T
     for k in range(pairs):
         start = pl.multiple_of((pair ^ k) * strip, strip)
         outs[k][0] = turned[pl.ds(start, strip), :]
 
-    @pl.when(pl.program_id(0) == 0)
-    def _():
-        for out, place in ((own, side), (other, side ^ 1)):
-            for r in range(out.shape[1] // half):
-                start = pl.multiple_of(r * block + place * half, half)
-                out[:, r * half : (r + 1) * half] = context_ref[:, pl.ds(start, half)]
-
-
-def prepare(meta, cotangent, context, pairs, block):
+
+def cot_strips(cotangent, pairs, block):
     tokens, width = cotangent.shape
-    band_rows = context.shape[1]
     bands, strip = width // block, block // pairs
-    outs = pl.pallas_call(
-        functools.partial(prepare_kernel, pairs, block),
-        grid_spec=pltpu.PrefetchScalarGridSpec(
-            num_scalar_prefetch=1,
-            grid=(bands,),
-            in_specs=[
-                pl.BlockSpec((tokens, block), lambda c, meta: (0, c)),
-                pl.BlockSpec((tokens, band_rows), lambda c, meta: (0, 0)),
-            ],
-            out_specs=[pl.BlockSpec((1, strip, tokens), lambda c, meta: (c, 0, 0))] * pairs
-            + [pl.BlockSpec((tokens, band_rows // 2), lambda c, meta: (0, 0))] * 2,
-            scratch_shapes=[pltpu.VMEM((block, tokens), jnp.bfloat16)],
-        ),
-        out_shape=[jax.ShapeDtypeStruct((bands, strip, tokens), jnp.bfloat16)] * pairs
-        + [jax.ShapeDtypeStruct((tokens, band_rows // 2), jnp.bfloat16)] * 2,
+    return pl.pallas_call(
+        functools.partial(strip_kernel, pairs),
+        grid=(bands,),
+        in_specs=[pl.BlockSpec((tokens, block), lambda c: (0, c))],
+        out_specs=[pl.BlockSpec((1, strip, tokens), lambda c: (c, 0, 0))] * pairs,
+        scratch_shapes=[pltpu.VMEM((block, tokens), jnp.bfloat16)],
+        out_shape=[jax.ShapeDtypeStruct((bands, strip, tokens), jnp.bfloat16)] * pairs,
         compiler_params=pltpu.CompilerParams(vmem_limit_bytes=8 * MIB),
         cost_estimate=pl.CostEstimate(
-            flops=0, bytes_accessed=4 * tokens * (width + band_rows), transcendentals=0
-        ),
-        name="prepare",
-    )(meta, cotangent, context)
-    return outs[:pairs], outs[pairs], outs[pairs + 1]
-
-
-def gradient_kernel(groups, ranks, sources, chunks, bands, meta, *refs):
+            flops=0, bytes_accessed=4 * tokens * width, transcendentals=0
+        ),
+        name="cot_strips",
+    )(cotangent)
+
+
+def column_kernel(block, context_ref, own, other):
+    half = block // 2
+    side = lax.rem(lax.axis_index("fsdp"), 2)
+    for out, place in ((own, side), (other, side ^ 1)):
+        for r in range(out.shape[1] // half):
+            start = pl.multiple_of(r * block + place * half, half)
+            out[:, r * half : (r + 1) * half] = context_ref[:, pl.ds(start, half)]
+
+
+def column_halves(context, block):
+    tokens, width = context.shape
+    return pl.pallas_call(
+        functools.partial(column_kernel, block),
+        in_specs=[pl.BlockSpec(memory_space=pltpu.VMEM)],
+        out_specs=[pl.BlockSpec(memory_space=pltpu.VMEM)] * 2,
+        out_shape=[jax.ShapeDtypeStruct((tokens, width // 2), jnp.bfloat16)] * 2,
+        compiler_params=pltpu.CompilerParams(vmem_limit_bytes=8 * MIB),
+        cost_estimate=pl.CostEstimate(
+            flops=0, bytes_accessed=4 * tokens * width, transcendentals=0
+        ),
+        name="column_halves",
+    )(context)
+
+
+def gradient_kernel(groups, ranks, sources, chunks, bands, table, *refs):
     pairs = groups // 2
     count = 1 + max(source for source, _ in sources)
     order = pair_order(pairs)
@@ -141,7 +148,7 @@
     slots = sum(chunks)
     rows = cots[0].shape[1]
     strip, part = outs[0].shape[1:]
-    position, rank = meta[0], meta[1]
+    position, rank = lax.axis_index("fsdp"), lax.axis_index("tensor")
     rhs = jnp.concatenate([ctxs[k // 2][k % 2] for k in range(groups)], axis=0)
     for t in range(ranks):
         found = sources[t * groups : (t + 1) * groups]
@@ -154,7 +161,7 @@
 
     def place(first, pieces, s, carry):
         for k in range(groups):
-            block_id = meta[2 + (position ^ offsets[k]) * slots + first + s]
+            block_id = table[(position ^ offsets[k]) * slots + first + s]
             row_band, col_band = lax.div(block_id, bands), lax.rem(block_id, bands)
             piece = lax.div(col_band, own_bands) ^ rank
             start = piece * rows + lax.rem(col_band, own_bands) * strip
@@ -169,7 +176,7 @@
         lax.fori_loop(0, count, functools.partial(place, sum(chunks[:i]), pieces), 0)
 
 
-def gradient_strips(meta, cots, ctxs, chunks, bands, block):
+def gradient_strips(table, cots, ctxs, chunks, bands, block):
     ranks, pairs = len(cots), len(ctxs)
     groups = 2 * pairs
     sources, first = [], 0
@@ -205,7 +212,7 @@
             transcendentals=0,
         ),
         name="gradient_strips",
-    )(meta, *[ctxs[k] for k in pair_order(pairs)], *[piece for rank in cots for piece in rank])
+    )(table, *[ctxs[k] for k in pair_order(pairs)], *[piece for rank in cots for piece in rank])
     return [outs[i * groups : (i + 1) * groups] for i in range(len(chunks))]
 
 
@@ -218,9 +225,9 @@
         turned[rows, columns] = piece[0]
 
 
-def direction_kernel(groups, halves, meta, second_ref, left_ref, right_ref, *refs):
+def direction_kernel(groups, halves, table, second_ref, left_ref, right_ref, *refs):
     grads, outs, turned, rows = refs[:groups], refs[groups : 2 * groups], refs[-2], refs[-1]
-    position = meta[0]
+    position = lax.axis_index("fsdp")
     gather_block(position, grads, turned)
     grad_bf16 = turned[...].T
     grad = grad_bf16.astype(jnp.float32)
@@ -246,19 +253,19 @@
         outs[k][0] = rows[pl.ds(pl.multiple_of(start, sub), sub), :]
 
 
-def directions(meta, grads, first, second, root_left, root_right, halves, sub):
+def directions(table, grads, first, second, root_left, root_right, halves, sub):
     groups = len(grads)
     slots, strip, part = grads[0].shape
     block = second.shape[-1]
-    stat = pl.BlockSpec((1, 1, block, block), lambda s, meta: (0, first + s, 0, 0))
+    stat = pl.BlockSpec((1, 1, block, block), lambda s, table: (0, first + s, 0, 0))
     return pl.pallas_call(
         functools.partial(direction_kernel, groups, halves),
         grid_spec=pltpu.PrefetchScalarGridSpec(
             num_scalar_prefetch=1,
             grid=(slots,),
             in_specs=[stat] * 3
-            + [pl.BlockSpec((1, strip, part), lambda s, meta: (s, 0, 0))] * groups,
-            out_specs=[pl.BlockSpec((1, sub, block), lambda s, meta: (s, 0, 0))] * groups,
+            + [pl.BlockSpec((1, strip, part), lambda s, table: (s, 0, 0))] * groups,
+            out_specs=[pl.BlockSpec((1, sub, block), lambda s, table: (s, 0, 0))] * groups,
             scratch_shapes=[
                 pltpu.VMEM((block, block), jnp.bfloat16),
                 pltpu.VMEM((block, block), jnp.bfloat16),
@@ -272,10 +279,10 @@
             transcendentals=0,
         ),
         name="directions",
-    )(meta, second, root_left, root_right, *grads)
-
-
-def statistics_kernel(groups, chunks, meta, left_ref, right_ref, second_ref, *refs):
+    )(table, second, root_left, root_right, *grads)
+
+
+def statistics_kernel(groups, chunks, table, left_ref, right_ref, second_ref, *refs):
     grads = refs[: groups * len(chunks)]
     left_out, right_out, second_out, turned = refs[groups * len(chunks) :]
     slot = pl.program_id(0)
@@ -284,7 +291,7 @@
 
         @pl.when(jnp.logical_and(slot >= first, slot < first + count))
         def _():
-            gather_block(meta[0], grads[i * groups : (i + 1) * groups], turned)
+            gather_block(lax.axis_index("fsdp"), grads[i * groups : (i + 1) * groups], turned)
 
     block = turned.shape[0]
     grad_t = turned[...]
@@ -297,16 +304,16 @@
     second_out[0, 0] = decay_rate * second_ref[0, 0] + (1.0 - decay_rate) * grad * grad
 
 
-def statistics(meta, grads, left_stat, right_stat, second):
+def statistics(table, grads, left_stat, right_stat, second):
     groups, chunks = len(grads[0]), [chunk[0].shape[0] for chunk in grads]
     _, strip, part = grads[0][0].shape
     block = second.shape[-1]
     slots = sum(chunks)
-    stat = pl.BlockSpec((1, 1, block, block), lambda s, meta: (0, s, 0, 0))
+    stat = pl.BlockSpec((1, 1, block, block), lambda s, table: (0, s, 0, 0))
 
     def strip_spec(first, count):
         return pl.BlockSpec(
-            (1, strip, part), lambda s, meta: (jnp.clip(s - first, 0, count - 1), 0, 0)
+            (1, strip, part), lambda s, table: (jnp.clip(s - first, 0, count - 1), 0, 0)
         )
 
     strip_specs = [
@@ -329,20 +336,20 @@
             transcendentals=0,
         ),
         name="statistics",
-    )(meta, left_stat, right_stat, second, *[piece for chunk in grads for piece in chunk])
-
-
-def regroup_kernel(groups, chunks, bands, halves, meta, *refs):
+    )(table, left_stat, right_stat, second, *[piece for chunk in grads for piece in chunk])
+
+
+def regroup_kernel(groups, chunks, bands, halves, table, *refs):
     inputs, outs, placed = refs[: groups * len(chunks)], refs[groups * len(chunks) : -1], refs[-1]
     block = inputs[0].shape[-1]
-    position = meta[0]
+    position = lax.axis_index("fsdp")
     own_band = lax.div(position, halves)
     slots = sum(chunks)
     offsets = offsets_of(groups)
 
     def place(first, pieces, s, carry):
         for k in range(groups):
-            block_id = meta[2 + (position ^ offsets[k]) * slots + first + s]
+            block_id = table[(position ^ offsets[k]) * slots + first + s]
             row_band, col_band = lax.div(block_id, bands), lax.rem(block_id, bands)
             columns = pl.ds(pl.multiple_of(col_band * block, block), block)
             placed[row_band ^ own_band, :, columns] = pieces[k][s]
@@ -355,7 +362,7 @@
         outs[k][...] = placed[k]
 
 
-def regroup(meta, pieces, bands, halves):
+def regroup(table, pieces, bands, halves):
     groups, chunks = len(pieces[0]), [chunk[0].shape[0] for chunk in pieces]
     _, sub, block = pieces[0][0].shape
     row_bands = groups // halves
@@ -376,13 +383,13 @@
             transcendentals=0,
         ),
         name="regroup",
-    )(meta, *[piece for chunk in pieces for piece in chunk])
-
-
-def stack_kernel(halves, meta, *refs):
+    )(table, *[piece for chunk in pieces for piece in chunk])
+
+
+def stack_kernel(halves, table, *refs):
     pieces, out, sems = refs[:-2], refs[-2], refs[-1]
     sub = pieces[0].shape[0]
-    own_band = lax.div(meta[0], halves)
+    own_band = lax.div(lax.axis_index("fsdp"), halves)
     copies = []
     for k, piece in enumerate(pieces):
         start = pl.multiple_of((own_band ^ k) * sub, sub)
@@ -393,7 +400,7 @@
         copy.wait()
 
 
-def stack_rows(meta, pieces, halves):
+def stack_rows(table, pieces, halves):
     count = len(pieces)
     sub, width = pieces[0].shape
     return pl.pallas_call(
@@ -411,7 +418,7 @@
             flops=0, bytes_accessed=4 * count * sub * width, transcendentals=0
         ),
         name="stack_rows",
-    )(meta, *pieces)
+    )(table, *pieces)
 
 
 def exchange(pieces, offsets):
@@ -426,12 +433,13 @@
     block, slots = left_stat.shape[-1], left_stat.shape[1]
     bands = cotangent.shape[1] * ranks // block
     strip_rows = band_rows // groups
-    place = jnp.stack([lax.axis_index("fsdp"), lax.axis_index("tensor")]).astype(jnp.int32)
-    meta = jnp.concatenate([place, block_table[0]])
+    table = block_table[0]
 
     pairs, tokens = groups // 2, context.shape[0]
     offsets = offsets_of(groups)
-    strips, own, other = prepare(meta, cotangent, context, pairs, block)
+    strips = cot_strips(cotangent, pairs, block)
+    context, _ = lax.optimization_barrier((context, strips[0]))
+    own, other = column_halves(context, block)
     strips = exchange(strips, range(0, groups, 2))
     other = swap(other, "fsdp", 1)
     strips, other = lax.optimization_barrier((strips, other))
@@ -467,20 +475,20 @@
 
     chunks = [slots - slots // 2, slots // 2]
     grads = [
-        exchange(chunk, offsets) for chunk in gradient_strips(meta, cots, ctxs, chunks, bands, block)
+        exchange(chunk, offsets) for chunk in gradient_strips(table, cots, ctxs, chunks, bands, block)
     ]
     halves = block // strip_rows
     sub = strip_rows * halves // groups
     pieces = []
     for i, chunk in enumerate(grads):
         stale = (second_moment, root_left, root_right)
-        parts = directions(meta, chunk, sum(chunks[:i]), *stale, halves, sub)
+        parts = directions(table, chunk, sum(chunks[:i]), *stale, halves, sub)
         pieces.append(exchange(parts, offsets))
     left_new, right_new, second_new = statistics(
-        meta, grads, left_stat, right_stat, second_moment
-    )
-    rows = exchange(regroup(meta, pieces, bands, halves), range(0, groups, halves))
-    return (left_new, right_new, second_new, stack_rows(meta, rows, halves))
+        table, grads, left_stat, right_stat, second_moment
+    )
+    rows = exchange(regroup(table, pieces, bands, halves), range(0, groups, halves))
+    return (left_new, right_new, second_new, stack_rows(table, rows, halves))
 
 
 def per_device(context, cotangent, block_table, left_stat, *rest):

time: 228 us -> 225 us (0.987)
  no operation moved by 1% of the time
where the time goes in v7:
time: 225 us
  waiting for transfers between devices  123 us (55%)
  starting transfers between devices  64.1 us (28%)
  Pallas kernels  34.1 us (15%)
  local copies, waits for them, and re-layouts  2.36 us (1%)
    ppermute x47, waiting for transfers between devices, swap(): return lax.ppermute(value, axis, [(i, i ^ offset) for i in range(count)])  123 us
    ppermute x47, starting transfers between devices, swap(): return lax.ppermute(value, axis, [(i, i ^ offset) for i in range(count)])  64.1 us
    pallas_call x2, Pallas kernels, directions(): pl.pallas_call(functools.partial(direction_kernel, groups, halves), grid_...  12.6 us
    pallas_call x1, Pallas kernels, statistics(): pl.pallas_call(functools.partial(statistics_kernel, groups, chunks), grid...  10.3 us
    pallas_call x1, Pallas kernels, gradient_strips(): pl.pallas_call(functools.partial(gradient_kernel, groups, ranks, sources,...  6.53 us
  transfers between devices with their start and end apart: 47, of which 23 were waited for; matrix products, arithmetic and copies ran while one was open for 0% of the time, Pallas kernels for 10%

profile of v7, /device:TPU:8, one launch (start us, length us, event | category | flops | bytes accessed | tf_op | source)
XLA Modules:
  0.0 224.7 jit_solution(6428194382724298365)
XLA Ops:
  3.0 3.0 %collective-permute-start.1 = (bf16[8,64,256]{2,1,0:T(8,128)(2,1)S(1)}, bf16[8,64,256]{2,1,0:T(8,128)(2,1)S(1)}, u32[]{:S(2)}, u32[]{:S(2)}) collective-permute-start(bf16[8,64,256]{2,1,0:T(8,128)(2,1)S(1)} %get-tuple-element.61), channel_id=1, source_target_pairs={{0,16},{4,20},{8,24},{12,28},{16,0},{20,4},{24,8},{28,12},{1,17},{... | collective-permute-start | bytes 786440 | tf_op jit(solution)/shard_map/ppermute | solution.py:77
  7.6 1.6 collective-permute-start.3
  9.2 4.4 %collective-permute-done = bf16[8,64,256]{2,1,0:T(8,128)(2,1)S(1)} collective-permute-done((bf16[8,64,256]{2,1,0:T(8,128)(2,1)S(1)}, bf16[8,64,256]{2,1,0:T(8,128)(2,1)S(1)}, u32[]{:S(2)}, u32[]{:S(2)}) %collective-permute-start) | collective-permute-done | bytes 262176 | tf_op jit(solution)/shard_map/ppermute | solution.py:77
  13.7 10.3 %collective-permute-done.1 = bf16[8,64,256]{2,1,0:T(8,128)(2,1)S(1)} collective-permute-done((bf16[8,64,256]{2,1,0:T(8,128)(2,1)S(1)}, bf16[8,64,256]{2,1,0:T(8,128)(2,1)S(1)}, u32[]{:S(2)}, u32[]{:S(2)}) %collective-permute-start.1) | collective-permute-done | bytes 262176 | tf_op jit(solution)/shard_map/ppermute | solution.py:77
  24.0 5.1 %collective-permute-done.2 = bf16[8,64,256]{2,1,0:T(8,128)(2,1)S(1)} collective-permute-done((bf16[8,64,256]{2,1,0:T(8,128)(2,1)S(1)}, bf16[8,64,256]{2,1,0:T(8,128)(2,1)S(1)}, u32[]{:S(2)}, u32[]{:S(2)}) %collective-permute-start.2) | collective-permute-done | bytes 262176 | tf_op jit(solution)/shard_map/ppermute | solution.py:77
  29.2 1.6 collective-permute-start.7
  30.8 1.5 collective-permute-start.10
  32.4 3.0 %collective-permute-start.4 = (bf16[2,256,512]{2,1,0:T(8,128)(2,1)S(1)}, bf16[2,256,512]{2,1,0:T(8,128)(2,1)S(1)}, u32[]{:S(2)}, u32[]{:S(2)}) collective-permute-start(bf16[2,256,512]{2,1,0:T(8,128)(2,1)S(1)} %pad_maximum_fusion.1.refs_1_), channel_id=1, source_target_pairs={{0,16},{4,20},{8,24},{12,28},{16,0},{20,4},{24,8},{28,12},{1,17},{... | collective-permute-start | bytes 1572872 | tf_op jit(solution)/shard_map/ppermute | solution.py:77
  35.4 17.6 %collective-permute-done.7.refs_5_ = bf16[4,512,256]{2,1,0:T(8,128)(2,1)S(1)} collective-permute-done((bf16[4,512,256]{2,1,0:T(8,128)(2,1)S(1)}, bf16[4,512,256]{2,1,0:T(8,128)(2,1)S(1)}, u32[]{:S(2)}, u32[]{:S(2)}) %collective-permute-start.7) | collective-permute-done | bytes 1048608 | tf_op jit(solution)/shard_map/ppermute | solution.py:77
  53.3 1.4 collective-permute-start.11
  54.7 2.1 collective-permute-done.4.refs_0_
  56.7 1.6 collective-permute-start.6
  58.9 6.6 %collective-permute-done.11.refs_9_ = bf16[2,512,256]{2,1,0:T(8,128)(2,1)S(1)} collective-permute-done((bf16[2,512,256]{2,1,0:T(8,128)(2,1)S(1)}, bf16[2,512,256]{2,1,0:T(8,128)(2,1)S(1)}, u32[]{:S(2)}, u32[]{:S(2)}) %collective-permute-start.11) | collective-permute-done | bytes 524320 | tf_op jit(solution)/shard_map/ppermute | solution.py:77
  65.5 4.9 %collective-permute-done.12.refs_10_ = bf16[2,512,256]{2,1,0:T(8,128)(2,1)S(1)} collective-permute-done((bf16[2,512,256]{2,1,0:T(8,128)(2,1)S(1)}, bf16[2,512,256]{2,1,0:T(8,128)(2,1)S(1)}, u32[]{:S(2)}, u32[]{:S(2)}) %collective-permute-start.12) | collective-permute-done | bytes 524320 | tf_op jit(solution)/shard_map/ppermute | solution.py:77
  71.0 1.4 collective-permute-done.15.refs_13_
  73.2 6.5 %gradient_strips.1 = (bf16[8,64,128]{2,1,0:T(8,128)(2,1)S(1)}, bf16[8,64,128]{2,1,0:T(8,128)(2,1)S(1)}, bf16[8,64,128]{2,1,0:T(8,128)(2,1)S(1)}, bf16[8,64,128]{...) custom-call(s32[128]{0:T(128)S(1)} %bitcast.9, ...), custom_call_target="tpu_custom_call" | custom-call | flops 4294967296 | bytes 12582912 | tf_op jit(solution)/shard_map/gradient_strips/pallas_call | solution.py:192
  79.7 1.4 collective-permute-start.16
  81.1 1.5 collective-permute-start.17
  83.2 1.5 collective-permute-start.24
  84.7 2.3 %collective-permute-start.25 = (bf16[8,64,128]{2,1,0:T(8,128)(2,1)S(1)}, bf16[8,64,128]{2,1,0:T(8,128)(2,1)S(1)}, u32[]{:S(2)}, u32[]{:S(2)}) collective-permute-start(bf16[8,64,128]{2,1,0:T(8,128)(2,1)S(1)} %get-tuple-element.81), channel_id=1, source_target_pairs={{0,20},{4,16},{8,28},{12,24},{16,4},{20,0},{24,12},{28,8},{1,21},{... | collective-permute-start | bytes 393224 | tf_op jit(solution)/shard_map/ppermute | solution.py:77
  87.1 5.6 %collective-permute-done.16.refs_0_ = bf16[8,64,128]{2,1,0:T(8,128)(2,1)S(1)} collective-permute-done((bf16[8,64,128]{2,1,0:T(8,128)(2,1)S(1)}, bf16[8,64,128]{2,1,0:T(8,128)(2,1)S(1)}, u32[]{:S(2)}, u32[]{:S(2)}) %collective-permute-start.16) | collective-permute-done | bytes 131104 | tf_op jit(solution)/shard_map/ppermute | solution.py:77
  92.7 3.1 %collective-permute-start.26 = (bf16[8,64,128]{2,1,0:T(8,128)(2,1)S(1)}, bf16[8,64,128]{2,1,0:T(8,128)(2,1)S(1)}, u32[]{:S(2)}, u32[]{:S(2)}) collective-permute-start(bf16[8,64,128]{2,1,0:T(8,128)(2,1)S(1)} %get-tuple-element.82), channel_id=1, source_target_pairs={{0,8},{4,12},{8,0},{12,4},{16,24},{20,28},{24,16},{28,20},{1,9},{5... | collective-permute-start | bytes 393224 | tf_op jit(solution)/shard_map/ppermute | solution.py:77
  96.7 2.3 %collective-permute-start.28 = (bf16[8,64,128]{2,1,0:T(8,128)(2,1)S(1)}, bf16[8,64,128]{2,1,0:T(8,128)(2,1)S(1)}, u32[]{:S(2)}, u32[]{:S(2)}) collective-permute-start(bf16[8,64,128]{2,1,0:T(8,128)(2,1)S(1)} %get-tuple-element.84), channel_id=1, source_target_pairs={{0,12},{4,8},{8,4},{12,0},{16,28},{20,24},{24,20},{28,16},{1,13},{... | collective-permute-start | bytes 393224 | tf_op jit(solution)/shard_map/ppermute | solution.py:77
  99.0 1.4 collective-permute-start.29
  100.7 4.6 %collective-permute-start.18 = (bf16[8,64,128]{2,1,0:T(8,128)(2,1)S(1)}, bf16[8,64,128]{2,1,0:T(8,128)(2,1)S(1)}, u32[]{:S(2)}, u32[]{:S(2)}) collective-permute-start(bf16[8,64,128]{2,1,0:T(8,128)(2,1)S(1)} %get-tuple-element.73), channel_id=1, source_target_pairs={{0,20},{4,16},{8,28},{12,24},{16,4},{20,0},{24,12},{28,8},{1,21},{... | collective-permute-start | bytes 393224 | tf_op jit(solution)/shard_map/ppermute | solution.py:77
  105.3 1.2 collective-permute-start.19
  106.5 4.5 %collective-permute-done.27.refs_12_.refs_4_ = bf16[8,64,128]{2,1,0:T(8,128)(2,1)S(1)} collective-permute-done((bf16[8,64,128]{2,1,0:T(8,128)(2,1)S(1)}, bf16[8,64,128]{2,1,0:T(8,128)(2,1)S(1)}, u32[]{:S(2)}, u32[]{:S(2)}) %collective-permute-start.27) | collective-permute-done | bytes 131104 | tf_op jit(solution)/shard_map/ppermute | solution.py:77
  112.9 2.1 collective-permute-done.29.refs_14_.refs_6_
  114.9 3.4 %collective-permute-start.22 = (bf16[8,64,128]{2,1,0:T(8,128)(2,1)S(1)}, bf16[8,64,128]{2,1,0:T(8,128)(2,1)S(1)}, u32[]{:S(2)}, u32[]{:S(2)}) collective-permute-start(bf16[8,64,128]{2,1,0:T(8,128)(2,1)S(1)} %get-tuple-element.77), channel_id=1, source_target_pairs={{0,28},{4,24},{8,20},{12,16},{16,12},{20,8},{24,4},{28,0},{1,29},{... | collective-permute-start | bytes 393224 | tf_op jit(solution)/shard_map/ppermute | solution.py:77
  118.4 6.3 %directions.3 = (bf16[8,32,256]{2,1,0:T(8,128)(2,1)S(1)}, bf16[8,32,256]{2,1,0:T(8,128)(2,1)S(1)}, bf16[8,32,256]{2,1,0:T(8,128)(2,1)S(1)}, bf16[8,32,256]{2,1,0...) custom-call(s32[128]{0:T(128)S(1)} %bitcast.10, ...), custom_call_target="tpu_custom_call" | custom-call | flops 536870912 | bytes 8388608 | tf_op jit(solution)/shard_map/directions/pallas_call | solution.py:261
  125.9 3.2 %collective-permute-start.39 = (bf16[8,32,256]{2,1,0:T(8,128)(2,1)S(1)}, bf16[8,32,256]{2,1,0:T(8,128)(2,1)S(1)}, u32[]{:S(2)}, u32[]{:S(2)}) collective-permute-start(bf16[8,32,256]{2,1,0:T(8,128)(2,1)S(1)} %get-tuple-element.100), channel_id=1, source_target_pairs={{0,20},{4,16},{8,28},{12,24},{16,4},{20,0},{24,12},{28,8},{1,21},{... | collective-permute-start | bytes 393224 | tf_op jit(solution)/shard_map/ppermute | solution.py:77
  129.2 3.5 %collective-permute-done.22.refs_6_ = bf16[8,64,128]{2,1,0:T(8,128)(2,1)S(1)} collective-permute-done((bf16[8,64,128]{2,1,0:T(8,128)(2,1)S(1)}, bf16[8,64,128]{2,1,0:T(8,128)(2,1)S(1)}, u32[]{:S(2)}, u32[]{:S(2)}) %collective-permute-start.22) | collective-permute-done | bytes 131104 | tf_op jit(solution)/shard_map/ppermute | solution.py:77
  132.7 2.6 %collective-permute-start.41 = (bf16[8,32,256]{2,1,0:T(8,128)(2,1)S(1)}, bf16[8,32,256]{2,1,0:T(8,128)(2,1)S(1)}, u32[]{:S(2)}, u32[]{:S(2)}) collective-permute-start(bf16[8,32,256]{2,1,0:T(8,128)(2,1)S(1)} %get-tuple-element.102), channel_id=1, source_target_pairs={{0,24},{4,28},{8,16},{12,20},{16,8},{20,12},{24,0},{28,4},{1,25},{... | collective-permute-start | bytes 393224 | tf_op jit(solution)/shard_map/ppermute | solution.py:77
  135.3 6.3 %directions.2 = (bf16[8,32,256]{2,1,0:T(8,128)(2,1)S(1)}, bf16[8,32,256]{2,1,0:T(8,128)(2,1)S(1)}, bf16[8,32,256]{2,1,0:T(8,128)(2,1)S(1)}, bf16[8,32,256]{2,1,0...) custom-call(s32[128]{0:T(128)S(1)} %bitcast.11, ...), custom_call_target="tpu_custom_call" | custom-call | flops 536870912 | bytes 8388608 | tf_op jit(solution)/shard_map/directions/pallas_call | solution.py:261
  142.6 4.3 %collective-permute-start.30 = (bf16[8,32,256]{2,1,0:T(8,128)(2,1)S(1)}, bf16[8,32,256]{2,1,0:T(8,128)(2,1)S(1)}, u32[]{:S(2)}, u32[]{:S(2)}) collective-permute-start(bf16[8,32,256]{2,1,0:T(8,128)(2,1)S(1)} %get-tuple-element.90), channel_id=1, source_target_pairs={{0,16},{4,20},{8,24},{12,28},{16,0},{20,4},{24,8},{28,12},{1,17},{... | collective-permute-start | bytes 393224 | tf_op jit(solution)/shard_map/ppermute | solution.py:77
  146.9 1.5 collective-permute-start.32
  149.9 7.7 %collective-permute-done.43.refs_14_ = bf16[8,32,256]{2,1,0:T(8,128)(2,1)S(1)} collective-permute-done((bf16[8,32,256]{2,1,0:T(8,128)(2,1)S(1)}, bf16[8,32,256]{2,1,0:T(8,128)(2,1)S(1)}, u32[]{:S(2)}, u32[]{:S(2)}) %collective-permute-start.43) | collective-permute-done | bytes 131104 | tf_op jit(solution)/shard_map/ppermute | solution.py:77
  157.6 3.2 %collective-permute-done.30.refs_0_ = bf16[8,32,256]{2,1,0:T(8,128)(2,1)S(1)} collective-permute-done((bf16[8,32,256]{2,1,0:T(8,128)(2,1)S(1)}, bf16[8,32,256]{2,1,0:T(8,128)(2,1)S(1)}, u32[]{:S(2)}, u32[]{:S(2)}) %collective-permute-start.30) | collective-permute-done | bytes 131104 | tf_op jit(solution)/shard_map/ppermute | solution.py:77
  160.8 3.8 %collective-permute-start.35 = (bf16[8,32,256]{2,1,0:T(8,128)(2,1)S(1)}, bf16[8,32,256]{2,1,0:T(8,128)(2,1)S(1)}, u32[]{:S(2)}, u32[]{:S(2)}) collective-permute-start(bf16[8,32,256]{2,1,0:T(8,128)(2,1)S(1)} %get-tuple-element.95), channel_id=1, source_target_pairs={{0,12},{4,8},{8,4},{12,0},{16,28},{20,24},{24,20},{28,16},{1,13},{... | collective-permute-start | bytes 393224 | tf_op jit(solution)/shard_map/ppermute | solution.py:77
  165.6 5.2 %collective-permute-done.34.refs_4_ = bf16[8,32,256]{2,1,0:T(8,128)(2,1)S(1)} collective-permute-done((bf16[8,32,256]{2,1,0:T(8,128)(2,1)S(1)}, bf16[8,32,256]{2,1,0:T(8,128)(2,1)S(1)}, u32[]{:S(2)}, u32[]{:S(2)}) %collective-permute-start.34) | collective-permute-done | bytes 131104 | tf_op jit(solution)/shard_map/ppermute | solution.py:77
  170.8 2.5 %collective-permute-done.36.refs_6_ = bf16[8,32,256]{2,1,0:T(8,128)(2,1)S(1)} collective-permute-done((bf16[8,32,256]{2,1,0:T(8,128)(2,1)S(1)}, bf16[8,32,256]{2,1,0:T(8,128)(2,1)S(1)}, u32[]{:S(2)}, u32[]{:S(2)}) %collective-permute-start.36) | collective-permute-done | bytes 131104 | tf_op jit(solution)/shard_map/ppermute | solution.py:77
  173.3 1.6 regroup.1
  175.0 2.8 %collective-permute-start.45 = (bf16[32,8192]{1,0:T(8,128)(2,1)S(1)}, bf16[32,8192]{1,0:T(8,128)(2,1)S(1)}, u32[]{:S(2)}, u32[]{:S(2)}) collective-permute-start(bf16[32,8192]{1,0:T(8,128)(2,1)S(1)} %get-tuple-element.108), channel_id=1, source_target_pairs={{0,16},{4,20},{8,24},{12,28},{16,0},{20,4},{24,8},{28,12},{1,17},{... | collective-permute-start | bytes 1572872 | tf_op jit(solution)/shard_map/ppermute | solution.py:77
  178.5 10.3 %statistics.1 = (f32[1,16,256,256]{3,2,1,0:T(8,128)}, f32[1,16,256,256]{3,2,1,0:T(8,128)}, f32[1,16,256,256]{3,2,1,0:T(8,128)}) custom-call(s32[128]{0:T(128)S(1)} %bitcast.13, f32[1,16,256,256]{3,2,1,0:T(8,128)S(1)} %copy-done.3, f32[1,16,256,256]{3,2,1,0:T(8,128)S(1)} %copy-done.4, f32[1,16,256,256]{3,2,1,0:T(8,128)S(1)} %copy-done, ...), custom_call_target="tpu_custom_call" | custom-call | flops 1073741824 | bytes 27262976 | tf_op jit(solution)/shard_map/statistics/pallas_call | solution.py:322
  188.8 7.1 %collective-permute-done.44.refs_1_ = bf16[32,8192]{1,0:T(8,128)(2,1)S(1)} collective-permute-done((bf16[32,8192]{1,0:T(8,128)(2,1)S(1)}, bf16[32,8192]{1,0:T(8,128)(2,1)S(1)}, u32[]{:S(2)}, u32[]{:S(2)}) %collective-permute-start.44) | collective-permute-done | bytes 524320 | tf_op jit(solution)/shard_map/ppermute | solution.py:77
  195.9 16.8 %collective-permute-done.45.refs_2_ = bf16[32,8192]{1,0:T(8,128)(2,1)S(1)} collective-permute-done((bf16[32,8192]{1,0:T(8,128)(2,1)S(1)}, bf16[32,8192]{1,0:T(8,128)(2,1)S(1)}, u32[]{:S(2)}, u32[]{:S(2)}) %collective-permute-start.45) | collective-permute-done | bytes 524320 | tf_op jit(solution)/shard_map/ppermute | solution.py:77
  212.7 10.1 %collective-permute-done.46.refs_3_ = bf16[32,8192]{1,0:T(8,128)(2,1)S(1)} collective-permute-done((bf16[32,8192]{1,0:T(8,128)(2,1)S(1)}, bf16[32,8192]{1,0:T(8,128)(2,1)S(1)}, u32[]{:S(2)}, u32[]{:S(2)}) %collective-permute-start.46) | collective-permute-done | bytes 524320 | tf_op jit(solution)/shard_map/ppermute | solution.py:77
  222.8 1.9 stack_rows.1
  (74 shorter events, 15.4 us)
Async XLA Ops:
  1.9 71.3 %copy-start.7 = (s32[1,128]{1,0:T(1,128)S(1)}, s32[1,128]{1,0:T(1,128)}, u32[]{:S(2)}) copy-start(s32[1,128]{1,0:T(1,128)} %param.10) | copy-start | bytes 1540
  2.9 10.8 %collective-permute-start = (bf16[8,64,256]{2,1,0:T(8,128)(2,1)S(1)}, bf16[8,64,256]{2,1,0:T(8,128)(2,1)S(1)}, u32[]{:S(2)}, u32[]{:S(2)}) collective-permute-start(bf16[8,64,256]{2,1,0:T(8,128)(2,1)S(1)} %get-tuple-element.60), channel_id=1, source_target_pairs={{0,8},{4,12},{8,0},{12,4},{16,24},{20,28},{24,16},{28,20},{1,9},{5... | collective-permute-start | bytes 786440 | tf_op jit(solution)/shard_map/ppermute | solution.py:77
  3.0 21.0 %collective-permute-start.1 = (bf16[8,64,256]{2,1,0:T(8,128)(2,1)S(1)}, bf16[8,64,256]{2,1,0:T(8,128)(2,1)S(1)}, u32[]{:S(2)}, u32[]{:S(2)}) collective-permute-start(bf16[8,64,256]{2,1,0:T(8,128)(2,1)S(1)} %get-tuple-element.61), channel_id=1, source_target_pairs={{0,16},{4,20},{8,24},{12,28},{16,0},{20,4},{24,8},{28,12},{1,17},{... | collective-permute-start | bytes 786440 | tf_op jit(solution)/shard_map/ppermute | solution.py:77
  6.0 23.1 %collective-permute-start.2 = (bf16[8,64,256]{2,1,0:T(8,128)(2,1)S(1)}, bf16[8,64,256]{2,1,0:T(8,128)(2,1)S(1)}, u32[]{:S(2)}, u32[]{:S(2)}) collective-permute-start(bf16[8,64,256]{2,1,0:T(8,128)(2,1)S(1)} %get-tuple-element.62), channel_id=1, source_target_pairs={{0,24},{4,28},{8,16},{12,20},{16,8},{20,12},{24,0},{28,4},{1,25},{... | collective-permute-start | bytes 786440 | tf_op jit(solution)/shard_map/ppermute | solution.py:77
  7.6 21.5 %collective-permute-start.3 = (bf16[256,512]{1,0:T(8,128)(2,1)S(1)}, bf16[256,512]{1,0:T(8,128)(2,1)S(1)}, u32[]{:S(2)}, u32[]{:S(2)}) collective-permute-start(bf16[256,512]{1,0:T(8,128)(2,1)S(1)} %get-tuple-element.63), channel_id=1, source_target_pairs={{0,4},{4,0},{8,12},{12,8},{16,20},{20,16},{24,28},{28,24},{1,5},{5... | collective-permute-start | bytes 786440 | tf_op jit(solution)/shard_map/ppermute | solution.py:77
  29.2 23.8 %collective-permute-start.7 = (bf16[4,512,256]{2,1,0:T(8,128)(2,1)S(1)}, bf16[4,512,256]{2,1,0:T(8,128)(2,1)S(1)}, u32[]{:S(2)}, u32[]{:S(2)}) collective-permute-start(bf16[4,512,256]{2,1,0:T(8,128)(2,1)S(1)} %pad_maximum_fusion.refs_4_), channel_id=1, source_target_pairs={{0,4},{4,0},{8,12},{12,8},{16,20},{20,16},{24,28},{28,24},{1,5},{5... | collective-permute-start | bytes 3145736 | tf_op jit(solution)/shard_map/ppermute | solution.py:77
  30.8 27.5 %collective-permute-start.10 = (bf16[4,512,256]{2,1,0:T(8,128)(2,1)S(1)}, bf16[4,512,256]{2,1,0:T(8,128)(2,1)S(1)}, u32[]{:S(2)}, u32[]{:S(2)}) collective-permute-start(bf16[4,512,256]{2,1,0:T(8,128)(2,1)S(1)} %pad_maximum_fusion.refs_4_), channel_id=1, source_target_pairs={{0,2},{1,3},{2,0},{3,1},{4,6},{5,7},{6,4},{7,5},{8,10},{9,11},{10,... | collective-permute-start | bytes 3145736 | tf_op jit(solution)/shard_map/ppermute | solution.py:77
  32.4 20.9 %collective-permute-start.5 = (bf16[2,256,512]{2,1,0:T(8,128)(2,1)S(1)}, bf16[2,256,512]{2,1,0:T(8,128)(2,1)S(1)}, u32[]{:S(2)}, u32[]{:S(2)}) collective-permute-start(bf16[2,256,512]{2,1,0:T(8,128)(2,1)S(1)} %pad_maximum_fusion.1.refs_1_), channel_id=1, source_target_pairs={{0,8},{4,12},{8,0},{12,4},{16,24},{20,28},{24,16},{28,20},{1,9},{5... | collective-permute-start | bytes 1572872 | tf_op jit(solution)/shard_map/ppermute | solution.py:77
  32.4 24.3 %collective-permute-start.4 = (bf16[2,256,512]{2,1,0:T(8,128)(2,1)S(1)}, bf16[2,256,512]{2,1,0:T(8,128)(2,1)S(1)}, u32[]{:S(2)}, u32[]{:S(2)}) collective-permute-start(bf16[2,256,512]{2,1,0:T(8,128)(2,1)S(1)} %pad_maximum_fusion.1.refs_1_), channel_id=1, source_target_pairs={{0,16},{4,20},{8,24},{12,28},{16,0},{20,4},{24,8},{28,12},{1,17},{... | collective-permute-start | bytes 1572872 | tf_op jit(solution)/shard_map/ppermute | solution.py:77
  53.3 12.2 %collective-permute-start.11 = (bf16[2,512,256]{2,1,0:T(8,128)(2,1)S(1)}, bf16[2,512,256]{2,1,0:T(8,128)(2,1)S(1)}, u32[]{:S(2)}, u32[]{:S(2)}) collective-permute-start(bf16[2,512,256]{2,1,0:T(8,128)(2,1)S(1)} %slice.8), channel_id=1, source_target_pairs={{0,2},{1,3},{2,0},{3,1},{4,6},{5,7},{6,4},{7,5},{8,10},{9,11},{10,... | collective-permute-start | bytes 1572872 | tf_op jit(solution)/shard_map/ppermute | solution.py:77
  54.7 16.3 %collective-permute-start.8 = (bf16[4,512,256]{2,1,0:T(8,128)(2,1)S(1)}, bf16[4,512,256]{2,1,0:T(8,128)(2,1)S(1)}, u32[]{:S(2)}, u32[]{:S(2)}) collective-permute-start(bf16[4,512,256]{2,1,0:T(8,128)(2,1)S(1)} %pad_maximum_fusion.refs_4_), channel_id=1, source_target_pairs={{0,1},{1,0},{2,3},{3,2},{4,5},{5,4},{6,7},{7,6},{8,9},{9,8},{10,11... | collective-permute-start | bytes 3145736 | tf_op jit(solution)/shard_map/ppermute | solution.py:77
  56.7 13.8 %collective-permute-start.6 = (bf16[2,256,512]{2,1,0:T(8,128)(2,1)S(1)}, bf16[2,256,512]{2,1,0:T(8,128)(2,1)S(1)}, u32[]{:S(2)}, u32[]{:S(2)}) collective-permute-start(bf16[2,256,512]{2,1,0:T(8,128)(2,1)S(1)} %collective-permute-done.4.refs_0_), channel_id=1, source_target_pairs={{0,8},{4,12},{8,0},{12,4},{16,24},{20,28},{24,16},{28,20},{1,9},{5... | collective-permute-start | bytes 1572872 | tf_op jit(solution)/shard_map/ppermute | solution.py:77
  58.4 12.1 %collective-permute-start.12 = (bf16[2,512,256]{2,1,0:T(8,128)(2,1)S(1)}, bf16[2,512,256]{2,1,0:T(8,128)(2,1)S(1)}, u32[]{:S(2)}, u32[]{:S(2)}) collective-permute-start(bf16[2,512,256]{2,1,0:T(8,128)(2,1)S(1)} %slice.9), channel_id=1, source_target_pairs={{0,4},{4,0},{8,12},{12,8},{16,20},{20,16},{24,28},{28,24},{1,5},{5... | collective-permute-start | bytes 1572872 | tf_op jit(solution)/shard_map/ppermute | solution.py:77
  58.9 12.1 %collective-permute-start.9 = (bf16[4,512,256]{2,1,0:T(8,128)(2,1)S(1)}, bf16[4,512,256]{2,1,0:T(8,128)(2,1)S(1)}, u32[]{:S(2)}, u32[]{:S(2)}) collective-permute-start(bf16[4,512,256]{2,1,0:T(8,128)(2,1)S(1)} %collective-permute-done.7.refs_5_), channel_id=1, source_target_pairs={{0,1},{1,0},{2,3},{3,2},{4,5},{5,4},{6,7},{7,6},{8,9},{9,8},{10,11... | collective-permute-start | bytes 3145736 | tf_op jit(solution)/shard_map/ppermute | solution.py:77
  65.5 7.6 %collective-permute-start.13 = (bf16[4,512,256]{2,1,0:T(8,128)(2,1)S(1)}, bf16[4,512,256]{2,1,0:T(8,128)(2,1)S(1)}, u32[]{:S(2)}, u32[]{:S(2)}) collective-permute-start(bf16[4,512,256]{2,1,0:T(8,128)(2,1)S(1)} %collective-permute-done.10.refs_8_), channel_id=1, source_target_pairs={{0,1},{1,0},{2,3},{3,2},{4,5},{5,4},{6,7},{7,6},{8,9},{9,8},{10,11... | collective-permute-start | bytes 3145736 | tf_op jit(solution)/shard_map/ppermute | solution.py:77
  70.5 1.9 collective-permute-start.15
  70.5 2.7 %collective-permute-start.14 = (bf16[2,512,256]{2,1,0:T(8,128)(2,1)S(1)}, bf16[2,512,256]{2,1,0:T(8,128)(2,1)S(1)}, u32[]{:S(2)}, u32[]{:S(2)}) collective-permute-start(bf16[2,512,256]{2,1,0:T(8,128)(2,1)S(1)} %collective-permute-done.11.refs_9_), channel_id=1, source_target_pairs={{0,1},{1,0},{2,3},{3,2},{4,5},{5,4},{6,7},{7,6},{8,9},{9,8},{10,11... | collective-permute-start | bytes 1572872 | tf_op jit(solution)/shard_map/ppermute | solution.py:77
  79.7 13.0 %collective-permute-start.16 = (bf16[8,64,128]{2,1,0:T(8,128)(2,1)S(1)}, bf16[8,64,128]{2,1,0:T(8,128)(2,1)S(1)}, u32[]{:S(2)}, u32[]{:S(2)}) collective-permute-start(bf16[8,64,128]{2,1,0:T(8,128)(2,1)S(1)} %get-tuple-element.71), channel_id=1, source_target_pairs={{0,16},{4,20},{8,24},{12,28},{16,0},{20,4},{24,8},{28,12},{1,17},{... | collective-permute-start | bytes 393224 | tf_op jit(solution)/shard_map/ppermute | solution.py:77
  81.1 14.7 %collective-permute-start.17 = (bf16[8,64,128]{2,1,0:T(8,128)(2,1)S(1)}, bf16[8,64,128]{2,1,0:T(8,128)(2,1)S(1)}, u32[]{:S(2)}, u32[]{:S(2)}) collective-permute-start(bf16[8,64,128]{2,1,0:T(8,128)(2,1)S(1)} %get-tuple-element.72), channel_id=1, source_target_pairs={{0,4},{4,0},{8,12},{12,8},{16,20},{20,16},{24,28},{28,24},{1,5},{5... | collective-permute-start | bytes 393224 | tf_op jit(solution)/shard_map/ppermute | solution.py:77
  82.7 14.0 %collective-permute-start.23 = (bf16[8,64,128]{2,1,0:T(8,128)(2,1)S(1)}, bf16[8,64,128]{2,1,0:T(8,128)(2,1)S(1)}, u32[]{:S(2)}, u32[]{:S(2)}) collective-permute-start(bf16[8,64,128]{2,1,0:T(8,128)(2,1)S(1)} %get-tuple-element.79), channel_id=1, source_target_pairs={{0,16},{4,20},{8,24},{12,28},{16,0},{20,4},{24,8},{28,12},{1,17},{... | collective-permute-start | bytes 393224 | tf_op jit(solution)/shard_map/ppermute | solution.py:77
  83.2 15.8 %collective-permute-start.24 = (bf16[8,64,128]{2,1,0:T(8,128)(2,1)S(1)}, bf16[8,64,128]{2,1,0:T(8,128)(2,1)S(1)}, u32[]{:S(2)}, u32[]{:S(2)}) collective-permute-start(bf16[8,64,128]{2,1,0:T(8,128)(2,1)S(1)} %get-tuple-element.80), channel_id=1, source_target_pairs={{0,4},{4,0},{8,12},{12,8},{16,20},{20,16},{24,28},{28,24},{1,5},{5... | collective-permute-start | bytes 393224 | tf_op jit(solution)/shard_map/ppermute | solution.py:77
  84.7 16.0 %collective-permute-start.25 = (bf16[8,64,128]{2,1,0:T(8,128)(2,1)S(1)}, bf16[8,64,128]{2,1,0:T(8,128)(2,1)S(1)}, u32[]{:S(2)}, u32[]{:S(2)}) collective-permute-start(bf16[8,64,128]{2,1,0:T(8,128)(2,1)S(1)} %get-tuple-element.81), channel_id=1, source_target_pairs={{0,20},{4,16},{8,28},{12,24},{16,4},{20,0},{24,12},{28,8},{1,21},{... | collective-permute-start | bytes 393224 | tf_op jit(solution)/shard_map/ppermute | solution.py:77
  92.7 12.6 %collective-permute-start.26 = (bf16[8,64,128]{2,1,0:T(8,128)(2,1)S(1)}, bf16[8,64,128]{2,1,0:T(8,128)(2,1)S(1)}, u32[]{:S(2)}, u32[]{:S(2)}) collective-permute-start(bf16[8,64,128]{2,1,0:T(8,128)(2,1)S(1)} %get-tuple-element.82), channel_id=1, source_target_pairs={{0,8},{4,12},{8,0},{12,4},{16,24},{20,28},{24,16},{28,20},{1,9},{5... | collective-permute-start | bytes 393224 | tf_op jit(solution)/shard_map/ppermute | solution.py:77
  95.8 15.2 %collective-permute-start.27 = (bf16[8,64,128]{2,1,0:T(8,128)(2,1)S(1)}, bf16[8,64,128]{2,1,0:T(8,128)(2,1)S(1)}, u32[]{:S(2)}, u32[]{:S(2)}) collective-permute-start(bf16[8,64,128]{2,1,0:T(8,128)(2,1)S(1)} %get-tuple-element.83), channel_id=1, source_target_pairs={{0,24},{4,28},{8,16},{12,20},{16,8},{20,12},{24,0},{28,4},{1,25},{... | collective-permute-start | bytes 393224 | tf_op jit(solution)/shard_map/ppermute | solution.py:77
  96.7 15.2 %collective-permute-start.28 = (bf16[8,64,128]{2,1,0:T(8,128)(2,1)S(1)}, bf16[8,64,128]{2,1,0:T(8,128)(2,1)S(1)}, u32[]{:S(2)}, u32[]{:S(2)}) collective-permute-start(bf16[8,64,128]{2,1,0:T(8,128)(2,1)S(1)} %get-tuple-element.84), channel_id=1, source_target_pairs={{0,12},{4,8},{8,4},{12,0},{16,28},{20,24},{24,20},{28,16},{1,13},{... | collective-permute-start | bytes 393224 | tf_op jit(solution)/shard_map/ppermute | solution.py:77
  99.0 15.9 %collective-permute-start.29 = (bf16[8,64,128]{2,1,0:T(8,128)(2,1)S(1)}, bf16[8,64,128]{2,1,0:T(8,128)(2,1)S(1)}, u32[]{:S(2)}, u32[]{:S(2)}) collective-permute-start(bf16[8,64,128]{2,1,0:T(8,128)(2,1)S(1)} %get-tuple-element.85), channel_id=1, source_target_pairs={{0,28},{4,24},{8,20},{12,16},{16,12},{20,8},{24,4},{28,0},{1,29},{... | collective-permute-start | bytes 393224 | tf_op jit(solution)/shard_map/ppermute | solution.py:77
  100.7 23.9 %collective-permute-start.18 = (bf16[8,64,128]{2,1,0:T(8,128)(2,1)S(1)}, bf16[8,64,128]{2,1,0:T(8,128)(2,1)S(1)}, u32[]{:S(2)}, u32[]{:S(2)}) collective-permute-start(bf16[8,64,128]{2,1,0:T(8,128)(2,1)S(1)} %get-tuple-element.73), channel_id=1, source_target_pairs={{0,20},{4,16},{8,28},{12,24},{16,4},{20,0},{24,12},{28,8},{1,21},{... | collective-permute-start | bytes 393224 | tf_op jit(solution)/shard_map/ppermute | solution.py:77
  105.3 19.6 %collective-permute-start.19 = (bf16[8,64,128]{2,1,0:T(8,128)(2,1)S(1)}, bf16[8,64,128]{2,1,0:T(8,128)(2,1)S(1)}, u32[]{:S(2)}, u32[]{:S(2)}) collective-permute-start(bf16[8,64,128]{2,1,0:T(8,128)(2,1)S(1)} %get-tuple-element.74), channel_id=1, source_target_pairs={{0,8},{4,12},{8,0},{12,4},{16,24},{20,28},{24,16},{28,20},{1,9},{5... | collective-permute-start | bytes 393224 | tf_op jit(solution)/shard_map/ppermute | solution.py:77
  111.0 14.9 %collective-permute-start.20 = (bf16[8,64,128]{2,1,0:T(8,128)(2,1)S(1)}, bf16[8,64,128]{2,1,0:T(8,128)(2,1)S(1)}, u32[]{:S(2)}, u32[]{:S(2)}) collective-permute-start(bf16[8,64,128]{2,1,0:T(8,128)(2,1)S(1)} %get-tuple-element.75), channel_id=1, source_target_pairs={{0,24},{4,28},{8,16},{12,20},{16,8},{20,12},{24,0},{28,4},{1,25},{... | collective-permute-start | bytes 393224 | tf_op jit(solution)/shard_map/ppermute | solution.py:77
  111.9 17.3 %collective-permute-start.21 = (bf16[8,64,128]{2,1,0:T(8,128)(2,1)S(1)}, bf16[8,64,128]{2,1,0:T(8,128)(2,1)S(1)}, u32[]{:S(2)}, u32[]{:S(2)}) collective-permute-start(bf16[8,64,128]{2,1,0:T(8,128)(2,1)S(1)} %get-tuple-element.76), channel_id=1, source_target_pairs={{0,12},{4,8},{8,4},{12,0},{16,28},{20,24},{24,20},{28,16},{1,13},{... | collective-permute-start | bytes 393224 | tf_op jit(solution)/shard_map/ppermute | solution.py:77
  114.9 17.7 %collective-permute-start.22 = (bf16[8,64,128]{2,1,0:T(8,128)(2,1)S(1)}, bf16[8,64,128]{2,1,0:T(8,128)(2,1)S(1)}, u32[]{:S(2)}, u32[]{:S(2)}) collective-permute-start(bf16[8,64,128]{2,1,0:T(8,128)(2,1)S(1)} %get-tuple-element.77), channel_id=1, source_target_pairs={{0,28},{4,24},{8,20},{12,16},{16,12},{20,8},{24,4},{28,0},{1,29},{... | collective-permute-start | bytes 393224 | tf_op jit(solution)/shard_map/ppermute | solution.py:77
  124.7 16.9 %collective-permute-start.37 = (bf16[8,32,256]{2,1,0:T(8,128)(2,1)S(1)}, bf16[8,32,256]{2,1,0:T(8,128)(2,1)S(1)}, u32[]{:S(2)}, u32[]{:S(2)}) collective-permute-start(bf16[8,32,256]{2,1,0:T(8,128)(2,1)S(1)} %get-tuple-element.98), channel_id=1, source_target_pairs={{0,16},{4,20},{8,24},{12,28},{16,0},{20,4},{24,8},{28,12},{1,17},{... | collective-permute-start | bytes 393224 | tf_op jit(solution)/shard_map/ppermute | solution.py:77
  124.9 16.7 %collective-permute-start.38 = (bf16[8,32,256]{2,1,0:T(8,128)(2,1)S(1)}, bf16[8,32,256]{2,1,0:T(8,128)(2,1)S(1)}, u32[]{:S(2)}, u32[]{:S(2)}) collective-permute-start(bf16[8,32,256]{2,1,0:T(8,128)(2,1)S(1)} %get-tuple-element.99), channel_id=1, source_target_pairs={{0,4},{4,0},{8,12},{12,8},{16,20},{20,16},{24,28},{28,24},{1,5},{5... | collective-permute-start | bytes 393224 | tf_op jit(solution)/shard_map/ppermute | solution.py:77
  125.9 16.6 %collective-permute-start.39 = (bf16[8,32,256]{2,1,0:T(8,128)(2,1)S(1)}, bf16[8,32,256]{2,1,0:T(8,128)(2,1)S(1)}, u32[]{:S(2)}, u32[]{:S(2)}) collective-permute-start(bf16[8,32,256]{2,1,0:T(8,128)(2,1)S(1)} %get-tuple-element.100), channel_id=1, source_target_pairs={{0,20},{4,16},{8,28},{12,24},{16,4},{20,0},{24,12},{28,8},{1,21},{... | collective-permute-start | bytes 393224 | tf_op jit(solution)/shard_map/ppermute | solution.py:77
  129.1 17.8 %collective-permute-start.40 = (bf16[8,32,256]{2,1,0:T(8,128)(2,1)S(1)}, bf16[8,32,256]{2,1,0:T(8,128)(2,1)S(1)}, u32[]{:S(2)}, u32[]{:S(2)}) collective-permute-start(bf16[8,32,256]{2,1,0:T(8,128)(2,1)S(1)} %get-tuple-element.101), channel_id=1, source_target_pairs={{0,8},{4,12},{8,0},{12,4},{16,24},{20,28},{24,16},{28,20},{1,9},{5... | collective-permute-start | bytes 393224 | tf_op jit(solution)/shard_map/ppermute | solution.py:77
  132.7 14.2 %collective-permute-start.41 = (bf16[8,32,256]{2,1,0:T(8,128)(2,1)S(1)}, bf16[8,32,256]{2,1,0:T(8,128)(2,1)S(1)}, u32[]{:S(2)}, u32[]{:S(2)}) collective-permute-start(bf16[8,32,256]{2,1,0:T(8,128)(2,1)S(1)} %get-tuple-element.102), channel_id=1, source_target_pairs={{0,24},{4,28},{8,16},{12,20},{16,8},{20,12},{24,0},{28,4},{1,25},{... | collective-permute-start | bytes 393224 | tf_op jit(solution)/shard_map/ppermute | solution.py:77
  141.5 8.0 %collective-permute-start.42 = (bf16[8,32,256]{2,1,0:T(8,128)(2,1)S(1)}, bf16[8,32,256]{2,1,0:T(8,128)(2,1)S(1)}, u32[]{:S(2)}, u32[]{:S(2)}) collective-permute-start(bf16[8,32,256]{2,1,0:T(8,128)(2,1)S(1)} %get-tuple-element.103), channel_id=1, source_target_pairs={{0,12},{4,8},{8,4},{12,0},{16,28},{20,24},{24,20},{28,16},{1,13},{... | collective-permute-start | bytes 393224 | tf_op jit(solution)/shard_map/ppermute | solution.py:77
  141.6 15.9 %collective-permute-start.43 = (bf16[8,32,256]{2,1,0:T(8,128)(2,1)S(1)}, bf16[8,32,256]{2,1,0:T(8,128)(2,1)S(1)}, u32[]{:S(2)}, u32[]{:S(2)}) collective-permute-start(bf16[8,32,256]{2,1,0:T(8,128)(2,1)S(1)} %get-tuple-element.104), channel_id=1, source_target_pairs={{0,28},{4,24},{8,20},{12,16},{16,12},{20,8},{24,4},{28,0},{1,29},{... | collective-permute-start | bytes 393224 | tf_op jit(solution)/shard_map/ppermute | solution.py:77
  142.6 18.2 %collective-permute-start.30 = (bf16[8,32,256]{2,1,0:T(8,128)(2,1)S(1)}, bf16[8,32,256]{2,1,0:T(8,128)(2,1)S(1)}, u32[]{:S(2)}, u32[]{:S(2)}) collective-permute-start(bf16[8,32,256]{2,1,0:T(8,128)(2,1)S(1)} %get-tuple-element.90), channel_id=1, source_target_pairs={{0,16},{4,20},{8,24},{12,28},{16,0},{20,4},{24,8},{28,12},{1,17},{... | collective-permute-start | bytes 393224 | tf_op jit(solution)/shard_map/ppermute | solution.py:77
  146.9 17.7 %collective-permute-start.31 = (bf16[8,32,256]{2,1,0:T(8,128)(2,1)S(1)}, bf16[8,32,256]{2,1,0:T(8,128)(2,1)S(1)}, u32[]{:S(2)}, u32[]{:S(2)}) collective-permute-start(bf16[8,32,256]{2,1,0:T(8,128)(2,1)S(1)} %get-tuple-element.91), channel_id=1, source_target_pairs={{0,4},{4,0},{8,12},{12,8},{16,20},{20,16},{24,28},{28,24},{1,5},{5... | collective-permute-start | bytes 393224 | tf_op jit(solution)/shard_map/ppermute | solution.py:77
  146.9 18.7 %collective-permute-start.32 = (bf16[8,32,256]{2,1,0:T(8,128)(2,1)S(1)}, bf16[8,32,256]{2,1,0:T(8,128)(2,1)S(1)}, u32[]{:S(2)}, u32[]{:S(2)}) collective-permute-start(bf16[8,32,256]{2,1,0:T(8,128)(2,1)S(1)} %get-tuple-element.92), channel_id=1, source_target_pairs={{0,20},{4,16},{8,28},{12,24},{16,4},{20,0},{24,12},{28,8},{1,21},{... | collective-permute-start | bytes 393224 | tf_op jit(solution)/shard_map/ppermute | solution.py:77
  149.6 16.0 %collective-permute-start.33 = (bf16[8,32,256]{2,1,0:T(8,128)(2,1)S(1)}, bf16[8,32,256]{2,1,0:T(8,128)(2,1)S(1)}, u32[]{:S(2)}, u32[]{:S(2)}) collective-permute-start(bf16[8,32,256]{2,1,0:T(8,128)(2,1)S(1)} %get-tuple-element.93), channel_id=1, source_target_pairs={{0,8},{4,12},{8,0},{12,4},{16,24},{20,28},{24,16},{28,20},{1,9},{5... | collective-permute-start | bytes 393224 | tf_op jit(solution)/shard_map/ppermute | solution.py:77
  157.5 13.3 %collective-permute-start.34 = (bf16[8,32,256]{2,1,0:T(8,128)(2,1)S(1)}, bf16[8,32,256]{2,1,0:T(8,128)(2,1)S(1)}, u32[]{:S(2)}, u32[]{:S(2)}) collective-permute-start(bf16[8,32,256]{2,1,0:T(8,128)(2,1)S(1)} %get-tuple-element.94), channel_id=1, source_target_pairs={{0,24},{4,28},{8,16},{12,20},{16,8},{20,12},{24,0},{28,4},{1,25},{... | collective-permute-start | bytes 393224 | tf_op jit(solution)/shard_map/ppermute | solution.py:77
  160.8 10.0 %collective-permute-start.35 = (bf16[8,32,256]{2,1,0:T(8,128)(2,1)S(1)}, bf16[8,32,256]{2,1,0:T(8,128)(2,1)S(1)}, u32[]{:S(2)}, u32[]{:S(2)}) collective-permute-start(bf16[8,32,256]{2,1,0:T(8,128)(2,1)S(1)} %get-tuple-element.95), channel_id=1, source_target_pairs={{0,12},{4,8},{8,4},{12,0},{16,28},{20,24},{24,20},{28,16},{1,13},{... | collective-permute-start | bytes 393224 | tf_op jit(solution)/shard_map/ppermute | solution.py:77
  164.6 8.7 %collective-permute-start.36 = (bf16[8,32,256]{2,1,0:T(8,128)(2,1)S(1)}, bf16[8,32,256]{2,1,0:T(8,128)(2,1)S(1)}, u32[]{:S(2)}, u32[]{:S(2)}) collective-permute-start(bf16[8,32,256]{2,1,0:T(8,128)(2,1)S(1)} %get-tuple-element.96), channel_id=1, source_target_pairs={{0,28},{4,24},{8,20},{12,16},{16,12},{20,8},{24,4},{28,0},{1,29},{... | collective-permute-start | bytes 393224 | tf_op jit(solution)/shard_map/ppermute | solution.py:77
  174.9 21.0 %collective-permute-start.44 = (bf16[32,8192]{1,0:T(8,128)(2,1)S(1)}, bf16[32,8192]{1,0:T(8,128)(2,1)S(1)}, u32[]{:S(2)}, u32[]{:S(2)}) collective-permute-start(bf16[32,8192]{1,0:T(8,128)(2,1)S(1)} %get-tuple-element.107), channel_id=1, source_target_pairs={{0,8},{4,12},{8,0},{12,4},{16,24},{20,28},{24,16},{28,20},{1,9},{5... | collective-permute-start | bytes 1572872 | tf_op jit(solution)/shard_map/ppermute | solution.py:77
  175.0 37.7 %collective-permute-start.45 = (bf16[32,8192]{1,0:T(8,128)(2,1)S(1)}, bf16[32,8192]{1,0:T(8,128)(2,1)S(1)}, u32[]{:S(2)}, u32[]{:S(2)}) collective-permute-start(bf16[32,8192]{1,0:T(8,128)(2,1)S(1)} %get-tuple-element.108), channel_id=1, source_target_pairs={{0,16},{4,20},{8,24},{12,28},{16,0},{20,4},{24,8},{28,12},{1,17},{... | collective-permute-start | bytes 1572872 | tf_op jit(solution)/shard_map/ppermute | solution.py:77
  177.8 45.0 %collective-permute-start.46 = (bf16[32,8192]{1,0:T(8,128)(2,1)S(1)}, bf16[32,8192]{1,0:T(8,128)(2,1)S(1)}, u32[]{:S(2)}, u32[]{:S(2)}) collective-permute-start(bf16[32,8192]{1,0:T(8,128)(2,1)S(1)} %get-tuple-element.109), channel_id=1, source_target_pairs={{0,24},{4,28},{8,16},{12,20},{16,8},{20,12},{24,0},{28,4},{1,25},{... | collective-permute-start | bytes 1572872 | tf_op jit(solution)/shard_map/ppermute | solution.py:77
  (7 other events, 224.4 us)

commit v8 on v7

--- a/solution.py
+++ b/solution.py
@@ -9,6 +9,7 @@
 
 decay_rate = 0.95
 MIB = 1024 * 1024
+TOGETHER = 4
 
 
 def general_plan(
@@ -173,7 +174,7 @@
 
     for i, count in enumerate(chunks):
         pieces = outs[i * groups : (i + 1) * groups]
-        lax.fori_loop(0, count, functools.partial(place, sum(chunks[:i]), pieces), 0)
+        lax.fori_loop(0, count, functools.partial(place, sum(chunks[:i]), pieces), 0, unroll=4)
 
 
 def gradient_strips(table, cots, ctxs, chunks, bands, block):
@@ -216,63 +217,65 @@
     return [outs[i * groups : (i + 1) * groups] for i in range(len(chunks))]
 
 
-def gather_block(position, grads, turned):
+def gather_block(position, grads, slot, turned):
     for offset, piece in zip(offsets_of(len(grads)), grads):
         _, strip, part = piece.shape
         middle = position ^ offset
         rows = pl.ds(pl.multiple_of(lax.div(middle, 2) * strip, strip), strip)
         columns = pl.ds(pl.multiple_of(lax.rem(middle, 2) * part, part), part)
-        turned[rows, columns] = piece[0]
-
-
-def direction_kernel(groups, halves, table, second_ref, left_ref, right_ref, *refs):
+        turned[rows, columns] = piece[slot]
+
+
+def direction_kernel(groups, halves, together, table, second_ref, left_ref, right_ref, *refs):
     grads, outs, turned, rows = refs[:groups], refs[groups : 2 * groups], refs[-2], refs[-1]
     position = lax.axis_index("fsdp")
-    gather_block(position, grads, turned)
-    grad_bf16 = turned[...].T
-    grad = grad_bf16.astype(jnp.float32)
-    second = decay_rate * second_ref[0, 0] + (1.0 - decay_rate) * grad * grad
-    adam = grad / (jnp.sqrt(second) + 1e-08)
-    half = jnp.dot(
-        left_ref[0, 0].astype(jnp.bfloat16), grad_bf16, preferred_element_type=jnp.float32
-    )
-    shaped = jnp.dot(
-        half.astype(jnp.bfloat16),
-        right_ref[0, 0].astype(jnp.bfloat16),
-        preferred_element_type=jnp.float32,
-    )
-    adam_sum = jnp.sum(adam * adam, keepdims=True)
-    shaped_sum = jnp.sum(shaped * shaped, keepdims=True)
-    ratio = jnp.sqrt(adam_sum) / jnp.sqrt(shaped_sum + 1e-06)
-    rows[...] = (shaped * ratio).astype(jnp.bfloat16)
     sub = outs[0].shape[1]
-    for k, offset in enumerate(offsets_of(groups)):
-        middle = position ^ offset
-        half, quarter = lax.rem(middle, halves), lax.div(middle, halves)
-        start = (half * (groups // halves) + quarter) * sub
-        outs[k][0] = rows[pl.ds(pl.multiple_of(start, sub), sub), :]
+    for u in range(together):
+        slot = pl.program_id(0) * together + u
+        gather_block(position, grads, slot, turned.at[u])
+        grad_bf16 = turned[u].T
+        grad = grad_bf16.astype(jnp.float32)
+        second = decay_rate * second_ref[0, u] + (1.0 - decay_rate) * grad * grad
+        adam = grad / (jnp.sqrt(second) + 1e-08)
+        half = jnp.dot(
+            left_ref[0, u].astype(jnp.bfloat16), grad_bf16, preferred_element_type=jnp.float32
+        )
+        shaped = jnp.dot(
+            half.astype(jnp.bfloat16),
+            right_ref[0, u].astype(jnp.bfloat16),
+            preferred_element_type=jnp.float32,
+        )
+        adam_sum = jnp.sum(adam * adam, keepdims=True)
+        shaped_sum = jnp.sum(shaped * shaped, keepdims=True)
+        ratio = jnp.sqrt(adam_sum) / jnp.sqrt(shaped_sum + 1e-06)
+        rows[u] = (shaped * ratio).astype(jnp.bfloat16)
+        for k, offset in enumerate(offsets_of(groups)):
+            middle = position ^ offset
+            side, quarter = lax.rem(middle, halves), lax.div(middle, halves)
+            start = (side * (groups // halves) + quarter) * sub
+            outs[k][slot] = rows[u, pl.ds(pl.multiple_of(start, sub), sub), :]
 
 
 def directions(table, grads, first, second, root_left, root_right, halves, sub):
     groups = len(grads)
-    slots, strip, part = grads[0].shape
+    slots = grads[0].shape[0]
     block = second.shape[-1]
-    stat = pl.BlockSpec((1, 1, block, block), lambda s, table: (0, first + s, 0, 0))
+    together = TOGETHER if slots % TOGETHER == 0 and first % TOGETHER == 0 else 1
+    stat = pl.BlockSpec(
+        (1, together, block, block), lambda s, table: (0, first // together + s, 0, 0)
+    )
+    whole = pl.BlockSpec(memory_space=pltpu.VMEM)
     return pl.pallas_call(
-        functools.partial(direction_kernel, groups, halves),
+        functools.partial(direction_kernel, groups, halves, together),
         grid_spec=pltpu.PrefetchScalarGridSpec(
             num_scalar_prefetch=1,
-            grid=(slots,),
-            in_specs=[stat] * 3
-            + [pl.BlockSpec((1, strip, part), lambda s, table: (s, 0, 0))] * groups,
-            out_specs=[pl.BlockSpec((1, sub, block), lambda s, table: (s, 0, 0))] * groups,
-            scratch_shapes=[
-                pltpu.VMEM((block, block), jnp.bfloat16),
-                pltpu.VMEM((block, block), jnp.bfloat16),
-            ],
+            grid=(slots // together,),
+            in_specs=[stat] * 3 + [whole] * groups,
+            out_specs=[whole] * groups,
+            scratch_shapes=[pltpu.VMEM((together, block, block), jnp.bfloat16)] * 2,
         ),
         out_shape=[jax.ShapeDtypeStruct((slots, sub, block), jnp.bfloat16)] * groups,
-        compiler_params=pltpu.CompilerParams(vmem_limit_bytes=8 * MIB),
+        compiler_params=pltpu.CompilerParams(vmem_limit_bytes=16 * MIB),
         cost_estimate=pl.CostEstimate(
             flops=4 * slots * block**3,
             bytes_accessed=16 * slots * block * block,
@@ -291,7 +294,8 @@
 
         @pl.when(jnp.logical_and(slot >= first, slot < first + count))
         def _():
-            gather_block(lax.axis_index("fsdp"), grads[i * groups : (i + 1) * groups], turned)
+            pieces = grads[i * groups : (i + 1) * groups]
+            gather_block(lax.axis_index("fsdp"), pieces, 0, turned)
 
     block = turned.shape[0]
     grad_t = turned[...]
@@ -339,6 +343,10 @@
     )(table, left_stat, right_stat, second, *[piece for chunk in grads for piece in chunk])
 
 
+def row_order(pairs):
+    return [*reversed(range(pairs))]
+
+
 def regroup_kernel(groups, chunks, bands, halves, table, *refs):
     inputs, outs, placed = refs[: groups * len(chunks)], refs[groups * len(chunks) : -1], refs[-1]
     block = inputs[0].shape[-1]
@@ -357,9 +365,9 @@
 
     for i, count in enumerate(chunks):
         pieces = inputs[i * groups : (i + 1) * groups]
-        lax.fori_loop(0, count, functools.partial(place, sum(chunks[:i]), pieces), 0)
-    for k in range(len(outs)):
-        outs[k][...] = placed[k]
+        lax.fori_loop(0, count, functools.partial(place, sum(chunks[:i]), pieces), 0, unroll=4)
+    for k, out in zip(row_order(len(outs)), outs):
+        out[...] = placed[k]
 
 
 def regroup(table, pieces, bands, halves):
@@ -386,39 +394,42 @@
     )(table, *[piece for chunk in pieces for piece in chunk])
 
 
-def stack_kernel(halves, table, *refs):
-    pieces, out, sems = refs[:-2], refs[-2], refs[-1]
+def stack_kernel(halves, offsets, table, *refs):
+    pieces, out, sems = refs[: len(offsets)], refs[-2], refs[-1]
     sub = pieces[0].shape[0]
     own_band = lax.div(lax.axis_index("fsdp"), halves)
     copies = []
-    for k, piece in enumerate(pieces):
+    for i, (piece, k) in enumerate(zip(pieces, offsets)):
         start = pl.multiple_of((own_band ^ k) * sub, sub)
-        copies.append(pltpu.make_async_copy(piece, out.at[0, pl.ds(start, sub), :], sems.at[k]))
+        copies.append(pltpu.make_async_copy(piece, out.at[0, pl.ds(start, sub), :], sems.at[i]))
     for copy in copies:
         copy.start()
     for copy in copies:
         copy.wait()
 
 
-def stack_rows(table, pieces, halves):
-    count = len(pieces)
+def stack_rows(table, pieces, offsets, halves, count, known=None):
     sub, width = pieces[0].shape
+    anywhere = pl.BlockSpec(memory_space=pl.ANY)
+    before = [] if known is None else [known]
     return pl.pallas_call(
-        functools.partial(stack_kernel, halves),
+        functools.partial(stack_kernel, halves, offsets),
         grid_spec=pltpu.PrefetchScalarGridSpec(
             num_scalar_prefetch=1,
             grid=(),
-            in_specs=[pl.BlockSpec(memory_space=pltpu.VMEM)] * count,
-            out_specs=pl.BlockSpec(memory_space=pl.ANY),
-            scratch_shapes=[pltpu.SemaphoreType.DMA((count,))],
+            in_specs=[pl.BlockSpec(memory_space=pltpu.VMEM)] * len(pieces)
+            + [anywhere] * len(before),
+            out_specs=anywhere,
+            scratch_shapes=[pltpu.SemaphoreType.DMA((len(pieces),))],
         ),
         out_shape=jax.ShapeDtypeStruct((1, count * sub, width), jnp.bfloat16),
+        input_output_aliases={len(pieces) + 1: 0} if before else {},
         compiler_params=pltpu.CompilerParams(vmem_limit_bytes=4 * MIB),
         cost_estimate=pl.CostEstimate(
-            flops=0, bytes_accessed=4 * count * sub * width, transcendentals=0
+            flops=0, bytes_accessed=4 * len(pieces) * sub * width, transcendentals=0
         ),
         name="stack_rows",
-    )(table, *pieces)
+    )(table, *pieces, *before)
 
 
 def exchange(pieces, offsets):
@@ -487,8 +498,11 @@
     left_new, right_new, second_new = statistics(
         table, grads, left_stat, right_stat, second_moment
     )
-    rows = exchange(regroup(table, pieces, bands, halves), range(0, groups, halves))
-    return (left_new, right_new, second_new, stack_rows(table, rows, halves))
+    order = row_order(pairs)
+    rows = exchange(regroup(table, pieces, bands, halves), [k * halves for k in order])
+    found = stack_rows(table, rows[1:], order[1:], halves, pairs)
+    found = stack_rows(table, rows[:1], order[:1], halves, pairs, found)
+    return (left_new, right_new, second_new, found)
 
 
 def per_device(context, cotangent, block_table, left_stat, *rest):

time: 225 us -> 224 us (level)
  starting transfers between devices: 64.1 us -> 72.8 us
  Pallas kernels: 34.1 us -> 28.8 us
  waiting for transfers between devices: 123 us -> 118 us
    ppermute x47, starting transfers between devices: 64.1 us -> 72.8 us  [swap(): return lax.ppermute(value, axis, [(i, i ^ offset) for i in range(count)])]
    pallas_call x3 -> x4, Pallas kernels: 14.5 us -> 9.32 us  [the longest x2 6.26 us: directions(): pl.pallas_call(functools.partial(direction_kernel, groups, halves, togeth...]
    ppermute x47, waiting for transfers between devices: 123 us -> 118 us  [swap(): return lax.ppermute(value, axis, [(i, i ^ offset) for i in range(count)])]
  transfers between devices with their start and end apart: 47 -> 47, of which waited for: 23 -> 23; matrix products, arithmetic and copies ran while one was open for 0% -> 0% of each run, Pallas kernels for 10% -> 8%
where the time goes in v8:
time: 224 us; the launch traced here: 223 us
  waiting for transfers between devices  118 us (53%)
  starting transfers between devices  72.8 us (32%)
  Pallas kernels  28.8 us (13%)
  local copies, waits for them, and re-layouts  2.36 us (1%)
    ppermute x47, waiting for transfers between devices, swap(): return lax.ppermute(value, axis, [(i, i ^ offset) for i in range(count)])  118 us
    ppermute x47, starting transfers between devices, swap(): return lax.ppermute(value, axis, [(i, i ^ offset) for i in range(count)])  72.8 us
    pallas_call x1, Pallas kernels, statistics(): pl.pallas_call(functools.partial(statistics_kernel, groups, chunks), grid...  10.3 us
    pallas_call x1, Pallas kernels, gradient_strips(): pl.pallas_call(functools.partial(gradient_kernel, groups, ranks, sources,...  6.46 us
    pallas_call x2, Pallas kernels, directions(): pl.pallas_call(functools.partial(direction_kernel, groups, halves, togeth...  6.26 us
  transfers between devices with their start and end apart: 47, of which 23 were waited for; matrix products, arithmetic and copies ran while one was open for 0% of the time, Pallas kernels for 8%

profile of v8, /device:TPU:8, one launch (start us, length us, event | category | flops | bytes accessed | tf_op | source)
XLA Modules:
  0.0 223.3 jit_solution(139741082357456737)
XLA Ops:
  3.0 3.0 %collective-permute-start.1 = (bf16[8,64,256]{2,1,0:T(8,128)(2,1)S(1)}, bf16[8,64,256]{2,1,0:T(8,128)(2,1)S(1)}, u32[]{:S(2)}, u32[]{:S(2)}) collective-permute-start(bf16[8,64,256]{2,1,0:T(8,128)(2,1)S(1)} %get-tuple-element.61), channel_id=1, source_target_pairs={{0,16},{4,20},{8,24},{12,28},{16,0},{20,4},{24,8},{28,12},{1,17},{... | collective-permute-start | bytes 786440 | tf_op jit(solution)/shard_map/ppermute | solution.py:78
  7.6 1.6 collective-permute-start.3
  9.2 4.4 %collective-permute-done = bf16[8,64,256]{2,1,0:T(8,128)(2,1)S(1)} collective-permute-done((bf16[8,64,256]{2,1,0:T(8,128)(2,1)S(1)}, bf16[8,64,256]{2,1,0:T(8,128)(2,1)S(1)}, u32[]{:S(2)}, u32[]{:S(2)}) %collective-permute-start) | collective-permute-done | bytes 262176 | tf_op jit(solution)/shard_map/ppermute | solution.py:78
  13.7 10.3 %collective-permute-done.1 = bf16[8,64,256]{2,1,0:T(8,128)(2,1)S(1)} collective-permute-done((bf16[8,64,256]{2,1,0:T(8,128)(2,1)S(1)}, bf16[8,64,256]{2,1,0:T(8,128)(2,1)S(1)}, u32[]{:S(2)}, u32[]{:S(2)}) %collective-permute-start.1) | collective-permute-done | bytes 262176 | tf_op jit(solution)/shard_map/ppermute | solution.py:78
  24.0 5.1 %collective-permute-done.2 = bf16[8,64,256]{2,1,0:T(8,128)(2,1)S(1)} collective-permute-done((bf16[8,64,256]{2,1,0:T(8,128)(2,1)S(1)}, bf16[8,64,256]{2,1,0:T(8,128)(2,1)S(1)}, u32[]{:S(2)}, u32[]{:S(2)}) %collective-permute-start.2) | collective-permute-done | bytes 262176 | tf_op jit(solution)/shard_map/ppermute | solution.py:78
  29.2 1.6 collective-permute-start.7
  30.8 1.5 collective-permute-start.10
  32.4 3.0 %collective-permute-start.4 = (bf16[2,256,512]{2,1,0:T(8,128)(2,1)S(1)}, bf16[2,256,512]{2,1,0:T(8,128)(2,1)S(1)}, u32[]{:S(2)}, u32[]{:S(2)}) collective-permute-start(bf16[2,256,512]{2,1,0:T(8,128)(2,1)S(1)} %pad_maximum_fusion.1.refs_1_), channel_id=1, source_target_pairs={{0,16},{4,20},{8,24},{12,28},{16,0},{20,4},{24,8},{28,12},{1,17},{... | collective-permute-start | bytes 1572872 | tf_op jit(solution)/shard_map/ppermute | solution.py:78
  35.4 17.6 %collective-permute-done.7.refs_5_ = bf16[4,512,256]{2,1,0:T(8,128)(2,1)S(1)} collective-permute-done((bf16[4,512,256]{2,1,0:T(8,128)(2,1)S(1)}, bf16[4,512,256]{2,1,0:T(8,128)(2,1)S(1)}, u32[]{:S(2)}, u32[]{:S(2)}) %collective-permute-start.7) | collective-permute-done | bytes 1048608 | tf_op jit(solution)/shard_map/ppermute | solution.py:78
  54.7 2.1 collective-permute-done.4.refs_0_
  56.7 1.6 collective-permute-start.6
  58.9 6.6 %collective-permute-done.11.refs_9_ = bf16[2,512,256]{2,1,0:T(8,128)(2,1)S(1)} collective-permute-done((bf16[2,512,256]{2,1,0:T(8,128)(2,1)S(1)}, bf16[2,512,256]{2,1,0:T(8,128)(2,1)S(1)}, u32[]{:S(2)}, u32[]{:S(2)}) %collective-permute-start.11) | collective-permute-done | bytes 524320 | tf_op jit(solution)/shard_map/ppermute | solution.py:78
  65.5 4.9 %collective-permute-done.12.refs_10_ = bf16[2,512,256]{2,1,0:T(8,128)(2,1)S(1)} collective-permute-done((bf16[2,512,256]{2,1,0:T(8,128)(2,1)S(1)}, bf16[2,512,256]{2,1,0:T(8,128)(2,1)S(1)}, u32[]{:S(2)}, u32[]{:S(2)}) %collective-permute-start.12) | collective-permute-done | bytes 524320 | tf_op jit(solution)/shard_map/ppermute | solution.py:78
  71.0 1.4 collective-permute-done.15.refs_13_
  73.2 6.5 %gradient_strips.1 = (bf16[8,64,128]{2,1,0:T(8,128)(2,1)S(1)}, bf16[8,64,128]{2,1,0:T(8,128)(2,1)S(1)}, bf16[8,64,128]{2,1,0:T(8,128)(2,1)S(1)}, bf16[8,64,128]{...) custom-call(s32[128]{0:T(128)S(1)} %bitcast.9, ...), custom_call_target="tpu_custom_call" | custom-call | flops 4294967296 | bytes 12582912 | tf_op jit(solution)/shard_map/gradient_strips/pallas_call | solution.py:193
  79.6 1.4 collective-permute-start.16
  81.1 1.5 collective-permute-start.17
  83.1 1.5 collective-permute-start.24
  84.7 2.3 %collective-permute-start.25 = (bf16[8,64,128]{2,1,0:T(8,128)(2,1)S(1)}, bf16[8,64,128]{2,1,0:T(8,128)(2,1)S(1)}, u32[]{:S(2)}, u32[]{:S(2)}) collective-permute-start(bf16[8,64,128]{2,1,0:T(8,128)(2,1)S(1)} %get-tuple-element.81), channel_id=1, source_target_pairs={{0,20},{4,16},{8,28},{12,24},{16,4},{20,0},{24,12},{28,8},{1,21},{... | collective-permute-start | bytes 393224 | tf_op jit(solution)/shard_map/ppermute | solution.py:78
  87.0 5.6 %collective-permute-done.16.refs_0_ = bf16[8,64,128]{2,1,0:T(8,128)(2,1)S(1)} collective-permute-done((bf16[8,64,128]{2,1,0:T(8,128)(2,1)S(1)}, bf16[8,64,128]{2,1,0:T(8,128)(2,1)S(1)}, u32[]{:S(2)}, u32[]{:S(2)}) %collective-permute-start.16) | collective-permute-done | bytes 131104 | tf_op jit(solution)/shard_map/ppermute | solution.py:78
  92.6 3.1 %collective-permute-start.26 = (bf16[8,64,128]{2,1,0:T(8,128)(2,1)S(1)}, bf16[8,64,128]{2,1,0:T(8,128)(2,1)S(1)}, u32[]{:S(2)}, u32[]{:S(2)}) collective-permute-start(bf16[8,64,128]{2,1,0:T(8,128)(2,1)S(1)} %get-tuple-element.82), channel_id=1, source_target_pairs={{0,8},{4,12},{8,0},{12,4},{16,24},{20,28},{24,16},{28,20},{1,9},{5... | collective-permute-start | bytes 393224 | tf_op jit(solution)/shard_map/ppermute | solution.py:78
  96.6 2.3 %collective-permute-start.28 = (bf16[8,64,128]{2,1,0:T(8,128)(2,1)S(1)}, bf16[8,64,128]{2,1,0:T(8,128)(2,1)S(1)}, u32[]{:S(2)}, u32[]{:S(2)}) collective-permute-start(bf16[8,64,128]{2,1,0:T(8,128)(2,1)S(1)} %get-tuple-element.84), channel_id=1, source_target_pairs={{0,12},{4,8},{8,4},{12,0},{16,28},{20,24},{24,20},{28,16},{1,13},{... | collective-permute-start | bytes 393224 | tf_op jit(solution)/shard_map/ppermute | solution.py:78
  98.9 1.4 collective-permute-start.29
  100.7 4.6 %collective-permute-start.18 = (bf16[8,64,128]{2,1,0:T(8,128)(2,1)S(1)}, bf16[8,64,128]{2,1,0:T(8,128)(2,1)S(1)}, u32[]{:S(2)}, u32[]{:S(2)}) collective-permute-start(bf16[8,64,128]{2,1,0:T(8,128)(2,1)S(1)} %get-tuple-element.73), channel_id=1, source_target_pairs={{0,20},{4,16},{8,28},{12,24},{16,4},{20,0},{24,12},{28,8},{1,21},{... | collective-permute-start | bytes 393224 | tf_op jit(solution)/shard_map/ppermute | solution.py:78
  106.5 4.5 %collective-permute-done.27.refs_12_.refs_4_ = bf16[8,64,128]{2,1,0:T(8,128)(2,1)S(1)} collective-permute-done((bf16[8,64,128]{2,1,0:T(8,128)(2,1)S(1)}, bf16[8,64,128]{2,1,0:T(8,128)(2,1)S(1)}, u32[]{:S(2)}, u32[]{:S(2)}) %collective-permute-start.27) | collective-permute-done | bytes 131104 | tf_op jit(solution)/shard_map/ppermute | solution.py:78
  112.8 2.1 collective-permute-done.29.refs_14_.refs_6_
  114.9 3.4 %collective-permute-start.22 = (bf16[8,64,128]{2,1,0:T(8,128)(2,1)S(1)}, bf16[8,64,128]{2,1,0:T(8,128)(2,1)S(1)}, u32[]{:S(2)}, u32[]{:S(2)}) collective-permute-start(bf16[8,64,128]{2,1,0:T(8,128)(2,1)S(1)} %get-tuple-element.77), channel_id=1, source_target_pairs={{0,28},{4,24},{8,20},{12,16},{16,12},{20,8},{24,4},{28,0},{1,29},{... | collective-permute-start | bytes 393224 | tf_op jit(solution)/shard_map/ppermute | solution.py:78
  118.3 3.1 %directions.3 = (bf16[8,32,256]{2,1,0:T(8,128)(2,1)S(1)}, bf16[8,32,256]{2,1,0:T(8,128)(2,1)S(1)}, bf16[8,32,256]{2,1,0:T(8,128)(2,1)S(1)}, bf16[8,32,256]{2,1,0...) custom-call(s32[128]{0:T(128)S(1)} %bitcast.10, ...), custom_call_target="tpu_custom_call" | custom-call | flops 536870912 | bytes 8388608 | tf_op jit(solution)/shard_map/directions/pallas_call | solution.py:268
  121.5 3.4 %collective-permute-start.37 = (bf16[8,32,256]{2,1,0:T(8,128)(2,1)S(1)}, bf16[8,32,256]{2,1,0:T(8,128)(2,1)S(1)}, u32[]{:S(2)}, u32[]{:S(2)}) collective-permute-start(bf16[8,32,256]{2,1,0:T(8,128)(2,1)S(1)} %get-tuple-element.98), channel_id=1, source_target_pairs={{0,16},{4,20},{8,24},{12,28},{16,0},{20,4},{24,8},{28,12},{1,17},{... | collective-permute-start | bytes 393224 | tf_op jit(solution)/shard_map/ppermute | solution.py:78
  126.3 4.7 %collective-permute-start.40 = (bf16[8,32,256]{2,1,0:T(8,128)(2,1)S(1)}, bf16[8,32,256]{2,1,0:T(8,128)(2,1)S(1)}, u32[]{:S(2)}, u32[]{:S(2)}) collective-permute-start(bf16[8,32,256]{2,1,0:T(8,128)(2,1)S(1)} %get-tuple-element.101), channel_id=1, source_target_pairs={{0,8},{4,12},{8,0},{12,4},{16,24},{20,28},{24,16},{28,20},{1,9},{5... | collective-permute-start | bytes 393224 | tf_op jit(solution)/shard_map/ppermute | solution.py:78
  131.0 3.0 %collective-permute-done.22.refs_6_ = bf16[8,64,128]{2,1,0:T(8,128)(2,1)S(1)} collective-permute-done((bf16[8,64,128]{2,1,0:T(8,128)(2,1)S(1)}, bf16[8,64,128]{2,1,0:T(8,128)(2,1)S(1)}, u32[]{:S(2)}, u32[]{:S(2)}) %collective-permute-start.22) | collective-permute-done | bytes 131104 | tf_op jit(solution)/shard_map/ppermute | solution.py:78
  134.0 3.1 %directions.2 = (bf16[8,32,256]{2,1,0:T(8,128)(2,1)S(1)}, bf16[8,32,256]{2,1,0:T(8,128)(2,1)S(1)}, bf16[8,32,256]{2,1,0:T(8,128)(2,1)S(1)}, bf16[8,32,256]{2,1,0...) custom-call(s32[128]{0:T(128)S(1)} %bitcast.11, ...), custom_call_target="tpu_custom_call" | custom-call | flops 536870912 | bytes 8388608 | tf_op jit(solution)/shard_map/directions/pallas_call | solution.py:268
  137.2 4.0 %collective-permute-start.42 = (bf16[8,32,256]{2,1,0:T(8,128)(2,1)S(1)}, bf16[8,32,256]{2,1,0:T(8,128)(2,1)S(1)}, u32[]{:S(2)}, u32[]{:S(2)}) collective-permute-start(bf16[8,32,256]{2,1,0:T(8,128)(2,1)S(1)} %get-tuple-element.103), channel_id=1, source_target_pairs={{0,12},{4,8},{8,4},{12,0},{16,28},{20,24},{24,20},{28,16},{1,13},{... | collective-permute-start | bytes 393224 | tf_op jit(solution)/shard_map/ppermute | solution.py:78
  141.2 3.4 %collective-permute-start.30 = (bf16[8,32,256]{2,1,0:T(8,128)(2,1)S(1)}, bf16[8,32,256]{2,1,0:T(8,128)(2,1)S(1)}, u32[]{:S(2)}, u32[]{:S(2)}) collective-permute-start(bf16[8,32,256]{2,1,0:T(8,128)(2,1)S(1)} %get-tuple-element.90), channel_id=1, source_target_pairs={{0,16},{4,20},{8,24},{12,28},{16,0},{20,4},{24,8},{28,12},{1,17},{... | collective-permute-start | bytes 393224 | tf_op jit(solution)/shard_map/ppermute | solution.py:78
  145.4 5.2 %collective-permute-done.41.refs_12_ = bf16[8,32,256]{2,1,0:T(8,128)(2,1)S(1)} collective-permute-done((bf16[8,32,256]{2,1,0:T(8,128)(2,1)S(1)}, bf16[8,32,256]{2,1,0:T(8,128)(2,1)S(1)}, u32[]{:S(2)}, u32[]{:S(2)}) %collective-permute-start.41) | collective-permute-done | bytes 131104 | tf_op jit(solution)/shard_map/ppermute | solution.py:78
  150.6 3.0 %collective-permute-start.33 = (bf16[8,32,256]{2,1,0:T(8,128)(2,1)S(1)}, bf16[8,32,256]{2,1,0:T(8,128)(2,1)S(1)}, u32[]{:S(2)}, u32[]{:S(2)}) collective-permute-start(bf16[8,32,256]{2,1,0:T(8,128)(2,1)S(1)} %get-tuple-element.93), channel_id=1, source_target_pairs={{0,8},{4,12},{8,0},{12,4},{16,24},{20,28},{24,16},{28,20},{1,9},{5... | collective-permute-start | bytes 393224 | tf_op jit(solution)/shard_map/ppermute | solution.py:78
  153.6 1.6 collective-permute-done.43.refs_14_
  155.8 1.5 collective-permute-done.30.refs_0_
  157.3 6.3 %collective-permute-start.35 = (bf16[8,32,256]{2,1,0:T(8,128)(2,1)S(1)}, bf16[8,32,256]{2,1,0:T(8,128)(2,1)S(1)}, u32[]{:S(2)}, u32[]{:S(2)}) collective-permute-start(bf16[8,32,256]{2,1,0:T(8,128)(2,1)S(1)} %get-tuple-element.95), channel_id=1, source_target_pairs={{0,12},{4,8},{8,4},{12,0},{16,28},{20,24},{24,20},{28,16},{1,13},{... | collective-permute-start | bytes 393224 | tf_op jit(solution)/shard_map/ppermute | solution.py:78
  163.7 6.5 %collective-permute-done.34.refs_4_ = bf16[8,32,256]{2,1,0:T(8,128)(2,1)S(1)} collective-permute-done((bf16[8,32,256]{2,1,0:T(8,128)(2,1)S(1)}, bf16[8,32,256]{2,1,0:T(8,128)(2,1)S(1)}, u32[]{:S(2)}, u32[]{:S(2)}) %collective-permute-start.34) | collective-permute-done | bytes 131104 | tf_op jit(solution)/shard_map/ppermute | solution.py:78
  170.2 3.0 %collective-permute-done.36.refs_6_ = bf16[8,32,256]{2,1,0:T(8,128)(2,1)S(1)} collective-permute-done((bf16[8,32,256]{2,1,0:T(8,128)(2,1)S(1)}, bf16[8,32,256]{2,1,0:T(8,128)(2,1)S(1)}, u32[]{:S(2)}, u32[]{:S(2)}) %collective-permute-start.36) | collective-permute-done | bytes 131104 | tf_op jit(solution)/shard_map/ppermute | solution.py:78
  173.2 1.5 regroup.1
  174.8 2.8 %collective-permute-start.46 = (bf16[32,8192]{1,0:T(8,128)(2,1)S(1)}, bf16[32,8192]{1,0:T(8,128)(2,1)S(1)}, u32[]{:S(2)}, u32[]{:S(2)}) collective-permute-start(bf16[32,8192]{1,0:T(8,128)(2,1)S(1)} %get-tuple-element.108), channel_id=1, source_target_pairs={{0,8},{4,12},{8,0},{12,4},{16,24},{20,28},{24,16},{28,20},{1,9},{5... | collective-permute-start | bytes 1572872 | tf_op jit(solution)/shard_map/ppermute | solution.py:78
  178.2 10.3 %statistics.1 = (f32[1,16,256,256]{3,2,1,0:T(8,128)}, f32[1,16,256,256]{3,2,1,0:T(8,128)}, f32[1,16,256,256]{3,2,1,0:T(8,128)}) custom-call(s32[128]{0:T(128)S(1)} %bitcast.13, f32[1,16,256,256]{3,2,1,0:T(8,128)S(1)} %copy-done.3, f32[1,16,256,256]{3,2,1,0:T(8,128)S(1)} %copy-done.4, f32[1,16,256,256]{3,2,1,0:T(8,128)S(1)} %copy-done, ...), custom_call_target="tpu_custom_call" | custom-call | flops 1073741824 | bytes 27262976 | tf_op jit(solution)/shard_map/statistics/pallas_call | solution.py:326
  188.6 9.7 %collective-permute-done.45.refs_0_ = bf16[32,8192]{1,0:T(8,128)(2,1)S(1)} collective-permute-done((bf16[32,8192]{1,0:T(8,128)(2,1)S(1)}, bf16[32,8192]{1,0:T(8,128)(2,1)S(1)}, u32[]{:S(2)}, u32[]{:S(2)}) %collective-permute-start.45) | collective-permute-done | bytes 524320 | tf_op jit(solution)/shard_map/ppermute | solution.py:78
  198.3 3.3 %collective-permute-done.46.refs_1_ = bf16[32,8192]{1,0:T(8,128)(2,1)S(1)} collective-permute-done((bf16[32,8192]{1,0:T(8,128)(2,1)S(1)}, bf16[32,8192]{1,0:T(8,128)(2,1)S(1)}, u32[]{:S(2)}, u32[]{:S(2)}) %collective-permute-start.46) | collective-permute-done | bytes 524320 | tf_op jit(solution)/shard_map/ppermute | solution.py:78
  201.6 1.7 stack_rows.2.refs_1_
  203.3 18.6 %collective-permute-done.44.refs_0_ = bf16[32,8192]{1,0:T(8,128)(2,1)S(1)} collective-permute-done((bf16[32,8192]{1,0:T(8,128)(2,1)S(1)}, bf16[32,8192]{1,0:T(8,128)(2,1)S(1)}, u32[]{:S(2)}, u32[]{:S(2)}) %collective-permute-start.44) | collective-permute-done | bytes 524320 | tf_op jit(solution)/shard_map/ppermute | solution.py:78
  (75 shorter events, 17.6 us)
Async XLA Ops:
  1.9 71.3 %copy-start.7 = (s32[1,128]{1,0:T(1,128)S(1)}, s32[1,128]{1,0:T(1,128)}, u32[]{:S(2)}) copy-start(s32[1,128]{1,0:T(1,128)} %param.10) | copy-start | bytes 1540
  2.9 10.8 %collective-permute-start = (bf16[8,64,256]{2,1,0:T(8,128)(2,1)S(1)}, bf16[8,64,256]{2,1,0:T(8,128)(2,1)S(1)}, u32[]{:S(2)}, u32[]{:S(2)}) collective-permute-start(bf16[8,64,256]{2,1,0:T(8,128)(2,1)S(1)} %get-tuple-element.60), channel_id=1, source_target_pairs={{0,8},{4,12},{8,0},{12,4},{16,24},{20,28},{24,16},{28,20},{1,9},{5... | collective-permute-start | bytes 786440 | tf_op jit(solution)/shard_map/ppermute | solution.py:78
  3.0 21.0 %collective-permute-start.1 = (bf16[8,64,256]{2,1,0:T(8,128)(2,1)S(1)}, bf16[8,64,256]{2,1,0:T(8,128)(2,1)S(1)}, u32[]{:S(2)}, u32[]{:S(2)}) collective-permute-start(bf16[8,64,256]{2,1,0:T(8,128)(2,1)S(1)} %get-tuple-element.61), channel_id=1, source_target_pairs={{0,16},{4,20},{8,24},{12,28},{16,0},{20,4},{24,8},{28,12},{1,17},{... | collective-permute-start | bytes 786440 | tf_op jit(solution)/shard_map/ppermute | solution.py:78
  6.0 23.1 %collective-permute-start.2 = (bf16[8,64,256]{2,1,0:T(8,128)(2,1)S(1)}, bf16[8,64,256]{2,1,0:T(8,128)(2,1)S(1)}, u32[]{:S(2)}, u32[]{:S(2)}) collective-permute-start(bf16[8,64,256]{2,1,0:T(8,128)(2,1)S(1)} %get-tuple-element.62), channel_id=1, source_target_pairs={{0,24},{4,28},{8,16},{12,20},{16,8},{20,12},{24,0},{28,4},{1,25},{... | collective-permute-start | bytes 786440 | tf_op jit(solution)/shard_map/ppermute | solution.py:78
  7.6 21.5 %collective-permute-start.3 = (bf16[256,512]{1,0:T(8,128)(2,1)S(1)}, bf16[256,512]{1,0:T(8,128)(2,1)S(1)}, u32[]{:S(2)}, u32[]{:S(2)}) collective-permute-start(bf16[256,512]{1,0:T(8,128)(2,1)S(1)} %get-tuple-element.63), channel_id=1, source_target_pairs={{0,4},{4,0},{8,12},{12,8},{16,20},{20,16},{24,28},{28,24},{1,5},{5... | collective-permute-start | bytes 786440 | tf_op jit(solution)/shard_map/ppermute | solution.py:78
  29.2 23.8 %collective-permute-start.7 = (bf16[4,512,256]{2,1,0:T(8,128)(2,1)S(1)}, bf16[4,512,256]{2,1,0:T(8,128)(2,1)S(1)}, u32[]{:S(2)}, u32[]{:S(2)}) collective-permute-start(bf16[4,512,256]{2,1,0:T(8,128)(2,1)S(1)} %pad_maximum_fusion.refs_4_), channel_id=1, source_target_pairs={{0,4},{4,0},{8,12},{12,8},{16,20},{20,16},{24,28},{28,24},{1,5},{5... | collective-permute-start | bytes 3145736 | tf_op jit(solution)/shard_map/ppermute | solution.py:78
  30.8 27.5 %collective-permute-start.10 = (bf16[4,512,256]{2,1,0:T(8,128)(2,1)S(1)}, bf16[4,512,256]{2,1,0:T(8,128)(2,1)S(1)}, u32[]{:S(2)}, u32[]{:S(2)}) collective-permute-start(bf16[4,512,256]{2,1,0:T(8,128)(2,1)S(1)} %pad_maximum_fusion.refs_4_), channel_id=1, source_target_pairs={{0,2},{1,3},{2,0},{3,1},{4,6},{5,7},{6,4},{7,5},{8,10},{9,11},{10,... | collective-permute-start | bytes 3145736 | tf_op jit(solution)/shard_map/ppermute | solution.py:78
  32.4 20.9 %collective-permute-start.5 = (bf16[2,256,512]{2,1,0:T(8,128)(2,1)S(1)}, bf16[2,256,512]{2,1,0:T(8,128)(2,1)S(1)}, u32[]{:S(2)}, u32[]{:S(2)}) collective-permute-start(bf16[2,256,512]{2,1,0:T(8,128)(2,1)S(1)} %pad_maximum_fusion.1.refs_1_), channel_id=1, source_target_pairs={{0,8},{4,12},{8,0},{12,4},{16,24},{20,28},{24,16},{28,20},{1,9},{5... | collective-permute-start | bytes 1572872 | tf_op jit(solution)/shard_map/ppermute | solution.py:78
  32.4 24.3 %collective-permute-start.4 = (bf16[2,256,512]{2,1,0:T(8,128)(2,1)S(1)}, bf16[2,256,512]{2,1,0:T(8,128)(2,1)S(1)}, u32[]{:S(2)}, u32[]{:S(2)}) collective-permute-start(bf16[2,256,512]{2,1,0:T(8,128)(2,1)S(1)} %pad_maximum_fusion.1.refs_1_), channel_id=1, source_target_pairs={{0,16},{4,20},{8,24},{12,28},{16,0},{20,4},{24,8},{28,12},{1,17},{... | collective-permute-start | bytes 1572872 | tf_op jit(solution)/shard_map/ppermute | solution.py:78
  53.3 12.2 %collective-permute-start.11 = (bf16[2,512,256]{2,1,0:T(8,128)(2,1)S(1)}, bf16[2,512,256]{2,1,0:T(8,128)(2,1)S(1)}, u32[]{:S(2)}, u32[]{:S(2)}) collective-permute-start(bf16[2,512,256]{2,1,0:T(8,128)(2,1)S(1)} %slice.8), channel_id=1, source_target_pairs={{0,2},{1,3},{2,0},{3,1},{4,6},{5,7},{6,4},{7,5},{8,10},{9,11},{10,... | collective-permute-start | bytes 1572872 | tf_op jit(solution)/shard_map/ppermute | solution.py:78
  54.7 16.3 %collective-permute-start.8 = (bf16[4,512,256]{2,1,0:T(8,128)(2,1)S(1)}, bf16[4,512,256]{2,1,0:T(8,128)(2,1)S(1)}, u32[]{:S(2)}, u32[]{:S(2)}) collective-permute-start(bf16[4,512,256]{2,1,0:T(8,128)(2,1)S(1)} %pad_maximum_fusion.refs_4_), channel_id=1, source_target_pairs={{0,1},{1,0},{2,3},{3,2},{4,5},{5,4},{6,7},{7,6},{8,9},{9,8},{10,11... | collective-permute-start | bytes 3145736 | tf_op jit(solution)/shard_map/ppermute | solution.py:78
  56.7 13.8 %collective-permute-start.6 = (bf16[2,256,512]{2,1,0:T(8,128)(2,1)S(1)}, bf16[2,256,512]{2,1,0:T(8,128)(2,1)S(1)}, u32[]{:S(2)}, u32[]{:S(2)}) collective-permute-start(bf16[2,256,512]{2,1,0:T(8,128)(2,1)S(1)} %collective-permute-done.4.refs_0_), channel_id=1, source_target_pairs={{0,8},{4,12},{8,0},{12,4},{16,24},{20,28},{24,16},{28,20},{1,9},{5... | collective-permute-start | bytes 1572872 | tf_op jit(solution)/shard_map/ppermute | solution.py:78
  58.4 12.1 %collective-permute-start.12 = (bf16[2,512,256]{2,1,0:T(8,128)(2,1)S(1)}, bf16[2,512,256]{2,1,0:T(8,128)(2,1)S(1)}, u32[]{:S(2)}, u32[]{:S(2)}) collective-permute-start(bf16[2,512,256]{2,1,0:T(8,128)(2,1)S(1)} %slice.9), channel_id=1, source_target_pairs={{0,4},{4,0},{8,12},{12,8},{16,20},{20,16},{24,28},{28,24},{1,5},{5... | collective-permute-start | bytes 1572872 | tf_op jit(solution)/shard_map/ppermute | solution.py:78
  58.9 12.1 %collective-permute-start.9 = (bf16[4,512,256]{2,1,0:T(8,128)(2,1)S(1)}, bf16[4,512,256]{2,1,0:T(8,128)(2,1)S(1)}, u32[]{:S(2)}, u32[]{:S(2)}) collective-permute-start(bf16[4,512,256]{2,1,0:T(8,128)(2,1)S(1)} %collective-permute-done.7.refs_5_), channel_id=1, source_target_pairs={{0,1},{1,0},{2,3},{3,2},{4,5},{5,4},{6,7},{7,6},{8,9},{9,8},{10,11... | collective-permute-start | bytes 3145736 | tf_op jit(solution)/shard_map/ppermute | solution.py:78
  65.5 7.6 %collective-permute-start.13 = (bf16[4,512,256]{2,1,0:T(8,128)(2,1)S(1)}, bf16[4,512,256]{2,1,0:T(8,128)(2,1)S(1)}, u32[]{:S(2)}, u32[]{:S(2)}) collective-permute-start(bf16[4,512,256]{2,1,0:T(8,128)(2,1)S(1)} %collective-permute-done.10.refs_8_), channel_id=1, source_target_pairs={{0,1},{1,0},{2,3},{3,2},{4,5},{5,4},{6,7},{7,6},{8,9},{9,8},{10,11... | collective-permute-start | bytes 3145736 | tf_op jit(solution)/shard_map/ppermute | solution.py:78
  70.5 1.9 collective-permute-start.15
  70.5 2.7 %collective-permute-start.14 = (bf16[2,512,256]{2,1,0:T(8,128)(2,1)S(1)}, bf16[2,512,256]{2,1,0:T(8,128)(2,1)S(1)}, u32[]{:S(2)}, u32[]{:S(2)}) collective-permute-start(bf16[2,512,256]{2,1,0:T(8,128)(2,1)S(1)} %collective-permute-done.11.refs_9_), channel_id=1, source_target_pairs={{0,1},{1,0},{2,3},{3,2},{4,5},{5,4},{6,7},{7,6},{8,9},{9,8},{10,11... | collective-permute-start | bytes 1572872 | tf_op jit(solution)/shard_map/ppermute | solution.py:78
  79.6 13.0 %collective-permute-start.16 = (bf16[8,64,128]{2,1,0:T(8,128)(2,1)S(1)}, bf16[8,64,128]{2,1,0:T(8,128)(2,1)S(1)}, u32[]{:S(2)}, u32[]{:S(2)}) collective-permute-start(bf16[8,64,128]{2,1,0:T(8,128)(2,1)S(1)} %get-tuple-element.71), channel_id=1, source_target_pairs={{0,16},{4,20},{8,24},{12,28},{16,0},{20,4},{24,8},{28,12},{1,17},{... | collective-permute-start | bytes 393224 | tf_op jit(solution)/shard_map/ppermute | solution.py:78
  81.1 14.7 %collective-permute-start.17 = (bf16[8,64,128]{2,1,0:T(8,128)(2,1)S(1)}, bf16[8,64,128]{2,1,0:T(8,128)(2,1)S(1)}, u32[]{:S(2)}, u32[]{:S(2)}) collective-permute-start(bf16[8,64,128]{2,1,0:T(8,128)(2,1)S(1)} %get-tuple-element.72), channel_id=1, source_target_pairs={{0,4},{4,0},{8,12},{12,8},{16,20},{20,16},{24,28},{28,24},{1,5},{5... | collective-permute-start | bytes 393224 | tf_op jit(solution)/shard_map/ppermute | solution.py:78
  82.6 14.0 %collective-permute-start.23 = (bf16[8,64,128]{2,1,0:T(8,128)(2,1)S(1)}, bf16[8,64,128]{2,1,0:T(8,128)(2,1)S(1)}, u32[]{:S(2)}, u32[]{:S(2)}) collective-permute-start(bf16[8,64,128]{2,1,0:T(8,128)(2,1)S(1)} %get-tuple-element.79), channel_id=1, source_target_pairs={{0,16},{4,20},{8,24},{12,28},{16,0},{20,4},{24,8},{28,12},{1,17},{... | collective-permute-start | bytes 393224 | tf_op jit(solution)/shard_map/ppermute | solution.py:78
  83.1 15.8 %collective-permute-start.24 = (bf16[8,64,128]{2,1,0:T(8,128)(2,1)S(1)}, bf16[8,64,128]{2,1,0:T(8,128)(2,1)S(1)}, u32[]{:S(2)}, u32[]{:S(2)}) collective-permute-start(bf16[8,64,128]{2,1,0:T(8,128)(2,1)S(1)} %get-tuple-element.80), channel_id=1, source_target_pairs={{0,4},{4,0},{8,12},{12,8},{16,20},{20,16},{24,28},{28,24},{1,5},{5... | collective-permute-start | bytes 393224 | tf_op jit(solution)/shard_map/ppermute | solution.py:78
  84.7 16.0 %collective-permute-start.25 = (bf16[8,64,128]{2,1,0:T(8,128)(2,1)S(1)}, bf16[8,64,128]{2,1,0:T(8,128)(2,1)S(1)}, u32[]{:S(2)}, u32[]{:S(2)}) collective-permute-start(bf16[8,64,128]{2,1,0:T(8,128)(2,1)S(1)} %get-tuple-element.81), channel_id=1, source_target_pairs={{0,20},{4,16},{8,28},{12,24},{16,4},{20,0},{24,12},{28,8},{1,21},{... | collective-permute-start | bytes 393224 | tf_op jit(solution)/shard_map/ppermute | solution.py:78
  92.6 12.6 %collective-permute-start.26 = (bf16[8,64,128]{2,1,0:T(8,128)(2,1)S(1)}, bf16[8,64,128]{2,1,0:T(8,128)(2,1)S(1)}, u32[]{:S(2)}, u32[]{:S(2)}) collective-permute-start(bf16[8,64,128]{2,1,0:T(8,128)(2,1)S(1)} %get-tuple-element.82), channel_id=1, source_target_pairs={{0,8},{4,12},{8,0},{12,4},{16,24},{20,28},{24,16},{28,20},{1,9},{5... | collective-permute-start | bytes 393224 | tf_op jit(solution)/shard_map/ppermute | solution.py:78
  95.8 15.2 %collective-permute-start.27 = (bf16[8,64,128]{2,1,0:T(8,128)(2,1)S(1)}, bf16[8,64,128]{2,1,0:T(8,128)(2,1)S(1)}, u32[]{:S(2)}, u32[]{:S(2)}) collective-permute-start(bf16[8,64,128]{2,1,0:T(8,128)(2,1)S(1)} %get-tuple-element.83), channel_id=1, source_target_pairs={{0,24},{4,28},{8,16},{12,20},{16,8},{20,12},{24,0},{28,4},{1,25},{... | collective-permute-start | bytes 393224 | tf_op jit(solution)/shard_map/ppermute | solution.py:78
  96.6 15.2 %collective-permute-start.28 = (bf16[8,64,128]{2,1,0:T(8,128)(2,1)S(1)}, bf16[8,64,128]{2,1,0:T(8,128)(2,1)S(1)}, u32[]{:S(2)}, u32[]{:S(2)}) collective-permute-start(bf16[8,64,128]{2,1,0:T(8,128)(2,1)S(1)} %get-tuple-element.84), channel_id=1, source_target_pairs={{0,12},{4,8},{8,4},{12,0},{16,28},{20,24},{24,20},{28,16},{1,13},{... | collective-permute-start | bytes 393224 | tf_op jit(solution)/shard_map/ppermute | solution.py:78
  98.9 15.9 %collective-permute-start.29 = (bf16[8,64,128]{2,1,0:T(8,128)(2,1)S(1)}, bf16[8,64,128]{2,1,0:T(8,128)(2,1)S(1)}, u32[]{:S(2)}, u32[]{:S(2)}) collective-permute-start(bf16[8,64,128]{2,1,0:T(8,128)(2,1)S(1)} %get-tuple-element.85), channel_id=1, source_target_pairs={{0,28},{4,24},{8,20},{12,16},{16,12},{20,8},{24,4},{28,0},{1,29},{... | collective-permute-start | bytes 393224 | tf_op jit(solution)/shard_map/ppermute | solution.py:78
  100.7 20.8 %collective-permute-start.18 = (bf16[8,64,128]{2,1,0:T(8,128)(2,1)S(1)}, bf16[8,64,128]{2,1,0:T(8,128)(2,1)S(1)}, u32[]{:S(2)}, u32[]{:S(2)}) collective-permute-start(bf16[8,64,128]{2,1,0:T(8,128)(2,1)S(1)} %get-tuple-element.73), channel_id=1, source_target_pairs={{0,20},{4,16},{8,28},{12,24},{16,4},{20,0},{24,12},{28,8},{1,21},{... | collective-permute-start | bytes 393224 | tf_op jit(solution)/shard_map/ppermute | solution.py:78
  105.2 19.6 %collective-permute-start.19 = (bf16[8,64,128]{2,1,0:T(8,128)(2,1)S(1)}, bf16[8,64,128]{2,1,0:T(8,128)(2,1)S(1)}, u32[]{:S(2)}, u32[]{:S(2)}) collective-permute-start(bf16[8,64,128]{2,1,0:T(8,128)(2,1)S(1)} %get-tuple-element.74), channel_id=1, source_target_pairs={{0,8},{4,12},{8,0},{12,4},{16,24},{20,28},{24,16},{28,20},{1,9},{5... | collective-permute-start | bytes 393224 | tf_op jit(solution)/shard_map/ppermute | solution.py:78
  110.9 14.7 %collective-permute-start.20 = (bf16[8,64,128]{2,1,0:T(8,128)(2,1)S(1)}, bf16[8,64,128]{2,1,0:T(8,128)(2,1)S(1)}, u32[]{:S(2)}, u32[]{:S(2)}) collective-permute-start(bf16[8,64,128]{2,1,0:T(8,128)(2,1)S(1)} %get-tuple-element.75), channel_id=1, source_target_pairs={{0,24},{4,28},{8,16},{12,20},{16,8},{20,12},{24,0},{28,4},{1,25},{... | collective-permute-start | bytes 393224 | tf_op jit(solution)/shard_map/ppermute | solution.py:78
  111.8 14.5 %collective-permute-start.21 = (bf16[8,64,128]{2,1,0:T(8,128)(2,1)S(1)}, bf16[8,64,128]{2,1,0:T(8,128)(2,1)S(1)}, u32[]{:S(2)}, u32[]{:S(2)}) collective-permute-start(bf16[8,64,128]{2,1,0:T(8,128)(2,1)S(1)} %get-tuple-element.76), channel_id=1, source_target_pairs={{0,12},{4,8},{8,4},{12,0},{16,28},{20,24},{24,20},{28,16},{1,13},{... | collective-permute-start | bytes 393224 | tf_op jit(solution)/shard_map/ppermute | solution.py:78
  114.9 19.2 %collective-permute-start.22 = (bf16[8,64,128]{2,1,0:T(8,128)(2,1)S(1)}, bf16[8,64,128]{2,1,0:T(8,128)(2,1)S(1)}, u32[]{:S(2)}, u32[]{:S(2)}) collective-permute-start(bf16[8,64,128]{2,1,0:T(8,128)(2,1)S(1)} %get-tuple-element.77), channel_id=1, source_target_pairs={{0,28},{4,24},{8,20},{12,16},{16,12},{20,8},{24,4},{28,0},{1,29},{... | collective-permute-start | bytes 393224 | tf_op jit(solution)/shard_map/ppermute | solution.py:78
  121.5 15.7 %collective-permute-start.37 = (bf16[8,32,256]{2,1,0:T(8,128)(2,1)S(1)}, bf16[8,32,256]{2,1,0:T(8,128)(2,1)S(1)}, u32[]{:S(2)}, u32[]{:S(2)}) collective-permute-start(bf16[8,32,256]{2,1,0:T(8,128)(2,1)S(1)} %get-tuple-element.98), channel_id=1, source_target_pairs={{0,16},{4,20},{8,24},{12,28},{16,0},{20,4},{24,8},{28,12},{1,17},{... | collective-permute-start | bytes 393224 | tf_op jit(solution)/shard_map/ppermute | solution.py:78
  124.8 16.4 %collective-permute-start.38 = (bf16[8,32,256]{2,1,0:T(8,128)(2,1)S(1)}, bf16[8,32,256]{2,1,0:T(8,128)(2,1)S(1)}, u32[]{:S(2)}, u32[]{:S(2)}) collective-permute-start(bf16[8,32,256]{2,1,0:T(8,128)(2,1)S(1)} %get-tuple-element.99), channel_id=1, source_target_pairs={{0,4},{4,0},{8,12},{12,8},{16,20},{20,16},{24,28},{28,24},{1,5},{5... | collective-permute-start | bytes 393224 | tf_op jit(solution)/shard_map/ppermute | solution.py:78
  125.6 15.6 %collective-permute-start.39 = (bf16[8,32,256]{2,1,0:T(8,128)(2,1)S(1)}, bf16[8,32,256]{2,1,0:T(8,128)(2,1)S(1)}, u32[]{:S(2)}, u32[]{:S(2)}) collective-permute-start(bf16[8,32,256]{2,1,0:T(8,128)(2,1)S(1)} %get-tuple-element.100), channel_id=1, source_target_pairs={{0,20},{4,16},{8,28},{12,24},{16,4},{20,0},{24,12},{28,8},{1,21},{... | collective-permute-start | bytes 393224 | tf_op jit(solution)/shard_map/ppermute | solution.py:78
  126.3 18.3 %collective-permute-start.40 = (bf16[8,32,256]{2,1,0:T(8,128)(2,1)S(1)}, bf16[8,32,256]{2,1,0:T(8,128)(2,1)S(1)}, u32[]{:S(2)}, u32[]{:S(2)}) collective-permute-start(bf16[8,32,256]{2,1,0:T(8,128)(2,1)S(1)} %get-tuple-element.101), channel_id=1, source_target_pairs={{0,8},{4,12},{8,0},{12,4},{16,24},{20,28},{24,16},{28,20},{1,9},{5... | collective-permute-start | bytes 393224 | tf_op jit(solution)/shard_map/ppermute | solution.py:78
  134.0 16.6 %collective-permute-start.41 = (bf16[8,32,256]{2,1,0:T(8,128)(2,1)S(1)}, bf16[8,32,256]{2,1,0:T(8,128)(2,1)S(1)}, u32[]{:S(2)}, u32[]{:S(2)}) collective-permute-start(bf16[8,32,256]{2,1,0:T(8,128)(2,1)S(1)} %get-tuple-element.102), channel_id=1, source_target_pairs={{0,24},{4,28},{8,16},{12,20},{16,8},{20,12},{24,0},{28,4},{1,25},{... | collective-permute-start | bytes 393224 | tf_op jit(solution)/shard_map/ppermute | solution.py:78
  137.2 13.4 %collective-permute-start.42 = (bf16[8,32,256]{2,1,0:T(8,128)(2,1)S(1)}, bf16[8,32,256]{2,1,0:T(8,128)(2,1)S(1)}, u32[]{:S(2)}, u32[]{:S(2)}) collective-permute-start(bf16[8,32,256]{2,1,0:T(8,128)(2,1)S(1)} %get-tuple-element.103), channel_id=1, source_target_pairs={{0,12},{4,8},{8,4},{12,0},{16,28},{20,24},{24,20},{28,16},{1,13},{... | collective-permute-start | bytes 393224 | tf_op jit(solution)/shard_map/ppermute | solution.py:78
  141.2 13.9 %collective-permute-start.43 = (bf16[8,32,256]{2,1,0:T(8,128)(2,1)S(1)}, bf16[8,32,256]{2,1,0:T(8,128)(2,1)S(1)}, u32[]{:S(2)}, u32[]{:S(2)}) collective-permute-start(bf16[8,32,256]{2,1,0:T(8,128)(2,1)S(1)} %get-tuple-element.104), channel_id=1, source_target_pairs={{0,28},{4,24},{8,20},{12,16},{16,12},{20,8},{24,4},{28,0},{1,29},{... | collective-permute-start | bytes 393224 | tf_op jit(solution)/shard_map/ppermute | solution.py:78
  141.2 16.1 %collective-permute-start.30 = (bf16[8,32,256]{2,1,0:T(8,128)(2,1)S(1)}, bf16[8,32,256]{2,1,0:T(8,128)(2,1)S(1)}, u32[]{:S(2)}, u32[]{:S(2)}) collective-permute-start(bf16[8,32,256]{2,1,0:T(8,128)(2,1)S(1)} %get-tuple-element.90), channel_id=1, source_target_pairs={{0,16},{4,20},{8,24},{12,28},{16,0},{20,4},{24,8},{28,12},{1,17},{... | collective-permute-start | bytes 393224 | tf_op jit(solution)/shard_map/ppermute | solution.py:78
  144.6 19.1 %collective-permute-start.31 = (bf16[8,32,256]{2,1,0:T(8,128)(2,1)S(1)}, bf16[8,32,256]{2,1,0:T(8,128)(2,1)S(1)}, u32[]{:S(2)}, u32[]{:S(2)}) collective-permute-start(bf16[8,32,256]{2,1,0:T(8,128)(2,1)S(1)} %get-tuple-element.91), channel_id=1, source_target_pairs={{0,4},{4,0},{8,12},{12,8},{16,20},{20,16},{24,28},{28,24},{1,5},{5... | collective-permute-start | bytes 393224 | tf_op jit(solution)/shard_map/ppermute | solution.py:78
  150.6 13.1 %collective-permute-start.32 = (bf16[8,32,256]{2,1,0:T(8,128)(2,1)S(1)}, bf16[8,32,256]{2,1,0:T(8,128)(2,1)S(1)}, u32[]{:S(2)}, u32[]{:S(2)}) collective-permute-start(bf16[8,32,256]{2,1,0:T(8,128)(2,1)S(1)} %get-tuple-element.92), channel_id=1, source_target_pairs={{0,20},{4,16},{8,28},{12,24},{16,4},{20,0},{24,12},{28,8},{1,21},{... | collective-permute-start | bytes 393224 | tf_op jit(solution)/shard_map/ppermute | solution.py:78
  150.6 13.1 %collective-permute-start.33 = (bf16[8,32,256]{2,1,0:T(8,128)(2,1)S(1)}, bf16[8,32,256]{2,1,0:T(8,128)(2,1)S(1)}, u32[]{:S(2)}, u32[]{:S(2)}) collective-permute-start(bf16[8,32,256]{2,1,0:T(8,128)(2,1)S(1)} %get-tuple-element.93), channel_id=1, source_target_pairs={{0,8},{4,12},{8,0},{12,4},{16,24},{20,28},{24,16},{28,20},{1,9},{5... | collective-permute-start | bytes 393224 | tf_op jit(solution)/shard_map/ppermute | solution.py:78
  155.1 15.1 %collective-permute-start.34 = (bf16[8,32,256]{2,1,0:T(8,128)(2,1)S(1)}, bf16[8,32,256]{2,1,0:T(8,128)(2,1)S(1)}, u32[]{:S(2)}, u32[]{:S(2)}) collective-permute-start(bf16[8,32,256]{2,1,0:T(8,128)(2,1)S(1)} %get-tuple-element.94), channel_id=1, source_target_pairs={{0,24},{4,28},{8,16},{12,20},{16,8},{20,12},{24,0},{28,4},{1,25},{... | collective-permute-start | bytes 393224 | tf_op jit(solution)/shard_map/ppermute | solution.py:78
  157.3 12.9 %collective-permute-start.35 = (bf16[8,32,256]{2,1,0:T(8,128)(2,1)S(1)}, bf16[8,32,256]{2,1,0:T(8,128)(2,1)S(1)}, u32[]{:S(2)}, u32[]{:S(2)}) collective-permute-start(bf16[8,32,256]{2,1,0:T(8,128)(2,1)S(1)} %get-tuple-element.95), channel_id=1, source_target_pairs={{0,12},{4,8},{8,4},{12,0},{16,28},{20,24},{24,20},{28,16},{1,13},{... | collective-permute-start | bytes 393224 | tf_op jit(solution)/shard_map/ppermute | solution.py:78
  163.7 9.5 %collective-permute-start.36 = (bf16[8,32,256]{2,1,0:T(8,128)(2,1)S(1)}, bf16[8,32,256]{2,1,0:T(8,128)(2,1)S(1)}, u32[]{:S(2)}, u32[]{:S(2)}) collective-permute-start(bf16[8,32,256]{2,1,0:T(8,128)(2,1)S(1)} %get-tuple-element.96), channel_id=1, source_target_pairs={{0,28},{4,24},{8,20},{12,16},{16,12},{20,8},{24,4},{28,0},{1,29},{... | collective-permute-start | bytes 393224 | tf_op jit(solution)/shard_map/ppermute | solution.py:78
  174.7 23.6 %collective-permute-start.45 = (bf16[32,8192]{1,0:T(8,128)(2,1)S(1)}, bf16[32,8192]{1,0:T(8,128)(2,1)S(1)}, u32[]{:S(2)}, u32[]{:S(2)}) collective-permute-start(bf16[32,8192]{1,0:T(8,128)(2,1)S(1)} %get-tuple-element.107), channel_id=1, source_target_pairs={{0,16},{4,20},{8,24},{12,28},{16,0},{20,4},{24,8},{28,12},{1,17},{... | collective-permute-start | bytes 1572872 | tf_op jit(solution)/shard_map/ppermute | solution.py:78
  174.8 26.8 %collective-permute-start.46 = (bf16[32,8192]{1,0:T(8,128)(2,1)S(1)}, bf16[32,8192]{1,0:T(8,128)(2,1)S(1)}, u32[]{:S(2)}, u32[]{:S(2)}) collective-permute-start(bf16[32,8192]{1,0:T(8,128)(2,1)S(1)} %get-tuple-element.108), channel_id=1, source_target_pairs={{0,8},{4,12},{8,0},{12,4},{16,24},{20,28},{24,16},{28,20},{1,9},{5... | collective-permute-start | bytes 1572872 | tf_op jit(solution)/shard_map/ppermute | solution.py:78
  177.5 44.4 %collective-permute-start.44 = (bf16[32,8192]{1,0:T(8,128)(2,1)S(1)}, bf16[32,8192]{1,0:T(8,128)(2,1)S(1)}, u32[]{:S(2)}, u32[]{:S(2)}) collective-permute-start(bf16[32,8192]{1,0:T(8,128)(2,1)S(1)} %get-tuple-element.106), channel_id=1, source_target_pairs={{0,24},{4,28},{8,16},{12,20},{16,8},{20,12},{24,0},{28,4},{1,25},{... | collective-permute-start | bytes 1572872 | tf_op jit(solution)/shard_map/ppermute | solution.py:78
  (7 other events, 226.2 us)

commit v9 on v8

--- a/solution.py
+++ b/solution.py
@@ -93,9 +93,9 @@
     strip = turned.shape[0] // pairs
     pair = lax.div(lax.axis_index("fsdp"), 2)
     turned[...] = cot_ref[...].T
-    for k in range(pairs):
+    for k, out in zip(row_order(pairs), outs):
         start = pl.multiple_of((pair ^ k) * strip, strip)
-        outs[k][0] = turned[pl.ds(start, strip), :]
+        out[0] = turned[pl.ds(start, strip), :]
 
 
 def cot_strips(cotangent, pairs, block):
@@ -451,7 +451,7 @@
     strips = cot_strips(cotangent, pairs, block)
     context, _ = lax.optimization_barrier((context, strips[0]))
     own, other = column_halves(context, block)
-    strips = exchange(strips, range(0, groups, 2))
+    strips = exchange(strips, [2 * k for k in row_order(pairs)])[::-1]
     other = swap(other, "fsdp", 1)
     strips, other = lax.optimization_barrier((strips, other))
     strips = jnp.stack(strips).reshape(pairs, -1, tokens)

time: 224 us -> 224 us (level)
  no operation moved by 1% of the time
where the time goes in v9:
time: 224 us; the launch traced here: 223 us
  waiting for transfers between devices  118 us (53%)
  starting transfers between devices  72.9 us (33%)
  Pallas kernels  28.7 us (13%)
  local copies, waits for them, and re-layouts  2.36 us (1%)
    ppermute x47, waiting for transfers between devices, swap(): return lax.ppermute(value, axis, [(i, i ^ offset) for i in range(count)])  118 us
    ppermute x47, starting transfers between devices, swap(): return lax.ppermute(value, axis, [(i, i ^ offset) for i in range(count)])  72.9 us
    pallas_call x1, Pallas kernels, statistics(): pl.pallas_call(functools.partial(statistics_kernel, groups, chunks), grid...  10.3 us
    pallas_call x1, Pallas kernels, gradient_strips(): pl.pallas_call(functools.partial(gradient_kernel, groups, ranks, sources,...  6.46 us
    pallas_call x2, Pallas kernels, directions(): pl.pallas_call(functools.partial(direction_kernel, groups, halves, togeth...  6.26 us
  transfers between devices with their start and end apart: 47, of which 23 were waited for; matrix products, arithmetic and copies ran while one was open for 0% of the time, Pallas kernels for 8%

profile of v9, /device:TPU:8, one launch (start us, length us, event | category | flops | bytes accessed | tf_op | source)
XLA Modules:
  0.0 223.3 jit_solution(12033739786858170481)
XLA Ops:
  3.0 3.0 %collective-permute-start.1 = (bf16[8,64,256]{2,1,0:T(8,128)(2,1)S(1)}, bf16[8,64,256]{2,1,0:T(8,128)(2,1)S(1)}, u32[]{:S(2)}, u32[]{:S(2)}) collective-permute-start(bf16[8,64,256]{2,1,0:T(8,128)(2,1)S(1)} %get-tuple-element.62), channel_id=1, source_target_pairs={{0,16},{4,20},{8,24},{12,28},{16,0},{20,4},{24,8},{28,12},{1,17},{... | collective-permute-start | bytes 786440 | tf_op jit(solution)/shard_map/ppermute | solution.py:78
  7.6 1.6 collective-permute-start.3
  9.2 4.4 %collective-permute-done = bf16[8,64,256]{2,1,0:T(8,128)(2,1)S(1)} collective-permute-done((bf16[8,64,256]{2,1,0:T(8,128)(2,1)S(1)}, bf16[8,64,256]{2,1,0:T(8,128)(2,1)S(1)}, u32[]{:S(2)}, u32[]{:S(2)}) %collective-permute-start) | collective-permute-done | bytes 262176 | tf_op jit(solution)/shard_map/ppermute | solution.py:78
  13.7 10.3 %collective-permute-done.1 = bf16[8,64,256]{2,1,0:T(8,128)(2,1)S(1)} collective-permute-done((bf16[8,64,256]{2,1,0:T(8,128)(2,1)S(1)}, bf16[8,64,256]{2,1,0:T(8,128)(2,1)S(1)}, u32[]{:S(2)}, u32[]{:S(2)}) %collective-permute-start.1) | collective-permute-done | bytes 262176 | tf_op jit(solution)/shard_map/ppermute | solution.py:78
  24.0 5.1 %collective-permute-done.2 = bf16[8,64,256]{2,1,0:T(8,128)(2,1)S(1)} collective-permute-done((bf16[8,64,256]{2,1,0:T(8,128)(2,1)S(1)}, bf16[8,64,256]{2,1,0:T(8,128)(2,1)S(1)}, u32[]{:S(2)}, u32[]{:S(2)}) %collective-permute-start.2) | collective-permute-done | bytes 262176 | tf_op jit(solution)/shard_map/ppermute | solution.py:78
  29.2 1.6 collective-permute-start.7
  30.8 1.5 collective-permute-start.10
  32.4 3.0 %collective-permute-start.4 = (bf16[2,256,512]{2,1,0:T(8,128)(2,1)S(1)}, bf16[2,256,512]{2,1,0:T(8,128)(2,1)S(1)}, u32[]{:S(2)}, u32[]{:S(2)}) collective-permute-start(bf16[2,256,512]{2,1,0:T(8,128)(2,1)S(1)} %pad_maximum_fusion.1.refs_1_), channel_id=1, source_target_pairs={{0,16},{4,20},{8,24},{12,28},{16,0},{20,4},{24,8},{28,12},{1,17},{... | collective-permute-start | bytes 1572872 | tf_op jit(solution)/shard_map/ppermute | solution.py:78
  35.5 17.6 %collective-permute-done.7.refs_5_ = bf16[4,512,256]{2,1,0:T(8,128)(2,1)S(1)} collective-permute-done((bf16[4,512,256]{2,1,0:T(8,128)(2,1)S(1)}, bf16[4,512,256]{2,1,0:T(8,128)(2,1)S(1)}, u32[]{:S(2)}, u32[]{:S(2)}) %collective-permute-start.7) | collective-permute-done | bytes 1048608 | tf_op jit(solution)/shard_map/ppermute | solution.py:78
  54.6 2.1 collective-permute-done.4.refs_0_
  56.7 1.6 collective-permute-start.6
  58.9 6.6 %collective-permute-done.11.refs_9_ = bf16[2,512,256]{2,1,0:T(8,128)(2,1)S(1)} collective-permute-done((bf16[2,512,256]{2,1,0:T(8,128)(2,1)S(1)}, bf16[2,512,256]{2,1,0:T(8,128)(2,1)S(1)}, u32[]{:S(2)}, u32[]{:S(2)}) %collective-permute-start.11) | collective-permute-done | bytes 524320 | tf_op jit(solution)/shard_map/ppermute | solution.py:78
  65.5 5.0 %collective-permute-done.12.refs_10_ = bf16[2,512,256]{2,1,0:T(8,128)(2,1)S(1)} collective-permute-done((bf16[2,512,256]{2,1,0:T(8,128)(2,1)S(1)}, bf16[2,512,256]{2,1,0:T(8,128)(2,1)S(1)}, u32[]{:S(2)}, u32[]{:S(2)}) %collective-permute-start.12) | collective-permute-done | bytes 524320 | tf_op jit(solution)/shard_map/ppermute | solution.py:78
  71.0 1.4 collective-permute-done.15.refs_13_
  73.2 6.5 %gradient_strips.1 = (bf16[8,64,128]{2,1,0:T(8,128)(2,1)S(1)}, bf16[8,64,128]{2,1,0:T(8,128)(2,1)S(1)}, bf16[8,64,128]{2,1,0:T(8,128)(2,1)S(1)}, bf16[8,64,128]{...) custom-call(s32[128]{0:T(128)S(1)} %bitcast.9, ...), custom_call_target="tpu_custom_call" | custom-call | flops 4294967296 | bytes 12582912 | tf_op jit(solution)/shard_map/gradient_strips/pallas_call | solution.py:193
  79.7 1.4 collective-permute-start.16
  81.1 1.5 collective-permute-start.17
  83.1 1.5 collective-permute-start.24
  84.7 2.3 %collective-permute-start.25 = (bf16[8,64,128]{2,1,0:T(8,128)(2,1)S(1)}, bf16[8,64,128]{2,1,0:T(8,128)(2,1)S(1)}, u32[]{:S(2)}, u32[]{:S(2)}) collective-permute-start(bf16[8,64,128]{2,1,0:T(8,128)(2,1)S(1)} %get-tuple-element.81), channel_id=1, source_target_pairs={{0,20},{4,16},{8,28},{12,24},{16,4},{20,0},{24,12},{28,8},{1,21},{... | collective-permute-start | bytes 393224 | tf_op jit(solution)/shard_map/ppermute | solution.py:78
  87.0 5.6 %collective-permute-done.16.refs_0_ = bf16[8,64,128]{2,1,0:T(8,128)(2,1)S(1)} collective-permute-done((bf16[8,64,128]{2,1,0:T(8,128)(2,1)S(1)}, bf16[8,64,128]{2,1,0:T(8,128)(2,1)S(1)}, u32[]{:S(2)}, u32[]{:S(2)}) %collective-permute-start.16) | collective-permute-done | bytes 131104 | tf_op jit(solution)/shard_map/ppermute | solution.py:78
  92.6 3.1 %collective-permute-start.26 = (bf16[8,64,128]{2,1,0:T(8,128)(2,1)S(1)}, bf16[8,64,128]{2,1,0:T(8,128)(2,1)S(1)}, u32[]{:S(2)}, u32[]{:S(2)}) collective-permute-start(bf16[8,64,128]{2,1,0:T(8,128)(2,1)S(1)} %get-tuple-element.82), channel_id=1, source_target_pairs={{0,8},{4,12},{8,0},{12,4},{16,24},{20,28},{24,16},{28,20},{1,9},{5... | collective-permute-start | bytes 393224 | tf_op jit(solution)/shard_map/ppermute | solution.py:78
  96.6 2.4 %collective-permute-start.28 = (bf16[8,64,128]{2,1,0:T(8,128)(2,1)S(1)}, bf16[8,64,128]{2,1,0:T(8,128)(2,1)S(1)}, u32[]{:S(2)}, u32[]{:S(2)}) collective-permute-start(bf16[8,64,128]{2,1,0:T(8,128)(2,1)S(1)} %get-tuple-element.84), channel_id=1, source_target_pairs={{0,12},{4,8},{8,4},{12,0},{16,28},{20,24},{24,20},{28,16},{1,13},{... | collective-permute-start | bytes 393224 | tf_op jit(solution)/shard_map/ppermute | solution.py:78
  100.6 4.6 %collective-permute-start.18 = (bf16[8,64,128]{2,1,0:T(8,128)(2,1)S(1)}, bf16[8,64,128]{2,1,0:T(8,128)(2,1)S(1)}, u32[]{:S(2)}, u32[]{:S(2)}) collective-permute-start(bf16[8,64,128]{2,1,0:T(8,128)(2,1)S(1)} %get-tuple-element.73), channel_id=1, source_target_pairs={{0,20},{4,16},{8,28},{12,24},{16,4},{20,0},{24,12},{28,8},{1,21},{... | collective-permute-start | bytes 393224 | tf_op jit(solution)/shard_map/ppermute | solution.py:78
  106.5 4.4 %collective-permute-done.27.refs_12_.refs_4_ = bf16[8,64,128]{2,1,0:T(8,128)(2,1)S(1)} collective-permute-done((bf16[8,64,128]{2,1,0:T(8,128)(2,1)S(1)}, bf16[8,64,128]{2,1,0:T(8,128)(2,1)S(1)}, u32[]{:S(2)}, u32[]{:S(2)}) %collective-permute-start.27) | collective-permute-done | bytes 131104 | tf_op jit(solution)/shard_map/ppermute | solution.py:78
  112.8 1.9 collective-permute-done.29.refs_14_.refs_6_
  114.7 3.5 %collective-permute-start.22 = (bf16[8,64,128]{2,1,0:T(8,128)(2,1)S(1)}, bf16[8,64,128]{2,1,0:T(8,128)(2,1)S(1)}, u32[]{:S(2)}, u32[]{:S(2)}) collective-permute-start(bf16[8,64,128]{2,1,0:T(8,128)(2,1)S(1)} %get-tuple-element.77), channel_id=1, source_target_pairs={{0,28},{4,24},{8,20},{12,16},{16,12},{20,8},{24,4},{28,0},{1,29},{... | collective-permute-start | bytes 393224 | tf_op jit(solution)/shard_map/ppermute | solution.py:78
  118.3 3.1 %directions.3 = (bf16[8,32,256]{2,1,0:T(8,128)(2,1)S(1)}, bf16[8,32,256]{2,1,0:T(8,128)(2,1)S(1)}, bf16[8,32,256]{2,1,0:T(8,128)(2,1)S(1)}, bf16[8,32,256]{2,1,0...) custom-call(s32[128]{0:T(128)S(1)} %bitcast.10, ...), custom_call_target="tpu_custom_call" | custom-call | flops 536870912 | bytes 8388608 | tf_op jit(solution)/shard_map/directions/pallas_call | solution.py:268
  121.4 3.4 %collective-permute-start.37 = (bf16[8,32,256]{2,1,0:T(8,128)(2,1)S(1)}, bf16[8,32,256]{2,1,0:T(8,128)(2,1)S(1)}, u32[]{:S(2)}, u32[]{:S(2)}) collective-permute-start(bf16[8,32,256]{2,1,0:T(8,128)(2,1)S(1)} %get-tuple-element.98), channel_id=1, source_target_pairs={{0,16},{4,20},{8,24},{12,28},{16,0},{20,4},{24,8},{28,12},{1,17},{... | collective-permute-start | bytes 393224 | tf_op jit(solution)/shard_map/ppermute | solution.py:78
  126.3 4.7 %collective-permute-start.40 = (bf16[8,32,256]{2,1,0:T(8,128)(2,1)S(1)}, bf16[8,32,256]{2,1,0:T(8,128)(2,1)S(1)}, u32[]{:S(2)}, u32[]{:S(2)}) collective-permute-start(bf16[8,32,256]{2,1,0:T(8,128)(2,1)S(1)} %get-tuple-element.101), channel_id=1, source_target_pairs={{0,8},{4,12},{8,0},{12,4},{16,24},{20,28},{24,16},{28,20},{1,9},{5... | collective-permute-start | bytes 393224 | tf_op jit(solution)/shard_map/ppermute | solution.py:78
  131.0 3.0 %collective-permute-done.22.refs_6_ = bf16[8,64,128]{2,1,0:T(8,128)(2,1)S(1)} collective-permute-done((bf16[8,64,128]{2,1,0:T(8,128)(2,1)S(1)}, bf16[8,64,128]{2,1,0:T(8,128)(2,1)S(1)}, u32[]{:S(2)}, u32[]{:S(2)}) %collective-permute-start.22) | collective-permute-done | bytes 131104 | tf_op jit(solution)/shard_map/ppermute | solution.py:78
  134.0 3.1 %directions.2 = (bf16[8,32,256]{2,1,0:T(8,128)(2,1)S(1)}, bf16[8,32,256]{2,1,0:T(8,128)(2,1)S(1)}, bf16[8,32,256]{2,1,0:T(8,128)(2,1)S(1)}, bf16[8,32,256]{2,1,0...) custom-call(s32[128]{0:T(128)S(1)} %bitcast.11, ...), custom_call_target="tpu_custom_call" | custom-call | flops 536870912 | bytes 8388608 | tf_op jit(solution)/shard_map/directions/pallas_call | solution.py:268
  137.2 4.0 %collective-permute-start.42 = (bf16[8,32,256]{2,1,0:T(8,128)(2,1)S(1)}, bf16[8,32,256]{2,1,0:T(8,128)(2,1)S(1)}, u32[]{:S(2)}, u32[]{:S(2)}) collective-permute-start(bf16[8,32,256]{2,1,0:T(8,128)(2,1)S(1)} %get-tuple-element.103), channel_id=1, source_target_pairs={{0,12},{4,8},{8,4},{12,0},{16,28},{20,24},{24,20},{28,16},{1,13},{... | collective-permute-start | bytes 393224 | tf_op jit(solution)/shard_map/ppermute | solution.py:78
  141.2 3.4 %collective-permute-start.30 = (bf16[8,32,256]{2,1,0:T(8,128)(2,1)S(1)}, bf16[8,32,256]{2,1,0:T(8,128)(2,1)S(1)}, u32[]{:S(2)}, u32[]{:S(2)}) collective-permute-start(bf16[8,32,256]{2,1,0:T(8,128)(2,1)S(1)} %get-tuple-element.90), channel_id=1, source_target_pairs={{0,16},{4,20},{8,24},{12,28},{16,0},{20,4},{24,8},{28,12},{1,17},{... | collective-permute-start | bytes 393224 | tf_op jit(solution)/shard_map/ppermute | solution.py:78
  145.3 5.2 %collective-permute-done.41.refs_12_ = bf16[8,32,256]{2,1,0:T(8,128)(2,1)S(1)} collective-permute-done((bf16[8,32,256]{2,1,0:T(8,128)(2,1)S(1)}, bf16[8,32,256]{2,1,0:T(8,128)(2,1)S(1)}, u32[]{:S(2)}, u32[]{:S(2)}) %collective-permute-start.41) | collective-permute-done | bytes 131104 | tf_op jit(solution)/shard_map/ppermute | solution.py:78
  150.5 3.0 %collective-permute-start.33 = (bf16[8,32,256]{2,1,0:T(8,128)(2,1)S(1)}, bf16[8,32,256]{2,1,0:T(8,128)(2,1)S(1)}, u32[]{:S(2)}, u32[]{:S(2)}) collective-permute-start(bf16[8,32,256]{2,1,0:T(8,128)(2,1)S(1)} %get-tuple-element.93), channel_id=1, source_target_pairs={{0,8},{4,12},{8,0},{12,4},{16,24},{20,28},{24,16},{28,20},{1,9},{5... | collective-permute-start | bytes 393224 | tf_op jit(solution)/shard_map/ppermute | solution.py:78
  153.6 1.6 collective-permute-done.43.refs_14_
  155.8 1.5 collective-permute-done.30.refs_0_
  157.3 6.4 %collective-permute-start.35 = (bf16[8,32,256]{2,1,0:T(8,128)(2,1)S(1)}, bf16[8,32,256]{2,1,0:T(8,128)(2,1)S(1)}, u32[]{:S(2)}, u32[]{:S(2)}) collective-permute-start(bf16[8,32,256]{2,1,0:T(8,128)(2,1)S(1)} %get-tuple-element.95), channel_id=1, source_target_pairs={{0,12},{4,8},{8,4},{12,0},{16,28},{20,24},{24,20},{28,16},{1,13},{... | collective-permute-start | bytes 393224 | tf_op jit(solution)/shard_map/ppermute | solution.py:78
  163.7 6.5 %collective-permute-done.34.refs_4_ = bf16[8,32,256]{2,1,0:T(8,128)(2,1)S(1)} collective-permute-done((bf16[8,32,256]{2,1,0:T(8,128)(2,1)S(1)}, bf16[8,32,256]{2,1,0:T(8,128)(2,1)S(1)}, u32[]{:S(2)}, u32[]{:S(2)}) %collective-permute-start.34) | collective-permute-done | bytes 131104 | tf_op jit(solution)/shard_map/ppermute | solution.py:78
  170.2 3.0 %collective-permute-done.36.refs_6_ = bf16[8,32,256]{2,1,0:T(8,128)(2,1)S(1)} collective-permute-done((bf16[8,32,256]{2,1,0:T(8,128)(2,1)S(1)}, bf16[8,32,256]{2,1,0:T(8,128)(2,1)S(1)}, u32[]{:S(2)}, u32[]{:S(2)}) %collective-permute-start.36) | collective-permute-done | bytes 131104 | tf_op jit(solution)/shard_map/ppermute | solution.py:78
  173.2 1.5 regroup.1
  174.7 2.8 %collective-permute-start.46 = (bf16[32,8192]{1,0:T(8,128)(2,1)S(1)}, bf16[32,8192]{1,0:T(8,128)(2,1)S(1)}, u32[]{:S(2)}, u32[]{:S(2)}) collective-permute-start(bf16[32,8192]{1,0:T(8,128)(2,1)S(1)} %get-tuple-element.108), channel_id=1, source_target_pairs={{0,8},{4,12},{8,0},{12,4},{16,24},{20,28},{24,16},{28,20},{1,9},{5... | collective-permute-start | bytes 1572872 | tf_op jit(solution)/shard_map/ppermute | solution.py:78
  178.2 10.3 %statistics.1 = (f32[1,16,256,256]{3,2,1,0:T(8,128)}, f32[1,16,256,256]{3,2,1,0:T(8,128)}, f32[1,16,256,256]{3,2,1,0:T(8,128)}) custom-call(s32[128]{0:T(128)S(1)} %bitcast.13, f32[1,16,256,256]{3,2,1,0:T(8,128)S(1)} %copy-done.3, f32[1,16,256,256]{3,2,1,0:T(8,128)S(1)} %copy-done.4, f32[1,16,256,256]{3,2,1,0:T(8,128)S(1)} %copy-done, ...), custom_call_target="tpu_custom_call" | custom-call | flops 1073741824 | bytes 27262976 | tf_op jit(solution)/shard_map/statistics/pallas_call | solution.py:326
  188.6 9.7 %collective-permute-done.45.refs_0_ = bf16[32,8192]{1,0:T(8,128)(2,1)S(1)} collective-permute-done((bf16[32,8192]{1,0:T(8,128)(2,1)S(1)}, bf16[32,8192]{1,0:T(8,128)(2,1)S(1)}, u32[]{:S(2)}, u32[]{:S(2)}) %collective-permute-start.45) | collective-permute-done | bytes 524320 | tf_op jit(solution)/shard_map/ppermute | solution.py:78
  198.3 3.3 %collective-permute-done.46.refs_1_ = bf16[32,8192]{1,0:T(8,128)(2,1)S(1)} collective-permute-done((bf16[32,8192]{1,0:T(8,128)(2,1)S(1)}, bf16[32,8192]{1,0:T(8,128)(2,1)S(1)}, u32[]{:S(2)}, u32[]{:S(2)}) %collective-permute-start.46) | collective-permute-done | bytes 524320 | tf_op jit(solution)/shard_map/ppermute | solution.py:78
  201.6 1.7 stack_rows.2.refs_1_
  203.3 18.6 %collective-permute-done.44.refs_0_ = bf16[32,8192]{1,0:T(8,128)(2,1)S(1)} collective-permute-done((bf16[32,8192]{1,0:T(8,128)(2,1)S(1)}, bf16[32,8192]{1,0:T(8,128)(2,1)S(1)}, u32[]{:S(2)}, u32[]{:S(2)}) %collective-permute-start.44) | collective-permute-done | bytes 524320 | tf_op jit(solution)/shard_map/ppermute | solution.py:78
  222.0 1.4 stack_rows.3
  (75 shorter events, 17.5 us)
Async XLA Ops:
  1.9 71.3 %copy-start.7 = (s32[1,128]{1,0:T(1,128)S(1)}, s32[1,128]{1,0:T(1,128)}, u32[]{:S(2)}) copy-start(s32[1,128]{1,0:T(1,128)} %param.10) | copy-start | bytes 1540
  2.9 10.8 %collective-permute-start = (bf16[8,64,256]{2,1,0:T(8,128)(2,1)S(1)}, bf16[8,64,256]{2,1,0:T(8,128)(2,1)S(1)}, u32[]{:S(2)}, u32[]{:S(2)}) collective-permute-start(bf16[8,64,256]{2,1,0:T(8,128)(2,1)S(1)} %get-tuple-element.61), channel_id=1, source_target_pairs={{0,8},{4,12},{8,0},{12,4},{16,24},{20,28},{24,16},{28,20},{1,9},{5... | collective-permute-start | bytes 786440 | tf_op jit(solution)/shard_map/ppermute | solution.py:78
  3.0 21.0 %collective-permute-start.1 = (bf16[8,64,256]{2,1,0:T(8,128)(2,1)S(1)}, bf16[8,64,256]{2,1,0:T(8,128)(2,1)S(1)}, u32[]{:S(2)}, u32[]{:S(2)}) collective-permute-start(bf16[8,64,256]{2,1,0:T(8,128)(2,1)S(1)} %get-tuple-element.62), channel_id=1, source_target_pairs={{0,16},{4,20},{8,24},{12,28},{16,0},{20,4},{24,8},{28,12},{1,17},{... | collective-permute-start | bytes 786440 | tf_op jit(solution)/shard_map/ppermute | solution.py:78
  6.0 23.1 %collective-permute-start.2 = (bf16[8,64,256]{2,1,0:T(8,128)(2,1)S(1)}, bf16[8,64,256]{2,1,0:T(8,128)(2,1)S(1)}, u32[]{:S(2)}, u32[]{:S(2)}) collective-permute-start(bf16[8,64,256]{2,1,0:T(8,128)(2,1)S(1)} %get-tuple-element.57), channel_id=1, source_target_pairs={{0,24},{4,28},{8,16},{12,20},{16,8},{20,12},{24,0},{28,4},{1,25},{... | collective-permute-start | bytes 786440 | tf_op jit(solution)/shard_map/ppermute | solution.py:78
  7.6 21.5 %collective-permute-start.3 = (bf16[256,512]{1,0:T(8,128)(2,1)S(1)}, bf16[256,512]{1,0:T(8,128)(2,1)S(1)}, u32[]{:S(2)}, u32[]{:S(2)}) collective-permute-start(bf16[256,512]{1,0:T(8,128)(2,1)S(1)} %get-tuple-element.63), channel_id=1, source_target_pairs={{0,4},{4,0},{8,12},{12,8},{16,20},{20,16},{24,28},{28,24},{1,5},{5... | collective-permute-start | bytes 786440 | tf_op jit(solution)/shard_map/ppermute | solution.py:78
  29.2 23.8 %collective-permute-start.7 = (bf16[4,512,256]{2,1,0:T(8,128)(2,1)S(1)}, bf16[4,512,256]{2,1,0:T(8,128)(2,1)S(1)}, u32[]{:S(2)}, u32[]{:S(2)}) collective-permute-start(bf16[4,512,256]{2,1,0:T(8,128)(2,1)S(1)} %pad_maximum_fusion.refs_4_), channel_id=1, source_target_pairs={{0,4},{4,0},{8,12},{12,8},{16,20},{20,16},{24,28},{28,24},{1,5},{5... | collective-permute-start | bytes 3145736 | tf_op jit(solution)/shard_map/ppermute | solution.py:78
  30.8 27.5 %collective-permute-start.10 = (bf16[4,512,256]{2,1,0:T(8,128)(2,1)S(1)}, bf16[4,512,256]{2,1,0:T(8,128)(2,1)S(1)}, u32[]{:S(2)}, u32[]{:S(2)}) collective-permute-start(bf16[4,512,256]{2,1,0:T(8,128)(2,1)S(1)} %pad_maximum_fusion.refs_4_), channel_id=1, source_target_pairs={{0,2},{1,3},{2,0},{3,1},{4,6},{5,7},{6,4},{7,5},{8,10},{9,11},{10,... | collective-permute-start | bytes 3145736 | tf_op jit(solution)/shard_map/ppermute | solution.py:78
  32.3 21.0 %collective-permute-start.5 = (bf16[2,256,512]{2,1,0:T(8,128)(2,1)S(1)}, bf16[2,256,512]{2,1,0:T(8,128)(2,1)S(1)}, u32[]{:S(2)}, u32[]{:S(2)}) collective-permute-start(bf16[2,256,512]{2,1,0:T(8,128)(2,1)S(1)} %pad_maximum_fusion.1.refs_1_), channel_id=1, source_target_pairs={{0,8},{4,12},{8,0},{12,4},{16,24},{20,28},{24,16},{28,20},{1,9},{5... | collective-permute-start | bytes 1572872 | tf_op jit(solution)/shard_map/ppermute | solution.py:78
  32.4 24.3 %collective-permute-start.4 = (bf16[2,256,512]{2,1,0:T(8,128)(2,1)S(1)}, bf16[2,256,512]{2,1,0:T(8,128)(2,1)S(1)}, u32[]{:S(2)}, u32[]{:S(2)}) collective-permute-start(bf16[2,256,512]{2,1,0:T(8,128)(2,1)S(1)} %pad_maximum_fusion.1.refs_1_), channel_id=1, source_target_pairs={{0,16},{4,20},{8,24},{12,28},{16,0},{20,4},{24,8},{28,12},{1,17},{... | collective-permute-start | bytes 1572872 | tf_op jit(solution)/shard_map/ppermute | solution.py:78
  53.3 12.2 %collective-permute-start.11 = (bf16[2,512,256]{2,1,0:T(8,128)(2,1)S(1)}, bf16[2,512,256]{2,1,0:T(8,128)(2,1)S(1)}, u32[]{:S(2)}, u32[]{:S(2)}) collective-permute-start(bf16[2,512,256]{2,1,0:T(8,128)(2,1)S(1)} %slice.8), channel_id=1, source_target_pairs={{0,2},{1,3},{2,0},{3,1},{4,6},{5,7},{6,4},{7,5},{8,10},{9,11},{10,... | collective-permute-start | bytes 1572872 | tf_op jit(solution)/shard_map/ppermute | solution.py:78
  54.6 16.4 %collective-permute-start.8 = (bf16[4,512,256]{2,1,0:T(8,128)(2,1)S(1)}, bf16[4,512,256]{2,1,0:T(8,128)(2,1)S(1)}, u32[]{:S(2)}, u32[]{:S(2)}) collective-permute-start(bf16[4,512,256]{2,1,0:T(8,128)(2,1)S(1)} %pad_maximum_fusion.refs_4_), channel_id=1, source_target_pairs={{0,1},{1,0},{2,3},{3,2},{4,5},{5,4},{6,7},{7,6},{8,9},{9,8},{10,11... | collective-permute-start | bytes 3145736 | tf_op jit(solution)/shard_map/ppermute | solution.py:78
  56.7 13.8 %collective-permute-start.6 = (bf16[2,256,512]{2,1,0:T(8,128)(2,1)S(1)}, bf16[2,256,512]{2,1,0:T(8,128)(2,1)S(1)}, u32[]{:S(2)}, u32[]{:S(2)}) collective-permute-start(bf16[2,256,512]{2,1,0:T(8,128)(2,1)S(1)} %collective-permute-done.4.refs_0_), channel_id=1, source_target_pairs={{0,8},{4,12},{8,0},{12,4},{16,24},{20,28},{24,16},{28,20},{1,9},{5... | collective-permute-start | bytes 1572872 | tf_op jit(solution)/shard_map/ppermute | solution.py:78
  58.3 12.2 %collective-permute-start.12 = (bf16[2,512,256]{2,1,0:T(8,128)(2,1)S(1)}, bf16[2,512,256]{2,1,0:T(8,128)(2,1)S(1)}, u32[]{:S(2)}, u32[]{:S(2)}) collective-permute-start(bf16[2,512,256]{2,1,0:T(8,128)(2,1)S(1)} %slice.9), channel_id=1, source_target_pairs={{0,4},{4,0},{8,12},{12,8},{16,20},{20,16},{24,28},{28,24},{1,5},{5... | collective-permute-start | bytes 1572872 | tf_op jit(solution)/shard_map/ppermute | solution.py:78
  58.9 12.1 %collective-permute-start.9 = (bf16[4,512,256]{2,1,0:T(8,128)(2,1)S(1)}, bf16[4,512,256]{2,1,0:T(8,128)(2,1)S(1)}, u32[]{:S(2)}, u32[]{:S(2)}) collective-permute-start(bf16[4,512,256]{2,1,0:T(8,128)(2,1)S(1)} %collective-permute-done.7.refs_5_), channel_id=1, source_target_pairs={{0,1},{1,0},{2,3},{3,2},{4,5},{5,4},{6,7},{7,6},{8,9},{9,8},{10,11... | collective-permute-start | bytes 3145736 | tf_op jit(solution)/shard_map/ppermute | solution.py:78
  65.5 7.7 %collective-permute-start.13 = (bf16[4,512,256]{2,1,0:T(8,128)(2,1)S(1)}, bf16[4,512,256]{2,1,0:T(8,128)(2,1)S(1)}, u32[]{:S(2)}, u32[]{:S(2)}) collective-permute-start(bf16[4,512,256]{2,1,0:T(8,128)(2,1)S(1)} %collective-permute-done.10.refs_8_), channel_id=1, source_target_pairs={{0,1},{1,0},{2,3},{3,2},{4,5},{5,4},{6,7},{7,6},{8,9},{9,8},{10,11... | collective-permute-start | bytes 3145736 | tf_op jit(solution)/shard_map/ppermute | solution.py:78
  70.5 1.9 collective-permute-start.15
  70.5 2.7 %collective-permute-start.14 = (bf16[2,512,256]{2,1,0:T(8,128)(2,1)S(1)}, bf16[2,512,256]{2,1,0:T(8,128)(2,1)S(1)}, u32[]{:S(2)}, u32[]{:S(2)}) collective-permute-start(bf16[2,512,256]{2,1,0:T(8,128)(2,1)S(1)} %collective-permute-done.11.refs_9_), channel_id=1, source_target_pairs={{0,1},{1,0},{2,3},{3,2},{4,5},{5,4},{6,7},{7,6},{8,9},{9,8},{10,11... | collective-permute-start | bytes 1572872 | tf_op jit(solution)/shard_map/ppermute | solution.py:78
  79.7 12.9 %collective-permute-start.16 = (bf16[8,64,128]{2,1,0:T(8,128)(2,1)S(1)}, bf16[8,64,128]{2,1,0:T(8,128)(2,1)S(1)}, u32[]{:S(2)}, u32[]{:S(2)}) collective-permute-start(bf16[8,64,128]{2,1,0:T(8,128)(2,1)S(1)} %get-tuple-element.71), channel_id=1, source_target_pairs={{0,16},{4,20},{8,24},{12,28},{16,0},{20,4},{24,8},{28,12},{1,17},{... | collective-permute-start | bytes 393224 | tf_op jit(solution)/shard_map/ppermute | solution.py:78
  81.1 14.6 %collective-permute-start.17 = (bf16[8,64,128]{2,1,0:T(8,128)(2,1)S(1)}, bf16[8,64,128]{2,1,0:T(8,128)(2,1)S(1)}, u32[]{:S(2)}, u32[]{:S(2)}) collective-permute-start(bf16[8,64,128]{2,1,0:T(8,128)(2,1)S(1)} %get-tuple-element.72), channel_id=1, source_target_pairs={{0,4},{4,0},{8,12},{12,8},{16,20},{20,16},{24,28},{28,24},{1,5},{5... | collective-permute-start | bytes 393224 | tf_op jit(solution)/shard_map/ppermute | solution.py:78
  82.6 13.9 %collective-permute-start.23 = (bf16[8,64,128]{2,1,0:T(8,128)(2,1)S(1)}, bf16[8,64,128]{2,1,0:T(8,128)(2,1)S(1)}, u32[]{:S(2)}, u32[]{:S(2)}) collective-permute-start(bf16[8,64,128]{2,1,0:T(8,128)(2,1)S(1)} %get-tuple-element.79), channel_id=1, source_target_pairs={{0,16},{4,20},{8,24},{12,28},{16,0},{20,4},{24,8},{28,12},{1,17},{... | collective-permute-start | bytes 393224 | tf_op jit(solution)/shard_map/ppermute | solution.py:78
  83.1 15.8 %collective-permute-start.24 = (bf16[8,64,128]{2,1,0:T(8,128)(2,1)S(1)}, bf16[8,64,128]{2,1,0:T(8,128)(2,1)S(1)}, u32[]{:S(2)}, u32[]{:S(2)}) collective-permute-start(bf16[8,64,128]{2,1,0:T(8,128)(2,1)S(1)} %get-tuple-element.80), channel_id=1, source_target_pairs={{0,4},{4,0},{8,12},{12,8},{16,20},{20,16},{24,28},{28,24},{1,5},{5... | collective-permute-start | bytes 393224 | tf_op jit(solution)/shard_map/ppermute | solution.py:78
  84.7 15.9 %collective-permute-start.25 = (bf16[8,64,128]{2,1,0:T(8,128)(2,1)S(1)}, bf16[8,64,128]{2,1,0:T(8,128)(2,1)S(1)}, u32[]{:S(2)}, u32[]{:S(2)}) collective-permute-start(bf16[8,64,128]{2,1,0:T(8,128)(2,1)S(1)} %get-tuple-element.81), channel_id=1, source_target_pairs={{0,20},{4,16},{8,28},{12,24},{16,4},{20,0},{24,12},{28,8},{1,21},{... | collective-permute-start | bytes 393224 | tf_op jit(solution)/shard_map/ppermute | solution.py:78
  92.6 12.6 %collective-permute-start.26 = (bf16[8,64,128]{2,1,0:T(8,128)(2,1)S(1)}, bf16[8,64,128]{2,1,0:T(8,128)(2,1)S(1)}, u32[]{:S(2)}, u32[]{:S(2)}) collective-permute-start(bf16[8,64,128]{2,1,0:T(8,128)(2,1)S(1)} %get-tuple-element.82), channel_id=1, source_target_pairs={{0,8},{4,12},{8,0},{12,4},{16,24},{20,28},{24,16},{28,20},{1,9},{5... | collective-permute-start | bytes 393224 | tf_op jit(solution)/shard_map/ppermute | solution.py:78
  95.7 15.2 %collective-permute-start.27 = (bf16[8,64,128]{2,1,0:T(8,128)(2,1)S(1)}, bf16[8,64,128]{2,1,0:T(8,128)(2,1)S(1)}, u32[]{:S(2)}, u32[]{:S(2)}) collective-permute-start(bf16[8,64,128]{2,1,0:T(8,128)(2,1)S(1)} %get-tuple-element.83), channel_id=1, source_target_pairs={{0,24},{4,28},{8,16},{12,20},{16,8},{20,12},{24,0},{28,4},{1,25},{... | collective-permute-start | bytes 393224 | tf_op jit(solution)/shard_map/ppermute | solution.py:78
  96.6 15.2 %collective-permute-start.28 = (bf16[8,64,128]{2,1,0:T(8,128)(2,1)S(1)}, bf16[8,64,128]{2,1,0:T(8,128)(2,1)S(1)}, u32[]{:S(2)}, u32[]{:S(2)}) collective-permute-start(bf16[8,64,128]{2,1,0:T(8,128)(2,1)S(1)} %get-tuple-element.84), channel_id=1, source_target_pairs={{0,12},{4,8},{8,4},{12,0},{16,28},{20,24},{24,20},{28,16},{1,13},{... | collective-permute-start | bytes 393224 | tf_op jit(solution)/shard_map/ppermute | solution.py:78
  98.9 15.8 %collective-permute-start.29 = (bf16[8,64,128]{2,1,0:T(8,128)(2,1)S(1)}, bf16[8,64,128]{2,1,0:T(8,128)(2,1)S(1)}, u32[]{:S(2)}, u32[]{:S(2)}) collective-permute-start(bf16[8,64,128]{2,1,0:T(8,128)(2,1)S(1)} %get-tuple-element.85), channel_id=1, source_target_pairs={{0,28},{4,24},{8,20},{12,16},{16,12},{20,8},{24,4},{28,0},{1,29},{... | collective-permute-start | bytes 393224 | tf_op jit(solution)/shard_map/ppermute | solution.py:78
  100.6 20.8 %collective-permute-start.18 = (bf16[8,64,128]{2,1,0:T(8,128)(2,1)S(1)}, bf16[8,64,128]{2,1,0:T(8,128)(2,1)S(1)}, u32[]{:S(2)}, u32[]{:S(2)}) collective-permute-start(bf16[8,64,128]{2,1,0:T(8,128)(2,1)S(1)} %get-tuple-element.73), channel_id=1, source_target_pairs={{0,20},{4,16},{8,28},{12,24},{16,4},{20,0},{24,12},{28,8},{1,21},{... | collective-permute-start | bytes 393224 | tf_op jit(solution)/shard_map/ppermute | solution.py:78
  105.2 19.6 %collective-permute-start.19 = (bf16[8,64,128]{2,1,0:T(8,128)(2,1)S(1)}, bf16[8,64,128]{2,1,0:T(8,128)(2,1)S(1)}, u32[]{:S(2)}, u32[]{:S(2)}) collective-permute-start(bf16[8,64,128]{2,1,0:T(8,128)(2,1)S(1)} %get-tuple-element.74), channel_id=1, source_target_pairs={{0,8},{4,12},{8,0},{12,4},{16,24},{20,28},{24,16},{28,20},{1,9},{5... | collective-permute-start | bytes 393224 | tf_op jit(solution)/shard_map/ppermute | solution.py:78
  110.9 14.7 %collective-permute-start.20 = (bf16[8,64,128]{2,1,0:T(8,128)(2,1)S(1)}, bf16[8,64,128]{2,1,0:T(8,128)(2,1)S(1)}, u32[]{:S(2)}, u32[]{:S(2)}) collective-permute-start(bf16[8,64,128]{2,1,0:T(8,128)(2,1)S(1)} %get-tuple-element.75), channel_id=1, source_target_pairs={{0,24},{4,28},{8,16},{12,20},{16,8},{20,12},{24,0},{28,4},{1,25},{... | collective-permute-start | bytes 393224 | tf_op jit(solution)/shard_map/ppermute | solution.py:78
  111.8 14.5 %collective-permute-start.21 = (bf16[8,64,128]{2,1,0:T(8,128)(2,1)S(1)}, bf16[8,64,128]{2,1,0:T(8,128)(2,1)S(1)}, u32[]{:S(2)}, u32[]{:S(2)}) collective-permute-start(bf16[8,64,128]{2,1,0:T(8,128)(2,1)S(1)} %get-tuple-element.76), channel_id=1, source_target_pairs={{0,12},{4,8},{8,4},{12,0},{16,28},{20,24},{24,20},{28,16},{1,13},{... | collective-permute-start | bytes 393224 | tf_op jit(solution)/shard_map/ppermute | solution.py:78
  114.7 19.3 %collective-permute-start.22 = (bf16[8,64,128]{2,1,0:T(8,128)(2,1)S(1)}, bf16[8,64,128]{2,1,0:T(8,128)(2,1)S(1)}, u32[]{:S(2)}, u32[]{:S(2)}) collective-permute-start(bf16[8,64,128]{2,1,0:T(8,128)(2,1)S(1)} %get-tuple-element.77), channel_id=1, source_target_pairs={{0,28},{4,24},{8,20},{12,16},{16,12},{20,8},{24,4},{28,0},{1,29},{... | collective-permute-start | bytes 393224 | tf_op jit(solution)/shard_map/ppermute | solution.py:78
  121.4 15.8 %collective-permute-start.37 = (bf16[8,32,256]{2,1,0:T(8,128)(2,1)S(1)}, bf16[8,32,256]{2,1,0:T(8,128)(2,1)S(1)}, u32[]{:S(2)}, u32[]{:S(2)}) collective-permute-start(bf16[8,32,256]{2,1,0:T(8,128)(2,1)S(1)} %get-tuple-element.98), channel_id=1, source_target_pairs={{0,16},{4,20},{8,24},{12,28},{16,0},{20,4},{24,8},{28,12},{1,17},{... | collective-permute-start | bytes 393224 | tf_op jit(solution)/shard_map/ppermute | solution.py:78
  124.8 16.4 %collective-permute-start.38 = (bf16[8,32,256]{2,1,0:T(8,128)(2,1)S(1)}, bf16[8,32,256]{2,1,0:T(8,128)(2,1)S(1)}, u32[]{:S(2)}, u32[]{:S(2)}) collective-permute-start(bf16[8,32,256]{2,1,0:T(8,128)(2,1)S(1)} %get-tuple-element.99), channel_id=1, source_target_pairs={{0,4},{4,0},{8,12},{12,8},{16,20},{20,16},{24,28},{28,24},{1,5},{5... | collective-permute-start | bytes 393224 | tf_op jit(solution)/shard_map/ppermute | solution.py:78
  125.6 15.6 %collective-permute-start.39 = (bf16[8,32,256]{2,1,0:T(8,128)(2,1)S(1)}, bf16[8,32,256]{2,1,0:T(8,128)(2,1)S(1)}, u32[]{:S(2)}, u32[]{:S(2)}) collective-permute-start(bf16[8,32,256]{2,1,0:T(8,128)(2,1)S(1)} %get-tuple-element.100), channel_id=1, source_target_pairs={{0,20},{4,16},{8,28},{12,24},{16,4},{20,0},{24,12},{28,8},{1,21},{... | collective-permute-start | bytes 393224 | tf_op jit(solution)/shard_map/ppermute | solution.py:78
  126.3 18.3 %collective-permute-start.40 = (bf16[8,32,256]{2,1,0:T(8,128)(2,1)S(1)}, bf16[8,32,256]{2,1,0:T(8,128)(2,1)S(1)}, u32[]{:S(2)}, u32[]{:S(2)}) collective-permute-start(bf16[8,32,256]{2,1,0:T(8,128)(2,1)S(1)} %get-tuple-element.101), channel_id=1, source_target_pairs={{0,8},{4,12},{8,0},{12,4},{16,24},{20,28},{24,16},{28,20},{1,9},{5... | collective-permute-start | bytes 393224 | tf_op jit(solution)/shard_map/ppermute | solution.py:78
  134.0 16.5 %collective-permute-start.41 = (bf16[8,32,256]{2,1,0:T(8,128)(2,1)S(1)}, bf16[8,32,256]{2,1,0:T(8,128)(2,1)S(1)}, u32[]{:S(2)}, u32[]{:S(2)}) collective-permute-start(bf16[8,32,256]{2,1,0:T(8,128)(2,1)S(1)} %get-tuple-element.102), channel_id=1, source_target_pairs={{0,24},{4,28},{8,16},{12,20},{16,8},{20,12},{24,0},{28,4},{1,25},{... | collective-permute-start | bytes 393224 | tf_op jit(solution)/shard_map/ppermute | solution.py:78
  137.2 13.4 %collective-permute-start.42 = (bf16[8,32,256]{2,1,0:T(8,128)(2,1)S(1)}, bf16[8,32,256]{2,1,0:T(8,128)(2,1)S(1)}, u32[]{:S(2)}, u32[]{:S(2)}) collective-permute-start(bf16[8,32,256]{2,1,0:T(8,128)(2,1)S(1)} %get-tuple-element.103), channel_id=1, source_target_pairs={{0,12},{4,8},{8,4},{12,0},{16,28},{20,24},{24,20},{28,16},{1,13},{... | collective-permute-start | bytes 393224 | tf_op jit(solution)/shard_map/ppermute | solution.py:78
  141.2 13.9 %collective-permute-start.43 = (bf16[8,32,256]{2,1,0:T(8,128)(2,1)S(1)}, bf16[8,32,256]{2,1,0:T(8,128)(2,1)S(1)}, u32[]{:S(2)}, u32[]{:S(2)}) collective-permute-start(bf16[8,32,256]{2,1,0:T(8,128)(2,1)S(1)} %get-tuple-element.104), channel_id=1, source_target_pairs={{0,28},{4,24},{8,20},{12,16},{16,12},{20,8},{24,4},{28,0},{1,29},{... | collective-permute-start | bytes 393224 | tf_op jit(solution)/shard_map/ppermute | solution.py:78
  141.2 16.1 %collective-permute-start.30 = (bf16[8,32,256]{2,1,0:T(8,128)(2,1)S(1)}, bf16[8,32,256]{2,1,0:T(8,128)(2,1)S(1)}, u32[]{:S(2)}, u32[]{:S(2)}) collective-permute-start(bf16[8,32,256]{2,1,0:T(8,128)(2,1)S(1)} %get-tuple-element.90), channel_id=1, source_target_pairs={{0,16},{4,20},{8,24},{12,28},{16,0},{20,4},{24,8},{28,12},{1,17},{... | collective-permute-start | bytes 393224 | tf_op jit(solution)/shard_map/ppermute | solution.py:78
  144.6 19.1 %collective-permute-start.31 = (bf16[8,32,256]{2,1,0:T(8,128)(2,1)S(1)}, bf16[8,32,256]{2,1,0:T(8,128)(2,1)S(1)}, u32[]{:S(2)}, u32[]{:S(2)}) collective-permute-start(bf16[8,32,256]{2,1,0:T(8,128)(2,1)S(1)} %get-tuple-element.91), channel_id=1, source_target_pairs={{0,4},{4,0},{8,12},{12,8},{16,20},{20,16},{24,28},{28,24},{1,5},{5... | collective-permute-start | bytes 393224 | tf_op jit(solution)/shard_map/ppermute | solution.py:78
  150.5 13.2 %collective-permute-start.32 = (bf16[8,32,256]{2,1,0:T(8,128)(2,1)S(1)}, bf16[8,32,256]{2,1,0:T(8,128)(2,1)S(1)}, u32[]{:S(2)}, u32[]{:S(2)}) collective-permute-start(bf16[8,32,256]{2,1,0:T(8,128)(2,1)S(1)} %get-tuple-element.92), channel_id=1, source_target_pairs={{0,20},{4,16},{8,28},{12,24},{16,4},{20,0},{24,12},{28,8},{1,21},{... | collective-permute-start | bytes 393224 | tf_op jit(solution)/shard_map/ppermute | solution.py:78
  150.5 13.2 %collective-permute-start.33 = (bf16[8,32,256]{2,1,0:T(8,128)(2,1)S(1)}, bf16[8,32,256]{2,1,0:T(8,128)(2,1)S(1)}, u32[]{:S(2)}, u32[]{:S(2)}) collective-permute-start(bf16[8,32,256]{2,1,0:T(8,128)(2,1)S(1)} %get-tuple-element.93), channel_id=1, source_target_pairs={{0,8},{4,12},{8,0},{12,4},{16,24},{20,28},{24,16},{28,20},{1,9},{5... | collective-permute-start | bytes 393224 | tf_op jit(solution)/shard_map/ppermute | solution.py:78
  155.1 15.1 %collective-permute-start.34 = (bf16[8,32,256]{2,1,0:T(8,128)(2,1)S(1)}, bf16[8,32,256]{2,1,0:T(8,128)(2,1)S(1)}, u32[]{:S(2)}, u32[]{:S(2)}) collective-permute-start(bf16[8,32,256]{2,1,0:T(8,128)(2,1)S(1)} %get-tuple-element.94), channel_id=1, source_target_pairs={{0,24},{4,28},{8,16},{12,20},{16,8},{20,12},{24,0},{28,4},{1,25},{... | collective-permute-start | bytes 393224 | tf_op jit(solution)/shard_map/ppermute | solution.py:78
  157.3 12.9 %collective-permute-start.35 = (bf16[8,32,256]{2,1,0:T(8,128)(2,1)S(1)}, bf16[8,32,256]{2,1,0:T(8,128)(2,1)S(1)}, u32[]{:S(2)}, u32[]{:S(2)}) collective-permute-start(bf16[8,32,256]{2,1,0:T(8,128)(2,1)S(1)} %get-tuple-element.95), channel_id=1, source_target_pairs={{0,12},{4,8},{8,4},{12,0},{16,28},{20,24},{24,20},{28,16},{1,13},{... | collective-permute-start | bytes 393224 | tf_op jit(solution)/shard_map/ppermute | solution.py:78
  163.7 9.5 %collective-permute-start.36 = (bf16[8,32,256]{2,1,0:T(8,128)(2,1)S(1)}, bf16[8,32,256]{2,1,0:T(8,128)(2,1)S(1)}, u32[]{:S(2)}, u32[]{:S(2)}) collective-permute-start(bf16[8,32,256]{2,1,0:T(8,128)(2,1)S(1)} %get-tuple-element.96), channel_id=1, source_target_pairs={{0,28},{4,24},{8,20},{12,16},{16,12},{20,8},{24,4},{28,0},{1,29},{... | collective-permute-start | bytes 393224 | tf_op jit(solution)/shard_map/ppermute | solution.py:78
  174.7 23.6 %collective-permute-start.45 = (bf16[32,8192]{1,0:T(8,128)(2,1)S(1)}, bf16[32,8192]{1,0:T(8,128)(2,1)S(1)}, u32[]{:S(2)}, u32[]{:S(2)}) collective-permute-start(bf16[32,8192]{1,0:T(8,128)(2,1)S(1)} %get-tuple-element.107), channel_id=1, source_target_pairs={{0,16},{4,20},{8,24},{12,28},{16,0},{20,4},{24,8},{28,12},{1,17},{... | collective-permute-start | bytes 1572872 | tf_op jit(solution)/shard_map/ppermute | solution.py:78
  174.7 26.9 %collective-permute-start.46 = (bf16[32,8192]{1,0:T(8,128)(2,1)S(1)}, bf16[32,8192]{1,0:T(8,128)(2,1)S(1)}, u32[]{:S(2)}, u32[]{:S(2)}) collective-permute-start(bf16[32,8192]{1,0:T(8,128)(2,1)S(1)} %get-tuple-element.108), channel_id=1, source_target_pairs={{0,8},{4,12},{8,0},{12,4},{16,24},{20,28},{24,16},{28,20},{1,9},{5... | collective-permute-start | bytes 1572872 | tf_op jit(solution)/shard_map/ppermute | solution.py:78
  177.6 44.4 %collective-permute-start.44 = (bf16[32,8192]{1,0:T(8,128)(2,1)S(1)}, bf16[32,8192]{1,0:T(8,128)(2,1)S(1)}, u32[]{:S(2)}, u32[]{:S(2)}) collective-permute-start(bf16[32,8192]{1,0:T(8,128)(2,1)S(1)} %get-tuple-element.106), channel_id=1, source_target_pairs={{0,24},{4,28},{8,16},{12,20},{16,8},{20,12},{24,0},{28,4},{1,25},{... | collective-permute-start | bytes 1572872 | tf_op jit(solution)/shard_map/ppermute | solution.py:78
  (7 other events, 225.9 us)
